TPU v7x, 32 devices: a whole 2x2x4 slice. The times are simulated.
32 devices in a mesh: row: 4 (over y, core), col: 2 (over x), layer: 4 (over z).
Axes of the slice: x: 2, y: 2, z: 4, core: 2. Of those that a mesh axis runs over, the one named last changes fastest.
Arguments:
- a_blocks: bfloat16 [768, 128, 128], P(('row', 'col', 'layer')), may hold values from -0.5 to 0.5
- a_rows: int32 [768], P(('row', 'col', 'layer')), may hold values from 0 to 31, as said below
- a_cols: int32 [768], P(('row', 'col', 'layer')), may hold values from 0 to 31, as said below
- s_blocks: bfloat16 [32, 4, 128, 128], P(('row', 'layer'), 'col'), may hold values from -6 to 6
- s_cols: int32 [32, 4], P(('row', 'layer'), 'col'), may hold values from 0 to 31, as said below
- c_cols: int32 [32, 4], P('row', 'col'), may hold values from 0 to 31, as said below
Outputs:
- c_blocks: bfloat16 [32, 4, 128, 128], P(('row', 'layer'), 'col')
Inputs may be any that keep to these rules, and one draw needn't show every extreme that they name: The pairs (a_rows[n], a_cols[n]) are all distinct. The blocks held by device (r, c, l) have block rows in [r * 32 / 4, (r + 1) * 32 / 4) and block columns k with (k // (32 / (4 * 4))) % 4 == l. `a_cols`: see a_rows. `s_cols`: in each row, the entries t with t // 2 == c are distinct block columns in [c * 32 / 2, (c + 1) * 32 / 2). `c_cols`: in each row, the entries t with t // 2 == c are distinct block columns in [c * 32 / 2, (c + 1) * 32 / 2).
All inputs are finite; a program needn't handle non-finite values.
Results may differ from a plain program's by a relative error of at most 0.001.
Values may be sent and summed in bfloat16 or wider, within the bound.
No kernel may reach another device: no remote copies, remote signals or barrier semaphores. Data moves between devices by JAX's collectives and lax.ppermute only.
A program may use at most 192 MiB of HBM per device.

v0:
```python
import jax
import jax.numpy as jnp
from jax import lax
from jax.sharding import PartitionSpec as P


def per_device(a_blocks, a_rows, a_cols, s_blocks, s_cols, c_cols):
    right_panel, panel_cols = (
        lax.all_gather(s_blocks, "row", axis=0, tiled=True),
        lax.all_gather(s_cols, "row", axis=0, tiled=True),
    )
    piece_rows = s_blocks.shape[0]
    layers = lax.axis_size("layer")
    local_rows = c_cols.shape[0]
    kept_width = c_cols.shape[1]
    right_width = panel_cols.shape[1]
    block_order = a_blocks.shape[1]
    slot_total = local_rows * kept_width
    row_base = lax.axis_index("row") * local_rows
    zero_sum = jnp.zeros((slot_total, block_order, block_order), jnp.float32)
    all_blocks = lax.all_gather(a_blocks, "col", axis=0, tiled=True)
    all_rows = lax.all_gather(a_rows, "col", axis=0, tiled=True)
    all_cols = lax.all_gather(a_cols, "col", axis=0, tiled=True)
    how_many = all_blocks.shape[0]
    owner_group = all_cols // piece_rows
    pair_panel_index = owner_group // layers * piece_rows + all_cols % piece_rows
    right_cols = jnp.take(panel_cols, pair_panel_index, axis=0)
    local_row = all_rows - row_base
    kept_cols = jnp.take(c_cols, local_row, axis=0)
    matches = right_cols[:, :, None] == kept_cols[:, None, :]
    landed = jnp.any(matches, axis=2)
    slot_index = jnp.sum(
        jnp.where(matches, jnp.arange(kept_width, dtype=jnp.int32)[None, None, :], 0), axis=2
    )
    targets = jnp.where(landed, local_row[:, None] * kept_width + slot_index, slot_total).astype(
        jnp.int32
    )
    panel_index, landed, targets = (pair_panel_index, landed, targets)
    pair_total = how_many * right_width
    group_size = 32
    padded_total = (pair_total + group_size - 1) // group_size * group_size
    flat_landed = landed.reshape(-1)
    flat_targets = targets.reshape(-1)
    ordering = jnp.argsort(jnp.where(flat_landed, 0, 1).astype(jnp.int32), stable=True)
    ordering = jnp.concatenate([ordering, jnp.zeros((padded_total - pair_total,), jnp.int32)])
    landed_count = jnp.sum(flat_landed.astype(jnp.int32))
    group_count = (landed_count + group_size - 1) // group_size

    def one_group(group_index, totals):
        start = group_index * group_size
        picked = lax.dynamic_slice_in_dim(ordering, start, group_size, 0)
        block_index = picked // right_width
        slot_right = picked % right_width
        position = start + jnp.arange(group_size, dtype=jnp.int32)
        goal = jnp.where(
            position < landed_count, jnp.take(flat_targets, picked, axis=0), slot_total
        )
        left_blocks = jnp.take(all_blocks, block_index, axis=0)
        right_blocks = right_panel[jnp.take(panel_index, block_index, axis=0), slot_right]
        products = jnp.einsum(
            "mab,mbc->mac", left_blocks, right_blocks, preferred_element_type=jnp.float32
        )
        return totals.at[goal].add(products, mode="drop")

    running = lax.fori_loop(0, group_count, one_group, zero_sum)
    partial_value = running.reshape(local_rows, kept_width, block_order, block_order)
    return lax.psum_scatter(partial_value, "layer", scatter_dimension=0, tiled=True).astype(
        jnp.bfloat16
    )


def solution(mesh):
    placed = (
        P(("row", "col", "layer"), None, None),
        P(("row", "col", "layer")),
        P(("row", "col", "layer")),
        P(("row", "layer"), "col", None, None),
        P(("row", "layer"), "col"),
        P("row", "col"),
    )
    return jax.shard_map(
        per_device,
        mesh=mesh,
        in_specs=placed,
        out_specs=P(("row", "layer"), "col", None, None),
        check_vma=False,
    )
```

profile of v0, /device:TPU:0, one launch (start us, length us, event | category | flops | bytes accessed | tf_op | source)
XLA Modules:
  0.0 88.5 jit_solution(18364751577820142306)
XLA Ops:
  6.5 0.0 all-gather.3.cloned.1.call-start
  6.5 0.7 all-gather.3.cloned.1.call-update
  7.3 0.0 reduce-scatter.2.cloned.1.call-start
  7.3 1.3 %dynamic-slice = u32[1]{0:T(128)} dynamic-slice(u32[32]{0:T(128)} %constant.222, u32[]{:T(128)S(6)} %add.132), dynamic_slice_sizes={1} | dynamic-slice | bytes 12
  9.2 0.9 dynamic-update-slice.1
  10.1 0.8 dynamic-update-slice
  10.9 5.2 %all-reduce.2 = (s32[48]{0:T(128)S(1)}, s32[48]{0:T(128)S(1)}) all-reduce(s32[48]{0:T(128)S(1)} %dynamic-update-slice.1, s32[48]{0:T(128)S(1)} %dynamic-update-slice), channel_id=1, replica_groups=mesh['row'=4,'col'=2,'layer'=4] {'col'}, use_global_device_ids=true, to_apply=%add.1 | all-reduce | flops 96 | bytes 768
  16.1 5.3 %all-gather = s32[4,2,2]{2,1,0:T(2,128)S(1)} all-gather(s32[1,2,2]{2,1,0:T(2,128)} %bitcast.9), channel_id=1, replica_groups=mesh['row'=4,'col'=2,'layer'=4] {'row'}, dimensions={0}, use_global_device_ids=true | all-gather | bytes 80 | tf_op jit(solution)/shard_map/all_gather | solution.py:10
  21.5 0.8 copy.19
  22.2 0.6 gather_fusion.5
  22.8 0.1 broadcast_select_fusion
  22.9 0.1 copy.20
  23.0 0.6 gather_fusion.4
  23.6 0.1 broadcast_select_fusion.1
  23.7 0.1 copy.18
  23.8 0.7 add_select_fusion
  25.1 0.1 copy.22
  25.2 0.1 select_n.154
  25.3 0.1 copy.21
  25.4 0.1 select_n.151
  25.6 2.6 %sort.17 = (s32[96]{0:T(128)}, s32[96]{0:T(128)S(1)}) sort(s32[96]{0:T(128)S(1)} %select_n.151, s32[96]{0:T(128)S(1)} %iota.16), dimensions={0}, to_apply=%region_2.4 | sort | flops 672 | bytes 1536 | tf_op jit(solution)/shard_map/jit(argsort)/sort | solution.py:44
  28.1 9.6 %all_gather.19 = bf16[8,2,128,128]{3,2,1,0:T(8,128)(2,1)} all-gather(bf16[2,2,128,128]{3,2,1,0:T(8,128)(2,1)} %param.13), channel_id=1, replica_groups=mesh['row'=4,'col'=2,'layer'=4] {'row'}, dimensions={0}, use_global_device_ids=true | all-gather | bytes 655360 | tf_op jit(solution)/shard_map/all_gather | solution.py:9
  37.7 1.1 %all-gather.3.cloned.1.call-done = bf16[48,128,128]{2,1,0:T(8,128)(2,1)} async-done(((bf16[24,128,128]{2,1,0:T(8,128)(2,1)}), bf16[48,128,128]{2,1,0:T(8,128)(2,1)}) %all-gather.3.cloned.1.call-update) | async-done | bytes 1572880 | tf_op jit(solution)/shard_map/all_gather | solution.py:21
  38.8 0.1 broadcast_in_dim.88
  38.9 12.7 %while.12 = (s32[]{:T(128)}, f32[16,128,128]{2,1,0:T(8,128)S(1)}, s32[]{:T(128)}, s32[]{:T(128)}, s32[96]{0:T(128)S(1)}, /*index=5*/s32[96]{0:T(128)S(1)}, bf16[...) while((s32[]{:T(128)}, f32[16,128,128]{2,1,0:T(8,128)S(1)}, ...), condition=%wide.region_6.8_spmd, body=%wide.region_4.7_spmd.sunk | while | flops 135270240 | bytes 14691323 | solution.py:65
  39.0 0.1 compare_and_fusion.4
  39.1 0.7 gather_fusion
  39.8 0.1 fusion.20
  39.9 0.7 gather_fusion.1
  40.6 0.6 compare_select_fusion.21
  41.2 3.1 %gather_fusion.3 = bf16[32,128,128]{2,1,0:T(8,128)(2,1)} fusion(bf16[48,128,128]{2,1,0:T(8,128)(2,1)} %get-tuple-element.255, s32[1024]{0:T(1024)S(1)} %pad_clamp_fusion.6), kind=kCustom, calls=%fused_computation.2.clone.1 | custom fusion | bytes 2097280 | tf_op jit(solution)/shard_map/while/body/jit(_take)/gather | solution.py:58
  44.3 2.7 %gather_fusion.2 = bf16[32,128,128]{2,1,0:T(8,128)(2,1)} fusion(bf16[8,2,128,128]{3,2,1,0:T(8,128)(2,1)} %get-tuple-element.257, s32[32]{0:T(128)S(1)} %get-tuple-element.221), kind=kCustom, calls=%fused_computation.4.clone.1 | custom fusion | bytes 2097408 | tf_op jit(solution)/shard_map/while/body/gather | solution.py:59
  47.0 2.0 %fusion.21 = f32[32,128,128]{2,1,0:T(8,128)S(1)} fusion(bf16[32,128,128]{2,1,0:T(8,128)(2,1)} %gather_fusion.2, bf16[32,128,128]{2,1,0:T(8,128)(2,1)} %gather_fusion.3, pred[32]{0:T(512)(128)(4,1)S(1)} %get-tuple-element.222), kind=kOutput, calls=%fused_computation.7.clone.1 | convolution fusion | flops 134742016 | bytes 4194336 | tf_op jit(solution)/shard_map/while/body/mab,mbc->mac/dot_general | solution.py:60
  49.0 2.7 %scatter_fusion = f32[16,128,128]{2,1,0:T(8,128)S(1)} fusion(f32[16,128,128]{2,1,0:T(8,128)S(1)} %get-tuple-element.237, s32[32]{0:T(128)S(1)} %compare_select_fusion.21, f32[32,128,128]{2,1,0:T(8,128)S(1)} %fusion.21), kind=kCustom, calls=%fused_computation.6.clone.1 | custom fusion | flops 524288 | bytes 6291584 | tf_op jit(solution)/shard_map/while/body/scatter-add | solution.py:63
  51.7 0.0 copy-start
  51.7 1.0 %copy-done = f32[16,128,128]{2,1,0:T(8,128)} copy-done((f32[16,128,128]{2,1,0:T(8,128)}, f32[16,128,128]{2,1,0:T(8,128)S(1)}, u32[]{:S(2)}) %copy-start) | copy-done | bytes 1048600
  52.7 0.0 reduce-scatter.2.cloned.1.call-update
  52.7 27.3 %reduce-scatter.2.cloned.1.call-done = f32[2,2,128,128]{3,2,1,0:T(8,128)} async-done(((f32[8,2,128,128]{3,2,1,0:T(8,128)}), f32[2,2,128,128]{3,2,1,0:T(8,128)}) %reduce-scatter.2.cloned.1.call-update) | async-done | bytes 262160 | tf_op jit(solution)/shard_map/reduce_scatter | solution.py:67
  80.0 1.6 %convert_element_type.8 = bf16[2,2,128,128]{3,2,1,0:T(8,128)(2,1)} convert(f32[2,2,128,128]{3,2,1,0:T(8,128)} %reduce-scatter.2.cloned.1.call-done) | non-fusion elementwise | flops 65536 | bytes 393216 | tf_op jit(solution)/shard_map/convert_element_type | solution.py:67
  (13 shorter events, 0.1 us)
Async XLA Ops:
  6.5 32.3 %all-gather.3.cloned.1.call-start = ((), (), s32[]{:S(2)}) async-start(), calls=%async_computation.1 | async-start | bytes 2359296 | tf_op jit(solution)/shard_map/all_gather | solution.py:21
  7.3 72.7 %reduce-scatter.2.cloned.1.call-start = ((), (), s32[]{:S(2)}) async-start(), calls=%async_computation.2 | async-start | bytes 1310720 | tf_op jit(solution)/shard_map/reduce_scatter | solution.py:67
  51.7 1.0 %copy-start = (f32[16,128,128]{2,1,0:T(8,128)}, f32[16,128,128]{2,1,0:T(8,128)S(1)}, u32[]{:S(2)}) copy-start(f32[16,128,128]{2,1,0:T(8,128)S(1)} %get-tuple-element.127) | copy-start | bytes 3145732
Sparse Core Ops, SparseCore 0:
  8.9 29.8 all-gather.2
  52.8 27.1 reduce-scatter.1
where the time goes:
time: 88.8 us; the launch traced here: 88.5 us
  waiting for transfers between devices  29.1 us (33%)
  blocking collectives  20.2 us (23%)
  between operations  14.8 us (17%)
  local copies, waits for them, and re-layouts  13.7 us (15%)
  other arithmetic  8.58 us (10%)
  matrix products  2.03 us (2%)
    reduce_scatter x1, waiting for transfers between devices, per_device(): lax.psum_scatter(partial_value, 'layer', scatter_dimension=0, tiled=True)  27.3 us
    all_gather x1, blocking collectives, per_device(): lax.all_gather(s_blocks, 'row', axis=0, tiled=True)  9.62 us
    all_gather x1, blocking collectives, per_device(): lax.all_gather(s_cols, 'row', axis=0, tiled=True)  5.35 us
    unnamed x1, blocking collectives  5.19 us
    unnamed x8, local copies, waits for them, and re-layouts  4.71 us
    gather x1, local copies, waits for them, and re-layouts, one_group(): left_blocks = jnp.take(all_blocks, block_index, axis=0)  3.08 us
    gather x1, local copies, waits for them, and re-layouts, one_group(): right_panel[jnp.take(panel_index, block_index, axis=0), slot_right]  2.68 us
    scatter-add x1, other arithmetic, one_group(): return totals.at[goal].add(products, mode='drop')  2.66 us
  transfers between devices with their start and end apart: 2, of which 2 were waited for; matrix products, arithmetic and copies ran while one was open for 10% of the time, Pallas kernels for 0%

commit v1 on v0

v1 whole, which is shorter than its diff:
```python
import functools

import jax
import jax.numpy as jnp
from jax import lax
from jax.experimental import pallas as pl
from jax.experimental.pallas import tpu as pltpu
from jax.sharding import PartitionSpec as P


def shifted(value, axis, offset):
    size = lax.axis_size(axis)
    return lax.ppermute(value, axis, [((i + offset) % size, i) for i in range(size)])


def product_kernel(sizes, *refs):
    rows, cols, layers, count, piece_rows, width, local_rows, kept = sizes
    refs = list(refs)
    a_rows, refs = refs[:cols], refs[cols:]
    a_cols, refs = refs[:cols], refs[cols:]
    s_cols, refs = refs[:rows], refs[rows:]
    c_cols, refs = refs[0], refs[1:]
    x_in, refs = refs[:cols], refs[cols:]
    s_in, refs = refs[:rows], refs[rows:]
    outs, refs = refs[:layers], refs[layers:]
    x_held, s_held, totals, x_sem, s_sem, out_sem = refs

    loads = [pltpu.make_async_copy(s_in[d], s_held.at[d], s_sem.at[d]) for d in range(rows)]
    loads += [pltpu.make_async_copy(x_in[j], x_held.at[j], x_sem.at[j]) for j in range(cols)]
    for load in loads:
        load.start()
    totals[...] = jnp.zeros_like(totals)
    here = lax.div(a_rows[0][0], local_rows)
    layer = lax.rem(lax.div(a_cols[0][0], piece_rows), layers)
    own_rows = local_rows // layers
    for load in loads:
        load.wait()

    for j in range(cols):

        def one_block(n, carry):
            row = a_rows[j][n] - here * local_rows
            inner = a_cols[j][n]
            owner = lax.div(lax.div(inner, piece_rows), layers)
            piece = lax.rem(owner - here + rows, rows)
            inner = lax.rem(inner, piece_rows)
            goal = lax.rem(lax.div(row, own_rows) - layer + layers, layers)
            goal = (goal * own_rows + lax.rem(row, own_rows)) * kept
            for s in range(width):
                wanted = s_cols[0][inner, s]
                for d in range(1, rows):
                    wanted = jnp.where(piece == d, s_cols[d][inner, s], wanted)
                for t in range(kept):

                    @pl.when(c_cols[row, t] == wanted)
                    def _():
                        totals[goal + t] += jnp.dot(
                            x_held[j, n],
                            s_held[piece, inner, s],
                            preferred_element_type=jnp.float32,
                        )

            return carry

        lax.fori_loop(0, count, one_block, 0)

    slots = own_rows * kept
    stores = [
        pltpu.make_async_copy(totals.at[pl.ds(d * slots, slots)], outs[d], out_sem.at[d])
        for d in range(layers)
    ]
    for store in stores:
        store.start()
    for store in stores:
        store.wait()


def per_device(a_blocks, a_rows, a_cols, s_blocks, s_cols, c_cols):
    rows, cols, layers = (lax.axis_size(axis) for axis in ("row", "col", "layer"))
    count, order = a_blocks.shape[:2]
    piece_rows, width = s_cols.shape
    local_rows, kept = c_cols.shape
    own_rows = local_rows // layers
    slots = own_rows * kept

    x_pieces = [a_blocks] + [shifted(a_blocks, "col", j) for j in range(1, cols)]
    row_pieces = [a_rows] + [shifted(a_rows, "col", j) for j in range(1, cols)]
    col_pieces = [a_cols] + [shifted(a_cols, "col", j) for j in range(1, cols)]
    s_pieces = [s_blocks] + [shifted(s_blocks, "row", d) for d in range(1, rows)]
    s_col_pieces = [s_cols] + [shifted(s_cols, "row", d) for d in range(1, rows)]

    scalars = pl.BlockSpec(memory_space=pltpu.SMEM)
    anywhere = pl.BlockSpec(memory_space=pl.ANY)
    sizes = (rows, cols, layers, count, piece_rows, width, local_rows, kept)
    held_bytes = 2 * order * order * (cols * count + rows * piece_rows * width)
    total_bytes = 4 * order * order * local_rows * kept
    pairs = cols * count * width
    parts = pl.pallas_call(
        functools.partial(product_kernel, sizes),
        out_shape=[jax.ShapeDtypeStruct((slots, order, order), jnp.float32)] * layers,
        in_specs=[scalars] * (2 * cols + rows + 1) + [anywhere] * (cols + rows),
        out_specs=[anywhere] * layers,
        scratch_shapes=[
            pltpu.VMEM((cols, count, order, order), jnp.bfloat16),
            pltpu.VMEM((rows, piece_rows, width, order, order), jnp.bfloat16),
            pltpu.VMEM((layers * slots, order, order), jnp.float32),
            pltpu.SemaphoreType.DMA((cols,)),
            pltpu.SemaphoreType.DMA((rows,)),
            pltpu.SemaphoreType.DMA((layers,)),
        ],
        compiler_params=pltpu.CompilerParams(
            vmem_limit_bytes=held_bytes + total_bytes + 4 * 2**20
        ),
        cost_estimate=pl.CostEstimate(
            flops=2 * order**3 * pairs // 4,
            bytes_accessed=held_bytes + total_bytes,
            transcendentals=0,
        ),
        name="products",
    )(*row_pieces, *col_pieces, *s_col_pieces, c_cols, *x_pieces, *s_pieces)

    result = parts[0]
    for d in range(1, layers):
        result = result + shifted(parts[d], "layer", layers - d)
    return result.reshape(own_rows, kept, order, order).astype(jnp.bfloat16)


def solution(mesh):
    placed = (
        P(("row", "col", "layer"), None, None),
        P(("row", "col", "layer")),
        P(("row", "col", "layer")),
        P(("row", "layer"), "col", None, None),
        P(("row", "layer"), "col"),
        P("row", "col"),
    )
    return jax.shard_map(
        per_device,
        mesh=mesh,
        in_specs=placed,
        out_specs=P(("row", "layer"), "col", None, None),
        check_vma=False,
    )
```

time: 88.8 us -> 55.3 us (0.62)
  the two profiles are of different devices: /device:TPU:0 before, /device:TPU:13 now
where the time goes in v1:
time: 55.3 us; the launch traced here: 54.9 us
  waiting for transfers between devices  35.3 us (64%)
  starting transfers between devices  10.7 us (19%)
  Pallas kernels  5.28 us (10%)
  local copies, waits for them, and re-layouts  2.8 us (5%)
  other arithmetic  0.71 us (1%)
    ppermute x12, waiting for transfers between devices, shifted(): lax.ppermute(value, axis, [((i + offset) % size, i) for i in range(size)])  35.3 us
    ppermute x12, starting transfers between devices, shifted(): lax.ppermute(value, axis, [((i + offset) % size, i) for i in range(size)])  10.7 us
    pallas_call x1, Pallas kernels, per_device(): pl.pallas_call(functools.partial(product_kernel, sizes), out_shape=[jax.S...  5.28 us
    unnamed x11, local copies, waits for them, and re-layouts  2.8 us
  transfers between devices with their start and end apart: 12, of which 8 were waited for; matrix products, arithmetic and copies ran while one was open for 1% of the time, Pallas kernels for 0%

profile of v1, /device:TPU:13, one launch (start us, length us, event | category | flops | bytes accessed | tf_op | source)
XLA Modules:
  0.0 54.9 jit_solution(16244474890770945298)
XLA Ops:
  0.0 0.0 copy-start.2
  0.0 0.0 copy-start.3
  0.0 0.0 copy-start.4
  0.0 1.3 %collective-permute-start.5 = (bf16[24,128,128]{2,1,0:T(8,128)(2,1)}, bf16[24,128,128]{2,1,0:T(8,128)(2,1)S(1)}, u32[]{:S(2)}, u32[]{:S(2)}) collective-permute-start(bf16[24,128,128]{2,1,0:T(8,128)(2,1)} %refs_9_.1), channel_id=1, source_target_pairs={{4,0},{0,4},{5,1},{1,5},{6,2},{2,6},{7,3},{3,7},{12,8},{8,12},{13,... | collective-permute-start | bytes 2359304 | tf_op jit(solution)/shard_map/ppermute | solution.py:13
  1.3 0.2 collective-permute-start.7
  1.5 1.2 %collective-permute-start.6 = (bf16[2,2,128,128]{3,2,1,0:T(8,128)(2,1)}, bf16[2,2,128,128]{3,2,1,0:T(8,128)(2,1)S(1)}, u32[]{:S(2)}, u32[]{:S(2)}) collective-permute-start(bf16[2,2,128,128]{3,2,1,0:T(8,128)(2,1)} %refs_11_.1), channel_id=1, source_target_pairs={{8,0},{16,8},{24,16},{0,24},{9,1},{17,9},{25,17},{1,25},{10,2},{18... | collective-permute-start | bytes 393224 | tf_op jit(solution)/shard_map/ppermute | solution.py:13
  2.7 1.1 %collective-permute-start.8 = (bf16[2,2,128,128]{3,2,1,0:T(8,128)(2,1)}, bf16[2,2,128,128]{3,2,1,0:T(8,128)(2,1)S(1)}, u32[]{:S(2)}, u32[]{:S(2)}) collective-permute-start(bf16[2,2,128,128]{3,2,1,0:T(8,128)(2,1)} %refs_11_.1), channel_id=1, source_target_pairs={{24,0},{0,8},{8,16},{16,24},{25,1},{1,9},{9,17},{17,25},{26,2},{2,... | collective-permute-start | bytes 393224 | tf_op jit(solution)/shard_map/ppermute | solution.py:13
  3.9 0.6 %collective-permute-start.3 = (s32[2,2]{1,0:T(2,128)}, s32[2,2]{1,0:T(2,128)S(1)}, u32[]{:S(2)}, u32[]{:S(2)}) collective-permute-start(s32[2,2]{1,0:T(2,128)} %refs_4_.1), channel_id=1, source_target_pairs={{16,0},{24,8},{0,16},{8,24},{17,1},{25,9},{1,17},{9,25},{18,2},{26... | collective-permute-start | bytes 56 | tf_op jit(solution)/shard_map/ppermute | solution.py:13
  4.5 4.3 %collective-permute-done.3.refs_6_ = s32[2,2]{1,0:T(2,128)S(1)} collective-permute-done((s32[2,2]{1,0:T(2,128)}, s32[2,2]{1,0:T(2,128)S(1)}, u32[]{:S(2)}, u32[]{:S(2)}) %collective-permute-start.3) | collective-permute-done | bytes 48 | tf_op jit(solution)/shard_map/ppermute | solution.py:13
  8.8 1.5 %collective-permute-start.2 = (s32[2,2]{1,0:T(2,128)}, s32[2,2]{1,0:T(2,128)S(1)}, u32[]{:S(2)}, u32[]{:S(2)}) collective-permute-start(s32[2,2]{1,0:T(2,128)} %refs_4_.1), channel_id=1, source_target_pairs={{8,0},{16,8},{24,16},{0,24},{9,1},{17,9},{25,17},{1,25},{10,2},{18... | collective-permute-start | bytes 56 | tf_op jit(solution)/shard_map/ppermute | solution.py:13
  10.2 2.0 %collective-permute-done.2.refs_5_ = s32[2,2]{1,0:T(2,128)S(1)} collective-permute-done((s32[2,2]{1,0:T(2,128)}, s32[2,2]{1,0:T(2,128)S(1)}, u32[]{:S(2)}, u32[]{:S(2)}) %collective-permute-start.2) | collective-permute-done | bytes 48 | tf_op jit(solution)/shard_map/ppermute | solution.py:13
  12.3 0.0 collective-permute-start.4
  12.3 1.3 %collective-permute-done.4.refs_7_ = s32[2,2]{1,0:T(2,128)S(1)} collective-permute-done((s32[2,2]{1,0:T(2,128)}, s32[2,2]{1,0:T(2,128)S(1)}, u32[]{:S(2)}, u32[]{:S(2)}) %collective-permute-start.4) | collective-permute-done | bytes 48 | tf_op jit(solution)/shard_map/ppermute | solution.py:13
  13.6 0.3 collective-permute-start
  13.9 4.8 %collective-permute-done.refs_1_ = s32[24]{0:T(128)S(1)} collective-permute-done((s32[24]{0:T(128)}, s32[24]{0:T(128)S(1)}, u32[]{:S(2)}, u32[]{:S(2)}) %collective-permute-start) | collective-permute-done | bytes 128 | tf_op jit(solution)/shard_map/ppermute | solution.py:13
  18.7 1.2 %collective-permute-start.1 = (s32[24]{0:T(128)}, s32[24]{0:T(128)S(1)}, u32[]{:S(2)}, u32[]{:S(2)}) collective-permute-start(s32[24]{0:T(128)} %refs_2_.1), channel_id=1, source_target_pairs={{4,0},{0,4},{5,1},{1,5},{6,2},{2,6},{7,3},{3,7},{12,8},{8,12},{13,... | collective-permute-start | bytes 296 | tf_op jit(solution)/shard_map/ppermute | solution.py:13
  19.9 0.8 %copy.7.refs_8_ = s32[8,2]{1,0:T(8,128)S(1)} copy(s32[8,2]{0,1:T(2,128)} %param.11) | data formatting | bytes 128 | tf_op args[5]
  20.7 0.6 %collective-permute-done.1.refs_3_ = s32[24]{0:T(128)S(1)} collective-permute-done((s32[24]{0:T(128)}, s32[24]{0:T(128)S(1)}, u32[]{:S(2)}, u32[]{:S(2)}) %collective-permute-start.1) | collective-permute-done | bytes 128 | tf_op jit(solution)/shard_map/ppermute | solution.py:13
  21.2 0.0 collective-permute-done.7.refs_13_
  21.2 0.0 collective-permute-done.6.refs_12_
  21.2 0.0 collective-permute-done.8.refs_14_
  21.2 0.0 collective-permute-done.5.refs_10_
  21.2 0.0 copy-done.2
  21.3 0.0 copy-done.3
  21.3 0.0 copy-done.4
  21.3 0.0 copy-start
  21.3 1.1 %copy-done = bf16[24,128,128]{2,1,0:T(8,128)(2,1)S(1)} copy-done((bf16[24,128,128]{2,1,0:T(8,128)(2,1)S(1)}, bf16[24,128,128]{2,1,0:T(8,128)(2,1)}, u32[]{:S(2)}) %copy-start) | copy-done | bytes 786456
  22.4 0.0 copy-start.1
  22.4 0.9 %copy-done.1 = bf16[2,2,128,128]{3,2,1,0:T(8,128)(2,1)S(1)} copy-done((bf16[2,2,128,128]{3,2,1,0:T(8,128)(2,1)S(1)}, bf16[2,2,128,128]{3,2,1,0:T(8,128)(2,1)}, u32[]{:S(2)}) %copy-start.1) | copy-done | bytes 131096
  23.3 5.3 %products.1 = (f32[4,128,128]{2,1,0:T(8,128)S(1)}, f32[4,128,128]{2,1,0:T(8,128)S(1)}, f32[4,128,128]{2,1,0:T(8,128)S(1)}, f32[4,128,128]{2,1,0:T(8,128)S(1)}) custom-call(s32[24]{0:T(128)S(1)} %copy-done.3, s32[24]{0:T(128)S(1)} %collective-permute-done.refs_1_, s32[24]{0:T(128)S(1)} %copy-done.4, s32[24]{0:T(128)S(1)} %collective-permute-done.1.refs_3_, ...), custom_call_target="tpu_custom_call" | custom-call | flops 100663296 | bytes 3145728 | tf_op jit(solution)/shard_map/products/pallas_call | solution.py:98
  28.6 1.7 %collective-permute-start.9 = (f32[4,128,128]{2,1,0:T(8,128)S(1)}, f32[4,128,128]{2,1,0:T(8,128)S(1)}, u32[]{:S(2)}, u32[]{:S(2)}) collective-permute-start(f32[4,128,128]{2,1,0:T(8,128)S(1)} %get-tuple-element.10), channel_id=1, source_target_pairs={{3,0},{0,1},{1,2},{2,3},{7,4},{4,5},{5,6},{6,7},{11,8},{8,9},{9,10... | collective-permute-start | bytes 786440 | tf_op jit(solution)/shard_map/ppermute | solution.py:13
  30.4 0.2 collective-permute-start.10
  30.6 1.4 %collective-permute-start.11 = (f32[4,128,128]{2,1,0:T(8,128)S(1)}, f32[4,128,128]{2,1,0:T(8,128)S(1)}, u32[]{:S(2)}, u32[]{:S(2)}) collective-permute-start(f32[4,128,128]{2,1,0:T(8,128)S(1)} %get-tuple-element.12), channel_id=1, source_target_pairs={{1,0},{2,1},{3,2},{0,3},{5,4},{6,5},{7,6},{4,7},{9,8},{10,9},{11,1... | collective-permute-start | bytes 786440 | tf_op jit(solution)/shard_map/ppermute | solution.py:13
  31.9 3.0 %collective-permute-done.9 = f32[4,128,128]{2,1,0:T(8,128)S(1)} collective-permute-done((f32[4,128,128]{2,1,0:T(8,128)S(1)}, f32[4,128,128]{2,1,0:T(8,128)S(1)}, u32[]{:S(2)}, u32[]{:S(2)}) %collective-permute-start.9) | collective-permute-done | bytes 262176 | tf_op jit(solution)/shard_map/ppermute | solution.py:13
  34.9 16.0 %collective-permute-done.10 = f32[4,128,128]{2,1,0:T(8,128)S(1)} collective-permute-done((f32[4,128,128]{2,1,0:T(8,128)S(1)}, f32[4,128,128]{2,1,0:T(8,128)S(1)}, u32[]{:S(2)}, u32[]{:S(2)}) %collective-permute-start.10) | collective-permute-done | bytes 262176 | tf_op jit(solution)/shard_map/ppermute | solution.py:13
  50.9 3.4 %collective-permute-done.11 = f32[4,128,128]{2,1,0:T(8,128)S(1)} collective-permute-done((f32[4,128,128]{2,1,0:T(8,128)S(1)}, f32[4,128,128]{2,1,0:T(8,128)S(1)}, u32[]{:S(2)}, u32[]{:S(2)}) %collective-permute-start.11) | collective-permute-done | bytes 262176 | tf_op jit(solution)/shard_map/ppermute | solution.py:13
  54.2 0.7 %add_convert_fusion = bf16[4,128,128]{2,1,0:T(8,128)(2,1)} fusion(f32[4,128,128]{2,1,0:T(8,128)S(1)} %collective-permute-done.11, f32[4,128,128]{2,1,0:T(8,128)S(1)} %collective-permute-done.10, f32[4,128,128]{2,1,0:T(8,128)S(1)} %get-tuple-element.9, f32[4,128,128]{2,1,0:T(8,128)S(1)} %collective-permute-done.9), kind=kLoop, calls=%fused_computation | loop fusion | flops 262144 | bytes 1179648 | tf_op jit(solution)/shard_map/convert_element_type | solution.py:125
Async XLA Ops:
  0.0 21.2 %copy-start.2 = (s32[2,2]{1,0:T(2,128)S(1)}, s32[2,2]{1,0:T(2,128)}, u32[]{:S(2)}) copy-start(s32[2,2]{1,0:T(2,128)} %refs_4_.1) | copy-start | bytes 52
  0.0 21.3 %copy-start.3 = (s32[24]{0:T(128)S(1)}, s32[24]{0:T(128)}, u32[]{:S(2)}) copy-start(s32[24]{0:T(128)} %refs_0_.1) | copy-start | bytes 292
  0.0 21.3 %copy-start.4 = (s32[24]{0:T(128)S(1)}, s32[24]{0:T(128)}, u32[]{:S(2)}) copy-start(s32[24]{0:T(128)} %refs_2_.1) | copy-start | bytes 292
  0.0 21.2 %collective-permute-start.5 = (bf16[24,128,128]{2,1,0:T(8,128)(2,1)}, bf16[24,128,128]{2,1,0:T(8,128)(2,1)S(1)}, u32[]{:S(2)}, u32[]{:S(2)}) collective-permute-start(bf16[24,128,128]{2,1,0:T(8,128)(2,1)} %refs_9_.1), channel_id=1, source_target_pairs={{4,0},{0,4},{5,1},{1,5},{6,2},{2,6},{7,3},{3,7},{12,8},{8,12},{13,... | collective-permute-start | bytes 2359304 | tf_op jit(solution)/shard_map/ppermute | solution.py:13
  1.3 19.9 %collective-permute-start.7 = (bf16[2,2,128,128]{3,2,1,0:T(8,128)(2,1)}, bf16[2,2,128,128]{3,2,1,0:T(8,128)(2,1)S(1)}, u32[]{:S(2)}, u32[]{:S(2)}) collective-permute-start(bf16[2,2,128,128]{3,2,1,0:T(8,128)(2,1)} %refs_11_.1), channel_id=1, source_target_pairs={{16,0},{24,8},{0,16},{8,24},{17,1},{25,9},{1,17},{9,25},{18,2},{26... | collective-permute-start | bytes 393224 | tf_op jit(solution)/shard_map/ppermute | solution.py:13
  1.5 19.7 %collective-permute-start.6 = (bf16[2,2,128,128]{3,2,1,0:T(8,128)(2,1)}, bf16[2,2,128,128]{3,2,1,0:T(8,128)(2,1)S(1)}, u32[]{:S(2)}, u32[]{:S(2)}) collective-permute-start(bf16[2,2,128,128]{3,2,1,0:T(8,128)(2,1)} %refs_11_.1), channel_id=1, source_target_pairs={{8,0},{16,8},{24,16},{0,24},{9,1},{17,9},{25,17},{1,25},{10,2},{18... | collective-permute-start | bytes 393224 | tf_op jit(solution)/shard_map/ppermute | solution.py:13
  2.7 18.5 %collective-permute-start.8 = (bf16[2,2,128,128]{3,2,1,0:T(8,128)(2,1)}, bf16[2,2,128,128]{3,2,1,0:T(8,128)(2,1)S(1)}, u32[]{:S(2)}, u32[]{:S(2)}) collective-permute-start(bf16[2,2,128,128]{3,2,1,0:T(8,128)(2,1)} %refs_11_.1), channel_id=1, source_target_pairs={{24,0},{0,8},{8,16},{16,24},{25,1},{1,9},{9,17},{17,25},{26,2},{2,... | collective-permute-start | bytes 393224 | tf_op jit(solution)/shard_map/ppermute | solution.py:13
  3.9 4.9 %collective-permute-start.3 = (s32[2,2]{1,0:T(2,128)}, s32[2,2]{1,0:T(2,128)S(1)}, u32[]{:S(2)}, u32[]{:S(2)}) collective-permute-start(s32[2,2]{1,0:T(2,128)} %refs_4_.1), channel_id=1, source_target_pairs={{16,0},{24,8},{0,16},{8,24},{17,1},{25,9},{1,17},{9,25},{18,2},{26... | collective-permute-start | bytes 56 | tf_op jit(solution)/shard_map/ppermute | solution.py:13
  8.8 3.5 %collective-permute-start.2 = (s32[2,2]{1,0:T(2,128)}, s32[2,2]{1,0:T(2,128)S(1)}, u32[]{:S(2)}, u32[]{:S(2)}) collective-permute-start(s32[2,2]{1,0:T(2,128)} %refs_4_.1), channel_id=1, source_target_pairs={{8,0},{16,8},{24,16},{0,24},{9,1},{17,9},{25,17},{1,25},{10,2},{18... | collective-permute-start | bytes 56 | tf_op jit(solution)/shard_map/ppermute | solution.py:13
  12.3 1.4 %collective-permute-start.4 = (s32[2,2]{1,0:T(2,128)}, s32[2,2]{1,0:T(2,128)S(1)}, u32[]{:S(2)}, u32[]{:S(2)}) collective-permute-start(s32[2,2]{1,0:T(2,128)} %refs_4_.1), channel_id=1, source_target_pairs={{24,0},{0,8},{8,16},{16,24},{25,1},{1,9},{9,17},{17,25},{26,2},{2,... | collective-permute-start | bytes 56 | tf_op jit(solution)/shard_map/ppermute | solution.py:13
  13.6 5.1 %collective-permute-start = (s32[24]{0:T(128)}, s32[24]{0:T(128)S(1)}, u32[]{:S(2)}, u32[]{:S(2)}) collective-permute-start(s32[24]{0:T(128)} %refs_0_.1), channel_id=1, source_target_pairs={{4,0},{0,4},{5,1},{1,5},{6,2},{2,6},{7,3},{3,7},{12,8},{8,12},{13,... | collective-permute-start | bytes 296 | tf_op jit(solution)/shard_map/ppermute | solution.py:13
  18.7 2.5 %collective-permute-start.1 = (s32[24]{0:T(128)}, s32[24]{0:T(128)S(1)}, u32[]{:S(2)}, u32[]{:S(2)}) collective-permute-start(s32[24]{0:T(128)} %refs_2_.1), channel_id=1, source_target_pairs={{4,0},{0,4},{5,1},{1,5},{6,2},{2,6},{7,3},{3,7},{12,8},{8,12},{13,... | collective-permute-start | bytes 296 | tf_op jit(solution)/shard_map/ppermute | solution.py:13
  21.3 1.1 %copy-start = (bf16[24,128,128]{2,1,0:T(8,128)(2,1)S(1)}, bf16[24,128,128]{2,1,0:T(8,128)(2,1)}, u32[]{:S(2)}) copy-start(bf16[24,128,128]{2,1,0:T(8,128)(2,1)} %refs_9_.1) | copy-start | bytes 2359300
  22.4 0.9 %copy-start.1 = (bf16[2,2,128,128]{3,2,1,0:T(8,128)(2,1)S(1)}, bf16[2,2,128,128]{3,2,1,0:T(8,128)(2,1)}, u32[]{:S(2)}) copy-start(bf16[2,2,128,128]{3,2,1,0:T(8,128)(2,1)} %refs_11_.1) | copy-start | bytes 393220
  28.6 6.3 %collective-permute-start.9 = (f32[4,128,128]{2,1,0:T(8,128)S(1)}, f32[4,128,128]{2,1,0:T(8,128)S(1)}, u32[]{:S(2)}, u32[]{:S(2)}) collective-permute-start(f32[4,128,128]{2,1,0:T(8,128)S(1)} %get-tuple-element.10), channel_id=1, source_target_pairs={{3,0},{0,1},{1,2},{2,3},{7,4},{4,5},{5,6},{6,7},{11,8},{8,9},{9,10... | collective-permute-start | bytes 786440 | tf_op jit(solution)/shard_map/ppermute | solution.py:13
  30.4 20.5 %collective-permute-start.10 = (f32[4,128,128]{2,1,0:T(8,128)S(1)}, f32[4,128,128]{2,1,0:T(8,128)S(1)}, u32[]{:S(2)}, u32[]{:S(2)}) collective-permute-start(f32[4,128,128]{2,1,0:T(8,128)S(1)} %get-tuple-element.11), channel_id=1, source_target_pairs={{2,0},{3,1},{0,2},{1,3},{6,4},{7,5},{4,6},{5,7},{10,8},{11,9},{8,1... | collective-permute-start | bytes 786440 | tf_op jit(solution)/shard_map/ppermute | solution.py:13
  30.6 23.7 %collective-permute-start.11 = (f32[4,128,128]{2,1,0:T(8,128)S(1)}, f32[4,128,128]{2,1,0:T(8,128)S(1)}, u32[]{:S(2)}, u32[]{:S(2)}) collective-permute-start(f32[4,128,128]{2,1,0:T(8,128)S(1)} %get-tuple-element.12), channel_id=1, source_target_pairs={{1,0},{2,1},{3,2},{0,3},{5,4},{6,5},{7,6},{4,7},{9,8},{10,9},{11,1... | collective-permute-start | bytes 786440 | tf_op jit(solution)/shard_map/ppermute | solution.py:13

commit v2 on v1

v2 whole, which is shorter than its diff:
```python
import functools

import jax
import jax.numpy as jnp
from jax import lax
from jax.experimental import pallas as pl
from jax.experimental.pallas import tpu as pltpu
from jax.sharding import PartitionSpec as P

CHUNKS = 2
GROUP = 4
MIB = 2**20


def shifted(value, axis, offset):
    size = lax.axis_size(axis)
    return lax.ppermute(value, axis, [((i + offset) % size, i) for i in range(size)])


def plan_kernel(sizes, *refs):
    rows, cols, layers, count, piece_rows, width, local_rows, kept = sizes
    row_packs, col_packs = (refs[0],) + refs[1:rows], (refs[0],) + refs[rows : rows + cols - 1]
    c_cols, pairs, tally, panel_cols = refs[rows + cols - 1 :]
    piece = piece_rows * width
    for d in range(rows):
        for q in range(piece):
            panel_cols[d * piece + q] = row_packs[d][2 * count + q]
    here = lax.div(refs[0][0], local_rows)
    layer = lax.rem(lax.div(refs[0][count], piece_rows), layers)
    own_rows = local_rows // layers
    total = jnp.int32(0)
    for j in range(cols):

        def one_block(n, total):
            row = col_packs[j][n] - here * local_rows
            inner = col_packs[j][count + n]
            owner = lax.div(inner, piece_rows * layers)
            inner = lax.rem(inner, piece_rows)
            right = (lax.rem(owner - here + rows, rows) * piece_rows + inner) * width
            goal = lax.rem(lax.div(row, own_rows) - layer + layers, layers)
            goal = (goal * own_rows + lax.rem(row, own_rows)) * kept
            for s in range(width):
                wanted = panel_cols[right + s]
                hit, slot = jnp.int32(0), goal
                for t in range(kept):
                    same = (c_cols[row, t] == wanted).astype(jnp.int32)
                    hit += same
                    slot += t * same
                pairs[0, total] = j * count + n
                pairs[1, total] = right + s
                pairs[2, total] = slot
                total += hit
            return total

        total = lax.fori_loop(0, count, one_block, total)
    for g in range(GROUP):
        pairs[0, total + g] = 0
        pairs[1, total + g] = 0
        pairs[2, total + g] = local_rows * kept
    tally[0] = total


def product_kernel(sizes, first, *refs):
    rows, cols, layers, count, slots, height = sizes
    pairs, tally, refs = refs[0], refs[1], refs[2:]
    x_in, refs = refs[:cols], refs[cols:]
    s_in, refs = refs[:rows], refs[rows:]
    own, sent, refs = refs[0], refs[1:layers], refs[layers:]
    x_held, s_held, totals, x_sem, s_sem = refs

    piece = s_held.shape[0] // rows
    loads = [
        pltpu.make_async_copy(s_in[d], s_held.at[pl.ds(d * piece, piece)], s_sem.at[d])
        for d in range(rows)
    ]
    loads.append(
        pltpu.make_async_copy(
            x_in[0].at[:, pl.ds(first, height), :], x_held.at[pl.ds(0, count)], x_sem.at[0]
        )
    )
    loads += [
        pltpu.make_async_copy(x_in[j], x_held.at[pl.ds(j * count, count)], x_sem.at[j])
        for j in range(1, cols)
    ]
    for load in loads:
        load.start()
    totals[...] = jnp.zeros_like(totals)
    for load in loads:
        load.wait()

    def one_group(group, carry):
        base = group * GROUP
        products = [
            jnp.dot(
                x_held[pairs[0, base + g]],
                s_held[pairs[1, base + g]],
                preferred_element_type=jnp.float32,
            )
            for g in range(GROUP)
        ]
        for g in range(GROUP):
            totals[pairs[2, base + g]] += products[g]
        return carry

    lax.fori_loop(0, lax.div(tally[0] + GROUP - 1, GROUP), one_group, 0)

    own[...] = totals[:slots]
    half = height // 2
    for d in range(1, layers):
        code = sent[d - 1]
        code[slots * half :] = jnp.zeros((code.shape[0] - slots * half, code.shape[1]), jnp.int32)
        for u in range(slots):
            value = totals[d * slots + u]
            peak = jnp.max(jnp.abs(value), axis=0, keepdims=True)
            power = jnp.floor(jnp.log2(jnp.maximum(peak, 1e-30)) + 1e-3) + 1.0
            whole = jnp.floor(value * jnp.exp2(15.0 - power) + 0.5).astype(jnp.int32)
            code[pl.ds(u * half, half)] = (whole[:half] << 16) | (whole[half:] & 0xFFFF)
            code[pl.ds(slots * half + u, 1)] = power.astype(jnp.int32)


def finish_kernel(sizes, *refs):
    layers, chunks, slots, height = sizes
    result = refs[-1]
    kept = result.shape[1]
    half = height // 2
    for c in range(chunks):
        own, codes = refs[c * layers], refs[c * layers + 1 : (c + 1) * layers]
        for u in range(slots):
            high, low = own[u, :half], own[u, half:]
            for code in codes:
                word = code[pl.ds(u * half, half)]
                power = code[pl.ds(slots * half + u, 1)].astype(jnp.float32)
                scale = jnp.exp2(power - 15.0)
                high += (word >> 16).astype(jnp.float32) * scale
                low += ((word << 16) >> 16).astype(jnp.float32) * scale
            at = c * height
            result[u // kept, u % kept, at : at + half] = high.astype(jnp.bfloat16)
            result[u // kept, u % kept, at + half : at + height] = low.astype(jnp.bfloat16)


def per_device(a_blocks, a_rows, a_cols, s_blocks, s_cols, c_cols):
    rows, cols, layers = (lax.axis_size(axis) for axis in ("row", "col", "layer"))
    count, order = a_blocks.shape[:2]
    piece_rows, width = s_cols.shape
    local_rows, kept = c_cols.shape
    own_rows = local_rows // layers
    slots = own_rows * kept
    height = order // CHUNKS
    panel = rows * piece_rows * width

    x_pieces = []
    for c in range(CHUNKS):
        part = lax.slice_in_dim(a_blocks, c * height, (c + 1) * height, axis=1)
        x_pieces.append([shifted(part, "col", j) for j in range(1, cols)])
    pack = jnp.concatenate([a_rows, a_cols, s_cols.reshape(-1)])
    row_packs = [shifted(pack, "row", d) for d in range(1, rows)]
    col_packs = [shifted(pack, "col", j) for j in range(1, cols)]
    flat_s = s_blocks.reshape(piece_rows * width, order, order)
    s_pieces = [flat_s] + [shifted(flat_s, "row", d) for d in range(1, rows)]

    scalars = pl.BlockSpec(memory_space=pltpu.SMEM)
    anywhere = pl.BlockSpec(memory_space=pl.ANY)
    vector = pl.BlockSpec(memory_space=pltpu.VMEM)
    most = cols * count * width
    pairs, tally = pl.pallas_call(
        functools.partial(
            plan_kernel, (rows, cols, layers, count, piece_rows, width, local_rows, kept)
        ),
        out_shape=[
            jax.ShapeDtypeStruct((3, most + GROUP), jnp.int32),
            jax.ShapeDtypeStruct((1,), jnp.int32),
        ],
        in_specs=[scalars] * (rows + cols),
        out_specs=[scalars] * 2,
        scratch_shapes=[pltpu.SMEM((panel,), jnp.int32)],
        name="plan",
    )(pack, *row_packs, *col_packs, c_cols)

    held_bytes = 2 * order * (cols * count * height + panel * order)
    total_bytes = 4 * order * height * (local_rows * kept + 1)
    code_rows = slots * (height // 2) + (slots + 7) // 8 * 8
    parts = []
    for c in range(CHUNKS):
        parts.append(
            pl.pallas_call(
                functools.partial(
                    product_kernel, (rows, cols, layers, count, slots, height), c * height
                ),
                out_shape=[jax.ShapeDtypeStruct((slots, height, order), jnp.float32)]
                + [jax.ShapeDtypeStruct((code_rows, order), jnp.int32)] * (layers - 1),
                in_specs=[scalars] * 2 + [anywhere] * (cols + rows),
                out_specs=[vector] * layers,
                scratch_shapes=[
                    pltpu.VMEM((cols * count, height, order), jnp.bfloat16),
                    pltpu.VMEM((panel, order, order), jnp.bfloat16),
                    pltpu.VMEM((layers * slots + 1, height, order), jnp.float32),
                    pltpu.SemaphoreType.DMA((cols,)),
                    pltpu.SemaphoreType.DMA((rows,)),
                ],
                compiler_params=pltpu.CompilerParams(
                    vmem_limit_bytes=held_bytes + 2 * total_bytes + 4 * MIB
                ),
                cost_estimate=pl.CostEstimate(
                    flops=2 * order**2 * height * most // 4,
                    bytes_accessed=held_bytes + total_bytes,
                    transcendentals=0,
                ),
                name=f"products_{c}",
            )(pairs, tally, a_blocks, *x_pieces[c], *s_pieces)
        )

    final = []
    for part in parts:
        final.append(part[0])
        final += [shifted(part[d], "layer", layers - d) for d in range(1, layers)]
    return pl.pallas_call(
        functools.partial(finish_kernel, (layers, CHUNKS, slots, height)),
        out_shape=jax.ShapeDtypeStruct((own_rows, kept, order, order), jnp.bfloat16),
        in_specs=[vector] * len(final),
        out_specs=vector,
        compiler_params=pltpu.CompilerParams(
            vmem_limit_bytes=16 * slots * order * order + 4 * MIB
        ),
        name="finish",
    )(*final)


def solution(mesh):
    placed = (
        P(("row", "col", "layer"), None, None),
        P(("row", "col", "layer")),
        P(("row", "col", "layer")),
        P(("row", "layer"), "col", None, None),
        P(("row", "layer"), "col"),
        P("row", "col"),
    )
    return jax.shard_map(
        per_device,
        mesh=mesh,
        in_specs=placed,
        out_specs=P(("row", "layer"), "col", None, None),
        check_vma=False,
    )
```

time: 55.3 us -> 48.6 us (0.88)
  the two profiles are of different devices: /device:TPU:13 before, /device:TPU:0 now
where the time goes in v2:
time: 48.6 us; the launch traced here: 48.5 us
  waiting for transfers between devices  18 us (37%)
  starting transfers between devices  17.4 us (36%)
  Pallas kernels  9.78 us (20%)
  local copies, waits for them, and re-layouts  3.1 us (6%)
    ppermute x15, waiting for transfers between devices, shifted(): lax.ppermute(value, axis, [((i + offset) % size, i) for i in range(size)])  18 us
    ppermute x15, starting transfers between devices, shifted(): lax.ppermute(value, axis, [((i + offset) % size, i) for i in range(size)])  17.4 us
    pallas_call x2, Pallas kernels, per_device(): pl.pallas_call(functools.partial(product_kernel, (rows, cols, layers, cou...  6.13 us
    pallas_call x1, Pallas kernels, per_device(): pl.pallas_call(functools.partial(plan_kernel, (rows, cols, layers, count,...  2.86 us
    unnamed x25, local copies, waits for them, and re-layouts  1.77 us
    slice x1, local copies, waits for them, and re-layouts, per_device(): part = lax.slice_in_dim(a_blocks, c * height, (c + 1) * height, axis=1)  1.25 us
  transfers between devices with their start and end apart: 15, of which 6 were waited for; matrix products, arithmetic and copies ran while one was open for 2% of the time, Pallas kernels for 19%

profile of v2, /device:TPU:0, one launch (start us, length us, event | category | flops | bytes accessed | tf_op | source)
XLA Modules:
  0.0 48.5 jit_solution(16417871745583608112)
XLA Ops:
  0.0 1.3 %fusion = (bf16[24,64,128]{2,1,0:T(8,128)(2,1)S(1)}, bf16[24,64,128]{2,1,0:T(8,128)(2,1)S(1)}) fusion(bf16[24,128,128]{2,1,0:T(8,128)(2,1)} %refs_2_.3), kind=kLoop, calls=%fused_computation.1 | loop fusion | bytes 1572864 | tf_op jit(solution)/shard_map/slice | solution.py:153
  1.3 0.0 copy-start.11
  1.3 3.0 %collective-permute-start.4 = (bf16[24,64,128]{2,1,0:T(8,128)(2,1)S(1)}, bf16[24,64,128]{2,1,0:T(8,128)(2,1)S(1)}, u32[]{:S(2)}, u32[]{:S(2)}) collective-permute-start(bf16[24,64,128]{2,1,0:T(8,128)(2,1)S(1)} %get-tuple-element.26), channel_id=1, source_target_pairs={{4,0},{0,4},{5,1},{1,5},{6,2},{2,6},{7,3},{3,7},{12,8},{8,12},{13,... | collective-permute-start | bytes 1179656 | tf_op jit(solution)/shard_map/ppermute | solution.py:17
  4.3 0.1 collective-permute-start.11
  4.4 0.0 copy-done.11
  4.4 0.1 reshape.6
  4.5 0.5 copy-done.5
  4.9 0.0 copy-done.6
  4.9 0.1 pad_add_fusion.refs_0_
  5.0 0.7 %collective-permute-start = (s32[52]{0:T(128)S(1)}, s32[52]{0:T(128)S(1)}, u32[]{:S(2)}, u32[]{:S(2)}) collective-permute-start(s32[52]{0:T(128)S(1)} %pad_add_fusion.refs_0_), channel_id=1, source_target_pairs={{8,0},{16,8},{24,16},{0,24},{9,1},{17,9},{25,17},{1,25},{10,2},{18... | collective-permute-start | bytes 632 | tf_op jit(solution)/shard_map/ppermute | solution.py:17
  5.7 0.9 %collective-permute-start.1 = (s32[52]{0:T(128)S(1)}, s32[52]{0:T(128)S(1)}, u32[]{:S(2)}, u32[]{:S(2)}) collective-permute-start(s32[52]{0:T(128)S(1)} %pad_add_fusion.refs_0_), channel_id=1, source_target_pairs={{16,0},{24,8},{0,16},{8,24},{17,1},{25,9},{1,17},{9,25},{18,2},{26... | collective-permute-start | bytes 632 | tf_op jit(solution)/shard_map/ppermute | solution.py:17
  6.6 0.2 collective-permute-start.2
  6.8 0.2 collective-permute-done.refs_1_
  7.0 1.2 %collective-permute-start.3 = (s32[52]{0:T(128)S(1)}, s32[52]{0:T(128)S(1)}, u32[]{:S(2)}, u32[]{:S(2)}) collective-permute-start(s32[52]{0:T(128)S(1)} %pad_add_fusion.refs_0_), channel_id=1, source_target_pairs={{4,0},{0,4},{5,1},{1,5},{6,2},{2,6},{7,3},{3,7},{12,8},{8,12},{13,... | collective-permute-start | bytes 632 | tf_op jit(solution)/shard_map/ppermute | solution.py:17
  8.3 1.0 %collective-permute-done.1.refs_2_ = s32[52]{0:T(128)S(1)} collective-permute-done((s32[52]{0:T(128)S(1)}, s32[52]{0:T(128)S(1)}, u32[]{:S(2)}, u32[]{:S(2)}) %collective-permute-start.1) | collective-permute-done | bytes 240 | tf_op jit(solution)/shard_map/ppermute | solution.py:17
  9.3 0.0 copy-done.3
  9.3 0.0 copy-done.7
  9.3 0.6 %copy-done.8 = s32[52]{0:T(128)} copy-done((s32[52]{0:T(128)}, s32[52]{0:T(128)S(1)}, u32[]{:S(2)}) %copy-start.8) | copy-done | bytes 232
  9.8 0.0 copy-done.1
  9.8 0.6 %collective-permute-start.5 = (bf16[4,128,128]{2,1,0:T(8,128)(2,1)S(1)}, bf16[4,128,128]{2,1,0:T(8,128)(2,1)S(1)}, u32[]{:S(2)}, u32[]{:S(2)}) collective-permute-start(bf16[4,128,128]{2,1,0:T(8,128)(2,1)S(1)} %bitcast.1), channel_id=1, source_target_pairs={{8,0},{16,8},{24,16},{0,24},{9,1},{17,9},{25,17},{1,25},{10,2},{18... | collective-permute-start | bytes 393224 | tf_op jit(solution)/shard_map/ppermute | solution.py:17
  10.5 0.0 collective-permute-done.2.refs_3_
  10.5 1.1 %collective-permute-start.6 = (bf16[4,128,128]{2,1,0:T(8,128)(2,1)S(1)}, bf16[4,128,128]{2,1,0:T(8,128)(2,1)S(1)}, u32[]{:S(2)}, u32[]{:S(2)}) collective-permute-start(bf16[4,128,128]{2,1,0:T(8,128)(2,1)S(1)} %bitcast.2), channel_id=1, source_target_pairs={{16,0},{24,8},{0,16},{8,24},{17,1},{25,9},{1,17},{9,25},{18,2},{26... | collective-permute-start | bytes 393224 | tf_op jit(solution)/shard_map/ppermute | solution.py:17
  11.6 10.3 %collective-permute-done.3.refs_4_ = s32[52]{0:T(128)S(1)} collective-permute-done((s32[52]{0:T(128)S(1)}, s32[52]{0:T(128)S(1)}, u32[]{:S(2)}, u32[]{:S(2)}) %collective-permute-start.3) | collective-permute-done | bytes 240 | tf_op jit(solution)/shard_map/ppermute | solution.py:17
  21.9 0.0 collective-permute-start.7
  21.9 0.0 copy-done.4
  21.9 0.7 %copy.7.refs_5_ = s32[8,2]{1,0:T(8,128)} copy(s32[8,2]{0,1:T(2,128)S(1)} %copy-done.4) | data formatting | bytes 128 | tf_op args[5]
  22.6 2.9 %plan.1 = (s32[3,100]{1,0:T(4,128)}, s32[1]{0:T(128)}) custom-call(s32[52]{0:T(128)} %copy-done.3, s32[52]{0:T(128)} %copy-done.7, s32[52]{0:T(128)} %copy-done.8, s32[52]{0:T(128)} %copy-done.9, s32[52]{0:T(128)} %copy-done.10, s32[8,2]{1,0:T(8,128)} %copy.7.refs_5_), custom_call_target="tpu_custom_call" | custom-call | tf_op jit(solution)/shard_map/plan/pallas_call | solution.py:165
  25.4 0.0 collective-permute-done.5.refs_5_
  25.5 0.0 collective-permute-done.6.refs_6_
  25.5 0.8 %collective-permute-done.7.refs_7_ = bf16[4,128,128]{2,1,0:T(8,128)(2,1)S(1)} collective-permute-done((bf16[4,128,128]{2,1,0:T(8,128)(2,1)S(1)}, bf16[4,128,128]{2,1,0:T(8,128)(2,1)S(1)}, u32[]{:S(2)}, u32[]{:S(2)}) %collective-permute-start.7) | collective-permute-done | bytes 131104 | tf_op jit(solution)/shard_map/ppermute | solution.py:17
  26.3 0.0 collective-permute-done.4.refs_3_
  26.3 0.0 copy-done
  26.3 3.1 %products_0.1 = (f32[4,64,128]{2,1,0:T(8,128)S(1)}, s32[136,128]{1,0:T(8,128)S(1)}, s32[136,128]{1,0:T(8,128)S(1)}, s32[136,128]{1,0:T(8,128)S(1)}) custom-call(s32[3,100]{1,0:T(4,128)S(1)} %copy-done.2, s32[1]{0:T(128)} %get-tuple-element.16.refs_1_, bf16[24,128,128]{2,1,0:T(8,128)(2,1)S(1)} %copy-done, ...), custom_call_target="tpu_custom_call" | custom-call | flops 50331648 | bytes 1867776 | tf_op jit(solution)/shard_map/products_0/pallas_call | solution.py:185
  29.4 1.7 %collective-permute-start.8 = (s32[136,128]{1,0:T(8,128)S(1)}, s32[136,128]{1,0:T(8,128)S(1)}, u32[]{:S(2)}, u32[]{:S(2)}) collective-permute-start(s32[136,128]{1,0:T(8,128)S(1)} %get-tuple-element.18), channel_id=1, source_target_pairs={{3,0},{0,1},{1,2},{2,3},{7,4},{4,5},{5,6},{6,7},{11,8},{8,9},{9,10... | collective-permute-start | bytes 208904 | tf_op jit(solution)/shard_map/ppermute | solution.py:17
  31.1 2.8 %collective-permute-start.9 = (s32[136,128]{1,0:T(8,128)S(1)}, s32[136,128]{1,0:T(8,128)S(1)}, u32[]{:S(2)}, u32[]{:S(2)}) collective-permute-start(s32[136,128]{1,0:T(8,128)S(1)} %get-tuple-element.19), channel_id=1, source_target_pairs={{2,0},{3,1},{0,2},{1,3},{6,4},{7,5},{4,6},{5,7},{10,8},{11,9},{8,1... | collective-permute-start | bytes 208904 | tf_op jit(solution)/shard_map/ppermute | solution.py:17
  33.8 1.2 %collective-permute-start.10 = (s32[136,128]{1,0:T(8,128)S(1)}, s32[136,128]{1,0:T(8,128)S(1)}, u32[]{:S(2)}, u32[]{:S(2)}) collective-permute-start(s32[136,128]{1,0:T(8,128)S(1)} %get-tuple-element.20), channel_id=1, source_target_pairs={{1,0},{2,1},{3,2},{0,3},{5,4},{6,5},{7,6},{4,7},{9,8},{10,9},{11,1... | collective-permute-start | bytes 208904 | tf_op jit(solution)/shard_map/ppermute | solution.py:17
  35.0 0.0 collective-permute-done.11.refs_3_
  35.0 3.1 %products_1.1 = (f32[4,64,128]{2,1,0:T(8,128)S(1)}, s32[136,128]{1,0:T(8,128)S(1)}, s32[136,128]{1,0:T(8,128)S(1)}, s32[136,128]{1,0:T(8,128)S(1)}) custom-call(s32[3,100]{1,0:T(4,128)S(1)} %copy-done.2, s32[1]{0:T(128)} %get-tuple-element.16.refs_1_, bf16[24,128,128]{2,1,0:T(8,128)(2,1)S(1)} %copy-done, ...), custom_call_target="tpu_custom_call" | custom-call | flops 50331648 | bytes 1867776 | tf_op jit(solution)/shard_map/products_1/pallas_call | solution.py:185
  38.1 0.7 %collective-permute-start.12 = (s32[136,128]{1,0:T(8,128)S(1)}, s32[136,128]{1,0:T(8,128)S(1)}, u32[]{:S(2)}, u32[]{:S(2)}) collective-permute-start(s32[136,128]{1,0:T(8,128)S(1)} %get-tuple-element.22), channel_id=1, source_target_pairs={{3,0},{0,1},{1,2},{2,3},{7,4},{4,5},{5,6},{6,7},{11,8},{8,9},{9,10... | collective-permute-start | bytes 208904 | tf_op jit(solution)/shard_map/ppermute | solution.py:17
  38.8 0.3 collective-permute-start.13
  39.2 0.0 collective-permute-done.8.refs_1_
  39.2 2.8 %collective-permute-start.14 = (s32[136,128]{1,0:T(8,128)S(1)}, s32[136,128]{1,0:T(8,128)S(1)}, u32[]{:S(2)}, u32[]{:S(2)}) collective-permute-start(s32[136,128]{1,0:T(8,128)S(1)} %get-tuple-element.24), channel_id=1, source_target_pairs={{1,0},{2,1},{3,2},{0,3},{5,4},{6,5},{7,6},{4,7},{9,8},{10,9},{11,1... | collective-permute-start | bytes 208904 | tf_op jit(solution)/shard_map/ppermute | solution.py:17
  42.0 0.0 collective-permute-done.9.refs_2_
  42.0 0.0 collective-permute-done.10.refs_3_
  42.0 3.0 %collective-permute-done.12.refs_5_ = s32[136,128]{1,0:T(8,128)S(1)} collective-permute-done((s32[136,128]{1,0:T(8,128)S(1)}, s32[136,128]{1,0:T(8,128)S(1)}, u32[]{:S(2)}, u32[]{:S(2)}) %collective-permute-start.12) | collective-permute-done | bytes 69664 | tf_op jit(solution)/shard_map/ppermute | solution.py:17
  45.0 2.7 %collective-permute-done.13.refs_6_ = s32[136,128]{1,0:T(8,128)S(1)} collective-permute-done((s32[136,128]{1,0:T(8,128)S(1)}, s32[136,128]{1,0:T(8,128)S(1)}, u32[]{:S(2)}, u32[]{:S(2)}) %collective-permute-start.13) | collective-permute-done | bytes 69664 | tf_op jit(solution)/shard_map/ppermute | solution.py:17
  47.7 0.0 collective-permute-done.14.refs_7_
  47.7 0.8 %finish.1 = bf16[2,2,128,128]{3,2,1,0:T(8,128)(2,1)} custom-call(f32[4,64,128]{2,1,0:T(8,128)S(1)} %get-tuple-element.17.refs_0_, s32[136,128]{1,0:T(8,128)S(1)} %collective-permute-done.8.refs_1_, s32[136,128]{1,0:T(8,128)S(1)} %collective-permute-done.9.refs_2_, s32[136,128]{1,0:T(8,128)S(1)} %collective-permute-done.10.refs_3_, ...), custom_call_target="tpu_custom_call" | custom-call | tf_op jit(solution)/shard_map/finish/pallas_call | solution.py:216
  (14 shorter events, 0.0 us)
Async XLA Ops:
  0.0 26.3 %copy-start = (bf16[24,128,128]{2,1,0:T(8,128)(2,1)S(1)}, bf16[24,128,128]{2,1,0:T(8,128)(2,1)}, u32[]{:S(2)}) copy-start(bf16[24,128,128]{2,1,0:T(8,128)(2,1)} %refs_2_.3) | copy-start | bytes 2359300
  0.0 9.8 %copy-start.1 = (bf16[2,2,128,128]{3,2,1,0:T(8,128)(2,1)S(1)}, bf16[2,2,128,128]{3,2,1,0:T(8,128)(2,1)}, u32[]{:S(2)}) copy-start(bf16[2,2,128,128]{3,2,1,0:T(8,128)(2,1)} %param.9) | copy-start | bytes 393220
  1.3 3.1 %copy-start.11 = (s32[2,2]{1,0:T(2,128)S(1)}, s32[2,2]{1,0:T(2,128)}, u32[]{:S(2)}) copy-start(s32[2,2]{1,0:T(2,128)} %param.10) | copy-start | bytes 52
  1.3 25.0 %collective-permute-start.4 = (bf16[24,64,128]{2,1,0:T(8,128)(2,1)S(1)}, bf16[24,64,128]{2,1,0:T(8,128)(2,1)S(1)}, u32[]{:S(2)}, u32[]{:S(2)}) collective-permute-start(bf16[24,64,128]{2,1,0:T(8,128)(2,1)S(1)} %get-tuple-element.26), channel_id=1, source_target_pairs={{4,0},{0,4},{5,1},{1,5},{6,2},{2,6},{7,3},{3,7},{12,8},{8,12},{13,... | collective-permute-start | bytes 1179656 | tf_op jit(solution)/shard_map/ppermute | solution.py:17
  4.3 0.7 %copy-start.5 = (s32[24]{0:T(128)S(1)}, s32[24]{0:T(128)}, u32[]{:S(2)}) copy-start(s32[24]{0:T(128)} %param.8) | copy-start | bytes 292
  4.3 0.7 %copy-start.6 = (s32[24]{0:T(128)S(1)}, s32[24]{0:T(128)}, u32[]{:S(2)}) copy-start(s32[24]{0:T(128)} %param.7) | copy-start | bytes 292
  4.3 30.7 %collective-permute-start.11 = (bf16[24,64,128]{2,1,0:T(8,128)(2,1)S(1)}, bf16[24,64,128]{2,1,0:T(8,128)(2,1)S(1)}, u32[]{:S(2)}, u32[]{:S(2)}) collective-permute-start(bf16[24,64,128]{2,1,0:T(8,128)(2,1)S(1)} %get-tuple-element.25), channel_id=1, source_target_pairs={{4,0},{0,4},{5,1},{1,5},{6,2},{2,6},{7,3},{3,7},{12,8},{8,12},{13,... | collective-permute-start | bytes 1179656 | tf_op jit(solution)/shard_map/ppermute | solution.py:17
  5.0 4.2 %copy-start.3 = (s32[52]{0:T(128)}, s32[52]{0:T(128)S(1)}, u32[]{:S(2)}) copy-start(s32[52]{0:T(128)S(1)} %pad_add_fusion.refs_0_) | copy-start | bytes 628
  5.0 16.9 %copy-start.4 = (s32[8,2]{0,1:T(2,128)S(1)}, s32[8,2]{0,1:T(2,128)}, u32[]{:S(2)}) copy-start(s32[8,2]{0,1:T(2,128)} %param.11) | copy-start | bytes 196
  5.0 2.0 %collective-permute-start = (s32[52]{0:T(128)S(1)}, s32[52]{0:T(128)S(1)}, u32[]{:S(2)}, u32[]{:S(2)}) collective-permute-start(s32[52]{0:T(128)S(1)} %pad_add_fusion.refs_0_), channel_id=1, source_target_pairs={{8,0},{16,8},{24,16},{0,24},{9,1},{17,9},{25,17},{1,25},{10,2},{18... | collective-permute-start | bytes 632 | tf_op jit(solution)/shard_map/ppermute | solution.py:17
  5.7 3.5 %collective-permute-start.1 = (s32[52]{0:T(128)S(1)}, s32[52]{0:T(128)S(1)}, u32[]{:S(2)}, u32[]{:S(2)}) collective-permute-start(s32[52]{0:T(128)S(1)} %pad_add_fusion.refs_0_), channel_id=1, source_target_pairs={{16,0},{24,8},{0,16},{8,24},{17,1},{25,9},{1,17},{9,25},{18,2},{26... | collective-permute-start | bytes 632 | tf_op jit(solution)/shard_map/ppermute | solution.py:17
  6.6 3.8 %collective-permute-start.2 = (s32[52]{0:T(128)S(1)}, s32[52]{0:T(128)S(1)}, u32[]{:S(2)}, u32[]{:S(2)}) collective-permute-start(s32[52]{0:T(128)S(1)} %pad_add_fusion.refs_0_), channel_id=1, source_target_pairs={{24,0},{0,8},{8,16},{16,24},{25,1},{1,9},{9,17},{17,25},{26,2},{2,... | collective-permute-start | bytes 632 | tf_op jit(solution)/shard_map/ppermute | solution.py:17
  7.0 2.3 %copy-start.7 = (s32[52]{0:T(128)}, s32[52]{0:T(128)S(1)}, u32[]{:S(2)}) copy-start(s32[52]{0:T(128)S(1)} %collective-permute-done.refs_1_) | copy-start | bytes 628
  7.0 14.9 %collective-permute-start.3 = (s32[52]{0:T(128)S(1)}, s32[52]{0:T(128)S(1)}, u32[]{:S(2)}, u32[]{:S(2)}) collective-permute-start(s32[52]{0:T(128)S(1)} %pad_add_fusion.refs_0_), channel_id=1, source_target_pairs={{4,0},{0,4},{5,1},{1,5},{6,2},{2,6},{7,3},{3,7},{12,8},{8,12},{13,... | collective-permute-start | bytes 632 | tf_op jit(solution)/shard_map/ppermute | solution.py:17
  9.3 0.6 %copy-start.8 = (s32[52]{0:T(128)}, s32[52]{0:T(128)S(1)}, u32[]{:S(2)}) copy-start(s32[52]{0:T(128)S(1)} %collective-permute-done.1.refs_2_) | copy-start | bytes 628
  9.8 15.6 %collective-permute-start.5 = (bf16[4,128,128]{2,1,0:T(8,128)(2,1)S(1)}, bf16[4,128,128]{2,1,0:T(8,128)(2,1)S(1)}, u32[]{:S(2)}, u32[]{:S(2)}) collective-permute-start(bf16[4,128,128]{2,1,0:T(8,128)(2,1)S(1)} %bitcast.1), channel_id=1, source_target_pairs={{8,0},{16,8},{24,16},{0,24},{9,1},{17,9},{25,17},{1,25},{10,2},{18... | collective-permute-start | bytes 393224 | tf_op jit(solution)/shard_map/ppermute | solution.py:17
  10.5 12.1 %copy-start.9 = (s32[52]{0:T(128)}, s32[52]{0:T(128)S(1)}, u32[]{:S(2)}) copy-start(s32[52]{0:T(128)S(1)} %collective-permute-done.2.refs_3_) | copy-start | bytes 628
  10.5 15.0 %collective-permute-start.6 = (bf16[4,128,128]{2,1,0:T(8,128)(2,1)S(1)}, bf16[4,128,128]{2,1,0:T(8,128)(2,1)S(1)}, u32[]{:S(2)}, u32[]{:S(2)}) collective-permute-start(bf16[4,128,128]{2,1,0:T(8,128)(2,1)S(1)} %bitcast.2), channel_id=1, source_target_pairs={{16,0},{24,8},{0,16},{8,24},{17,1},{25,9},{1,17},{9,25},{18,2},{26... | collective-permute-start | bytes 393224 | tf_op jit(solution)/shard_map/ppermute | solution.py:17
  21.9 0.7 %copy-start.10 = (s32[52]{0:T(128)}, s32[52]{0:T(128)S(1)}, u32[]{:S(2)}) copy-start(s32[52]{0:T(128)S(1)} %collective-permute-done.3.refs_4_) | copy-start | bytes 628
  21.9 4.4 %collective-permute-start.7 = (bf16[4,128,128]{2,1,0:T(8,128)(2,1)S(1)}, bf16[4,128,128]{2,1,0:T(8,128)(2,1)S(1)}, u32[]{:S(2)}, u32[]{:S(2)}) collective-permute-start(bf16[4,128,128]{2,1,0:T(8,128)(2,1)S(1)} %bitcast.3), channel_id=1, source_target_pairs={{24,0},{0,8},{8,16},{16,24},{25,1},{1,9},{9,17},{17,25},{26,2},{2,... | collective-permute-start | bytes 393224 | tf_op jit(solution)/shard_map/ppermute | solution.py:17
  25.4 0.9 %copy-start.2 = (s32[3,100]{1,0:T(4,128)S(1)}, s32[3,100]{1,0:T(4,128)}, u32[]{:S(2)}) copy-start(s32[3,100]{1,0:T(4,128)} %get-tuple-element.15.refs_0_) | copy-start | bytes 3604
  29.4 9.8 %collective-permute-start.8 = (s32[136,128]{1,0:T(8,128)S(1)}, s32[136,128]{1,0:T(8,128)S(1)}, u32[]{:S(2)}, u32[]{:S(2)}) collective-permute-start(s32[136,128]{1,0:T(8,128)S(1)} %get-tuple-element.18), channel_id=1, source_target_pairs={{3,0},{0,1},{1,2},{2,3},{7,4},{4,5},{5,6},{6,7},{11,8},{8,9},{9,10... | collective-permute-start | bytes 208904 | tf_op jit(solution)/shard_map/ppermute | solution.py:17
  31.1 10.9 %collective-permute-start.9 = (s32[136,128]{1,0:T(8,128)S(1)}, s32[136,128]{1,0:T(8,128)S(1)}, u32[]{:S(2)}, u32[]{:S(2)}) collective-permute-start(s32[136,128]{1,0:T(8,128)S(1)} %get-tuple-element.19), channel_id=1, source_target_pairs={{2,0},{3,1},{0,2},{1,3},{6,4},{7,5},{4,6},{5,7},{10,8},{11,9},{8,1... | collective-permute-start | bytes 208904 | tf_op jit(solution)/shard_map/ppermute | solution.py:17
  33.8 8.1 %collective-permute-start.10 = (s32[136,128]{1,0:T(8,128)S(1)}, s32[136,128]{1,0:T(8,128)S(1)}, u32[]{:S(2)}, u32[]{:S(2)}) collective-permute-start(s32[136,128]{1,0:T(8,128)S(1)} %get-tuple-element.20), channel_id=1, source_target_pairs={{1,0},{2,1},{3,2},{0,3},{5,4},{6,5},{7,6},{4,7},{9,8},{10,9},{11,1... | collective-permute-start | bytes 208904 | tf_op jit(solution)/shard_map/ppermute | solution.py:17
  38.1 6.9 %collective-permute-start.12 = (s32[136,128]{1,0:T(8,128)S(1)}, s32[136,128]{1,0:T(8,128)S(1)}, u32[]{:S(2)}, u32[]{:S(2)}) collective-permute-start(s32[136,128]{1,0:T(8,128)S(1)} %get-tuple-element.22), channel_id=1, source_target_pairs={{3,0},{0,1},{1,2},{2,3},{7,4},{4,5},{5,6},{6,7},{11,8},{8,9},{9,10... | collective-permute-start | bytes 208904 | tf_op jit(solution)/shard_map/ppermute | solution.py:17
  38.8 8.9 %collective-permute-start.13 = (s32[136,128]{1,0:T(8,128)S(1)}, s32[136,128]{1,0:T(8,128)S(1)}, u32[]{:S(2)}, u32[]{:S(2)}) collective-permute-start(s32[136,128]{1,0:T(8,128)S(1)} %get-tuple-element.23), channel_id=1, source_target_pairs={{2,0},{3,1},{0,2},{1,3},{6,4},{7,5},{4,6},{5,7},{10,8},{11,9},{8,1... | collective-permute-start | bytes 208904 | tf_op jit(solution)/shard_map/ppermute | solution.py:17
  39.2 8.5 %collective-permute-start.14 = (s32[136,128]{1,0:T(8,128)S(1)}, s32[136,128]{1,0:T(8,128)S(1)}, u32[]{:S(2)}, u32[]{:S(2)}) collective-permute-start(s32[136,128]{1,0:T(8,128)S(1)} %get-tuple-element.24), channel_id=1, source_target_pairs={{1,0},{2,1},{3,2},{0,3},{5,4},{6,5},{7,6},{4,7},{9,8},{10,9},{11,1... | collective-permute-start | bytes 208904 | tf_op jit(solution)/shard_map/ppermute | solution.py:17

commit v3 on v2

v3 whole, which is shorter than its diff:
```python
import functools

import jax
import jax.numpy as jnp
from jax import lax
from jax.experimental import pallas as pl
from jax.experimental.pallas import tpu as pltpu
from jax.sharding import PartitionSpec as P

CHUNKS = 2
GROUP = 4
LANES = 128
MIB = 2**20


def shifted(value, axis, offset):
    size = lax.axis_size(axis)
    return lax.ppermute(value, axis, [((i + offset) % size, i) for i in range(size)])


def note_rows(how_many):
    digits = (how_many + LANES - 1) // LANES
    return (2 * digits + 15) // 16 * 16, digits


def write_notes(payload, start, values):
    height, digits = note_rows(len(values))
    row = lax.broadcasted_iota(jnp.int32, (height, LANES), 0)
    lane = lax.broadcasted_iota(jnp.int32, (height, LANES), 1)
    tile = jnp.zeros((height, LANES), jnp.int32)
    for p, value in enumerate(values):
        high = value >> 7
        here = lane == p % LANES
        tile = jnp.where(here & (row == p // LANES), value & 127, tile)
        tile = jnp.where(here & (row == digits + p // LANES), high, tile)
    payload[start : start + height] = tile.astype(jnp.float32).astype(jnp.bfloat16)


def read_notes(payload, start, how_many, whole, notes, sem):
    height, _ = note_rows(how_many)
    whole[...] = payload[start : start + height].astype(jnp.float32).astype(jnp.int32)
    copy = pltpu.make_async_copy(whole, notes, sem)
    copy.start()
    return copy


def note(notes, how_many, p):
    _, digits = note_rows(how_many)
    if isinstance(p, int) or digits > 1:
        row, lane = (p // LANES, p % LANES) if isinstance(p, int) else (p >> 7, p & 127)
    else:
        row, lane = 0, p
    return notes[row, lane] + (notes[digits + row, lane] << 7)


def pack_kernel(sizes, rights, goals, s_cols, x_in, s_in, x_out, s_out, x_sem, s_sem):
    count, height, order, piece_rows, width = sizes
    piece = piece_rows * width
    loads = [
        pltpu.make_async_copy(
            x_in.at[n, pl.ds(0, height)], x_out.at[pl.ds(n * height, height)], x_sem.at[n]
        )
        for n in range(count)
    ]
    loads += [
        pltpu.make_async_copy(s_in.at[q], s_out.at[pl.ds(q * order, order)], s_sem.at[q])
        for q in range(piece)
    ]
    for load in loads:
        load.start()
    write_notes(
        x_out, count * height, [rights[n] for n in range(count)] + [goals[n] for n in range(count)]
    )
    write_notes(
        s_out, piece * order, [s_cols[q, s] for q in range(piece_rows) for s in range(width)]
    )
    for load in loads:
        load.wait()


def list_pairs(sizes, target, panel_cols, kept_cols, pairs, tally, j):
    count, width, kept, trash = sizes

    def one_block(n, total):
        right, goal = target(n)
        for s in range(width):
            wanted = panel_cols[right + s]
            hit, slot = jnp.int32(0), goal
            for t in range(kept):
                same = (kept_cols[goal + t] == wanted).astype(jnp.int32)
                hit += same
                slot += t * same
            pairs[j, 0, total] = n
            pairs[j, 1, total] = right + s
            pairs[j, 2, total] = slot
            total += hit
        return total

    total = lax.fori_loop(0, count, one_block, jnp.int32(0))
    for g in range(GROUP):
        pairs[j, 0, total + g] = 0
        pairs[j, 1, total + g] = 0
        pairs[j, 2, total + g] = trash
    tally[j] = total


def add_products(left, panel, totals, pairs, tally, j):
    def one_group(group, carry):
        base = group * GROUP
        products = [
            jnp.dot(
                left(pairs[j, 0, base + g]),
                panel[pairs[j, 1, base + g]],
                preferred_element_type=jnp.float32,
            )
            for g in range(GROUP)
        ]
        for g in range(GROUP):
            totals[pairs[j, 2, base + g]] += products[g]
        return carry

    lax.fori_loop(0, lax.div(tally[j] + GROUP - 1, GROUP), one_group, 0)


def own_kernel(sizes, *refs):
    rows, layers, count, piece_rows, width, local_rows, kept, order = sizes
    layer, rights, goals, s_cols, c_cols, x_in, s_in = refs[:7]
    s_other = refs[7 : 6 + rows]
    totals, panel, panel_cols, kept_cols = refs[6 + rows : 10 + rows]
    whole, notes, pairs, tally, s_sem, note_sem = refs[10 + rows :]
    piece = piece_rows * width
    loads = [pltpu.make_async_copy(s_in, panel.at[pl.ds(0, piece)], s_sem.at[0])]
    for d in range(1, rows):
        loads += [
            pltpu.make_async_copy(
                s_other[d - 1].at[pl.ds(q * order, order)],
                panel.at[d * piece + q],
                s_sem.at[d * piece + q],
            )
            for q in range(piece)
        ]
    for load in loads:
        load.start()
    reads = [
        read_notes(s_other[d], piece * order, piece, whole.at[d], notes.at[d], note_sem.at[d])
        for d in range(rows - 1)
    ]
    totals[...] = jnp.zeros_like(totals)
    own_rows = local_rows // layers
    for g in range(layers):
        base = lax.rem(layer[0] + g, layers) * own_rows
        for i in range(own_rows):
            for t in range(kept):
                kept_cols[(g * own_rows + i) * kept + t] = c_cols[base + i, t]
    for read in reads:
        read.wait()
    for q in range(piece):
        panel_cols[q] = s_cols[q // width, q % width]
        for d in range(1, rows):
            panel_cols[d * piece + q] = note(notes.at[d - 1], piece, q)
    trash = local_rows * kept
    list_pairs(
        (count, width, kept, trash),
        lambda n: (rights[n], goals[n]),
        panel_cols,
        kept_cols,
        pairs,
        tally,
        0,
    )
    for load in loads:
        load.wait()
    add_products(lambda n: x_in[n], panel, totals, pairs, tally, 0)


def peer_kernel(sizes, first, *refs):
    cols, layers, count, width, kept, slots, height = sizes
    if first == 0:
        panel_cols, kept_cols, refs = refs[0], refs[1], refs[2:]
    else:
        pairs, tally, refs = refs[0], refs[1], refs[2:]
    x_in, refs = refs[: cols - 1], refs[cols - 1 :]
    panel, before, own, sent, refs = refs[0], refs[1], refs[2], refs[3 : 2 + layers], refs[2 + layers :]
    if first == 0:
        pairs, tally, totals, whole, notes, note_sem = refs
        reads = [
            read_notes(x_in[j], count * height, 2 * count, whole.at[j], notes.at[j], note_sem.at[j])
            for j in range(cols - 1)
        ]
    else:
        (totals,) = refs
    totals[...] = before[:, first : first + height]
    if first == 0:
        for j in range(cols - 1):
            reads[j].wait()
            list_pairs(
                (count, width, kept, layers * slots),
                lambda n: (
                    note(notes.at[j], 2 * count, n),
                    note(notes.at[j], 2 * count, count + n),
                ),
                panel_cols,
                kept_cols,
                pairs,
                tally,
                j,
            )

    for j in range(cols - 1):

        def left(n):
            return x_in[j][pl.ds(pl.multiple_of(n * height, height), height)]

        add_products(left, panel, totals, pairs, tally, j)

    own[...] = totals[:slots]
    half = height // 2
    for d in range(1, layers):
        code = sent[d - 1]
        code[slots * half :] = jnp.zeros((code.shape[0] - slots * half, code.shape[1]), jnp.int32)
        for u in range(slots):
            value = totals[d * slots + u]
            peak = jnp.max(jnp.abs(value), axis=0, keepdims=True)
            power = jnp.floor(jnp.log2(jnp.maximum(peak, 1e-30)) + 1e-3) + 1.0
            whole_value = jnp.floor(value * jnp.exp2(15.0 - power) + 0.5).astype(jnp.int32)
            code[pl.ds(u * half, half)] = (whole_value[:half] << 16) | (whole_value[half:] & 0xFFFF)
            code[pl.ds(slots * half + u, 1)] = power.astype(jnp.int32)


def finish_kernel(sizes, *refs):
    layers, chunks, slots, height = sizes
    result = refs[-1]
    kept = result.shape[1]
    half = height // 2
    for c in range(chunks):
        own, codes = refs[c * layers], refs[c * layers + 1 : (c + 1) * layers]
        for u in range(slots):
            high, low = own[u, :half], own[u, half:]
            for code in codes:
                word = code[pl.ds(u * half, half)]
                power = code[pl.ds(slots * half + u, 1)].astype(jnp.float32)
                scale = jnp.exp2(power - 15.0)
                high += (word >> 16).astype(jnp.float32) * scale
                low += ((word << 16) >> 16).astype(jnp.float32) * scale
            at = c * height
            result[u // kept, u % kept, at : at + half] = high.astype(jnp.bfloat16)
            result[u // kept, u % kept, at + half : at + height] = low.astype(jnp.bfloat16)


def per_device(a_blocks, a_rows, a_cols, s_blocks, s_cols, c_cols):
    rows, cols, layers = (lax.axis_size(axis) for axis in ("row", "col", "layer"))
    count, order = a_blocks.shape[:2]
    piece_rows, width = s_cols.shape
    local_rows, kept = c_cols.shape
    own_rows = local_rows // layers
    slots = own_rows * kept
    height = order // CHUNKS
    piece = piece_rows * width
    panel_size = rows * piece

    row_at, layer_at = lax.axis_index("row"), lax.axis_index("layer")
    owner = a_cols // (piece_rows * layers)
    rights = ((owner - row_at + rows) % rows * piece_rows + a_cols % piece_rows) * width
    local = a_rows - row_at * local_rows
    goals = (local // own_rows - layer_at + layers) % layers * own_rows + local % own_rows
    goals = goals * kept
    flat_s = s_blocks.reshape(piece, order, order)

    scalars = pl.BlockSpec(memory_space=pltpu.SMEM)
    anywhere = pl.BlockSpec(memory_space=pl.ANY)
    vector = pl.BlockSpec(memory_space=pltpu.VMEM)
    x_note_rows, _ = note_rows(2 * count)
    s_note_rows, _ = note_rows(piece)

    x_first, s_sent = pl.pallas_call(
        functools.partial(pack_kernel, (count, height, order, piece_rows, width)),
        out_shape=[
            jax.ShapeDtypeStruct((count * height + x_note_rows, order), jnp.bfloat16),
            jax.ShapeDtypeStruct((piece * order + s_note_rows, order), jnp.bfloat16),
        ],
        in_specs=[scalars] * 3 + [anywhere] * 2,
        out_specs=[vector] * 2,
        scratch_shapes=[pltpu.SemaphoreType.DMA((count,)), pltpu.SemaphoreType.DMA((piece,))],
        name="pack",
    )(rights, goals, s_cols, a_blocks, flat_s)
    x_pieces = [[shifted(x_first, "col", j) for j in range(1, cols)]]
    s_pieces = [shifted(s_sent, "row", d) for d in range(1, rows)]
    for c in range(1, CHUNKS):
        part = lax.slice_in_dim(a_blocks, c * height, (c + 1) * height, axis=1)
        part = part.reshape(count * height, order)
        x_pieces.append([shifted(part, "col", j) for j in range(1, cols)])

    all_slots = layers * slots
    block_bytes = order * order
    totals, panel, panel_cols, kept_cols = pl.pallas_call(
        functools.partial(
            own_kernel, (rows, layers, count, piece_rows, width, local_rows, kept, order)
        ),
        out_shape=[
            jax.ShapeDtypeStruct((all_slots + 1, order, order), jnp.float32),
            jax.ShapeDtypeStruct((panel_size, order, order), jnp.bfloat16),
            jax.ShapeDtypeStruct((panel_size,), jnp.int32),
            jax.ShapeDtypeStruct((all_slots,), jnp.int32),
        ],
        in_specs=[scalars] * 5 + [vector] * (1 + rows),
        out_specs=[vector] * 2 + [scalars] * 2,
        scratch_shapes=[
            pltpu.VMEM((rows - 1, s_note_rows, LANES), jnp.int32),
            pltpu.SMEM((rows - 1, s_note_rows, LANES), jnp.int32),
            pltpu.SMEM((1, 3, count * width + GROUP), jnp.int32),
            pltpu.SMEM((1,), jnp.int32),
            pltpu.SemaphoreType.DMA((panel_size,)),
            pltpu.SemaphoreType.DMA((rows - 1,)),
        ],
        compiler_params=pltpu.CompilerParams(
            vmem_limit_bytes=block_bytes * (4 * all_slots + 4 * panel_size + 2 * count) + 4 * MIB
        ),
        cost_estimate=pl.CostEstimate(
            flops=2 * order**3 * count * width // 4,
            bytes_accessed=block_bytes * (4 * all_slots + 4 * panel_size + 2 * count),
            transcendentals=0,
        ),
        name="own_products",
    )(layer_at.reshape(1), rights, goals, s_cols, c_cols, a_blocks, flat_s, *s_pieces)

    code_rows = slots * (height // 2) + (slots + 7) // 8 * 8
    pair_shapes = [(cols - 1, 3, count * width + GROUP), (cols - 1,)]
    parts, plan = [], []
    for c in range(CHUNKS):
        out_shape = [jax.ShapeDtypeStruct((slots, height, order), jnp.float32)]
        out_shape += [jax.ShapeDtypeStruct((code_rows, order), jnp.int32)] * (layers - 1)
        out_specs = [vector] * layers
        scratch = [pltpu.VMEM((all_slots + 1, height, order), jnp.float32)]
        if c == 0:
            out_shape += [jax.ShapeDtypeStruct(shape, jnp.int32) for shape in pair_shapes]
            out_specs += [scalars] * 2
            scratch += [
                pltpu.VMEM((cols - 1, x_note_rows, LANES), jnp.int32),
                pltpu.SMEM((cols - 1, x_note_rows, LANES), jnp.int32),
                pltpu.SemaphoreType.DMA((cols - 1,)),
            ]
        moved = block_bytes * (8 * all_slots + 2 * panel_size + 2 * count * (cols - 1))
        out = pl.pallas_call(
            functools.partial(
                peer_kernel, (cols, layers, count, width, kept, slots, height), c * height
            ),
            out_shape=out_shape,
            in_specs=[scalars] * 2 + [vector] * (cols + 1),
            out_specs=out_specs,
            scratch_shapes=scratch,
            compiler_params=pltpu.CompilerParams(vmem_limit_bytes=moved + 4 * MIB),
            cost_estimate=pl.CostEstimate(
                flops=2 * order**2 * height * count * width // 4 * (cols - 1),
                bytes_accessed=moved // CHUNKS,
                transcendentals=0,
            ),
            name=f"peer_products_{c}",
        )(*(plan or (panel_cols, kept_cols)), *x_pieces[c], panel, totals)
        if c == 0:
            plan = out[layers:]
        parts.append(out[:layers])

    final = []
    for part in parts:
        final.append(part[0])
        final += [shifted(part[d], "layer", layers - d) for d in range(1, layers)]
    return pl.pallas_call(
        functools.partial(finish_kernel, (layers, CHUNKS, slots, height)),
        out_shape=jax.ShapeDtypeStruct((own_rows, kept, order, order), jnp.bfloat16),
        in_specs=[vector] * len(final),
        out_specs=vector,
        compiler_params=pltpu.CompilerParams(
            vmem_limit_bytes=16 * slots * order * order + 4 * MIB
        ),
        name="finish",
    )(*final)


def solution(mesh):
    placed = (
        P(("row", "col", "layer"), None, None),
        P(("row", "col", "layer")),
        P(("row", "col", "layer")),
        P(("row", "layer"), "col", None, None),
        P(("row", "layer"), "col"),
        P("row", "col"),
    )
    return jax.shard_map(
        per_device,
        mesh=mesh,
        in_specs=placed,
        out_specs=P(("row", "layer"), "col", None, None),
        check_vma=False,
    )
```

time: 48.6 us -> 39.6 us (0.81)
  waiting for transfers between devices: 18 us -> 10.8 us
  local copies, waits for them, and re-layouts: 3.1 us -> 0.13 us
  starting transfers between devices: 17.4 us -> 15.3 us
  Pallas kernels: 9.78 us -> 11.8 us
  other arithmetic: 0.08 us -> 1.35 us
    ppermute x15 -> x11, waiting for transfers between devices: 18 us -> 10.8 us  [shifted(): lax.ppermute(value, axis, [((i + offset) % size, i) for i in range(size)])]
    ppermute x15 -> x11, starting transfers between devices: 17.4 us -> 15.3 us  [shifted(): lax.ppermute(value, axis, [((i + offset) % size, i) for i in range(size)])]
    pallas_call x3 -> x4, Pallas kernels: 8.98 us -> 11 us  [the longest x2 4.23 us: per_device(): pl.pallas_call(functools.partial(peer_kernel, (cols, layers, count, width...]
    unnamed x25 -> x13, local copies, waits for them, and re-layouts: 1.77 us -> 0.1 us
    mul x0 -> x1, other arithmetic: none -> 1.35 us  [per_device(): goals = goals * kept]
    slice x1, local copies, waits for them, and re-layouts: 1.25 us -> 0.03 us  [per_device(): part = lax.slice_in_dim(a_blocks, c * height, (c + 1) * height, axis=1)]
  transfers between devices with their start and end apart: 15 -> 11, of which waited for: 6 -> 4; matrix products, arithmetic and copies ran while one was open for 2% -> 0% of each run, Pallas kernels for 19% -> 20%
where the time goes in v3:
time: 39.6 us; the launch traced here: 39.4 us
  starting transfers between devices  15.3 us (39%)
  Pallas kernels  11.8 us (30%)
  waiting for transfers between devices  10.8 us (27%)
  other arithmetic  1.35 us (3%)
    ppermute x11, starting transfers between devices, shifted(): lax.ppermute(value, axis, [((i + offset) % size, i) for i in range(size)])  15.3 us
    ppermute x11, waiting for transfers between devices, shifted(): lax.ppermute(value, axis, [((i + offset) % size, i) for i in range(size)])  10.8 us
    pallas_call x2, Pallas kernels, per_device(): pl.pallas_call(functools.partial(peer_kernel, (cols, layers, count, width...  4.23 us
    pallas_call x1, Pallas kernels, per_device(): pl.pallas_call(functools.partial(own_kernel, (rows, layers, count, piece_...  3.83 us
    pallas_call x1, Pallas kernels, per_device(): pl.pallas_call(functools.partial(pack_kernel, (count, height, order, piec...  2.9 us
    mul x1, other arithmetic, per_device(): goals = goals * kept  1.35 us
    pallas_call x1, Pallas kernels, per_device(): pl.pallas_call(functools.partial(finish_kernel, (layers, CHUNKS, slots, h...  0.8 us
  transfers between devices with their start and end apart: 11, of which 4 were waited for; matrix products, arithmetic and copies ran while one was open for 0% of the time, Pallas kernels for 20%

profile of v3, /device:TPU:0, one launch (start us, length us, event | category | flops | bytes accessed | tf_op | source)
XLA Modules:
  0.0 39.4 jit_solution(9820689016410262277)
XLA Ops:
  0.0 0.0 copy-start.4
  0.0 0.0 copy-start
  0.0 0.0 copy-start.1
  0.0 0.0 copy-start.5
  0.0 1.3 %fusion.6 = (s32[24]{0:T(128)}, s32[24]{0:T(128)}) fusion(s32[24]{0:T(128)} %param.7, s32[]{:T(128)} %axis_index.22, s32[]{:T(128)S(6)} %mul.17, s32[]{:T(128)S(6)} %axis_index.25, s32[24]{0:T(128)} %param.8), kind=kLoop, calls=%fused_computation.23 | loop fusion | flops 1800 | bytes 396 | tf_op jit(solution)/shard_map/mul | solution.py:266
  1.4 0.0 copy-start.2
  1.4 0.0 copy-start.3
  1.4 2.9 %pack.1 = (bf16[1552,128]{1,0:T(8,128)(2,1)}, bf16[528,128]{1,0:T(8,128)(2,1)}) custom-call(s32[24]{0:T(128)} %get-tuple-element.38.rights.refs_1_, s32[24]{0:T(128)} %get-tuple-element.37.goals.refs_2_, s32[2,2]{1,0:T(2,128)} %refs_3_.1, bf16[24,128,128]{2,1,0:T(8,128)(2,1)} %refs_5_.1, bf16[4,128,128]{2,1,0:T(8,128)(2,1)} %bitcast.3), custom_call_target="tpu_custom_call" | custom-call | tf_op jit(solution)/shard_map/pack/pallas_call | solution.py:275
  4.3 3.0 %collective-permute-start.3 = (bf16[1552,128]{1,0:T(8,128)(2,1)}, bf16[1552,128]{1,0:T(8,128)(2,1)S(1)}, u32[]{:S(2)}, u32[]{:S(2)}) collective-permute-start(bf16[1552,128]{1,0:T(8,128)(2,1)} %get-tuple-element.24), channel_id=1, source_target_pairs={{4,0},{0,4},{5,1},{1,5},{6,2},{2,6},{7,3},{3,7},{12,8},{8,12},{13,... | collective-permute-start | bytes 1191944 | tf_op jit(solution)/shard_map/ppermute | solution.py:18
  7.3 0.0 copy-done
  7.3 0.1 collective-permute-start.7
  7.4 0.9 %collective-permute-start = (bf16[528,128]{1,0:T(8,128)(2,1)}, bf16[528,128]{1,0:T(8,128)(2,1)S(1)}, u32[]{:S(2)}, u32[]{:S(2)}) collective-permute-start(bf16[528,128]{1,0:T(8,128)(2,1)} %get-tuple-element.21), channel_id=1, source_target_pairs={{8,0},{16,8},{24,16},{0,24},{9,1},{17,9},{25,17},{1,25},{10,2},{18... | collective-permute-start | bytes 405512 | tf_op jit(solution)/shard_map/ppermute | solution.py:18
  8.3 1.1 %collective-permute-start.1 = (bf16[528,128]{1,0:T(8,128)(2,1)}, bf16[528,128]{1,0:T(8,128)(2,1)S(1)}, u32[]{:S(2)}, u32[]{:S(2)}) collective-permute-start(bf16[528,128]{1,0:T(8,128)(2,1)} %get-tuple-element.21), channel_id=1, source_target_pairs={{16,0},{24,8},{0,16},{8,24},{17,1},{25,9},{1,17},{9,25},{18,2},{26... | collective-permute-start | bytes 405512 | tf_op jit(solution)/shard_map/ppermute | solution.py:18
  9.5 0.2 collective-permute-start.2
  9.7 0.0 copy-done.5
  9.7 0.1 copy.7.refs_4_
  9.8 2.2 %collective-permute-done.refs_7_ = bf16[528,128]{1,0:T(8,128)(2,1)S(1)} collective-permute-done((bf16[528,128]{1,0:T(8,128)(2,1)}, bf16[528,128]{1,0:T(8,128)(2,1)S(1)}, u32[]{:S(2)}, u32[]{:S(2)}) %collective-permute-start) | collective-permute-done | bytes 135200 | tf_op jit(solution)/shard_map/ppermute | solution.py:18
  12.0 4.8 %collective-permute-done.1.refs_8_ = bf16[528,128]{1,0:T(8,128)(2,1)S(1)} collective-permute-done((bf16[528,128]{1,0:T(8,128)(2,1)}, bf16[528,128]{1,0:T(8,128)(2,1)S(1)}, u32[]{:S(2)}, u32[]{:S(2)}) %collective-permute-start.1) | collective-permute-done | bytes 135200 | tf_op jit(solution)/shard_map/ppermute | solution.py:18
  16.8 0.0 collective-permute-done.2.refs_9_
  16.8 0.0 copy-done.4
  16.8 0.0 copy-done.1
  16.8 0.0 copy-done.2
  16.8 0.0 copy-done.3
  16.8 3.8 %own_products.1 = (f32[17,128,128]{2,1,0:T(8,128)S(1)}, bf16[16,128,128]{2,1,0:T(8,128)(2,1)S(1)}, s32[16]{0:T(128)S(1)}, s32[16]{0:T(128)S(1)}) custom-call(s32[1]{0:T(128)} %bitcast.refs_0_, s32[24]{0:T(128)S(1)} %copy-done.3, s32[24]{0:T(128)S(1)} %copy-done.2, s32[2,2]{1,0:T(2,128)S(1)} %copy-done.4, s32[8,2]{1,0:T(8,128)S(1)} %copy.7.refs_4_, ...), custom_call_target="tpu_custom_call" | custom-call | flops 50331648 | bytes 2883584 | tf_op jit(solution)/shard_map/own_products/pallas_call | solution.py:295
  20.7 0.0 collective-permute-done.3.refs_2_
  20.7 2.7 %peer_products_0.1 = (f32[4,64,128]{2,1,0:T(8,128)S(1)}, s32[136,128]{1,0:T(8,128)S(1)}, s32[136,128]{1,0:T(8,128)S(1)}, s32[136,128]{1,0:T(8,128)S(1)}, s32[1,3,52]{2,1,0:T(4,128)S(1)}, /*index=5*/s32[1]{0:T(128)}) custom-call(s32[16]{0:T(128)S(1)} %get-tuple-element.22.refs_0_, s32[16]{0:T(128)S(1)} %get-tuple-element.23.refs_1_, ...), custom_call_target="tpu_custom_call" | custom-call | flops 25165824 | bytes 1703936 | tf_op jit(solution)/shard_map/peer_products_0/pallas_call | solution.py:343
  23.4 2.2 %collective-permute-start.4 = (s32[136,128]{1,0:T(8,128)S(1)}, s32[136,128]{1,0:T(8,128)S(1)}, u32[]{:S(2)}, u32[]{:S(2)}) collective-permute-start(s32[136,128]{1,0:T(8,128)S(1)} %get-tuple-element.28), channel_id=1, source_target_pairs={{3,0},{0,1},{1,2},{2,3},{7,4},{4,5},{5,6},{6,7},{11,8},{8,9},{9,10... | collective-permute-start | bytes 208904 | tf_op jit(solution)/shard_map/ppermute | solution.py:18
  25.5 2.6 %collective-permute-start.5 = (s32[136,128]{1,0:T(8,128)S(1)}, s32[136,128]{1,0:T(8,128)S(1)}, u32[]{:S(2)}, u32[]{:S(2)}) collective-permute-start(s32[136,128]{1,0:T(8,128)S(1)} %get-tuple-element.29), channel_id=1, source_target_pairs={{2,0},{3,1},{0,2},{1,3},{6,4},{7,5},{4,6},{5,7},{10,8},{11,9},{8,1... | collective-permute-start | bytes 208904 | tf_op jit(solution)/shard_map/ppermute | solution.py:18
  28.1 1.3 %collective-permute-start.6 = (s32[136,128]{1,0:T(8,128)S(1)}, s32[136,128]{1,0:T(8,128)S(1)}, u32[]{:S(2)}, u32[]{:S(2)}) collective-permute-start(s32[136,128]{1,0:T(8,128)S(1)} %get-tuple-element.30), channel_id=1, source_target_pairs={{1,0},{2,1},{3,2},{0,3},{5,4},{6,5},{7,6},{4,7},{9,8},{10,9},{11,1... | collective-permute-start | bytes 208904 | tf_op jit(solution)/shard_map/ppermute | solution.py:18
  29.5 0.0 collective-permute-done.7.refs_2_
  29.5 1.6 %peer_products_1.1 = (f32[4,64,128]{2,1,0:T(8,128)S(1)}, s32[136,128]{1,0:T(8,128)S(1)}, s32[136,128]{1,0:T(8,128)S(1)}, s32[136,128]{1,0:T(8,128)S(1)}) custom-call(s32[1,3,52]{2,1,0:T(4,128)S(1)} %get-tuple-element.31.refs_0_, s32[1]{0:T(128)} %get-tuple-element.32.refs_1_, bf16[1536,128]{1,0:T(8,128)(2,1)S(1)} %collective-permute-done.7.refs_2_, ...), custom_call_target="tpu_custom_call" | custom-call | flops 25165824 | bytes 1703936 | tf_op jit(solution)/shard_map/peer_products_1/pallas_call | solution.py:343
  31.0 0.9 %collective-permute-start.8 = (s32[136,128]{1,0:T(8,128)S(1)}, s32[136,128]{1,0:T(8,128)S(1)}, u32[]{:S(2)}, u32[]{:S(2)}) collective-permute-start(s32[136,128]{1,0:T(8,128)S(1)} %get-tuple-element.34), channel_id=1, source_target_pairs={{3,0},{0,1},{1,2},{2,3},{7,4},{4,5},{5,6},{6,7},{11,8},{8,9},{9,10... | collective-permute-start | bytes 208904 | tf_op jit(solution)/shard_map/ppermute | solution.py:18
  31.9 0.3 collective-permute-start.9
  32.3 0.0 collective-permute-done.4.refs_1_
  32.3 2.6 %collective-permute-start.10 = (s32[136,128]{1,0:T(8,128)S(1)}, s32[136,128]{1,0:T(8,128)S(1)}, u32[]{:S(2)}, u32[]{:S(2)}) collective-permute-start(s32[136,128]{1,0:T(8,128)S(1)} %get-tuple-element.36), channel_id=1, source_target_pairs={{1,0},{2,1},{3,2},{0,3},{5,4},{6,5},{7,6},{4,7},{9,8},{10,9},{11,1... | collective-permute-start | bytes 208904 | tf_op jit(solution)/shard_map/ppermute | solution.py:18
  34.9 0.0 collective-permute-done.5.refs_2_
  34.9 0.0 collective-permute-done.6.refs_3_
  34.9 2.4 %collective-permute-done.8.refs_5_ = s32[136,128]{1,0:T(8,128)S(1)} collective-permute-done((s32[136,128]{1,0:T(8,128)S(1)}, s32[136,128]{1,0:T(8,128)S(1)}, u32[]{:S(2)}, u32[]{:S(2)}) %collective-permute-start.8) | collective-permute-done | bytes 69664 | tf_op jit(solution)/shard_map/ppermute | solution.py:18
  37.3 1.3 %collective-permute-done.9.refs_6_ = s32[136,128]{1,0:T(8,128)S(1)} collective-permute-done((s32[136,128]{1,0:T(8,128)S(1)}, s32[136,128]{1,0:T(8,128)S(1)}, u32[]{:S(2)}, u32[]{:S(2)}) %collective-permute-start.9) | collective-permute-done | bytes 69664 | tf_op jit(solution)/shard_map/ppermute | solution.py:18
  38.6 0.0 collective-permute-done.10.refs_7_
  38.6 0.8 %finish.1 = bf16[2,2,128,128]{3,2,1,0:T(8,128)(2,1)} custom-call(f32[4,64,128]{2,1,0:T(8,128)S(1)} %get-tuple-element.27.refs_0_, s32[136,128]{1,0:T(8,128)S(1)} %collective-permute-done.4.refs_1_, s32[136,128]{1,0:T(8,128)S(1)} %collective-permute-done.5.refs_2_, s32[136,128]{1,0:T(8,128)S(1)} %collective-permute-done.6.refs_3_, ...), custom_call_target="tpu_custom_call" | custom-call | tf_op jit(solution)/shard_map/finish/pallas_call | solution.py:367
  (1 shorter events, 0.0 us)
Async XLA Ops:
  0.0 16.8 %copy-start.4 = (s32[2,2]{1,0:T(2,128)S(1)}, s32[2,2]{1,0:T(2,128)}, u32[]{:S(2)}) copy-start(s32[2,2]{1,0:T(2,128)} %refs_3_.1) | copy-start | bytes 52
  0.0 7.3 %copy-start = (bf16[24,128,128]{2,1,0:T(8,128)(2,1)S(1)}, bf16[24,128,128]{2,1,0:T(8,128)(2,1)}, u32[]{:S(2)}) copy-start(bf16[24,128,128]{2,1,0:T(8,128)(2,1)} %refs_5_.1) | copy-start | bytes 2359300
  0.0 16.8 %copy-start.1 = (bf16[2,2,128,128]{3,2,1,0:T(8,128)(2,1)S(1)}, bf16[2,2,128,128]{3,2,1,0:T(8,128)(2,1)}, u32[]{:S(2)}) copy-start(bf16[2,2,128,128]{3,2,1,0:T(8,128)(2,1)} %param.9) | copy-start | bytes 393220
  0.0 9.7 %copy-start.5 = (s32[8,2]{0,1:T(2,128)S(1)}, s32[8,2]{0,1:T(2,128)}, u32[]{:S(2)}) copy-start(s32[8,2]{0,1:T(2,128)} %param.11) | copy-start | bytes 196
  1.4 15.5 %copy-start.2 = (s32[24]{0:T(128)S(1)}, s32[24]{0:T(128)}, u32[]{:S(2)}) copy-start(s32[24]{0:T(128)} %get-tuple-element.37.goals.refs_2_) | copy-start | bytes 292
  1.4 15.5 %copy-start.3 = (s32[24]{0:T(128)S(1)}, s32[24]{0:T(128)}, u32[]{:S(2)}) copy-start(s32[24]{0:T(128)} %get-tuple-element.38.rights.refs_1_) | copy-start | bytes 292
  4.3 16.4 %collective-permute-start.3 = (bf16[1552,128]{1,0:T(8,128)(2,1)}, bf16[1552,128]{1,0:T(8,128)(2,1)S(1)}, u32[]{:S(2)}, u32[]{:S(2)}) collective-permute-start(bf16[1552,128]{1,0:T(8,128)(2,1)} %get-tuple-element.24), channel_id=1, source_target_pairs={{4,0},{0,4},{5,1},{1,5},{6,2},{2,6},{7,3},{3,7},{12,8},{8,12},{13,... | collective-permute-start | bytes 1191944 | tf_op jit(solution)/shard_map/ppermute | solution.py:18
  7.3 22.1 %collective-permute-start.7 = (bf16[1536,128]{1,0:T(8,128)(2,1)S(1)}, bf16[1536,128]{1,0:T(8,128)(2,1)S(1)}, u32[]{:S(2)}, u32[]{:S(2)}) collective-permute-start(bf16[1536,128]{1,0:T(8,128)(2,1)S(1)} %bitcast.5), channel_id=1, source_target_pairs={{4,0},{0,4},{5,1},{1,5},{6,2},{2,6},{7,3},{3,7},{12,8},{8,12},{13,... | collective-permute-start | bytes 1179656 | tf_op jit(solution)/shard_map/ppermute | solution.py:18
  7.4 4.6 %collective-permute-start = (bf16[528,128]{1,0:T(8,128)(2,1)}, bf16[528,128]{1,0:T(8,128)(2,1)S(1)}, u32[]{:S(2)}, u32[]{:S(2)}) collective-permute-start(bf16[528,128]{1,0:T(8,128)(2,1)} %get-tuple-element.21), channel_id=1, source_target_pairs={{8,0},{16,8},{24,16},{0,24},{9,1},{17,9},{25,17},{1,25},{10,2},{18... | collective-permute-start | bytes 405512 | tf_op jit(solution)/shard_map/ppermute | solution.py:18
  8.3 8.5 %collective-permute-start.1 = (bf16[528,128]{1,0:T(8,128)(2,1)}, bf16[528,128]{1,0:T(8,128)(2,1)S(1)}, u32[]{:S(2)}, u32[]{:S(2)}) collective-permute-start(bf16[528,128]{1,0:T(8,128)(2,1)} %get-tuple-element.21), channel_id=1, source_target_pairs={{16,0},{24,8},{0,16},{8,24},{17,1},{25,9},{1,17},{9,25},{18,2},{26... | collective-permute-start | bytes 405512 | tf_op jit(solution)/shard_map/ppermute | solution.py:18
  9.5 7.4 %collective-permute-start.2 = (bf16[528,128]{1,0:T(8,128)(2,1)}, bf16[528,128]{1,0:T(8,128)(2,1)S(1)}, u32[]{:S(2)}, u32[]{:S(2)}) collective-permute-start(bf16[528,128]{1,0:T(8,128)(2,1)} %get-tuple-element.21), channel_id=1, source_target_pairs={{24,0},{0,8},{8,16},{16,24},{25,1},{1,9},{9,17},{17,25},{26,2},{2,... | collective-permute-start | bytes 405512 | tf_op jit(solution)/shard_map/ppermute | solution.py:18
  23.4 8.9 %collective-permute-start.4 = (s32[136,128]{1,0:T(8,128)S(1)}, s32[136,128]{1,0:T(8,128)S(1)}, u32[]{:S(2)}, u32[]{:S(2)}) collective-permute-start(s32[136,128]{1,0:T(8,128)S(1)} %get-tuple-element.28), channel_id=1, source_target_pairs={{3,0},{0,1},{1,2},{2,3},{7,4},{4,5},{5,6},{6,7},{11,8},{8,9},{9,10... | collective-permute-start | bytes 208904 | tf_op jit(solution)/shard_map/ppermute | solution.py:18
  25.5 9.4 %collective-permute-start.5 = (s32[136,128]{1,0:T(8,128)S(1)}, s32[136,128]{1,0:T(8,128)S(1)}, u32[]{:S(2)}, u32[]{:S(2)}) collective-permute-start(s32[136,128]{1,0:T(8,128)S(1)} %get-tuple-element.29), channel_id=1, source_target_pairs={{2,0},{3,1},{0,2},{1,3},{6,4},{7,5},{4,6},{5,7},{10,8},{11,9},{8,1... | collective-permute-start | bytes 208904 | tf_op jit(solution)/shard_map/ppermute | solution.py:18
  28.1 6.8 %collective-permute-start.6 = (s32[136,128]{1,0:T(8,128)S(1)}, s32[136,128]{1,0:T(8,128)S(1)}, u32[]{:S(2)}, u32[]{:S(2)}) collective-permute-start(s32[136,128]{1,0:T(8,128)S(1)} %get-tuple-element.30), channel_id=1, source_target_pairs={{1,0},{2,1},{3,2},{0,3},{5,4},{6,5},{7,6},{4,7},{9,8},{10,9},{11,1... | collective-permute-start | bytes 208904 | tf_op jit(solution)/shard_map/ppermute | solution.py:18
  31.0 6.3 %collective-permute-start.8 = (s32[136,128]{1,0:T(8,128)S(1)}, s32[136,128]{1,0:T(8,128)S(1)}, u32[]{:S(2)}, u32[]{:S(2)}) collective-permute-start(s32[136,128]{1,0:T(8,128)S(1)} %get-tuple-element.34), channel_id=1, source_target_pairs={{3,0},{0,1},{1,2},{2,3},{7,4},{4,5},{5,6},{6,7},{11,8},{8,9},{9,10... | collective-permute-start | bytes 208904 | tf_op jit(solution)/shard_map/ppermute | solution.py:18
  31.9 6.7 %collective-permute-start.9 = (s32[136,128]{1,0:T(8,128)S(1)}, s32[136,128]{1,0:T(8,128)S(1)}, u32[]{:S(2)}, u32[]{:S(2)}) collective-permute-start(s32[136,128]{1,0:T(8,128)S(1)} %get-tuple-element.35), channel_id=1, source_target_pairs={{2,0},{3,1},{0,2},{1,3},{6,4},{7,5},{4,6},{5,7},{10,8},{11,9},{8,1... | collective-permute-start | bytes 208904 | tf_op jit(solution)/shard_map/ppermute | solution.py:18
  32.3 6.4 %collective-permute-start.10 = (s32[136,128]{1,0:T(8,128)S(1)}, s32[136,128]{1,0:T(8,128)S(1)}, u32[]{:S(2)}, u32[]{:S(2)}) collective-permute-start(s32[136,128]{1,0:T(8,128)S(1)} %get-tuple-element.36), channel_id=1, source_target_pairs={{1,0},{2,1},{3,2},{0,3},{5,4},{6,5},{7,6},{4,7},{9,8},{10,9},{11,1... | collective-permute-start | bytes 208904 | tf_op jit(solution)/shard_map/ppermute | solution.py:18

commit v4 on v3

v4 whole, which is shorter than its diff:
```python
import functools

import jax
import jax.numpy as jnp
from jax import lax
from jax.experimental import pallas as pl
from jax.experimental.pallas import tpu as pltpu
from jax.sharding import PartitionSpec as P

CHUNKS = 2
GROUP = 4
LANES = 128
MIB = 2**20


def shifted(value, axis, offset):
    size = lax.axis_size(axis)
    return lax.ppermute(value, axis, [((i + offset) % size, i) for i in range(size)])


def quotient(value, by):
    return value >> (by.bit_length() - 1) if by & (by - 1) == 0 else lax.div(value, by)


def remainder(value, by):
    return value & (by - 1) if by & (by - 1) == 0 else lax.rem(value, by)


def note_rows(how_many):
    digits = (how_many + LANES - 1) // LANES
    return (2 * digits + 15) // 16 * 16, digits


def write_notes(payload, start, values):
    height, digits = note_rows(len(values))
    row = lax.broadcasted_iota(jnp.int32, (height, LANES), 0)
    lane = lax.broadcasted_iota(jnp.int32, (height, LANES), 1)
    tile = jnp.zeros((height, LANES), jnp.int32)
    for p, value in enumerate(values):
        here = lane == p % LANES
        tile = jnp.where(here & (row == p // LANES), value & (LANES - 1), tile)
        tile = jnp.where(here & (row == digits + p // LANES), quotient(value, LANES), tile)
    payload[start : start + height] = tile.astype(jnp.float32).astype(jnp.bfloat16)


def read_notes(payload, start, how_many, whole, notes, sem):
    height, _ = note_rows(how_many)
    whole[...] = payload[start : start + height].astype(jnp.float32).astype(jnp.int32)
    copy = pltpu.make_async_copy(whole, notes, sem)
    copy.start()
    return copy


def note(notes, how_many, p):
    _, digits = note_rows(how_many)
    return notes[p // LANES, p % LANES] + notes[digits + p // LANES, p % LANES] * LANES


def pack_kernel(sizes, a_rows, a_cols, s_cols, s_in, index, s_out, s_sem):
    count, order, piece_rows, width = sizes
    piece = piece_rows * width
    loads = [
        pltpu.make_async_copy(s_in.at[q], s_out.at[pl.ds(q * order, order)], s_sem.at[q])
        for q in range(piece)
    ]
    for load in loads:
        load.start()
    for n in range(count):
        index[n] = a_rows[n]
        index[count + n] = a_cols[n]
    write_notes(
        s_out, piece * order, [s_cols[q, s] for q in range(piece_rows) for s in range(width)]
    )
    for load in loads:
        load.wait()


def list_pairs(sizes, index, here, layer, panel_cols, kept_cols, pairs, tally, j):
    rows, layers, count, piece_rows, width, local_rows, kept = sizes
    own_rows = local_rows // layers

    def one_block(n, total):
        row = index[n] - here * local_rows
        inner = index[count + n]
        owner = quotient(inner, piece_rows * layers)
        inner = remainder(inner, piece_rows)
        right = (remainder(owner - here + rows, rows) * piece_rows + inner) * width
        goal = remainder(quotient(row, own_rows) - layer + layers, layers)
        goal = (goal * own_rows + remainder(row, own_rows)) * kept
        for s in range(width):
            wanted = panel_cols[right + s]
            hit, slot = jnp.int32(0), goal
            for t in range(kept):
                same = (kept_cols[goal + t] == wanted).astype(jnp.int32)
                hit += same
                slot += t * same
            pairs[j, 0, total] = n
            pairs[j, 1, total] = right + s
            pairs[j, 2, total] = slot
            total += hit
        return total

    total = lax.fori_loop(0, count, one_block, jnp.int32(0))
    for g in range(GROUP):
        pairs[j, 0, total + g] = 0
        pairs[j, 1, total + g] = 0
        pairs[j, 2, total + g] = local_rows * kept
    tally[j] = total


def add_products(left, panel, totals, pairs, tally, j):
    def one_group(group, carry):
        base = group * GROUP
        products = [
            jnp.dot(
                left(pairs[j, 0, base + g]),
                panel[pairs[j, 1, base + g]],
                preferred_element_type=jnp.float32,
            )
            for g in range(GROUP)
        ]
        for g in range(GROUP):
            totals[pairs[j, 2, base + g]] += products[g]
        return carry

    lax.fori_loop(0, quotient(tally[j] + GROUP - 1, GROUP), one_group, 0)


def own_kernel(sizes, *refs):
    rows, cols, layers, count, piece_rows, width, local_rows, kept, order = sizes
    index, s_cols, c_cols, x_in, s_in = refs[:cols], *refs[cols : cols + 4]
    s_other, refs = refs[cols + 4 : cols + 3 + rows], refs[cols + 3 + rows :]
    totals, panel, pairs, tally = refs[:4]
    panel_cols, kept_cols, whole, notes, s_sem, note_sem = refs[4:]
    piece = piece_rows * width
    loads = [pltpu.make_async_copy(s_in, panel.at[pl.ds(0, piece)], s_sem.at[0])]
    for d in range(1, rows):
        loads += [
            pltpu.make_async_copy(
                s_other[d - 1].at[pl.ds(q * order, order)],
                panel.at[d * piece + q],
                s_sem.at[d * piece + q],
            )
            for q in range(piece)
        ]
    reads = [
        read_notes(s_other[d], piece * order, piece, whole.at[d], notes.at[d], note_sem.at[d])
        for d in range(rows - 1)
    ]
    for load in loads:
        load.start()
    totals[...] = jnp.zeros_like(totals)
    here = quotient(index[0][0], local_rows)
    layer = remainder(quotient(index[0][count], piece_rows), layers)
    own_rows = local_rows // layers
    for g in range(layers):
        base = remainder(layer + g, layers) * own_rows
        for i in range(own_rows):
            for t in range(kept):
                kept_cols[(g * own_rows + i) * kept + t] = c_cols[base + i, t]
    for read in reads:
        read.wait()
    for q in range(piece):
        panel_cols[q] = s_cols[q // width, q % width]
        for d in range(1, rows):
            panel_cols[d * piece + q] = note(notes.at[d - 1], piece, q)
    for j in range(cols):
        list_pairs(
            (rows, layers, count, piece_rows, width, local_rows, kept),
            index[j],
            here,
            layer,
            panel_cols,
            kept_cols,
            pairs,
            tally,
            j,
        )
    for load in loads:
        load.wait()
    add_products(lambda n: x_in[n], panel, totals, pairs, tally, 0)


def peer_kernel(sizes, first, pairs, tally, *refs):
    cols, layers, slots, height = sizes
    x_in, refs = refs[: cols - 1], refs[cols - 1 :]
    panel, before, own, sent, totals = refs[0], refs[1], refs[2], refs[3 : 2 + layers], refs[-1]
    totals[...] = before[:, first : first + height]
    for j in range(1, cols):
        add_products(lambda n: x_in[j - 1][n], panel, totals, pairs, tally, j)

    own[...] = totals[:slots]
    half = height // 2
    for d in range(1, layers):
        code = sent[d - 1]
        code[slots * half :] = jnp.zeros((code.shape[0] - slots * half, code.shape[1]), jnp.int32)
        for u in range(slots):
            value = totals[d * slots + u]
            peak = jnp.max(jnp.abs(value), axis=0, keepdims=True)
            power = jnp.floor(jnp.log2(jnp.maximum(peak, 1e-30)) + 1e-3) + 1.0
            whole = jnp.floor(value * jnp.exp2(15.0 - power) + 0.5).astype(jnp.int32)
            code[pl.ds(u * half, half)] = (whole[:half] << 16) | (whole[half:] & 0xFFFF)
            code[pl.ds(slots * half + u, 1)] = power.astype(jnp.int32)


def finish_kernel(sizes, *refs):
    layers, chunks, slots, height = sizes
    result = refs[-1]
    kept = result.shape[1]
    half = height // 2
    for c in range(chunks):
        own, codes = refs[c * layers], refs[c * layers + 1 : (c + 1) * layers]
        for u in range(slots):
            high, low = own[u, :half], own[u, half:]
            for code in codes:
                word = code[pl.ds(u * half, half)]
                power = code[pl.ds(slots * half + u, 1)].astype(jnp.float32)
                scale = jnp.exp2(power - 15.0)
                high += (word >> 16).astype(jnp.float32) * scale
                low += ((word << 16) >> 16).astype(jnp.float32) * scale
            at = c * height
            result[u // kept, u % kept, at : at + half] = high.astype(jnp.bfloat16)
            result[u // kept, u % kept, at + half : at + height] = low.astype(jnp.bfloat16)


def per_device(a_blocks, a_rows, a_cols, s_blocks, s_cols, c_cols):
    rows, cols, layers = (lax.axis_size(axis) for axis in ("row", "col", "layer"))
    count, order = a_blocks.shape[:2]
    piece_rows, width = s_cols.shape
    local_rows, kept = c_cols.shape
    own_rows = local_rows // layers
    slots = own_rows * kept
    all_slots = layers * slots
    height = order // CHUNKS
    piece = piece_rows * width
    panel_size = rows * piece
    block_size = order * order
    flat_s = s_blocks.reshape(piece, order, order)
    note_height, _ = note_rows(piece)

    scalars = pl.BlockSpec(memory_space=pltpu.SMEM)
    anywhere = pl.BlockSpec(memory_space=pl.ANY)
    vector = pl.BlockSpec(memory_space=pltpu.VMEM)

    def x_chunk(blocks, c):
        part = lax.slice_in_dim(blocks, c * height, (c + 1) * height, axis=1)
        return [shifted(part, "col", j) for j in range(1, cols)]

    x_pieces = [x_chunk(a_blocks, 0)]
    index, s_sent = pl.pallas_call(
        functools.partial(pack_kernel, (count, order, piece_rows, width)),
        out_shape=[
            jax.ShapeDtypeStruct((2 * count,), jnp.int32),
            jax.ShapeDtypeStruct((piece * order + note_height, order), jnp.bfloat16),
        ],
        in_specs=[scalars] * 3 + [anywhere],
        out_specs=[scalars, vector],
        scratch_shapes=[pltpu.SemaphoreType.DMA((piece,))],
        name="pack",
    )(a_rows, a_cols, s_cols, flat_s)
    indices = [index] + [shifted(index, "col", j) for j in range(1, cols)]
    s_pieces = [shifted(s_sent, "row", d) for d in range(1, rows)]
    later_blocks, _, s_pieces = lax.optimization_barrier((a_blocks, indices, s_pieces))
    x_pieces += [x_chunk(later_blocks, c) for c in range(1, CHUNKS)]

    moved = block_size * (4 * all_slots + 4 * panel_size + 2 * count)
    totals, panel, *plan = pl.pallas_call(
        functools.partial(
            own_kernel, (rows, cols, layers, count, piece_rows, width, local_rows, kept, order)
        ),
        out_shape=[
            jax.ShapeDtypeStruct((all_slots + 1, order, order), jnp.float32),
            jax.ShapeDtypeStruct((panel_size, order, order), jnp.bfloat16),
            jax.ShapeDtypeStruct((cols, 3, count * width + GROUP), jnp.int32),
            jax.ShapeDtypeStruct((cols,), jnp.int32),
        ],
        in_specs=[scalars] * (cols + 2) + [vector] * (1 + rows),
        out_specs=[vector] * 2 + [scalars] * 2,
        scratch_shapes=[
            pltpu.SMEM((panel_size,), jnp.int32),
            pltpu.SMEM((all_slots,), jnp.int32),
            pltpu.VMEM((rows - 1, note_height, LANES), jnp.int32),
            pltpu.SMEM((rows - 1, note_height, LANES), jnp.int32),
            pltpu.SemaphoreType.DMA((panel_size,)),
            pltpu.SemaphoreType.DMA((rows - 1,)),
        ],
        compiler_params=pltpu.CompilerParams(vmem_limit_bytes=moved + 4 * MIB),
        cost_estimate=pl.CostEstimate(
            flops=2 * order**3 * count * width // 4, bytes_accessed=moved, transcendentals=0
        ),
        name="own_products",
    )(*indices, s_cols, c_cols, a_blocks, flat_s, *s_pieces)

    code_rows = slots * (height // 2) + (slots + 7) // 8 * 8
    moved = block_size * (8 * all_slots + 2 * panel_size + 2 * count * (cols - 1))
    parts = []
    for c in range(CHUNKS):
        out_shape = [jax.ShapeDtypeStruct((slots, height, order), jnp.float32)]
        out_shape += [jax.ShapeDtypeStruct((code_rows, order), jnp.int32)] * (layers - 1)
        parts.append(
            pl.pallas_call(
                functools.partial(peer_kernel, (cols, layers, slots, height), c * height),
                out_shape=out_shape,
                in_specs=[scalars] * 2 + [vector] * (cols + 1),
                out_specs=[vector] * layers,
                scratch_shapes=[pltpu.VMEM((all_slots + 1, height, order), jnp.float32)],
                compiler_params=pltpu.CompilerParams(vmem_limit_bytes=moved + 4 * MIB),
                cost_estimate=pl.CostEstimate(
                    flops=2 * order**2 * height * count * width // 4 * (cols - 1),
                    bytes_accessed=moved // CHUNKS,
                    transcendentals=0,
                ),
                name=f"peer_products_{c}",
            )(*plan, *x_pieces[c], panel, totals)
        )

    final = []
    for part in parts:
        final.append(part[0])
        final += [shifted(part[d], "layer", layers - d) for d in range(1, layers)]
    return pl.pallas_call(
        functools.partial(finish_kernel, (layers, CHUNKS, slots, height)),
        out_shape=jax.ShapeDtypeStruct((own_rows, kept, order, order), jnp.bfloat16),
        in_specs=[vector] * len(final),
        out_specs=vector,
        compiler_params=pltpu.CompilerParams(
            vmem_limit_bytes=16 * slots * order * order + 4 * MIB
        ),
        name="finish",
    )(*final)


def solution(mesh):
    placed = (
        P(("row", "col", "layer"), None, None),
        P(("row", "col", "layer")),
        P(("row", "col", "layer")),
        P(("row", "layer"), "col", None, None),
        P(("row", "layer"), "col"),
        P("row", "col"),
    )
    return jax.shard_map(
        per_device,
        mesh=mesh,
        in_specs=placed,
        out_specs=P(("row", "layer"), "col", None, None),
        check_vma=False,
    )
```

time: 39.6 us -> 42.5 us (1.073)
  waiting for transfers between devices: 10.8 us -> 15.7 us
  Pallas kernels: 11.8 us -> 9.97 us
  other arithmetic: 1.35 us -> 0 us
  local copies, waits for them, and re-layouts: 0.13 us -> 1.15 us
    ppermute x11 -> x12, waiting for transfers between devices: 10.8 us -> 15.7 us  [shifted(): lax.ppermute(value, axis, [((i + offset) % size, i) for i in range(size)])]
    pallas_call x4, Pallas kernels: 11 us -> 9.17 us  [the longest x1 4.25 us: per_device(): pl.pallas_call(functools.partial(own_kernel, (rows, cols, layers, count,...]
    mul x1 -> x0, other arithmetic: 1.35 us -> none  [per_device(): goals = goals * kept]
    slice x1 -> x2, local copies, waits for them, and re-layouts: 0.03 us -> 1.05 us  [x_chunk(): part = lax.slice_in_dim(blocks, c * height, (c + 1) * height, axis=1)]
    ppermute x11 -> x12, starting transfers between devices: 15.3 us -> 15.6 us  [shifted(): lax.ppermute(value, axis, [((i + offset) % size, i) for i in range(size)])]
  transfers between devices with their start and end apart: 11 -> 12, of which waited for: 4 -> 4; matrix products, arithmetic and copies ran while one was open for 0% -> 3% of each run, Pallas kernels for 20% -> 16%
where the time goes in v4:
time: 42.5 us
  waiting for transfers between devices  15.7 us (37%)
  starting transfers between devices  15.6 us (37%)
  Pallas kernels  9.97 us (23%)
  local copies, waits for them, and re-layouts  1.15 us (3%)
    ppermute x12, waiting for transfers between devices, shifted(): lax.ppermute(value, axis, [((i + offset) % size, i) for i in range(size)])  15.7 us
    ppermute x12, starting transfers between devices, shifted(): lax.ppermute(value, axis, [((i + offset) % size, i) for i in range(size)])  15.6 us
    pallas_call x1, Pallas kernels, per_device(): pl.pallas_call(functools.partial(own_kernel, (rows, cols, layers, count,...  4.25 us
    pallas_call x2, Pallas kernels, per_device(): pl.pallas_call(functools.partial(peer_kernel, (cols, layers, slots, heigh...  2.59 us
    pallas_call x1, Pallas kernels, per_device(): pl.pallas_call(functools.partial(pack_kernel, (count, order, piece_rows,...  2.33 us
    slice x2, local copies, waits for them, and re-layouts, x_chunk(): part = lax.slice_in_dim(blocks, c * height, (c + 1) * height, axis=1)  1.05 us
  transfers between devices with their start and end apart: 12, of which 4 were waited for; matrix products, arithmetic and copies ran while one was open for 3% of the time, Pallas kernels for 16%

profile of v4, /device:TPU:0, one launch (start us, length us, event | category | flops | bytes accessed | tf_op | source)
XLA Modules:
  0.0 42.5 jit_solution(7296788648163095382)
XLA Ops:
  0.0 0.0 copy-start.1
  0.0 0.0 copy-start.2
  0.0 0.0 copy-start
  0.0 0.0 copy-start.4
  0.0 2.3 %pack.1 = (s32[48]{0:T(128)}, bf16[528,128]{1,0:T(8,128)(2,1)}) custom-call(s32[24]{0:T(128)} %a_rows.1, s32[24]{0:T(128)} %a_cols.1, s32[2,2]{1,0:T(2,128)} %refs_2_.1, bf16[4,128,128]{2,1,0:T(8,128)(2,1)} %bitcast.1), custom_call_target="tpu_custom_call" | custom-call | tf_op jit(solution)/shard_map/pack/pallas_call | solution.py:250
  2.3 0.0 copy-start.3
  2.4 2.5 %collective-permute-start.1 = (bf16[528,128]{1,0:T(8,128)(2,1)}, bf16[528,128]{1,0:T(8,128)(2,1)S(1)}, u32[]{:S(2)}, u32[]{:S(2)}) collective-permute-start(bf16[528,128]{1,0:T(8,128)(2,1)} %get-tuple-element.24), channel_id=1, source_target_pairs={{8,0},{16,8},{24,16},{0,24},{9,1},{17,9},{25,17},{1,25},{10,2},{18... | collective-permute-start | bytes 405512 | tf_op jit(solution)/shard_map/ppermute | solution.py:18
  4.8 0.6 %collective-permute-start.2 = (bf16[528,128]{1,0:T(8,128)(2,1)}, bf16[528,128]{1,0:T(8,128)(2,1)S(1)}, u32[]{:S(2)}, u32[]{:S(2)}) collective-permute-start(bf16[528,128]{1,0:T(8,128)(2,1)} %get-tuple-element.24), channel_id=1, source_target_pairs={{16,0},{24,8},{0,16},{8,24},{17,1},{25,9},{1,17},{9,25},{18,2},{26... | collective-permute-start | bytes 405512 | tf_op jit(solution)/shard_map/ppermute | solution.py:18
  5.5 0.2 collective-permute-start.3
  5.6 1.0 %slice.6 = bf16[24,64,128]{2,1,0:T(8,128)(2,1)S(1)} slice(bf16[24,128,128]{2,1,0:T(8,128)(2,1)} %refs_4_.1), slice={[0:24], [0:64], [0:128]} | slice | bytes 786432 | tf_op jit(solution)/shard_map/slice | solution.py:246
  6.7 1.6 %collective-permute-start.4 = (bf16[24,64,128]{2,1,0:T(8,128)(2,1)S(1)}, bf16[24,64,128]{2,1,0:T(8,128)(2,1)S(1)}, u32[]{:S(2)}, u32[]{:S(2)}) collective-permute-start(bf16[24,64,128]{2,1,0:T(8,128)(2,1)S(1)} %slice.6), channel_id=1, source_target_pairs={{4,0},{0,4},{5,1},{1,5},{6,2},{2,6},{7,3},{3,7},{12,8},{8,12},{13,... | collective-permute-start | bytes 1179656 | tf_op jit(solution)/shard_map/ppermute | solution.py:18
  8.2 0.5 %collective-permute-start = (s32[48]{0:T(128)}, s32[48]{0:T(128)S(1)}, u32[]{:S(2)}, u32[]{:S(2)}) collective-permute-start(s32[48]{0:T(128)} %get-tuple-element.23.refs_0_), channel_id=1, source_target_pairs={{4,0},{0,4},{5,1},{1,5},{6,2},{2,6},{7,3},{3,7},{12,8},{8,12},{13,... | collective-permute-start | bytes 584 | tf_op jit(solution)/shard_map/ppermute | solution.py:18
  8.8 9.8 %collective-permute-done.refs_1_ = s32[48]{0:T(128)S(1)} collective-permute-done((s32[48]{0:T(128)}, s32[48]{0:T(128)S(1)}, u32[]{:S(2)}, u32[]{:S(2)}) %collective-permute-start) | collective-permute-done | bytes 224 | tf_op jit(solution)/shard_map/ppermute | solution.py:18
  18.5 0.0 collective-permute-done.1.refs_6_
  18.5 0.0 collective-permute-done.2.refs_7_
  18.5 0.0 collective-permute-done.3.refs_8_
  18.5 0.0 copy-done
  18.6 1.6 %collective-permute-start.8 = (bf16[24,64,128]{2,1,0:T(8,128)(2,1)S(1)}, bf16[24,64,128]{2,1,0:T(8,128)(2,1)S(1)}, u32[]{:S(2)}, u32[]{:S(2)}) collective-permute-start(bf16[24,64,128]{2,1,0:T(8,128)(2,1)S(1)} %slice.7), channel_id=1, source_target_pairs={{4,0},{0,4},{5,1},{1,5},{6,2},{2,6},{7,3},{3,7},{12,8},{8,12},{13,... | collective-permute-start | bytes 1179656 | tf_op jit(solution)/shard_map/ppermute | solution.py:18
  20.1 0.0 copy-done.4
  20.1 0.1 copy.7.refs_3_
  20.2 0.0 copy-done.1
  20.2 0.0 copy-done.2
  20.2 0.0 copy-done.3
  20.2 4.2 %own_products.1 = (f32[17,128,128]{2,1,0:T(8,128)S(1)}, bf16[16,128,128]{2,1,0:T(8,128)(2,1)S(1)}, s32[2,3,52]{2,1,0:T(4,128)S(1)}, s32[2]{0:T(128)S(1)}) custom-call(s32[48]{0:T(128)S(1)} %copy-done.3, s32[48]{0:T(128)S(1)} %collective-permute-done.refs_1_, s32[2,2]{1,0:T(2,128)S(1)} %copy-done.2, s32[8,2]{1,0:T(8,128)S(1)} %copy.7.refs_3_, ...), custom_call_target="tpu_custom_call" | custom-call | flops 50331648 | bytes 2883584 | tf_op jit(solution)/shard_map/own_products/pallas_call | solution.py:267
  24.5 0.0 collective-permute-done.4.refs_0_
  24.5 1.3 %peer_products_0.1 = (f32[4,64,128]{2,1,0:T(8,128)S(1)}, s32[136,128]{1,0:T(8,128)S(1)}, s32[136,128]{1,0:T(8,128)S(1)}, s32[136,128]{1,0:T(8,128)S(1)}) custom-call(s32[2,3,52]{2,1,0:T(4,128)S(1)} %get-tuple-element.28.pairs, s32[2]{0:T(128)S(1)} %get-tuple-element.29.tally, bf16[24,64,128]{2,1,0:T(8,128)(2,1)S(1)} %collective-permute-done.4.refs_0_, ...), custom_call_target="tpu_custom_call" | custom-call | flops 25165824 | bytes 1703936 | tf_op jit(solution)/shard_map/peer_products_0/pallas_call | solution.py:301
  25.8 1.3 %collective-permute-start.5 = (s32[136,128]{1,0:T(8,128)S(1)}, s32[136,128]{1,0:T(8,128)S(1)}, u32[]{:S(2)}, u32[]{:S(2)}) collective-permute-start(s32[136,128]{1,0:T(8,128)S(1)} %get-tuple-element.33), channel_id=1, source_target_pairs={{3,0},{0,1},{1,2},{2,3},{7,4},{4,5},{5,6},{6,7},{11,8},{8,9},{9,10... | collective-permute-start | bytes 208904 | tf_op jit(solution)/shard_map/ppermute | solution.py:18
  27.0 2.8 %collective-permute-start.6 = (s32[136,128]{1,0:T(8,128)S(1)}, s32[136,128]{1,0:T(8,128)S(1)}, u32[]{:S(2)}, u32[]{:S(2)}) collective-permute-start(s32[136,128]{1,0:T(8,128)S(1)} %get-tuple-element.34), channel_id=1, source_target_pairs={{2,0},{3,1},{0,2},{1,3},{6,4},{7,5},{4,6},{5,7},{10,8},{11,9},{8,1... | collective-permute-start | bytes 208904 | tf_op jit(solution)/shard_map/ppermute | solution.py:18
  29.8 1.4 %collective-permute-start.7 = (s32[136,128]{1,0:T(8,128)S(1)}, s32[136,128]{1,0:T(8,128)S(1)}, u32[]{:S(2)}, u32[]{:S(2)}) collective-permute-start(s32[136,128]{1,0:T(8,128)S(1)} %get-tuple-element.35), channel_id=1, source_target_pairs={{1,0},{2,1},{3,2},{0,3},{5,4},{6,5},{7,6},{4,7},{9,8},{10,9},{11,1... | collective-permute-start | bytes 208904 | tf_op jit(solution)/shard_map/ppermute | solution.py:18
  31.2 0.0 collective-permute-done.8.refs_0_
  31.2 1.3 %peer_products_1.1 = (f32[4,64,128]{2,1,0:T(8,128)S(1)}, s32[136,128]{1,0:T(8,128)S(1)}, s32[136,128]{1,0:T(8,128)S(1)}, s32[136,128]{1,0:T(8,128)S(1)}) custom-call(s32[2,3,52]{2,1,0:T(4,128)S(1)} %get-tuple-element.28.pairs, s32[2]{0:T(128)S(1)} %get-tuple-element.29.tally, bf16[24,64,128]{2,1,0:T(8,128)(2,1)S(1)} %collective-permute-done.8.refs_0_, ...), custom_call_target="tpu_custom_call" | custom-call | flops 25165824 | bytes 1703936 | tf_op jit(solution)/shard_map/peer_products_1/pallas_call | solution.py:301
  32.5 1.2 %collective-permute-start.10 = (s32[136,128]{1,0:T(8,128)S(1)}, s32[136,128]{1,0:T(8,128)S(1)}, u32[]{:S(2)}, u32[]{:S(2)}) collective-permute-start(s32[136,128]{1,0:T(8,128)S(1)} %get-tuple-element.39), channel_id=1, source_target_pairs={{2,0},{3,1},{0,2},{1,3},{6,4},{7,5},{4,6},{5,7},{10,8},{11,9},{8,1... | collective-permute-start | bytes 208904 | tf_op jit(solution)/shard_map/ppermute | solution.py:18
  33.7 1.9 %collective-permute-start.11 = (s32[136,128]{1,0:T(8,128)S(1)}, s32[136,128]{1,0:T(8,128)S(1)}, u32[]{:S(2)}, u32[]{:S(2)}) collective-permute-start(s32[136,128]{1,0:T(8,128)S(1)} %get-tuple-element.40), channel_id=1, source_target_pairs={{1,0},{2,1},{3,2},{0,3},{5,4},{6,5},{7,6},{4,7},{9,8},{10,9},{11,1... | collective-permute-start | bytes 208904 | tf_op jit(solution)/shard_map/ppermute | solution.py:18
  35.6 0.0 collective-permute-done.5.refs_1_
  35.6 0.2 collective-permute-start.9
  35.7 0.1 collective-permute-done.6.refs_2_
  35.8 0.0 collective-permute-done.7.refs_3_
  35.8 4.3 %collective-permute-done.10.refs_6_ = s32[136,128]{1,0:T(8,128)S(1)} collective-permute-done((s32[136,128]{1,0:T(8,128)S(1)}, s32[136,128]{1,0:T(8,128)S(1)}, u32[]{:S(2)}, u32[]{:S(2)}) %collective-permute-start.10) | collective-permute-done | bytes 69664 | tf_op jit(solution)/shard_map/ppermute | solution.py:18
  40.2 0.0 collective-permute-done.11.refs_7_
  40.2 1.5 %collective-permute-done.9.refs_5_ = s32[136,128]{1,0:T(8,128)S(1)} collective-permute-done((s32[136,128]{1,0:T(8,128)S(1)}, s32[136,128]{1,0:T(8,128)S(1)}, u32[]{:S(2)}, u32[]{:S(2)}) %collective-permute-start.9) | collective-permute-done | bytes 69664 | tf_op jit(solution)/shard_map/ppermute | solution.py:18
  41.7 0.8 %finish.1 = bf16[2,2,128,128]{3,2,1,0:T(8,128)(2,1)} custom-call(f32[4,64,128]{2,1,0:T(8,128)S(1)} %get-tuple-element.32.refs_0_, s32[136,128]{1,0:T(8,128)S(1)} %collective-permute-done.5.refs_1_, s32[136,128]{1,0:T(8,128)S(1)} %collective-permute-done.6.refs_2_, s32[136,128]{1,0:T(8,128)S(1)} %collective-permute-done.7.refs_3_, ...), custom_call_target="tpu_custom_call" | custom-call | tf_op jit(solution)/shard_map/finish/pallas_call | solution.py:321
  (1 shorter events, 0.0 us)
Async XLA Ops:
  0.0 20.2 %copy-start.1 = (bf16[2,2,128,128]{3,2,1,0:T(8,128)(2,1)S(1)}, bf16[2,2,128,128]{3,2,1,0:T(8,128)(2,1)}, u32[]{:S(2)}) copy-start(bf16[2,2,128,128]{3,2,1,0:T(8,128)(2,1)} %param.9) | copy-start | bytes 393220
  0.0 20.2 %copy-start.2 = (s32[2,2]{1,0:T(2,128)S(1)}, s32[2,2]{1,0:T(2,128)}, u32[]{:S(2)}) copy-start(s32[2,2]{1,0:T(2,128)} %refs_2_.1) | copy-start | bytes 52
  0.0 18.5 %copy-start = (bf16[24,128,128]{2,1,0:T(8,128)(2,1)S(1)}, bf16[24,128,128]{2,1,0:T(8,128)(2,1)}, u32[]{:S(2)}) copy-start(bf16[24,128,128]{2,1,0:T(8,128)(2,1)} %refs_4_.1) | copy-start | bytes 2359300
  0.0 20.1 %copy-start.4 = (s32[8,2]{0,1:T(2,128)S(1)}, s32[8,2]{0,1:T(2,128)}, u32[]{:S(2)}) copy-start(s32[8,2]{0,1:T(2,128)} %param.11) | copy-start | bytes 196
  2.3 17.9 %copy-start.3 = (s32[48]{0:T(128)S(1)}, s32[48]{0:T(128)}, u32[]{:S(2)}) copy-start(s32[48]{0:T(128)} %get-tuple-element.23.refs_0_) | copy-start | bytes 580
  2.4 16.2 %collective-permute-start.1 = (bf16[528,128]{1,0:T(8,128)(2,1)}, bf16[528,128]{1,0:T(8,128)(2,1)S(1)}, u32[]{:S(2)}, u32[]{:S(2)}) collective-permute-start(bf16[528,128]{1,0:T(8,128)(2,1)} %get-tuple-element.24), channel_id=1, source_target_pairs={{8,0},{16,8},{24,16},{0,24},{9,1},{17,9},{25,17},{1,25},{10,2},{18... | collective-permute-start | bytes 405512 | tf_op jit(solution)/shard_map/ppermute | solution.py:18
  4.8 13.7 %collective-permute-start.2 = (bf16[528,128]{1,0:T(8,128)(2,1)}, bf16[528,128]{1,0:T(8,128)(2,1)S(1)}, u32[]{:S(2)}, u32[]{:S(2)}) collective-permute-start(bf16[528,128]{1,0:T(8,128)(2,1)} %get-tuple-element.24), channel_id=1, source_target_pairs={{16,0},{24,8},{0,16},{8,24},{17,1},{25,9},{1,17},{9,25},{18,2},{26... | collective-permute-start | bytes 405512 | tf_op jit(solution)/shard_map/ppermute | solution.py:18
  5.5 13.1 %collective-permute-start.3 = (bf16[528,128]{1,0:T(8,128)(2,1)}, bf16[528,128]{1,0:T(8,128)(2,1)S(1)}, u32[]{:S(2)}, u32[]{:S(2)}) collective-permute-start(bf16[528,128]{1,0:T(8,128)(2,1)} %get-tuple-element.24), channel_id=1, source_target_pairs={{24,0},{0,8},{8,16},{16,24},{25,1},{1,9},{9,17},{17,25},{26,2},{2,... | collective-permute-start | bytes 405512 | tf_op jit(solution)/shard_map/ppermute | solution.py:18
  6.7 17.8 %collective-permute-start.4 = (bf16[24,64,128]{2,1,0:T(8,128)(2,1)S(1)}, bf16[24,64,128]{2,1,0:T(8,128)(2,1)S(1)}, u32[]{:S(2)}, u32[]{:S(2)}) collective-permute-start(bf16[24,64,128]{2,1,0:T(8,128)(2,1)S(1)} %slice.6), channel_id=1, source_target_pairs={{4,0},{0,4},{5,1},{1,5},{6,2},{2,6},{7,3},{3,7},{12,8},{8,12},{13,... | collective-permute-start | bytes 1179656 | tf_op jit(solution)/shard_map/ppermute | solution.py:18
  8.2 10.3 %collective-permute-start = (s32[48]{0:T(128)}, s32[48]{0:T(128)S(1)}, u32[]{:S(2)}, u32[]{:S(2)}) collective-permute-start(s32[48]{0:T(128)} %get-tuple-element.23.refs_0_), channel_id=1, source_target_pairs={{4,0},{0,4},{5,1},{1,5},{6,2},{2,6},{7,3},{3,7},{12,8},{8,12},{13,... | collective-permute-start | bytes 584 | tf_op jit(solution)/shard_map/ppermute | solution.py:18
  18.6 12.6 %collective-permute-start.8 = (bf16[24,64,128]{2,1,0:T(8,128)(2,1)S(1)}, bf16[24,64,128]{2,1,0:T(8,128)(2,1)S(1)}, u32[]{:S(2)}, u32[]{:S(2)}) collective-permute-start(bf16[24,64,128]{2,1,0:T(8,128)(2,1)S(1)} %slice.7), channel_id=1, source_target_pairs={{4,0},{0,4},{5,1},{1,5},{6,2},{2,6},{7,3},{3,7},{12,8},{8,12},{13,... | collective-permute-start | bytes 1179656 | tf_op jit(solution)/shard_map/ppermute | solution.py:18
  25.8 9.8 %collective-permute-start.5 = (s32[136,128]{1,0:T(8,128)S(1)}, s32[136,128]{1,0:T(8,128)S(1)}, u32[]{:S(2)}, u32[]{:S(2)}) collective-permute-start(s32[136,128]{1,0:T(8,128)S(1)} %get-tuple-element.33), channel_id=1, source_target_pairs={{3,0},{0,1},{1,2},{2,3},{7,4},{4,5},{5,6},{6,7},{11,8},{8,9},{9,10... | collective-permute-start | bytes 208904 | tf_op jit(solution)/shard_map/ppermute | solution.py:18
  27.0 8.8 %collective-permute-start.6 = (s32[136,128]{1,0:T(8,128)S(1)}, s32[136,128]{1,0:T(8,128)S(1)}, u32[]{:S(2)}, u32[]{:S(2)}) collective-permute-start(s32[136,128]{1,0:T(8,128)S(1)} %get-tuple-element.34), channel_id=1, source_target_pairs={{2,0},{3,1},{0,2},{1,3},{6,4},{7,5},{4,6},{5,7},{10,8},{11,9},{8,1... | collective-permute-start | bytes 208904 | tf_op jit(solution)/shard_map/ppermute | solution.py:18
  29.8 6.0 %collective-permute-start.7 = (s32[136,128]{1,0:T(8,128)S(1)}, s32[136,128]{1,0:T(8,128)S(1)}, u32[]{:S(2)}, u32[]{:S(2)}) collective-permute-start(s32[136,128]{1,0:T(8,128)S(1)} %get-tuple-element.35), channel_id=1, source_target_pairs={{1,0},{2,1},{3,2},{0,3},{5,4},{6,5},{7,6},{4,7},{9,8},{10,9},{11,1... | collective-permute-start | bytes 208904 | tf_op jit(solution)/shard_map/ppermute | solution.py:18
  32.5 7.7 %collective-permute-start.10 = (s32[136,128]{1,0:T(8,128)S(1)}, s32[136,128]{1,0:T(8,128)S(1)}, u32[]{:S(2)}, u32[]{:S(2)}) collective-permute-start(s32[136,128]{1,0:T(8,128)S(1)} %get-tuple-element.39), channel_id=1, source_target_pairs={{2,0},{3,1},{0,2},{1,3},{6,4},{7,5},{4,6},{5,7},{10,8},{11,9},{8,1... | collective-permute-start | bytes 208904 | tf_op jit(solution)/shard_map/ppermute | solution.py:18
  33.7 6.5 %collective-permute-start.11 = (s32[136,128]{1,0:T(8,128)S(1)}, s32[136,128]{1,0:T(8,128)S(1)}, u32[]{:S(2)}, u32[]{:S(2)}) collective-permute-start(s32[136,128]{1,0:T(8,128)S(1)} %get-tuple-element.40), channel_id=1, source_target_pairs={{1,0},{2,1},{3,2},{0,3},{5,4},{6,5},{7,6},{4,7},{9,8},{10,9},{11,1... | collective-permute-start | bytes 208904 | tf_op jit(solution)/shard_map/ppermute | solution.py:18
  35.6 6.1 %collective-permute-start.9 = (s32[136,128]{1,0:T(8,128)S(1)}, s32[136,128]{1,0:T(8,128)S(1)}, u32[]{:S(2)}, u32[]{:S(2)}) collective-permute-start(s32[136,128]{1,0:T(8,128)S(1)} %get-tuple-element.38), channel_id=1, source_target_pairs={{3,0},{0,1},{1,2},{2,3},{7,4},{4,5},{5,6},{6,7},{11,8},{8,9},{9,10... | collective-permute-start | bytes 208904 | tf_op jit(solution)/shard_map/ppermute | solution.py:18

commit v5 on v3

v5 whole, which is shorter than its diff:
```python
import functools

import jax
import jax.numpy as jnp
from jax import lax
from jax.experimental import pallas as pl
from jax.experimental.pallas import tpu as pltpu
from jax.sharding import PartitionSpec as P

CHUNKS = 2
GROUP = 4
LANES = 128
MIB = 2**20


def shifted(value, axis, offset):
    size = lax.axis_size(axis)
    return lax.ppermute(value, axis, [((i + offset) % size, i) for i in range(size)])


def quotient(value, by):
    return value >> (by.bit_length() - 1) if by & (by - 1) == 0 else lax.div(value, by)


def remainder(value, by):
    return value & (by - 1) if by & (by - 1) == 0 else lax.rem(value, by)


def note_rows(how_many):
    digits = (how_many + LANES - 1) // LANES
    return (2 * digits + 15) // 16 * 16, digits


def with_notes(payload, values):
    (how_many,) = values.shape
    height, digits = note_rows(how_many)
    values = jnp.pad(values, (0, digits * LANES - how_many)).reshape(digits, LANES)
    tile = jnp.concatenate([values & (LANES - 1), values >> (LANES.bit_length() - 1)])
    tile = jnp.pad(tile, ((0, height - 2 * digits), (0, 0)))
    return jnp.concatenate([payload, tile.astype(payload.dtype)])


def read_notes(payload, start, how_many, whole, notes, sem):
    height, _ = note_rows(how_many)
    whole[...] = payload[start : start + height].astype(jnp.float32).astype(jnp.int32)
    copy = pltpu.make_async_copy(whole, notes, sem)
    copy.start()
    return copy


def note(notes, how_many, p):
    _, digits = note_rows(how_many)
    return notes[p // LANES, p % LANES] + notes[digits + p // LANES, p % LANES] * LANES


def list_pairs(sizes, row_of, col_of, context, panel_cols, kept_cols, pairs, tally, j):
    rows, layers, count, piece_rows, width, local_rows, kept = sizes
    own_rows = local_rows // layers
    here, layer = context[0], context[1]

    def one_block(n, total):
        row = row_of(n) - here * local_rows
        inner = col_of(n)
        owner = quotient(inner, piece_rows * layers)
        inner = remainder(inner, piece_rows)
        right = (remainder(owner - here + rows, rows) * piece_rows + inner) * width
        goal = remainder(quotient(row, own_rows) - layer + layers, layers)
        goal = (goal * own_rows + remainder(row, own_rows)) * kept
        for s in range(width):
            wanted = panel_cols[right + s]
            hit, slot = jnp.int32(0), goal
            for t in range(kept):
                same = (kept_cols[goal + t] == wanted).astype(jnp.int32)
                hit += same
                slot += t * same
            pairs[j, 0, total] = n
            pairs[j, 1, total] = right + s
            pairs[j, 2, total] = slot
            total += hit
        return total

    total = lax.fori_loop(0, count, one_block, jnp.int32(0))
    for g in range(GROUP):
        pairs[j, 0, total + g] = 0
        pairs[j, 1, total + g] = 0
        pairs[j, 2, total + g] = local_rows * kept
    tally[j] = total


def add_products(left, panel, totals, pairs, tally, j):
    def one_group(group, carry):
        base = group * GROUP
        products = [
            jnp.dot(
                left(pairs[j, 0, base + g]),
                panel[pairs[j, 1, base + g]],
                preferred_element_type=jnp.float32,
            )
            for g in range(GROUP)
        ]
        for g in range(GROUP):
            totals[pairs[j, 2, base + g]] += products[g]
        return carry

    lax.fori_loop(0, quotient(tally[j] + GROUP - 1, GROUP), one_group, 0)


def own_kernel(sizes, *refs):
    rows, layers, count, piece_rows, width, local_rows, kept, order = sizes
    a_rows, a_cols, s_cols, c_cols, x_in, s_in = refs[:6]
    s_other, refs = refs[6 : 5 + rows], refs[5 + rows :]
    totals, panel, panel_cols, kept_cols, context = refs[:5]
    pairs, tally, whole, notes, s_sem, note_sem = refs[5:]
    piece = piece_rows * width
    loads = [pltpu.make_async_copy(s_in, panel.at[pl.ds(0, piece)], s_sem.at[0])]
    for d in range(1, rows):
        loads += [
            pltpu.make_async_copy(
                s_other[d - 1].at[pl.ds(q * order, order)],
                panel.at[d * piece + q],
                s_sem.at[d * piece + q],
            )
            for q in range(piece)
        ]
    reads = [
        read_notes(s_other[d], piece * order, piece, whole.at[d], notes.at[d], note_sem.at[d])
        for d in range(rows - 1)
    ]
    for load in loads:
        load.start()
    totals[...] = jnp.zeros_like(totals)
    layer = remainder(quotient(a_cols[0], piece_rows), layers)
    context[0] = quotient(a_rows[0], local_rows)
    context[1] = layer
    own_rows = local_rows // layers
    for g in range(layers):
        base = remainder(layer + g, layers) * own_rows
        for i in range(own_rows):
            for t in range(kept):
                kept_cols[(g * own_rows + i) * kept + t] = c_cols[base + i, t]
    for read in reads:
        read.wait()
    for q in range(piece):
        panel_cols[q] = s_cols[q // width, q % width]
        for d in range(1, rows):
            panel_cols[d * piece + q] = note(notes.at[d - 1], piece, q)
    list_pairs(
        (rows, layers, count, piece_rows, width, local_rows, kept),
        lambda n: a_rows[n],
        lambda n: a_cols[n],
        context,
        panel_cols,
        kept_cols,
        pairs,
        tally,
        0,
    )
    for load in loads:
        load.wait()
    add_products(lambda n: x_in[n], panel, totals, pairs, tally, 0)


def peer_kernel(sizes, first, context, *refs):
    rows, cols, layers, count, piece_rows, width, local_rows, kept, height = sizes
    slots = local_rows * kept // layers
    if first == 0:
        panel_cols, kept_cols, *refs = refs
    else:
        pairs, tally, *refs = refs
    x_in, refs = refs[: cols - 1], refs[cols - 1 :]
    panel, before, own, sent, *refs = refs
    if first == 0:
        pairs, tally, totals, whole, notes, note_sem = refs
        reads = [
            read_notes(x_in[j], count * height, 2 * count, whole.at[j], notes.at[j], note_sem.at[j])
            for j in range(cols - 1)
        ]
    else:
        (totals,) = refs
    totals[...] = before[:, first : first + height]
    if first == 0:
        for j in range(cols - 1):
            reads[j].wait()
            list_pairs(
                (rows, layers, count, piece_rows, width, local_rows, kept),
                lambda n: note(notes.at[j], 2 * count, n),
                lambda n: note(notes.at[j], 2 * count, count + n),
                context,
                panel_cols,
                kept_cols,
                pairs,
                tally,
                j,
            )

    for j in range(cols - 1):

        def left(n):
            return x_in[j][pl.ds(pl.multiple_of(n * height, height), height)]

        add_products(left, panel, totals, pairs, tally, j)

    own[...] = totals[:slots]
    half = height // 2
    for d in range(1, layers):
        code = sent.at[remainder(context[1] + d, layers)]
        spare = code.shape[0] - slots * half
        code[slots * half :] = jnp.zeros((spare, code.shape[1]), jnp.int32)
        for u in range(slots):
            value = totals[d * slots + u]
            peak = jnp.max(jnp.abs(value), axis=0, keepdims=True)
            power = jnp.floor(jnp.log2(jnp.maximum(peak, 1e-30)) + 1e-3) + 1.0
            word = jnp.floor(value * jnp.exp2(15.0 - power) + 0.5).astype(jnp.int32)
            code[pl.ds(u * half, half)] = (word[:half] << 16) | (word[half:] & 0xFFFF)
            code[pl.ds(slots * half + u, 1)] = power.astype(jnp.int32)


def finish_kernel(sizes, context, *refs):
    layers, chunks, slots, height = sizes
    result = refs[-1]
    kept = result.shape[1]
    half = height // 2
    for c in range(chunks):
        own, codes = refs[2 * c], refs[2 * c + 1]
        for u in range(slots):
            high, low = own[u, :half], own[u, half:]
            for d in range(1, layers):
                code = codes.at[remainder(context[1] + d, layers)]
                word = code[pl.ds(u * half, half)]
                power = code[pl.ds(slots * half + u, 1)].astype(jnp.float32)
                scale = jnp.exp2(power - 15.0)
                high += (word >> 16).astype(jnp.float32) * scale
                low += ((word << 16) >> 16).astype(jnp.float32) * scale
            at = c * height
            result[u // kept, u % kept, at : at + half] = high.astype(jnp.bfloat16)
            result[u // kept, u % kept, at + half : at + height] = low.astype(jnp.bfloat16)


def per_device(a_blocks, a_rows, a_cols, s_blocks, s_cols, c_cols):
    rows, cols, layers = (lax.axis_size(axis) for axis in ("row", "col", "layer"))
    count, order = a_blocks.shape[:2]
    piece_rows, width = s_cols.shape
    local_rows, kept = c_cols.shape
    own_rows = local_rows // layers
    slots = own_rows * kept
    all_slots = layers * slots
    height = order // CHUNKS
    piece = piece_rows * width
    panel_size = rows * piece
    block_size = order * order
    flat_s = s_blocks.reshape(piece, order, order)
    x_note_rows, _ = note_rows(2 * count)
    s_note_rows, _ = note_rows(piece)

    scalars = pl.BlockSpec(memory_space=pltpu.SMEM)
    vector = pl.BlockSpec(memory_space=pltpu.VMEM)

    def x_chunk(blocks, c):
        part = lax.slice_in_dim(blocks, c * height, (c + 1) * height, axis=1)
        return part.reshape(count * height, order)

    x_first = with_notes(x_chunk(a_blocks, 0), jnp.concatenate([a_rows, a_cols]))
    x_pieces = [[shifted(x_first, "col", j) for j in range(1, cols)]]
    s_sent = with_notes(flat_s.reshape(piece * order, order), s_cols.reshape(-1))
    s_pieces = [shifted(s_sent, "row", d) for d in range(1, rows)]
    later_blocks, _ = lax.optimization_barrier((a_blocks, x_first))
    for c in range(1, CHUNKS):
        part = x_chunk(later_blocks, c)
        x_pieces.append([shifted(part, "col", j) for j in range(1, cols)])

    moved = block_size * (4 * all_slots + 4 * panel_size + 2 * count)
    totals, panel, panel_cols, kept_cols, context = pl.pallas_call(
        functools.partial(
            own_kernel, (rows, layers, count, piece_rows, width, local_rows, kept, order)
        ),
        out_shape=[
            jax.ShapeDtypeStruct((all_slots + 1, order, order), jnp.float32),
            jax.ShapeDtypeStruct((panel_size, order, order), jnp.bfloat16),
            jax.ShapeDtypeStruct((panel_size,), jnp.int32),
            jax.ShapeDtypeStruct((all_slots,), jnp.int32),
            jax.ShapeDtypeStruct((2,), jnp.int32),
        ],
        in_specs=[scalars] * 4 + [vector] * (1 + rows),
        out_specs=[vector] * 2 + [scalars] * 3,
        scratch_shapes=[
            pltpu.SMEM((1, 3, count * width + GROUP), jnp.int32),
            pltpu.SMEM((1,), jnp.int32),
            pltpu.VMEM((rows - 1, s_note_rows, LANES), jnp.int32),
            pltpu.SMEM((rows - 1, s_note_rows, LANES), jnp.int32),
            pltpu.SemaphoreType.DMA((panel_size,)),
            pltpu.SemaphoreType.DMA((rows - 1,)),
        ],
        compiler_params=pltpu.CompilerParams(vmem_limit_bytes=moved + 4 * MIB),
        cost_estimate=pl.CostEstimate(
            flops=2 * order**3 * count * width // 4, bytes_accessed=moved, transcendentals=0
        ),
        name="own_products",
    )(a_rows, a_cols, s_cols, c_cols, a_blocks, flat_s, *s_pieces)

    code_rows = slots * (height // 2) + (slots + 7) // 8 * 8
    moved = block_size * (8 * all_slots + 2 * panel_size + 2 * count * (cols - 1))
    pair_shapes = [(cols - 1, 3, count * width + GROUP), (cols - 1,)]
    final, plan = [], []
    for c in range(CHUNKS):
        out_shape = [
            jax.ShapeDtypeStruct((slots, height, order), jnp.float32),
            jax.ShapeDtypeStruct((layers, code_rows, order), jnp.int32),
        ]
        out_specs = [vector] * 2
        scratch = [pltpu.VMEM((all_slots + 1, height, order), jnp.float32)]
        if c == 0:
            out_shape += [jax.ShapeDtypeStruct(shape, jnp.int32) for shape in pair_shapes]
            out_specs += [scalars] * 2
            scratch += [
                pltpu.VMEM((cols - 1, x_note_rows, LANES), jnp.int32),
                pltpu.SMEM((cols - 1, x_note_rows, LANES), jnp.int32),
                pltpu.SemaphoreType.DMA((cols - 1,)),
            ]
        own, sent, *made = pl.pallas_call(
            functools.partial(
                peer_kernel,
                (rows, cols, layers, count, piece_rows, width, local_rows, kept, height),
                c * height,
            ),
            out_shape=out_shape,
            in_specs=[scalars] * 3 + [vector] * (cols + 1),
            out_specs=out_specs,
            scratch_shapes=scratch,
            compiler_params=pltpu.CompilerParams(vmem_limit_bytes=moved + 4 * MIB),
            cost_estimate=pl.CostEstimate(
                flops=2 * order**2 * height * count * width // 4 * (cols - 1),
                bytes_accessed=moved // CHUNKS,
                transcendentals=0,
            ),
            name=f"peer_products_{c}",
        )(context, *(plan or (panel_cols, kept_cols)), *x_pieces[c], panel, totals)
        plan = plan or made
        final += [own, lax.all_to_all(sent, "layer", 0, 0, tiled=True)]

    return pl.pallas_call(
        functools.partial(finish_kernel, (layers, CHUNKS, slots, height)),
        out_shape=jax.ShapeDtypeStruct((own_rows, kept, order, order), jnp.bfloat16),
        in_specs=[scalars] + [vector] * len(final),
        out_specs=vector,
        compiler_params=pltpu.CompilerParams(
            vmem_limit_bytes=16 * slots * order * order + 4 * MIB
        ),
        name="finish",
    )(context, *final)


def solution(mesh):
    placed = (
        P(("row", "col", "layer"), None, None),
        P(("row", "col", "layer")),
        P(("row", "col", "layer")),
        P(("row", "layer"), "col", None, None),
        P(("row", "layer"), "col"),
        P("row", "col"),
    )
    return jax.shard_map(
        per_device,
        mesh=mesh,
        in_specs=placed,
        out_specs=P(("row", "layer"), "col", None, None),
        check_vma=False,
    )
```

time: 39.6 us -> 51.8 us (1.31)
  blocking collectives: 0 us -> 12.3 us
  waiting for transfers between devices: 10.8 us -> 15.9 us
  starting transfers between devices: 15.3 us -> 10.4 us
  Pallas kernels: 11.8 us -> 9.96 us
  local copies, waits for them, and re-layouts: 0.13 us -> 1.23 us
    all_to_all x0 -> x1, blocking collectives: none -> 12.3 us  [per_device(): final += [own, lax.all_to_all(sent, 'layer', 0, 0, tiled=True)]]
    ppermute x11 -> x5, starting transfers between devices: 15.3 us -> 5.54 us  [shifted(): lax.ppermute(value, axis, [((i + offset) % size, i) for i in range(size)])]
    ppermute x11 -> x5, waiting for transfers between devices: 10.8 us -> 15.8 us  [shifted(): lax.ppermute(value, axis, [((i + offset) % size, i) for i in range(size)])]
    all_to_all x0 -> x1, starting transfers between devices: none -> 4.88 us  [per_device(): final += [own, lax.all_to_all(sent, 'layer', 0, 0, tiled=True)]]
    pallas_call x3 -> x2, Pallas kernels: 7.13 us -> 5.23 us  [per_device(): pl.pallas_call(functools.partial(peer_kernel, (rows, cols, layers, count,...]
    concatenate x0 -> x5, other arithmetic: none -> 1.64 us  [the longest x1 0.83 us: per_device(): jnp.concatenate([a_rows, a_cols])]
    mul x1 -> x0, other arithmetic: 1.35 us -> none  [per_device(): goals = goals * kept]
    slice x1 -> x2, local copies, waits for them, and re-layouts: 0.03 us -> 1.05 us  [x_chunk(): part = lax.slice_in_dim(blocks, c * height, (c + 1) * height, axis=1)]
  transfers between devices with their start and end apart: 11 -> 6, of which waited for: 4 -> 3; matrix products, arithmetic and copies ran while one was open for 0% -> 0% of each run, Pallas kernels for 20% -> 10%
where the time goes in v5:
time: 51.8 us; the launch traced here: 51.6 us
  waiting for transfers between devices  15.9 us (31%)
  blocking collectives  12.3 us (24%)
  starting transfers between devices  10.4 us (20%)
  Pallas kernels  9.96 us (19%)
  other arithmetic  1.66 us (3%)
  local copies, waits for them, and re-layouts  1.23 us (2%)
    ppermute x5, waiting for transfers between devices, shifted(): lax.ppermute(value, axis, [((i + offset) % size, i) for i in range(size)])  15.8 us
    all_to_all x1, blocking collectives, per_device(): final += [own, lax.all_to_all(sent, 'layer', 0, 0, tiled=True)]  12.3 us
    ppermute x5, starting transfers between devices, shifted(): lax.ppermute(value, axis, [((i + offset) % size, i) for i in range(size)])  5.54 us
    pallas_call x2, Pallas kernels, per_device(): pl.pallas_call(functools.partial(peer_kernel, (rows, cols, layers, count,...  5.23 us
    all_to_all x1, starting transfers between devices, per_device(): final += [own, lax.all_to_all(sent, 'layer', 0, 0, tiled=True)]  4.88 us
    pallas_call x1, Pallas kernels, per_device(): pl.pallas_call(functools.partial(own_kernel, (rows, layers, count, piece_...  3.38 us
    pallas_call x1, Pallas kernels, per_device(): pl.pallas_call(functools.partial(finish_kernel, (layers, CHUNKS, slots, h...  1.34 us
    slice x2, local copies, waits for them, and re-layouts, x_chunk(): part = lax.slice_in_dim(blocks, c * height, (c + 1) * height, axis=1)  1.05 us
  transfers between devices with their start and end apart: 6, of which 3 were waited for; matrix products, arithmetic and copies ran while one was open for 0% of the time, Pallas kernels for 10%

profile of v5, /device:TPU:0, one launch (start us, length us, event | category | flops | bytes accessed | tf_op | source)
XLA Modules:
  0.0 51.6 jit_solution(2265637893937105764)
XLA Ops:
  0.0 0.0 copy-start.3
  0.0 0.0 copy-start.4
  0.0 0.0 copy-start
  0.0 0.0 copy-start.2
  0.0 0.0 copy-start.1
  0.0 0.0 copy-start.5
  0.0 0.8 %pad_add_fusion = s32[48]{0:T(128)S(1)} fusion(s32[24]{0:T(128)} %refs_1_.1, s32[24]{0:T(128)} %refs_0_.1), kind=kLoop, calls=%fused_computation.9 | loop fusion | flops 48 | bytes 384 | tf_op jit(solution)/shard_map/concatenate | solution.py:262
  0.9 1.0 %slice.6 = bf16[24,64,128]{2,1,0:T(8,128)(2,1)S(1)} slice(bf16[24,128,128]{2,1,0:T(8,128)(2,1)} %refs_4_.1), slice={[0:24], [0:64], [0:128]} | slice | bytes 786432 | tf_op jit(solution)/shard_map/slice | solution.py:259
  1.9 0.8 %pad_maximum_fusion = bf16[1552,128]{1,0:T(8,128)(2,1)} fusion(bf16[16,128]{1,0:T(8,128)(2,1)S(1)} %fusion.5, bf16[1536,128]{1,0:T(8,128)(2,1)S(1)} %bitcast.14), kind=kLoop, calls=%fused_computation | loop fusion | flops 794624 | bytes 794624 | tf_op jit(solution)/shard_map/concatenate | solution.py:40
  2.7 3.0 %collective-permute-start.3 = (bf16[1552,128]{1,0:T(8,128)(2,1)}, bf16[1552,128]{1,0:T(8,128)(2,1)S(1)}, u32[]{:S(2)}, u32[]{:S(2)}) collective-permute-start(bf16[1552,128]{1,0:T(8,128)(2,1)} %pad_maximum_fusion), channel_id=1, source_target_pairs={{4,0},{0,4},{5,1},{1,5},{6,2},{2,6},{7,3},{3,7},{12,8},{8,12},{13,... | collective-permute-start | bytes 1191944 | tf_op jit(solution)/shard_map/ppermute | solution.py:18
  5.6 0.0 copy-done.2
  5.6 0.1 reshape.23
  5.7 0.0 copy-done.1
  5.8 0.7 %collective-permute-start = (bf16[528,128]{1,0:T(8,128)(2,1)S(1)}, bf16[528,128]{1,0:T(8,128)(2,1)S(1)}, u32[]{:S(2)}, u32[]{:S(2)}) collective-permute-start(bf16[528,128]{1,0:T(8,128)(2,1)S(1)} %pad_maximum_fusion.1), channel_id=1, source_target_pairs={{8,0},{16,8},{24,16},{0,24},{9,1},{17,9},{25,17},{1,25},{10,2},{18... | collective-permute-start | bytes 405512 | tf_op jit(solution)/shard_map/ppermute | solution.py:18
  6.5 0.9 %collective-permute-start.1 = (bf16[528,128]{1,0:T(8,128)(2,1)S(1)}, bf16[528,128]{1,0:T(8,128)(2,1)S(1)}, u32[]{:S(2)}, u32[]{:S(2)}) collective-permute-start(bf16[528,128]{1,0:T(8,128)(2,1)S(1)} %pad_maximum_fusion.1), channel_id=1, source_target_pairs={{16,0},{24,8},{0,16},{8,24},{17,1},{25,9},{1,17},{9,25},{18,2},{26... | collective-permute-start | bytes 405512 | tf_op jit(solution)/shard_map/ppermute | solution.py:18
  7.4 0.2 collective-permute-start.2
  7.6 0.0 copy-done.5
  7.6 0.1 copy.7.refs_3_
  7.7 2.5 %collective-permute-done.refs_6_ = bf16[528,128]{1,0:T(8,128)(2,1)S(1)} collective-permute-done((bf16[528,128]{1,0:T(8,128)(2,1)S(1)}, bf16[528,128]{1,0:T(8,128)(2,1)S(1)}, u32[]{:S(2)}, u32[]{:S(2)}) %collective-permute-start) | collective-permute-done | bytes 135200 | tf_op jit(solution)/shard_map/ppermute | solution.py:18
  10.2 4.5 %collective-permute-done.1.refs_7_ = bf16[528,128]{1,0:T(8,128)(2,1)S(1)} collective-permute-done((bf16[528,128]{1,0:T(8,128)(2,1)S(1)}, bf16[528,128]{1,0:T(8,128)(2,1)S(1)}, u32[]{:S(2)}, u32[]{:S(2)}) %collective-permute-start.1) | collective-permute-done | bytes 135200 | tf_op jit(solution)/shard_map/ppermute | solution.py:18
  14.6 0.0 collective-permute-done.2.refs_8_
  14.7 0.0 copy-done.3
  14.7 0.0 copy-done.4
  14.7 0.0 copy-done
  14.7 3.4 %own_products.1 = (f32[17,128,128]{2,1,0:T(8,128)S(1)}, bf16[16,128,128]{2,1,0:T(8,128)(2,1)S(1)}, s32[16]{0:T(128)S(1)}, s32[16]{0:T(128)S(1)}, s32[2]{0:T(128)S(1)}) custom-call(s32[24]{0:T(128)S(1)} %copy-done.3, s32[24]{0:T(128)S(1)} %copy-done.4, s32[2,2]{1,0:T(2,128)S(1)} %copy-done.2, s32[8,2]{1,0:T(8,128)S(1)} %copy.7.refs_3_, ...), custom_call_target="tpu_custom_call" | custom-call | flops 50331648 | bytes 2883584 | tf_op jit(solution)/shard_map/own_products/pallas_call | solution.py:272
  18.1 0.0 collective-permute-done.3.refs_2_
  18.1 3.5 %peer_products_0.1 = (f32[4,64,128]{2,1,0:T(8,128)S(1)}, s32[4,136,128]{2,1,0:T(8,128)}, s32[1,3,52]{2,1,0:T(4,128)S(1)}, s32[1]{0:T(128)}) custom-call(s32[2]{0:T(128)S(1)} %get-tuple-element.17.context, s32[16]{0:T(128)S(1)} %get-tuple-element.18.refs_0_, s32[16]{0:T(128)S(1)} %get-tuple-element.19.refs_1_, ...), custom_call_target="tpu_custom_call" | custom-call | flops 25165824 | bytes 1703936 | tf_op jit(solution)/shard_map/peer_products_0/pallas_call | solution.py:319
  21.6 4.9 %all-to-all-start = ((s32[4,136,128]{2,1,0:T(8,128)}), s32[4,136,128]{2,1,0:T(8,128)S(1)}, u32[]{:S(2)}, u32[]{:S(2)}) async-start(s32[4,136,128]{2,1,0:T(8,128)} %get-tuple-element.23), calls=%async_computation | async-start | bytes 557056 | tf_op jit(solution)/shard_map/all_to_all | solution.py:338
  26.5 0.8 %collective-permute-start.4 = (bf16[1536,128]{1,0:T(8,128)(2,1)S(1)}, bf16[1536,128]{1,0:T(8,128)(2,1)S(1)}, u32[]{:S(2)}, u32[]{:S(2)}) collective-permute-start(bf16[1536,128]{1,0:T(8,128)(2,1)S(1)} %bitcast.15), channel_id=1, source_target_pairs={{4,0},{0,4},{5,1},{1,5},{6,2},{2,6},{7,3},{3,7},{12,8},{8,12},{13,... | collective-permute-start | bytes 1179656 | tf_op jit(solution)/shard_map/ppermute | solution.py:18
  27.3 8.8 %collective-permute-done.4.refs_2_ = bf16[1536,128]{1,0:T(8,128)(2,1)S(1)} collective-permute-done((bf16[1536,128]{1,0:T(8,128)(2,1)S(1)}, bf16[1536,128]{1,0:T(8,128)(2,1)S(1)}, u32[]{:S(2)}, u32[]{:S(2)}) %collective-permute-start.4) | collective-permute-done | bytes 393248 | tf_op jit(solution)/shard_map/ppermute | solution.py:18
  36.1 1.7 %peer_products_1.1 = (f32[4,64,128]{2,1,0:T(8,128)S(1)}, s32[4,136,128]{2,1,0:T(8,128)S(1)}) custom-call(s32[2]{0:T(128)S(1)} %get-tuple-element.17.context, s32[1,3,52]{2,1,0:T(4,128)S(1)} %get-tuple-element.24.refs_0_, s32[1]{0:T(128)} %get-tuple-element.25.refs_1_, bf16[1536,128]{1,0:T(8,128)(2,1)S(1)} %collective-permute-done.4.refs_2_, ...), custom_call_target="tpu_custom_call" | custom-call | flops 25165824 | bytes 1703936 | tf_op jit(solution)/shard_map/peer_products_1/pallas_call | solution.py:319
  37.9 0.0 all-to-all-done.refs_1_
  37.9 12.3 %all_to_all.10.refs_3_ = s32[4,136,128]{2,1,0:T(8,128)S(1)} all-to-all(s32[4,136,128]{2,1,0:T(8,128)S(1)} %get-tuple-element.28), channel_id=1, replica_groups=mesh['row'=4,'col'=2,'layer'=4] {'layer'}, dimensions={0} | all-to-all | bytes 557056 | tf_op jit(solution)/shard_map/all_to_all | solution.py:338
  50.2 1.3 %finish.1 = bf16[2,2,128,128]{3,2,1,0:T(8,128)(2,1)} custom-call(s32[2]{0:T(128)S(1)} %get-tuple-element.17.context, f32[4,64,128]{2,1,0:T(8,128)S(1)} %get-tuple-element.22.refs_0_, s32[4,136,128]{2,1,0:T(8,128)S(1)} %all-to-all-done.refs_1_, f32[4,64,128]{2,1,0:T(8,128)S(1)} %get-tuple-element.27.refs_2_, s32[4,136,128]{2,1,0:T(8,128)S(1)} %all_to_all.10.refs_3_), custom_call_target="tpu_custom_call" | custom-call | tf_op jit(solution)/shard_map/finish/pallas_call | solution.py:340
  (6 shorter events, 0.1 us)
Async XLA Ops:
  0.0 14.7 %copy-start.3 = (s32[24]{0:T(128)S(1)}, s32[24]{0:T(128)}, u32[]{:S(2)}) copy-start(s32[24]{0:T(128)} %refs_0_.1) | copy-start | bytes 292
  0.0 14.7 %copy-start.4 = (s32[24]{0:T(128)S(1)}, s32[24]{0:T(128)}, u32[]{:S(2)}) copy-start(s32[24]{0:T(128)} %refs_1_.1) | copy-start | bytes 292
  0.0 14.7 %copy-start = (bf16[24,128,128]{2,1,0:T(8,128)(2,1)S(1)}, bf16[24,128,128]{2,1,0:T(8,128)(2,1)}, u32[]{:S(2)}) copy-start(bf16[24,128,128]{2,1,0:T(8,128)(2,1)} %refs_4_.1) | copy-start | bytes 2359300
  0.0 5.6 %copy-start.2 = (s32[2,2]{1,0:T(2,128)S(1)}, s32[2,2]{1,0:T(2,128)}, u32[]{:S(2)}) copy-start(s32[2,2]{1,0:T(2,128)} %refs_2_.1) | copy-start | bytes 52
  0.0 5.7 %copy-start.1 = (bf16[2,2,128,128]{3,2,1,0:T(8,128)(2,1)S(1)}, bf16[2,2,128,128]{3,2,1,0:T(8,128)(2,1)}, u32[]{:S(2)}) copy-start(bf16[2,2,128,128]{3,2,1,0:T(8,128)(2,1)} %param.9) | copy-start | bytes 393220
  0.0 7.6 %copy-start.5 = (s32[8,2]{0,1:T(2,128)S(1)}, s32[8,2]{0,1:T(2,128)}, u32[]{:S(2)}) copy-start(s32[8,2]{0,1:T(2,128)} %param.11) | copy-start | bytes 196
  2.7 15.4 %collective-permute-start.3 = (bf16[1552,128]{1,0:T(8,128)(2,1)}, bf16[1552,128]{1,0:T(8,128)(2,1)S(1)}, u32[]{:S(2)}, u32[]{:S(2)}) collective-permute-start(bf16[1552,128]{1,0:T(8,128)(2,1)} %pad_maximum_fusion), channel_id=1, source_target_pairs={{4,0},{0,4},{5,1},{1,5},{6,2},{2,6},{7,3},{3,7},{12,8},{8,12},{13,... | collective-permute-start | bytes 1191944 | tf_op jit(solution)/shard_map/ppermute | solution.py:18
  5.8 4.4 %collective-permute-start = (bf16[528,128]{1,0:T(8,128)(2,1)S(1)}, bf16[528,128]{1,0:T(8,128)(2,1)S(1)}, u32[]{:S(2)}, u32[]{:S(2)}) collective-permute-start(bf16[528,128]{1,0:T(8,128)(2,1)S(1)} %pad_maximum_fusion.1), channel_id=1, source_target_pairs={{8,0},{16,8},{24,16},{0,24},{9,1},{17,9},{25,17},{1,25},{10,2},{18... | collective-permute-start | bytes 405512 | tf_op jit(solution)/shard_map/ppermute | solution.py:18
  6.5 8.1 %collective-permute-start.1 = (bf16[528,128]{1,0:T(8,128)(2,1)S(1)}, bf16[528,128]{1,0:T(8,128)(2,1)S(1)}, u32[]{:S(2)}, u32[]{:S(2)}) collective-permute-start(bf16[528,128]{1,0:T(8,128)(2,1)S(1)} %pad_maximum_fusion.1), channel_id=1, source_target_pairs={{16,0},{24,8},{0,16},{8,24},{17,1},{25,9},{1,17},{9,25},{18,2},{26... | collective-permute-start | bytes 405512 | tf_op jit(solution)/shard_map/ppermute | solution.py:18
  7.4 7.3 %collective-permute-start.2 = (bf16[528,128]{1,0:T(8,128)(2,1)S(1)}, bf16[528,128]{1,0:T(8,128)(2,1)S(1)}, u32[]{:S(2)}, u32[]{:S(2)}) collective-permute-start(bf16[528,128]{1,0:T(8,128)(2,1)S(1)} %pad_maximum_fusion.1), channel_id=1, source_target_pairs={{24,0},{0,8},{8,16},{16,24},{25,1},{1,9},{9,17},{17,25},{26,2},{2,... | collective-permute-start | bytes 405512 | tf_op jit(solution)/shard_map/ppermute | solution.py:18
  21.6 16.3 %all-to-all-start = ((s32[4,136,128]{2,1,0:T(8,128)}), s32[4,136,128]{2,1,0:T(8,128)S(1)}, u32[]{:S(2)}, u32[]{:S(2)}) async-start(s32[4,136,128]{2,1,0:T(8,128)} %get-tuple-element.23), calls=%async_computation | async-start | bytes 557056 | tf_op jit(solution)/shard_map/all_to_all | solution.py:338
  26.5 9.6 %collective-permute-start.4 = (bf16[1536,128]{1,0:T(8,128)(2,1)S(1)}, bf16[1536,128]{1,0:T(8,128)(2,1)S(1)}, u32[]{:S(2)}, u32[]{:S(2)}) collective-permute-start(bf16[1536,128]{1,0:T(8,128)(2,1)S(1)} %bitcast.15), channel_id=1, source_target_pairs={{4,0},{0,4},{5,1},{1,5},{6,2},{2,6},{7,3},{3,7},{12,8},{8,12},{13,... | collective-permute-start | bytes 1179656 | tf_op jit(solution)/shard_map/ppermute | solution.py:18

commit v6 on v4

--- a/solution.py
+++ b/solution.py
@@ -13,6 +13,19 @@
 MIB = 2**20
 
 
+def flipped(value, axis, bits):
+    return lax.ppermute(value, axis, [(i, i ^ bits) for i in range(lax.axis_size(axis))])
+
+
+def gathered(value, axis):
+    values = {0: value}
+    bit = lax.axis_size(axis) // 2
+    while bit:
+        values |= {d ^ bit: flipped(held, axis, bit) for d, held in values.items()}
+        bit //= 2
+    return [values[d] for d in range(len(values))]
+
+
 def shifted(value, axis, offset):
     size = lax.axis_size(axis)
     return lax.ppermute(value, axis, [((i + offset) % size, i) for i in range(size)])
@@ -31,16 +44,13 @@
     return (2 * digits + 15) // 16 * 16, digits
 
 
-def write_notes(payload, start, values):
-    height, digits = note_rows(len(values))
-    row = lax.broadcasted_iota(jnp.int32, (height, LANES), 0)
-    lane = lax.broadcasted_iota(jnp.int32, (height, LANES), 1)
-    tile = jnp.zeros((height, LANES), jnp.int32)
-    for p, value in enumerate(values):
-        here = lane == p % LANES
-        tile = jnp.where(here & (row == p // LANES), value & (LANES - 1), tile)
-        tile = jnp.where(here & (row == digits + p // LANES), quotient(value, LANES), tile)
-    payload[start : start + height] = tile.astype(jnp.float32).astype(jnp.bfloat16)
+def with_notes(payload, values):
+    (how_many,) = values.shape
+    height, digits = note_rows(how_many)
+    values = jnp.pad(values, (0, digits * LANES - how_many)).reshape(digits, LANES)
+    tile = jnp.concatenate([values & (LANES - 1), values >> (LANES.bit_length() - 1)])
+    tile = jnp.pad(tile, ((0, height - 2 * digits), (0, 0)))
+    return jnp.concatenate([payload, tile.astype(payload.dtype)])
 
 
 def read_notes(payload, start, how_many, whole, notes, sem):
@@ -56,35 +66,17 @@
     return notes[p // LANES, p % LANES] + notes[digits + p // LANES, p % LANES] * LANES
 
 
-def pack_kernel(sizes, a_rows, a_cols, s_cols, s_in, index, s_out, s_sem):
-    count, order, piece_rows, width = sizes
-    piece = piece_rows * width
-    loads = [
-        pltpu.make_async_copy(s_in.at[q], s_out.at[pl.ds(q * order, order)], s_sem.at[q])
-        for q in range(piece)
-    ]
-    for load in loads:
-        load.start()
-    for n in range(count):
-        index[n] = a_rows[n]
-        index[count + n] = a_cols[n]
-    write_notes(
-        s_out, piece * order, [s_cols[q, s] for q in range(piece_rows) for s in range(width)]
-    )
-    for load in loads:
-        load.wait()
-
-
-def list_pairs(sizes, index, here, layer, panel_cols, kept_cols, pairs, tally, j):
+def list_pairs(sizes, a_rows, a_cols, context, panel_cols, kept_cols, pairs, tally, j):
     rows, layers, count, piece_rows, width, local_rows, kept = sizes
     own_rows = local_rows // layers
+    here, layer = context[0], context[1]
 
     def one_block(n, total):
-        row = index[n] - here * local_rows
-        inner = index[count + n]
+        row = a_rows[n] - here * local_rows
+        inner = a_cols[n]
         owner = quotient(inner, piece_rows * layers)
         inner = remainder(inner, piece_rows)
-        right = (remainder(owner - here + rows, rows) * piece_rows + inner) * width
+        right = ((owner ^ here) * piece_rows + inner) * width
         goal = remainder(quotient(row, own_rows) - layer + layers, layers)
         goal = (goal * own_rows + remainder(row, own_rows)) * kept
         for s in range(width):
@@ -128,10 +120,11 @@
 
 def own_kernel(sizes, *refs):
     rows, cols, layers, count, piece_rows, width, local_rows, kept, order = sizes
-    index, s_cols, c_cols, x_in, s_in = refs[:cols], *refs[cols : cols + 4]
-    s_other, refs = refs[cols + 4 : cols + 3 + rows], refs[cols + 3 + rows :]
+    a_rows, a_cols, refs = refs[:cols], refs[cols : 2 * cols], refs[2 * cols :]
+    s_cols, c_cols, x_in, s_in = refs[:4]
+    s_other, refs = refs[4 : 3 + rows], refs[3 + rows :]
     totals, panel, pairs, tally = refs[:4]
-    panel_cols, kept_cols, whole, notes, s_sem, note_sem = refs[4:]
+    panel_cols, kept_cols, context, whole, notes, s_sem, note_sem = refs[4:]
     piece = piece_rows * width
     loads = [pltpu.make_async_copy(s_in, panel.at[pl.ds(0, piece)], s_sem.at[0])]
     for d in range(1, rows):
@@ -150,8 +143,9 @@
     for load in loads:
         load.start()
     totals[...] = jnp.zeros_like(totals)
-    here = quotient(index[0][0], local_rows)
-    layer = remainder(quotient(index[0][count], piece_rows), layers)
+    layer = remainder(quotient(a_cols[0][0], piece_rows), layers)
+    context[0] = quotient(a_rows[0][0], local_rows)
+    context[1] = layer
     own_rows = local_rows // layers
     for g in range(layers):
         base = remainder(layer + g, layers) * own_rows
@@ -167,9 +161,9 @@
     for j in range(cols):
         list_pairs(
             (rows, layers, count, piece_rows, width, local_rows, kept),
-            index[j],
-            here,
-            layer,
+            a_rows[j],
+            a_cols[j],
+            context,
             panel_cols,
             kept_cols,
             pairs,
@@ -193,13 +187,14 @@
     half = height // 2
     for d in range(1, layers):
         code = sent[d - 1]
-        code[slots * half :] = jnp.zeros((code.shape[0] - slots * half, code.shape[1]), jnp.int32)
+        spare = code.shape[0] - slots * half
+        code[slots * half :] = jnp.zeros((spare, code.shape[1]), jnp.int32)
         for u in range(slots):
             value = totals[d * slots + u]
             peak = jnp.max(jnp.abs(value), axis=0, keepdims=True)
             power = jnp.floor(jnp.log2(jnp.maximum(peak, 1e-30)) + 1e-3) + 1.0
-            whole = jnp.floor(value * jnp.exp2(15.0 - power) + 0.5).astype(jnp.int32)
-            code[pl.ds(u * half, half)] = (whole[:half] << 16) | (whole[half:] & 0xFFFF)
+            word = jnp.floor(value * jnp.exp2(15.0 - power) + 0.5).astype(jnp.int32)
+            code[pl.ds(u * half, half)] = (word[:half] << 16) | (word[half:] & 0xFFFF)
             code[pl.ds(slots * half + u, 1)] = power.astype(jnp.int32)
 
 
@@ -239,29 +234,22 @@
     note_height, _ = note_rows(piece)
 
     scalars = pl.BlockSpec(memory_space=pltpu.SMEM)
-    anywhere = pl.BlockSpec(memory_space=pl.ANY)
     vector = pl.BlockSpec(memory_space=pltpu.VMEM)
 
     def x_chunk(blocks, c):
-        part = lax.slice_in_dim(blocks, c * height, (c + 1) * height, axis=1)
-        return [shifted(part, "col", j) for j in range(1, cols)]
-
-    x_pieces = [x_chunk(a_blocks, 0)]
-    index, s_sent = pl.pallas_call(
-        functools.partial(pack_kernel, (count, order, piece_rows, width)),
-        out_shape=[
-            jax.ShapeDtypeStruct((2 * count,), jnp.int32),
-            jax.ShapeDtypeStruct((piece * order + note_height, order), jnp.bfloat16),
-        ],
-        in_specs=[scalars] * 3 + [anywhere],
-        out_specs=[scalars, vector],
-        scratch_shapes=[pltpu.SemaphoreType.DMA((piece,))],
-        name="pack",
-    )(a_rows, a_cols, s_cols, flat_s)
-    indices = [index] + [shifted(index, "col", j) for j in range(1, cols)]
-    s_pieces = [shifted(s_sent, "row", d) for d in range(1, rows)]
-    later_blocks, _, s_pieces = lax.optimization_barrier((a_blocks, indices, s_pieces))
-    x_pieces += [x_chunk(later_blocks, c) for c in range(1, CHUNKS)]
+        return lax.slice_in_dim(blocks, c * height, (c + 1) * height, axis=1)
+
+    row_pieces = [a_rows] + [shifted(a_rows, "col", j) for j in range(1, cols)]
+    col_pieces = [a_cols] + [shifted(a_cols, "col", j) for j in range(1, cols)]
+    x_first, row_pieces, col_pieces = lax.optimization_barrier(
+        (x_chunk(a_blocks, 0), row_pieces, col_pieces)
+    )
+    x_pieces = [[shifted(x_first, "col", j) for j in range(1, cols)]]
+    s_sent = with_notes(flat_s.reshape(piece * order, order), s_cols.reshape(-1))
+    s_pieces = gathered(s_sent, "row")[1:]
+    for c in range(1, CHUNKS):
+        part = x_chunk(a_blocks, c)
+        x_pieces.append([shifted(part, "col", j) for j in range(1, cols)])
 
     moved = block_size * (4 * all_slots + 4 * panel_size + 2 * count)
     totals, panel, *plan = pl.pallas_call(
@@ -274,11 +262,12 @@
             jax.ShapeDtypeStruct((cols, 3, count * width + GROUP), jnp.int32),
             jax.ShapeDtypeStruct((cols,), jnp.int32),
         ],
-        in_specs=[scalars] * (cols + 2) + [vector] * (1 + rows),
+        in_specs=[scalars] * (2 * cols + 2) + [vector] * (1 + rows),
         out_specs=[vector] * 2 + [scalars] * 2,
         scratch_shapes=[
             pltpu.SMEM((panel_size,), jnp.int32),
             pltpu.SMEM((all_slots,), jnp.int32),
+            pltpu.SMEM((2,), jnp.int32),
             pltpu.VMEM((rows - 1, note_height, LANES), jnp.int32),
             pltpu.SMEM((rows - 1, note_height, LANES), jnp.int32),
             pltpu.SemaphoreType.DMA((panel_size,)),
@@ -289,35 +278,31 @@
             flops=2 * order**3 * count * width // 4, bytes_accessed=moved, transcendentals=0
         ),
         name="own_products",
-    )(*indices, s_cols, c_cols, a_blocks, flat_s, *s_pieces)
+    )(*row_pieces, *col_pieces, s_cols, c_cols, a_blocks, flat_s, *s_pieces)
 
     code_rows = slots * (height // 2) + (slots + 7) // 8 * 8
     moved = block_size * (8 * all_slots + 2 * panel_size + 2 * count * (cols - 1))
-    parts = []
+    final = []
     for c in range(CHUNKS):
         out_shape = [jax.ShapeDtypeStruct((slots, height, order), jnp.float32)]
         out_shape += [jax.ShapeDtypeStruct((code_rows, order), jnp.int32)] * (layers - 1)
-        parts.append(
-            pl.pallas_call(
-                functools.partial(peer_kernel, (cols, layers, slots, height), c * height),
-                out_shape=out_shape,
-                in_specs=[scalars] * 2 + [vector] * (cols + 1),
-                out_specs=[vector] * layers,
-                scratch_shapes=[pltpu.VMEM((all_slots + 1, height, order), jnp.float32)],
-                compiler_params=pltpu.CompilerParams(vmem_limit_bytes=moved + 4 * MIB),
-                cost_estimate=pl.CostEstimate(
-                    flops=2 * order**2 * height * count * width // 4 * (cols - 1),
-                    bytes_accessed=moved // CHUNKS,
-                    transcendentals=0,
-                ),
-                name=f"peer_products_{c}",
-            )(*plan, *x_pieces[c], panel, totals)
-        )
-
-    final = []
-    for part in parts:
-        final.append(part[0])
-        final += [shifted(part[d], "layer", layers - d) for d in range(1, layers)]
+        own, *sent = pl.pallas_call(
+            functools.partial(peer_kernel, (cols, layers, slots, height), c * height),
+            out_shape=out_shape,
+            in_specs=[scalars] * 2 + [vector] * (cols + 1),
+            out_specs=[vector] * layers,
+            scratch_shapes=[pltpu.VMEM((all_slots + 1, height, order), jnp.float32)],
+            compiler_params=pltpu.CompilerParams(vmem_limit_bytes=moved + 4 * MIB),
+            cost_estimate=pl.CostEstimate(
+                flops=2 * order**2 * height * count * width // 4 * (cols - 1),
+                bytes_accessed=moved // CHUNKS,
+                transcendentals=0,
+            ),
+            name=f"peer_products_{c}",
+        )(*plan, *x_pieces[c], panel, totals)
+        final.append(own)
+        final += [shifted(sent[d - 1], "layer", layers - d) for d in range(1, layers)]
+
     return pl.pallas_call(
         functools.partial(finish_kernel, (layers, CHUNKS, slots, height)),
         out_shape=jax.ShapeDtypeStruct((own_rows, kept, order, order), jnp.bfloat16),

time: 42.5 us -> 35 us (0.82)
  waiting for transfers between devices: 15.7 us -> 8.64 us
  Pallas kernels: 9.97 us -> 7.11 us
  starting transfers between devices: 15.6 us -> 17.8 us
    ppermute x12 -> x10, waiting for transfers between devices: 15.7 us -> 4.26 us  [shifted(): lax.ppermute(value, axis, [((i + offset) % size, i) for i in range(size)])]
    ppermute x0 -> x3, waiting for transfers between devices: none -> 4.38 us  [flipped(): lax.ppermute(value, axis, [(i, i ^ bits) for i in range(lax.axis_size(axi...]
    pallas_call x1 -> x0, Pallas kernels: 2.33 us -> none  [per_device(): pl.pallas_call(functools.partial(pack_kernel, (count, order, piece_rows,...]
    ppermute x0 -> x3, starting transfers between devices: none -> 1.96 us  [flipped(): lax.ppermute(value, axis, [(i, i ^ bits) for i in range(lax.axis_size(axi...]
    ppermute x12 -> x10, starting transfers between devices: 15.6 us -> 15.8 us  [shifted(): lax.ppermute(value, axis, [((i + offset) % size, i) for i in range(size)])]
    slice x2 -> x1, local copies, waits for them, and re-layouts: 1.05 us -> 1.17 us  [x_chunk(): return lax.slice_in_dim(blocks, c * height, (c + 1) * height, axis=1)]
  transfers between devices with their start and end apart: 12 -> 13, of which waited for: 4 -> 5; matrix products, arithmetic and copies ran while one was open for 3% -> 4% of each run, Pallas kernels for 16% -> 18%
where the time goes in v6:
time: 35 us
  starting transfers between devices  17.8 us (51%)
  waiting for transfers between devices  8.64 us (25%)
  Pallas kernels  7.11 us (20%)
  local copies, waits for them, and re-layouts  1.35 us (4%)
    ppermute x10, starting transfers between devices, shifted(): lax.ppermute(value, axis, [((i + offset) % size, i) for i in range(size)])  15.8 us
    ppermute x3, waiting for transfers between devices, flipped(): lax.ppermute(value, axis, [(i, i ^ bits) for i in range(lax.axis_size(axi...  4.38 us
    ppermute x10, waiting for transfers between devices, shifted(): lax.ppermute(value, axis, [((i + offset) % size, i) for i in range(size)])  4.26 us
    pallas_call x1, Pallas kernels, per_device(): pl.pallas_call(functools.partial(own_kernel, (rows, cols, layers, count,...  4.06 us
    pallas_call x2, Pallas kernels, per_device(): pl.pallas_call(functools.partial(peer_kernel, (cols, layers, slots, heigh...  2.25 us
    ppermute x3, starting transfers between devices, flipped(): lax.ppermute(value, axis, [(i, i ^ bits) for i in range(lax.axis_size(axi...  1.96 us
    slice x1, local copies, waits for them, and re-layouts, x_chunk(): return lax.slice_in_dim(blocks, c * height, (c + 1) * height, axis=1)  1.17 us
    pallas_call x1, Pallas kernels, per_device(): pl.pallas_call(functools.partial(finish_kernel, (layers, CHUNKS, slots, h...  0.8 us
  transfers between devices with their start and end apart: 13, of which 5 were waited for; matrix products, arithmetic and copies ran while one was open for 4% of the time, Pallas kernels for 18%

profile of v6, /device:TPU:0, one launch (start us, length us, event | category | flops | bytes accessed | tf_op | source)
XLA Modules:
  0.0 35.0 jit_solution(3085606522887757274)
XLA Ops:
  0.0 0.0 copy-start.3
  0.0 0.0 copy-start.4
  0.0 0.0 copy-start
  0.0 0.0 copy-start.2
  0.0 0.0 copy-start.1
  0.0 0.0 copy-start.5
  0.0 3.0 %collective-permute-start = (s32[24]{0:T(128)}, s32[24]{0:T(128)S(1)}, u32[]{:S(2)}, u32[]{:S(2)}) collective-permute-start(s32[24]{0:T(128)} %refs_0_), channel_id=1, source_target_pairs={{4,0},{0,4},{5,1},{1,5},{6,2},{2,6},{7,3},{3,7},{12,8},{8,12},{13,... | collective-permute-start | bytes 296 | tf_op jit(solution)/shard_map/ppermute | solution.py:31
  3.0 0.1 collective-permute-start.1
  3.1 1.2 %fusion.3 = (bf16[24,64,128]{2,1,0:T(8,128)(2,1)S(1)}, bf16[24,64,128]{2,1,0:T(8,128)(2,1)S(1)}) fusion(bf16[24,128,128]{2,1,0:T(8,128)(2,1)} %refs_6_.1), kind=kLoop, calls=%fused_computation.7 | loop fusion | bytes 1572864 | tf_op jit(solution)/shard_map/slice | solution.py:240
  4.3 2.0 %collective-permute-start.9 = (bf16[24,64,128]{2,1,0:T(8,128)(2,1)S(1)}, bf16[24,64,128]{2,1,0:T(8,128)(2,1)S(1)}, u32[]{:S(2)}, u32[]{:S(2)}) collective-permute-start(bf16[24,64,128]{2,1,0:T(8,128)(2,1)S(1)} %get-tuple-element.39), channel_id=1, source_target_pairs={{4,0},{0,4},{5,1},{1,5},{6,2},{2,6},{7,3},{3,7},{12,8},{8,12},{13,... | collective-permute-start | bytes 1179656 | tf_op jit(solution)/shard_map/ppermute | solution.py:31
  6.3 0.0 copy-done.2
  6.3 0.1 reshape.12
  6.4 0.0 collective-permute-done.refs_1_
  6.4 0.3 collective-permute-done.1.refs_3_
  6.7 0.2 collective-permute-start.5
  6.9 0.0 copy-done.1
  6.9 2.0 %collective-permute-start.3 = (bf16[528,128]{1,0:T(8,128)(2,1)S(1)}, bf16[528,128]{1,0:T(8,128)(2,1)S(1)}, u32[]{:S(2)}, u32[]{:S(2)}) collective-permute-start(bf16[528,128]{1,0:T(8,128)(2,1)S(1)} %pad_maximum_fusion), channel_id=1, source_target_pairs={{0,16},{8,24},{16,0},{24,8},{1,17},{9,25},{17,1},{25,9},{2,18},{10... | collective-permute-start | bytes 405512 | tf_op jit(solution)/shard_map/ppermute | solution.py:17
  8.9 0.0 collective-permute-start.2
  8.9 3.1 %collective-permute-done.3.refs_9_ = bf16[528,128]{1,0:T(8,128)(2,1)S(1)} collective-permute-done((bf16[528,128]{1,0:T(8,128)(2,1)S(1)}, bf16[528,128]{1,0:T(8,128)(2,1)S(1)}, u32[]{:S(2)}, u32[]{:S(2)}) %collective-permute-start.3) | collective-permute-done | bytes 135200 | tf_op jit(solution)/shard_map/ppermute | solution.py:17
  12.0 0.0 collective-permute-start.4
  12.0 0.0 copy-done.5
  12.0 0.1 copy.7.refs_5_
  12.1 0.0 collective-permute-done.2.refs_8_
  12.1 1.3 %collective-permute-done.4.refs_10_ = bf16[528,128]{1,0:T(8,128)(2,1)S(1)} collective-permute-done((bf16[528,128]{1,0:T(8,128)(2,1)S(1)}, bf16[528,128]{1,0:T(8,128)(2,1)S(1)}, u32[]{:S(2)}, u32[]{:S(2)}) %collective-permute-start.4) | collective-permute-done | bytes 135200 | tf_op jit(solution)/shard_map/ppermute | solution.py:17
  13.3 0.0 copy-done.3
  13.3 0.0 copy-done.4
  13.3 0.0 copy-done
  13.3 4.1 %own_products.1 = (f32[17,128,128]{2,1,0:T(8,128)S(1)}, bf16[16,128,128]{2,1,0:T(8,128)(2,1)S(1)}, s32[2,3,52]{2,1,0:T(4,128)S(1)}, s32[2]{0:T(128)S(1)}) custom-call(s32[24]{0:T(128)S(1)} %copy-done.3, s32[24]{0:T(128)S(1)} %collective-permute-done.refs_1_, s32[24]{0:T(128)S(1)} %copy-done.4, s32[24]{0:T(128)S(1)} %collective-permute-done.1.refs_3_, ...), custom_call_target="tpu_custom_call" | custom-call | flops 50331648 | bytes 2883584 | tf_op jit(solution)/shard_map/own_products/pallas_call | solution.py:255
  17.4 0.0 collective-permute-done.9.refs_0_
  17.4 1.1 %peer_products_1.1 = (f32[4,64,128]{2,1,0:T(8,128)S(1)}, s32[136,128]{1,0:T(8,128)S(1)}, s32[136,128]{1,0:T(8,128)S(1)}, s32[136,128]{1,0:T(8,128)S(1)}) custom-call(s32[2,3,52]{2,1,0:T(4,128)S(1)} %get-tuple-element.26.pairs, s32[2]{0:T(128)S(1)} %get-tuple-element.27.tally, bf16[24,64,128]{2,1,0:T(8,128)(2,1)S(1)} %collective-permute-done.9.refs_0_, ...), custom_call_target="tpu_custom_call" | custom-call | flops 25165824 | bytes 1703936 | tf_op jit(solution)/shard_map/peer_products_1/pallas_call | solution.py:289
  18.6 1.8 %collective-permute-start.10 = (s32[136,128]{1,0:T(8,128)S(1)}, s32[136,128]{1,0:T(8,128)S(1)}, u32[]{:S(2)}, u32[]{:S(2)}) collective-permute-start(s32[136,128]{1,0:T(8,128)S(1)} %get-tuple-element.36), channel_id=1, source_target_pairs={{3,0},{0,1},{1,2},{2,3},{7,4},{4,5},{5,6},{6,7},{11,8},{8,9},{9,10... | collective-permute-start | bytes 208904 | tf_op jit(solution)/shard_map/ppermute | solution.py:31
  20.4 2.6 %collective-permute-start.11 = (s32[136,128]{1,0:T(8,128)S(1)}, s32[136,128]{1,0:T(8,128)S(1)}, u32[]{:S(2)}, u32[]{:S(2)}) collective-permute-start(s32[136,128]{1,0:T(8,128)S(1)} %get-tuple-element.37), channel_id=1, source_target_pairs={{2,0},{3,1},{0,2},{1,3},{6,4},{7,5},{4,6},{5,7},{10,8},{11,9},{8,1... | collective-permute-start | bytes 208904 | tf_op jit(solution)/shard_map/ppermute | solution.py:31
  23.0 1.5 %collective-permute-start.12 = (s32[136,128]{1,0:T(8,128)S(1)}, s32[136,128]{1,0:T(8,128)S(1)}, u32[]{:S(2)}, u32[]{:S(2)}) collective-permute-start(s32[136,128]{1,0:T(8,128)S(1)} %get-tuple-element.38), channel_id=1, source_target_pairs={{1,0},{2,1},{3,2},{0,3},{5,4},{6,5},{7,6},{4,7},{9,8},{10,9},{11,1... | collective-permute-start | bytes 208904 | tf_op jit(solution)/shard_map/ppermute | solution.py:31
  24.5 0.0 collective-permute-done.5.refs_0_
  24.5 1.1 %peer_products_0.1 = (f32[4,64,128]{2,1,0:T(8,128)S(1)}, s32[136,128]{1,0:T(8,128)S(1)}, s32[136,128]{1,0:T(8,128)S(1)}, s32[136,128]{1,0:T(8,128)S(1)}) custom-call(s32[2,3,52]{2,1,0:T(4,128)S(1)} %get-tuple-element.26.pairs, s32[2]{0:T(128)S(1)} %get-tuple-element.27.tally, bf16[24,64,128]{2,1,0:T(8,128)(2,1)S(1)} %collective-permute-done.5.refs_0_, ...), custom_call_target="tpu_custom_call" | custom-call | flops 25165824 | bytes 1703936 | tf_op jit(solution)/shard_map/peer_products_0/pallas_call | solution.py:289
  25.6 0.7 %collective-permute-start.6 = (s32[136,128]{1,0:T(8,128)S(1)}, s32[136,128]{1,0:T(8,128)S(1)}, u32[]{:S(2)}, u32[]{:S(2)}) collective-permute-start(s32[136,128]{1,0:T(8,128)S(1)} %get-tuple-element.32), channel_id=1, source_target_pairs={{3,0},{0,1},{1,2},{2,3},{7,4},{4,5},{5,6},{6,7},{11,8},{8,9},{9,10... | collective-permute-start | bytes 208904 | tf_op jit(solution)/shard_map/ppermute | solution.py:31
  26.3 2.4 %collective-permute-start.7 = (s32[136,128]{1,0:T(8,128)S(1)}, s32[136,128]{1,0:T(8,128)S(1)}, u32[]{:S(2)}, u32[]{:S(2)}) collective-permute-start(s32[136,128]{1,0:T(8,128)S(1)} %get-tuple-element.33), channel_id=1, source_target_pairs={{2,0},{3,1},{0,2},{1,3},{6,4},{7,5},{4,6},{5,7},{10,8},{11,9},{8,1... | collective-permute-start | bytes 208904 | tf_op jit(solution)/shard_map/ppermute | solution.py:31
  28.7 0.0 collective-permute-done.10.refs_5_
  28.7 1.5 %collective-permute-start.8 = (s32[136,128]{1,0:T(8,128)S(1)}, s32[136,128]{1,0:T(8,128)S(1)}, u32[]{:S(2)}, u32[]{:S(2)}) collective-permute-start(s32[136,128]{1,0:T(8,128)S(1)} %get-tuple-element.34), channel_id=1, source_target_pairs={{1,0},{2,1},{3,2},{0,3},{5,4},{6,5},{7,6},{4,7},{9,8},{10,9},{11,1... | collective-permute-start | bytes 208904 | tf_op jit(solution)/shard_map/ppermute | solution.py:31
  30.2 0.0 collective-permute-done.11.refs_6_
  30.2 0.0 collective-permute-done.12.refs_7_
  30.3 2.4 %collective-permute-done.6.refs_1_ = s32[136,128]{1,0:T(8,128)S(1)} collective-permute-done((s32[136,128]{1,0:T(8,128)S(1)}, s32[136,128]{1,0:T(8,128)S(1)}, u32[]{:S(2)}, u32[]{:S(2)}) %collective-permute-start.6) | collective-permute-done | bytes 69664 | tf_op jit(solution)/shard_map/ppermute | solution.py:31
  32.6 1.6 %collective-permute-done.7.refs_2_ = s32[136,128]{1,0:T(8,128)S(1)} collective-permute-done((s32[136,128]{1,0:T(8,128)S(1)}, s32[136,128]{1,0:T(8,128)S(1)}, u32[]{:S(2)}, u32[]{:S(2)}) %collective-permute-start.7) | collective-permute-done | bytes 69664 | tf_op jit(solution)/shard_map/ppermute | solution.py:31
  34.2 0.0 collective-permute-done.8.refs_3_
  34.2 0.8 %finish.1 = bf16[2,2,128,128]{3,2,1,0:T(8,128)(2,1)} custom-call(f32[4,64,128]{2,1,0:T(8,128)S(1)} %get-tuple-element.31.refs_0_, s32[136,128]{1,0:T(8,128)S(1)} %collective-permute-done.6.refs_1_, s32[136,128]{1,0:T(8,128)S(1)} %collective-permute-done.7.refs_2_, s32[136,128]{1,0:T(8,128)S(1)} %collective-permute-done.8.refs_3_, ...), custom_call_target="tpu_custom_call" | custom-call | tf_op jit(solution)/shard_map/finish/pallas_call | solution.py:306
  (3 shorter events, 0.0 us)
Async XLA Ops:
  0.0 13.3 %copy-start.3 = (s32[24]{0:T(128)S(1)}, s32[24]{0:T(128)}, u32[]{:S(2)}) copy-start(s32[24]{0:T(128)} %refs_0_) | copy-start | bytes 292
  0.0 13.3 %copy-start.4 = (s32[24]{0:T(128)S(1)}, s32[24]{0:T(128)}, u32[]{:S(2)}) copy-start(s32[24]{0:T(128)} %refs_2_) | copy-start | bytes 292
  0.0 13.3 %copy-start = (bf16[24,128,128]{2,1,0:T(8,128)(2,1)S(1)}, bf16[24,128,128]{2,1,0:T(8,128)(2,1)}, u32[]{:S(2)}) copy-start(bf16[24,128,128]{2,1,0:T(8,128)(2,1)} %refs_6_.1) | copy-start | bytes 2359300
  0.0 6.3 %copy-start.2 = (s32[2,2]{1,0:T(2,128)S(1)}, s32[2,2]{1,0:T(2,128)}, u32[]{:S(2)}) copy-start(s32[2,2]{1,0:T(2,128)} %refs_4_.1) | copy-start | bytes 52
  0.0 6.9 %copy-start.1 = (bf16[2,2,128,128]{3,2,1,0:T(8,128)(2,1)S(1)}, bf16[2,2,128,128]{3,2,1,0:T(8,128)(2,1)}, u32[]{:S(2)}) copy-start(bf16[2,2,128,128]{3,2,1,0:T(8,128)(2,1)} %param.9) | copy-start | bytes 393220
  0.0 12.0 %copy-start.5 = (s32[8,2]{0,1:T(2,128)S(1)}, s32[8,2]{0,1:T(2,128)}, u32[]{:S(2)}) copy-start(s32[8,2]{0,1:T(2,128)} %param.11) | copy-start | bytes 196
  0.0 6.4 %collective-permute-start = (s32[24]{0:T(128)}, s32[24]{0:T(128)S(1)}, u32[]{:S(2)}, u32[]{:S(2)}) collective-permute-start(s32[24]{0:T(128)} %refs_0_), channel_id=1, source_target_pairs={{4,0},{0,4},{5,1},{1,5},{6,2},{2,6},{7,3},{3,7},{12,8},{8,12},{13,... | collective-permute-start | bytes 296 | tf_op jit(solution)/shard_map/ppermute | solution.py:31
  3.0 3.7 %collective-permute-start.1 = (s32[24]{0:T(128)}, s32[24]{0:T(128)S(1)}, u32[]{:S(2)}, u32[]{:S(2)}) collective-permute-start(s32[24]{0:T(128)} %refs_2_), channel_id=1, source_target_pairs={{4,0},{0,4},{5,1},{1,5},{6,2},{2,6},{7,3},{3,7},{12,8},{8,12},{13,... | collective-permute-start | bytes 296 | tf_op jit(solution)/shard_map/ppermute | solution.py:31
  4.3 13.1 %collective-permute-start.9 = (bf16[24,64,128]{2,1,0:T(8,128)(2,1)S(1)}, bf16[24,64,128]{2,1,0:T(8,128)(2,1)S(1)}, u32[]{:S(2)}, u32[]{:S(2)}) collective-permute-start(bf16[24,64,128]{2,1,0:T(8,128)(2,1)S(1)} %get-tuple-element.39), channel_id=1, source_target_pairs={{4,0},{0,4},{5,1},{1,5},{6,2},{2,6},{7,3},{3,7},{12,8},{8,12},{13,... | collective-permute-start | bytes 1179656 | tf_op jit(solution)/shard_map/ppermute | solution.py:31
  6.7 17.8 %collective-permute-start.5 = (bf16[24,64,128]{2,1,0:T(8,128)(2,1)S(1)}, bf16[24,64,128]{2,1,0:T(8,128)(2,1)S(1)}, u32[]{:S(2)}, u32[]{:S(2)}) collective-permute-start(bf16[24,64,128]{2,1,0:T(8,128)(2,1)S(1)} %get-tuple-element.28), channel_id=1, source_target_pairs={{4,0},{0,4},{5,1},{1,5},{6,2},{2,6},{7,3},{3,7},{12,8},{8,12},{13,... | collective-permute-start | bytes 1179656 | tf_op jit(solution)/shard_map/ppermute | solution.py:31
  6.9 5.1 %collective-permute-start.3 = (bf16[528,128]{1,0:T(8,128)(2,1)S(1)}, bf16[528,128]{1,0:T(8,128)(2,1)S(1)}, u32[]{:S(2)}, u32[]{:S(2)}) collective-permute-start(bf16[528,128]{1,0:T(8,128)(2,1)S(1)} %pad_maximum_fusion), channel_id=1, source_target_pairs={{0,16},{8,24},{16,0},{24,8},{1,17},{9,25},{17,1},{25,9},{2,18},{10... | collective-permute-start | bytes 405512 | tf_op jit(solution)/shard_map/ppermute | solution.py:17
  8.9 3.2 %collective-permute-start.2 = (bf16[528,128]{1,0:T(8,128)(2,1)S(1)}, bf16[528,128]{1,0:T(8,128)(2,1)S(1)}, u32[]{:S(2)}, u32[]{:S(2)}) collective-permute-start(bf16[528,128]{1,0:T(8,128)(2,1)S(1)} %pad_maximum_fusion), channel_id=1, source_target_pairs={{0,8},{8,0},{16,24},{24,16},{1,9},{9,1},{17,25},{25,17},{2,10},{10... | collective-permute-start | bytes 405512 | tf_op jit(solution)/shard_map/ppermute | solution.py:17
  12.0 1.4 %collective-permute-start.4 = (bf16[528,128]{1,0:T(8,128)(2,1)S(1)}, bf16[528,128]{1,0:T(8,128)(2,1)S(1)}, u32[]{:S(2)}, u32[]{:S(2)}) collective-permute-start(bf16[528,128]{1,0:T(8,128)(2,1)S(1)} %collective-permute-done.3.refs_9_), channel_id=1, source_target_pairs={{0,8},{8,0},{16,24},{24,16},{1,9},{9,1},{17,25},{25,17},{2,10},{10... | collective-permute-start | bytes 405512 | tf_op jit(solution)/shard_map/ppermute | solution.py:17
  18.6 10.2 %collective-permute-start.10 = (s32[136,128]{1,0:T(8,128)S(1)}, s32[136,128]{1,0:T(8,128)S(1)}, u32[]{:S(2)}, u32[]{:S(2)}) collective-permute-start(s32[136,128]{1,0:T(8,128)S(1)} %get-tuple-element.36), channel_id=1, source_target_pairs={{3,0},{0,1},{1,2},{2,3},{7,4},{4,5},{5,6},{6,7},{11,8},{8,9},{9,10... | collective-permute-start | bytes 208904 | tf_op jit(solution)/shard_map/ppermute | solution.py:31
  20.4 9.9 %collective-permute-start.11 = (s32[136,128]{1,0:T(8,128)S(1)}, s32[136,128]{1,0:T(8,128)S(1)}, u32[]{:S(2)}, u32[]{:S(2)}) collective-permute-start(s32[136,128]{1,0:T(8,128)S(1)} %get-tuple-element.37), channel_id=1, source_target_pairs={{2,0},{3,1},{0,2},{1,3},{6,4},{7,5},{4,6},{5,7},{10,8},{11,9},{8,1... | collective-permute-start | bytes 208904 | tf_op jit(solution)/shard_map/ppermute | solution.py:31
  23.0 7.3 %collective-permute-start.12 = (s32[136,128]{1,0:T(8,128)S(1)}, s32[136,128]{1,0:T(8,128)S(1)}, u32[]{:S(2)}, u32[]{:S(2)}) collective-permute-start(s32[136,128]{1,0:T(8,128)S(1)} %get-tuple-element.38), channel_id=1, source_target_pairs={{1,0},{2,1},{3,2},{0,3},{5,4},{6,5},{7,6},{4,7},{9,8},{10,9},{11,1... | collective-permute-start | bytes 208904 | tf_op jit(solution)/shard_map/ppermute | solution.py:31
  25.6 7.0 %collective-permute-start.6 = (s32[136,128]{1,0:T(8,128)S(1)}, s32[136,128]{1,0:T(8,128)S(1)}, u32[]{:S(2)}, u32[]{:S(2)}) collective-permute-start(s32[136,128]{1,0:T(8,128)S(1)} %get-tuple-element.32), channel_id=1, source_target_pairs={{3,0},{0,1},{1,2},{2,3},{7,4},{4,5},{5,6},{6,7},{11,8},{8,9},{9,10... | collective-permute-start | bytes 208904 | tf_op jit(solution)/shard_map/ppermute | solution.py:31
  26.3 7.9 %collective-permute-start.7 = (s32[136,128]{1,0:T(8,128)S(1)}, s32[136,128]{1,0:T(8,128)S(1)}, u32[]{:S(2)}, u32[]{:S(2)}) collective-permute-start(s32[136,128]{1,0:T(8,128)S(1)} %get-tuple-element.33), channel_id=1, source_target_pairs={{2,0},{3,1},{0,2},{1,3},{6,4},{7,5},{4,6},{5,7},{10,8},{11,9},{8,1... | collective-permute-start | bytes 208904 | tf_op jit(solution)/shard_map/ppermute | solution.py:31
  28.7 5.5 %collective-permute-start.8 = (s32[136,128]{1,0:T(8,128)S(1)}, s32[136,128]{1,0:T(8,128)S(1)}, u32[]{:S(2)}, u32[]{:S(2)}) collective-permute-start(s32[136,128]{1,0:T(8,128)S(1)} %get-tuple-element.34), channel_id=1, source_target_pairs={{1,0},{2,1},{3,2},{0,3},{5,4},{6,5},{7,6},{4,7},{9,8},{10,9},{11,1... | collective-permute-start | bytes 208904 | tf_op jit(solution)/shard_map/ppermute | solution.py:31

commit v7 on v5

v7 whole, which is shorter than its diff:
```python
import functools

import jax
import jax.numpy as jnp
from jax import lax
from jax.experimental import pallas as pl
from jax.experimental.pallas import tpu as pltpu
from jax.sharding import PartitionSpec as P

CHUNKS = 2
GROUP = 4
LANES = 128
MIB = 2**20


def flipped(value, axis, bits):
    return lax.ppermute(value, axis, [(i, i ^ bits) for i in range(lax.axis_size(axis))])


def gathered(value, axis):
    values = {0: value}
    bit = lax.axis_size(axis) // 2
    while bit:
        values |= {d ^ bit: flipped(held, axis, bit) for d, held in values.items()}
        bit //= 2
    return [values[d] for d in range(len(values))]


def shifted(value, axis, offset):
    size = lax.axis_size(axis)
    return lax.ppermute(value, axis, [((i + offset) % size, i) for i in range(size)])


def quotient(value, by):
    return value >> (by.bit_length() - 1) if by & (by - 1) == 0 else lax.div(value, by)


def remainder(value, by):
    return value & (by - 1) if by & (by - 1) == 0 else lax.rem(value, by)


def note_rows(how_many):
    digits = (how_many + LANES - 1) // LANES
    return (2 * digits + 15) // 16 * 16, digits


def with_notes(payload, values):
    (how_many,) = values.shape
    height, digits = note_rows(how_many)
    values = jnp.pad(values, (0, digits * LANES - how_many)).reshape(digits, LANES)
    tile = jnp.concatenate([remainder(values, LANES), quotient(values, LANES)])
    tile = jnp.pad(tile, ((0, height - 2 * digits), (0, 0)))
    return jnp.concatenate([payload, tile.astype(payload.dtype)])


def read_notes(payload, start, how_many, whole, notes, sem):
    height, _ = note_rows(how_many)
    whole[...] = payload[start : start + height].astype(jnp.float32).astype(jnp.int32)
    copy = pltpu.make_async_copy(whole, notes, sem)
    copy.start()
    return copy


def note(notes, how_many, p):
    _, digits = note_rows(how_many)
    return notes[p // LANES, p % LANES] + notes[digits + p // LANES, p % LANES] * LANES


def positions(sizes, a_rows, a_cols, row_at, layer_at):
    layers, piece_rows, width, local_rows, kept = sizes
    own_rows = local_rows // layers
    owner = quotient(a_cols, piece_rows * layers)
    rights = ((owner ^ row_at) * piece_rows + remainder(a_cols, piece_rows)) * width
    local = a_rows - row_at * local_rows
    goals = remainder(quotient(local, own_rows) - layer_at + layers, layers) * own_rows
    return rights, (goals + remainder(local, own_rows)) * kept


def pack_kernel(sizes, a_rows, a_cols, x_in, x_out, tile, sem):
    count, height = sizes
    spot = x_out.at[pl.ds(0, count * height)].reshape(count, height, x_out.shape[1])
    load = pltpu.make_async_copy(x_in.at[:, pl.ds(0, height), :], spot, sem)
    load.start()
    tile[...] = jnp.zeros_like(tile)
    for p, value in enumerate((a_rows[...], a_cols[...])):
        tile[2 * p : 2 * p + 1, :count] = remainder(value, LANES)
        tile[2 * p + 1 : 2 * p + 2, :count] = quotient(value, LANES)
    x_out[count * height :] = tile[...].astype(jnp.float32).astype(jnp.bfloat16)
    load.wait()


def list_pairs(sizes, index, row, panel_cols, kept_cols, pairs, tally, j):
    count, width, kept, trash = sizes
    total = jnp.int32(0)
    for n in range(count):
        right, goal = index[row, n], index[row + 1, n]
        for s in range(width):
            wanted = panel_cols[right + s]
            hit, slot = jnp.int32(0), goal
            for t in range(kept):
                same = (kept_cols[goal + t] == wanted).astype(jnp.int32)
                hit += same
                slot += t * same
            pairs[j, 0, total] = n
            pairs[j, 1, total] = right + s
            pairs[j, 2, total] = slot
            total += hit
    for g in range(GROUP):
        pairs[j, 0, total + g] = 0
        pairs[j, 1, total + g] = 0
        pairs[j, 2, total + g] = trash
    tally[j] = total


def add_products(left, panel, totals, pairs, tally, j):
    def one_group(group, carry):
        base = group * GROUP
        products = [
            jnp.dot(
                left(pairs[j, 0, base + g]),
                panel[pairs[j, 1, base + g]],
                preferred_element_type=jnp.float32,
            )
            for g in range(GROUP)
        ]
        for g in range(GROUP):
            totals[pairs[j, 2, base + g]] += products[g]
        return carry

    lax.fori_loop(0, quotient(tally[j] + GROUP - 1, GROUP), one_group, 0)


def own_kernel(sizes, *refs):
    rows, layers, count, piece_rows, width, local_rows, kept, order = sizes
    place, index, s_cols, c_cols, x_in, s_in = refs[:6]
    s_other, refs = refs[6 : 5 + rows], refs[5 + rows :]
    totals, panel, panel_cols, kept_cols = refs[:4]
    pairs, tally, whole, notes, s_sem, note_sem = refs[4:]
    piece = piece_rows * width
    loads = [pltpu.make_async_copy(s_in, panel.at[pl.ds(0, piece)], s_sem.at[0])]
    for d in range(1, rows):
        loads += [
            pltpu.make_async_copy(
                s_other[d - 1].at[pl.ds(q * order, order)],
                panel.at[d * piece + q],
                s_sem.at[d * piece + q],
            )
            for q in range(piece)
        ]
    reads = [
        read_notes(s_other[d], piece * order, piece, whole.at[d], notes.at[d], note_sem.at[d])
        for d in range(rows - 1)
    ]
    for load in loads:
        load.start()
    totals[...] = jnp.zeros_like(totals)
    own_rows = local_rows // layers
    for g in range(layers):
        base = remainder(place[1] + g, layers) * own_rows
        for i in range(own_rows):
            for t in range(kept):
                kept_cols[(g * own_rows + i) * kept + t] = c_cols[base + i, t]
    for read in reads:
        read.wait()
    for q in range(piece):
        panel_cols[q] = s_cols[q // width, q % width]
        for d in range(1, rows):
            panel_cols[d * piece + q] = note(notes.at[d - 1], piece, q)
    sizes = (count, width, kept, local_rows * kept)
    list_pairs(sizes, index, 0, panel_cols, kept_cols, pairs, tally, 0)
    for load in loads:
        load.wait()
    add_products(lambda n: x_in[n], panel, totals, pairs, tally, 0)


def peer_kernel(sizes, first, *refs):
    cols, layers, count, piece_rows, width, local_rows, kept, height = sizes
    slots = local_rows * kept // layers
    if first == 0:
        place, panel_cols, kept_cols, *refs = refs
    else:
        pairs, tally, *refs = refs
    x_in, refs = refs[: cols - 1], refs[cols - 1 :]
    panel, before, own, sent, refs = refs[0], refs[1], refs[2], refs[3 : 2 + layers], refs[2 + layers :]
    if first == 0:
        pairs, tally, totals, whole, index, note_sem = refs
        copies = []
        for j in range(cols - 1):
            digits = x_in[j][pl.ds(count * height, 16)].astype(jnp.float32).astype(jnp.int32)
            rights, goals = positions(
                (layers, piece_rows, width, local_rows, kept),
                digits[0:1] + digits[1:2] * LANES,
                digits[2:3] + digits[3:4] * LANES,
                place[0],
                place[1],
            )
            whole[j, 0:1] = rights
            whole[j, 1:2] = goals
            copies.append(pltpu.make_async_copy(whole.at[j], index.at[j], note_sem.at[j]))
            copies[-1].start()
    else:
        (totals,) = refs
    totals[...] = before[:, first : first + height]
    if first == 0:
        for j in range(cols - 1):
            copies[j].wait()
            list_pairs(
                (count, width, kept, layers * slots),
                index.at[j],
                0,
                panel_cols,
                kept_cols,
                pairs,
                tally,
                j,
            )

    for j in range(cols - 1):

        def left(n):
            return x_in[j][pl.ds(pl.multiple_of(n * height, height), height)]

        add_products(left, panel, totals, pairs, tally, j)

    own[...] = totals[:slots]
    half = height // 2
    for d in range(1, layers):
        code = sent[d - 1]
        spare = code.shape[0] - slots * half
        code[slots * half :] = jnp.zeros((spare, code.shape[1]), jnp.int32)
        for u in range(slots):
            value = totals[d * slots + u]
            peak = jnp.max(jnp.abs(value), axis=0, keepdims=True)
            power = jnp.floor(jnp.log2(jnp.maximum(peak, 1e-30)) + 1e-3) + 1.0
            word = jnp.floor(value * jnp.exp2(15.0 - power) + 0.5).astype(jnp.int32)
            code[pl.ds(u * half, half)] = (word[:half] << 16) | (word[half:] & 0xFFFF)
            code[pl.ds(slots * half + u, 1)] = power.astype(jnp.int32)


def finish_kernel(sizes, *refs):
    layers, chunks, slots, height = sizes
    result = refs[-1]
    kept = result.shape[1]
    half = height // 2
    for c in range(chunks):
        own, codes = refs[c * layers], refs[c * layers + 1 : (c + 1) * layers]
        for u in range(slots):
            high, low = own[u, :half], own[u, half:]
            for code in codes:
                word = code[pl.ds(u * half, half)]
                power = code[pl.ds(slots * half + u, 1)].astype(jnp.float32)
                scale = jnp.exp2(power - 15.0)
                high += (word >> 16).astype(jnp.float32) * scale
                low += ((word << 16) >> 16).astype(jnp.float32) * scale
            at = c * height
            result[u // kept, u % kept, at : at + half] = high.astype(jnp.bfloat16)
            result[u // kept, u % kept, at + half : at + height] = low.astype(jnp.bfloat16)


def per_device(a_blocks, a_rows, a_cols, s_blocks, s_cols, c_cols):
    rows, cols, layers = (lax.axis_size(axis) for axis in ("row", "col", "layer"))
    count, order = a_blocks.shape[:2]
    piece_rows, width = s_cols.shape
    local_rows, kept = c_cols.shape
    own_rows = local_rows // layers
    slots = own_rows * kept
    all_slots = layers * slots
    height = order // CHUNKS
    piece = piece_rows * width
    panel_size = rows * piece
    block_size = order * order
    flat_s = s_blocks.reshape(piece, order, order)
    note_height, _ = note_rows(piece)

    scalars = pl.BlockSpec(memory_space=pltpu.SMEM)
    vector = pl.BlockSpec(memory_space=pltpu.VMEM)
    anywhere = pl.BlockSpec(memory_space=pl.ANY)

    x_first = pl.pallas_call(
        functools.partial(pack_kernel, (count, height)),
        out_shape=jax.ShapeDtypeStruct((count * height + 16, order), jnp.bfloat16),
        in_specs=[vector] * 2 + [anywhere],
        out_specs=vector,
        scratch_shapes=[pltpu.VMEM((16, LANES), jnp.int32), pltpu.SemaphoreType.DMA],
        name="pack",
    )(a_rows.reshape(1, count), a_cols.reshape(1, count), a_blocks)
    x_pieces = [[shifted(x_first, "col", j) for j in range(1, cols)]]
    s_sent = with_notes(flat_s.reshape(piece * order, order), s_cols.reshape(-1))
    s_pieces = gathered(s_sent, "row")[1:]
    later_blocks, later_rows, later_cols, _ = lax.optimization_barrier(
        (a_blocks, a_rows, a_cols, x_first)
    )
    for c in range(1, CHUNKS):
        part = lax.slice_in_dim(later_blocks, c * height, (c + 1) * height, axis=1)
        part = part.reshape(count * height, order)
        x_pieces.append([shifted(part, "col", j) for j in range(1, cols)])

    place = jnp.stack([lax.axis_index("row"), lax.axis_index("layer")])
    index = jnp.stack(
        positions(
            (layers, piece_rows, width, local_rows, kept),
            later_rows,
            later_cols,
            lax.axis_index("row"),
            lax.axis_index("layer"),
        )
    )
    moved = block_size * (4 * all_slots + 4 * panel_size + 2 * count)
    totals, panel, panel_cols, kept_cols = pl.pallas_call(
        functools.partial(
            own_kernel, (rows, layers, count, piece_rows, width, local_rows, kept, order)
        ),
        out_shape=[
            jax.ShapeDtypeStruct((all_slots + 1, order, order), jnp.float32),
            jax.ShapeDtypeStruct((panel_size, order, order), jnp.bfloat16),
            jax.ShapeDtypeStruct((panel_size,), jnp.int32),
            jax.ShapeDtypeStruct((all_slots,), jnp.int32),
        ],
        in_specs=[scalars] * 4 + [vector] * (1 + rows),
        out_specs=[vector] * 2 + [scalars] * 2,
        scratch_shapes=[
            pltpu.SMEM((1, 3, count * width + GROUP), jnp.int32),
            pltpu.SMEM((1,), jnp.int32),
            pltpu.VMEM((rows - 1, note_height, LANES), jnp.int32),
            pltpu.SMEM((rows - 1, note_height, LANES), jnp.int32),
            pltpu.SemaphoreType.DMA((panel_size,)),
            pltpu.SemaphoreType.DMA((rows - 1,)),
        ],
        compiler_params=pltpu.CompilerParams(vmem_limit_bytes=moved + 4 * MIB),
        cost_estimate=pl.CostEstimate(
            flops=2 * order**3 * count * width // 4, bytes_accessed=moved, transcendentals=0
        ),
        name="own_products",
    )(place, index, s_cols, c_cols, a_blocks, flat_s, *s_pieces)

    code_rows = slots * (height // 2) + (slots + 7) // 8 * 8
    moved = block_size * (8 * all_slots + 2 * panel_size + 2 * count * (cols - 1))
    pair_shapes = [(cols - 1, 3, count * width + GROUP), (cols - 1,)]
    final, plan = [], []
    for c in range(CHUNKS):
        out_shape = [jax.ShapeDtypeStruct((slots, height, order), jnp.float32)]
        out_shape += [jax.ShapeDtypeStruct((code_rows, order), jnp.int32)] * (layers - 1)
        out_specs = [vector] * layers
        scratch = [pltpu.VMEM((all_slots + 1, height, order), jnp.float32)]
        if c == 0:
            out_shape += [jax.ShapeDtypeStruct(shape, jnp.int32) for shape in pair_shapes]
            out_specs += [scalars] * 2
            scratch += [
                pltpu.VMEM((cols - 1, 2, LANES), jnp.int32),
                pltpu.SMEM((cols - 1, 2, LANES), jnp.int32),
                pltpu.SemaphoreType.DMA((cols - 1,)),
            ]
        given = plan or (place, panel_cols, kept_cols)
        out = pl.pallas_call(
            functools.partial(
                peer_kernel,
                (cols, layers, count, piece_rows, width, local_rows, kept, height),
                c * height,
            ),
            out_shape=out_shape,
            in_specs=[scalars] * len(given) + [vector] * (cols + 1),
            out_specs=out_specs,
            scratch_shapes=scratch,
            compiler_params=pltpu.CompilerParams(vmem_limit_bytes=moved + 4 * MIB),
            cost_estimate=pl.CostEstimate(
                flops=2 * order**2 * height * count * width // 4 * (cols - 1),
                bytes_accessed=moved // CHUNKS,
                transcendentals=0,
            ),
            name=f"peer_products_{c}",
        )(*given, *x_pieces[c], panel, totals)
        plan = plan or out[layers:]
        final.append(out[0])
        final += [shifted(out[d], "layer", layers - d) for d in range(1, layers)]

    return pl.pallas_call(
        functools.partial(finish_kernel, (layers, CHUNKS, slots, height)),
        out_shape=jax.ShapeDtypeStruct((own_rows, kept, order, order), jnp.bfloat16),
        in_specs=[vector] * len(final),
        out_specs=vector,
        compiler_params=pltpu.CompilerParams(
            vmem_limit_bytes=16 * slots * order * order + 4 * MIB
        ),
        name="finish",
    )(*final)


def solution(mesh):
    placed = (
        P(("row", "col", "layer"), None, None),
        P(("row", "col", "layer")),
        P(("row", "col", "layer")),
        P(("row", "layer"), "col", None, None),
        P(("row", "layer"), "col"),
        P("row", "col"),
    )
    return jax.shard_map(
        per_device,
        mesh=mesh,
        in_specs=placed,
        out_specs=P(("row", "layer"), "col", None, None),
        check_vma=False,
    )
```

time: 51.8 us -> 39.2 us (0.76)
  blocking collectives: 12.3 us -> 0 us
  starting transfers between devices: 10.4 us -> 16.1 us
  waiting for transfers between devices: 15.9 us -> 10.4 us
  other arithmetic: 1.66 us -> 1.08 us
    all_to_all x1 -> x0, blocking collectives: 12.3 us -> none  [per_device(): final += [own, lax.all_to_all(sent, 'layer', 0, 0, tiled=True)]]
    ppermute x5 -> x8, starting transfers between devices: 5.54 us -> 12.9 us  [shifted(): lax.ppermute(value, axis, [((i + offset) % size, i) for i in range(size)])]
    ppermute x5 -> x8, waiting for transfers between devices: 15.8 us -> 9.26 us  [shifted(): lax.ppermute(value, axis, [((i + offset) % size, i) for i in range(size)])]
    all_to_all x1 -> x0, starting transfers between devices: 4.88 us -> none  [per_device(): final += [own, lax.all_to_all(sent, 'layer', 0, 0, tiled=True)]]
    ppermute x0 -> x3, starting transfers between devices: none -> 3.18 us  [flipped(): lax.ppermute(value, axis, [(i, i ^ bits) for i in range(lax.axis_size(axi...]
    pallas_call x2 -> x3, Pallas kernels: 5.23 us -> 6.61 us  [the longest x2 4.18 us: per_device(): pl.pallas_call(functools.partial(peer_kernel, (cols, layers, count, piece...]
    ppermute x0 -> x3, waiting for transfers between devices: none -> 1.17 us  [flipped(): lax.ppermute(value, axis, [(i, i ^ bits) for i in range(lax.axis_size(axi...]
    slice x2 -> x1, local copies, waits for them, and re-layouts: 1.05 us -> 0.03 us  [per_device(): part = lax.slice_in_dim(later_blocks, c * height, (c + 1) * height, axis=1)]
  transfers between devices with their start and end apart: 6 -> 11, of which waited for: 3 -> 4; matrix products, arithmetic and copies ran while one was open for 0% -> 1% of each run, Pallas kernels for 10% -> 24%
where the time goes in v7:
time: 39.2 us; the launch traced here: 39 us
  starting transfers between devices  16.1 us (41%)
  waiting for transfers between devices  10.4 us (27%)
  Pallas kernels  10.3 us (26%)
  other arithmetic  1.08 us (3%)
  local copies, waits for them, and re-layouts  0.97 us (2%)
    ppermute x8, starting transfers between devices, shifted(): lax.ppermute(value, axis, [((i + offset) % size, i) for i in range(size)])  12.9 us
    ppermute x8, waiting for transfers between devices, shifted(): lax.ppermute(value, axis, [((i + offset) % size, i) for i in range(size)])  9.26 us
    pallas_call x2, Pallas kernels, per_device(): pl.pallas_call(functools.partial(peer_kernel, (cols, layers, count, piece...  4.18 us
    ppermute x3, starting transfers between devices, flipped(): lax.ppermute(value, axis, [(i, i ^ bits) for i in range(lax.axis_size(axi...  3.18 us
    pallas_call x1, Pallas kernels, per_device(): pl.pallas_call(functools.partial(own_kernel, (rows, layers, count, piece_...  2.9 us
    pallas_call x1, Pallas kernels, per_device(): pl.pallas_call(functools.partial(pack_kernel, (count, height)), out_shape...  2.43 us
    ppermute x3, waiting for transfers between devices, flipped(): lax.ppermute(value, axis, [(i, i ^ bits) for i in range(lax.axis_size(axi...  1.17 us
    concatenate x1, other arithmetic, with_notes(): return jnp.concatenate([payload, tile.astype(payload.dtype)])  0.97 us
  transfers between devices with their start and end apart: 11, of which 4 were waited for; matrix products, arithmetic and copies ran while one was open for 1% of the time, Pallas kernels for 24%

profile of v7, /device:TPU:0, one launch (start us, length us, event | category | flops | bytes accessed | tf_op | source)
XLA Modules:
  0.0 39.0 jit_solution(15429191640384276304)
XLA Ops:
  0.0 0.0 copy-start
  0.0 0.8 %reshape.23 = s32[4]{0:T(128)S(1)} reshape(s32[2,2]{1,0:T(2,128)} %refs_2_.1) | data formatting | bytes 32 | tf_op jit(solution)/shard_map/reshape | solution.py:288
  0.9 0.0 copy-start.3
  0.9 0.0 copy-start.4
  0.9 0.0 copy-start.5
  0.9 0.0 copy-start.1
  0.9 0.0 copy-start.2
  0.9 1.0 %pad_maximum_fusion = bf16[528,128]{1,0:T(8,128)(2,1)S(1)} fusion(bf16[16,128]{1,0:T(8,128)(2,1)S(1)} %fusion.2, bf16[512,128]{1,0:T(8,128)(2,1)} %bitcast.15), kind=kLoop, calls=%fused_computation | loop fusion | flops 270336 | bytes 270336 | tf_op jit(solution)/shard_map/concatenate | solution.py:53
  1.9 0.5 %collective-permute-start = (bf16[528,128]{1,0:T(8,128)(2,1)S(1)}, bf16[528,128]{1,0:T(8,128)(2,1)S(1)}, u32[]{:S(2)}, u32[]{:S(2)}) collective-permute-start(bf16[528,128]{1,0:T(8,128)(2,1)S(1)} %pad_maximum_fusion), channel_id=1, source_target_pairs={{0,8},{8,0},{16,24},{24,16},{1,9},{9,1},{17,25},{25,17},{2,10},{10... | collective-permute-start | bytes 405512 | tf_op jit(solution)/shard_map/ppermute | solution.py:17
  2.4 2.6 %collective-permute-start.1 = (bf16[528,128]{1,0:T(8,128)(2,1)S(1)}, bf16[528,128]{1,0:T(8,128)(2,1)S(1)}, u32[]{:S(2)}, u32[]{:S(2)}) collective-permute-start(bf16[528,128]{1,0:T(8,128)(2,1)S(1)} %pad_maximum_fusion), channel_id=1, source_target_pairs={{0,16},{8,24},{16,0},{24,8},{1,17},{9,25},{17,1},{25,9},{2,18},{10... | collective-permute-start | bytes 405512 | tf_op jit(solution)/shard_map/ppermute | solution.py:17
  5.0 2.4 %pack.1 = bf16[1552,128]{1,0:T(8,128)(2,1)} custom-call(s32[1,24]{1,0:T(1,128)} %bitcast.18, s32[1,24]{1,0:T(1,128)} %bitcast.19, bf16[24,128,128]{2,1,0:T(8,128)(2,1)} %refs_4_.1), custom_call_target="tpu_custom_call" | custom-call | tf_op jit(solution)/shard_map/pack/pallas_call | solution.py:279
  7.4 1.6 %collective-permute-start.3 = (bf16[1552,128]{1,0:T(8,128)(2,1)}, bf16[1552,128]{1,0:T(8,128)(2,1)S(1)}, u32[]{:S(2)}, u32[]{:S(2)}) collective-permute-start(bf16[1552,128]{1,0:T(8,128)(2,1)} %pack.1), channel_id=1, source_target_pairs={{4,0},{0,4},{5,1},{1,5},{6,2},{2,6},{7,3},{3,7},{12,8},{8,12},{13,... | collective-permute-start | bytes 1191944 | tf_op jit(solution)/shard_map/ppermute | solution.py:31
  9.0 0.0 copy-done
  9.0 0.6 %collective-permute-start.7 = (bf16[1536,128]{1,0:T(8,128)(2,1)S(1)}, bf16[1536,128]{1,0:T(8,128)(2,1)S(1)}, u32[]{:S(2)}, u32[]{:S(2)}) collective-permute-start(bf16[1536,128]{1,0:T(8,128)(2,1)S(1)} %bitcast.17), channel_id=1, source_target_pairs={{4,0},{0,4},{5,1},{1,5},{6,2},{2,6},{7,3},{3,7},{12,8},{8,12},{13,... | collective-permute-start | bytes 1179656 | tf_op jit(solution)/shard_map/ppermute | solution.py:31
  9.6 0.0 copy-done.3
  9.6 0.0 copy-done.4
  9.6 0.0 collective-permute-done.1.refs_7_
  9.7 0.1 collective-permute-start.2
  9.7 0.1 pad_add_fusion.1.refs_0_
  9.8 0.0 copy-done.5
  9.8 0.1 copy.7.refs_3_
  9.9 0.0 collective-permute-done.refs_6_
  9.9 1.2 %collective-permute-done.2.refs_8_ = bf16[528,128]{1,0:T(8,128)(2,1)S(1)} collective-permute-done((bf16[528,128]{1,0:T(8,128)(2,1)S(1)}, bf16[528,128]{1,0:T(8,128)(2,1)S(1)}, u32[]{:S(2)}, u32[]{:S(2)}) %collective-permute-start.2) | collective-permute-done | bytes 135200 | tf_op jit(solution)/shard_map/ppermute | solution.py:17
  11.1 0.0 copy-done.1
  11.1 0.0 copy-done.2
  11.1 2.9 %own_products.1 = (f32[17,128,128]{2,1,0:T(8,128)S(1)}, bf16[16,128,128]{2,1,0:T(8,128)(2,1)S(1)}, s32[16]{0:T(128)S(1)}, s32[16]{0:T(128)S(1)}) custom-call(s32[2]{0:T(128)S(1)} %pad_add_fusion.1.refs_0_, s32[2,24]{1,0:T(2,128)S(1)} %pad_add_fusion.refs_1_, s32[2,2]{1,0:T(2,128)S(1)} %copy-done.2, s32[8,2]{1,0:T(8,128)S(1)} %copy.7.refs_3_, ...), custom_call_target="tpu_custom_call" | custom-call | flops 50331648 | bytes 2883584 | tf_op jit(solution)/shard_map/own_products/pallas_call | solution.py:309
  14.0 5.8 %collective-permute-done.3.refs_3_ = bf16[1552,128]{1,0:T(8,128)(2,1)S(1)} collective-permute-done((bf16[1552,128]{1,0:T(8,128)(2,1)}, bf16[1552,128]{1,0:T(8,128)(2,1)S(1)}, u32[]{:S(2)}, u32[]{:S(2)}) %collective-permute-start.3) | collective-permute-done | bytes 397344 | tf_op jit(solution)/shard_map/ppermute | solution.py:31
  19.8 2.5 %peer_products_0.1 = (f32[4,64,128]{2,1,0:T(8,128)S(1)}, s32[136,128]{1,0:T(8,128)S(1)}, s32[136,128]{1,0:T(8,128)S(1)}, s32[136,128]{1,0:T(8,128)S(1)}, s32[1,3,52]{2,1,0:T(4,128)S(1)}, /*index=5*/s32[1]{0:T(128)}) custom-call(s32[2]{0:T(128)S(1)} %pad_add_fusion.1.refs_0_, s32[16]{0:T(128)S(1)} %get-tuple-element.24.refs_1_, ...), custom_call_target="tpu_custom_call" | custom-call | flops 25165824 | bytes 1703936 | tf_op jit(solution)/shard_map/peer_products_0/pallas_call | solution.py:354
  22.2 1.5 %collective-permute-start.4 = (s32[136,128]{1,0:T(8,128)S(1)}, s32[136,128]{1,0:T(8,128)S(1)}, u32[]{:S(2)}, u32[]{:S(2)}) collective-permute-start(s32[136,128]{1,0:T(8,128)S(1)} %get-tuple-element.29), channel_id=1, source_target_pairs={{3,0},{0,1},{1,2},{2,3},{7,4},{4,5},{5,6},{6,7},{11,8},{8,9},{9,10... | collective-permute-start | bytes 208904 | tf_op jit(solution)/shard_map/ppermute | solution.py:31
  23.7 2.8 %collective-permute-start.5 = (s32[136,128]{1,0:T(8,128)S(1)}, s32[136,128]{1,0:T(8,128)S(1)}, u32[]{:S(2)}, u32[]{:S(2)}) collective-permute-start(s32[136,128]{1,0:T(8,128)S(1)} %get-tuple-element.30), channel_id=1, source_target_pairs={{2,0},{3,1},{0,2},{1,3},{6,4},{7,5},{4,6},{5,7},{10,8},{11,9},{8,1... | collective-permute-start | bytes 208904 | tf_op jit(solution)/shard_map/ppermute | solution.py:31
  26.4 1.4 %collective-permute-start.6 = (s32[136,128]{1,0:T(8,128)S(1)}, s32[136,128]{1,0:T(8,128)S(1)}, u32[]{:S(2)}, u32[]{:S(2)}) collective-permute-start(s32[136,128]{1,0:T(8,128)S(1)} %get-tuple-element.31), channel_id=1, source_target_pairs={{1,0},{2,1},{3,2},{0,3},{5,4},{6,5},{7,6},{4,7},{9,8},{10,9},{11,1... | collective-permute-start | bytes 208904 | tf_op jit(solution)/shard_map/ppermute | solution.py:31
  27.8 0.0 collective-permute-done.7.refs_2_
  27.8 1.7 %peer_products_1.1 = (f32[4,64,128]{2,1,0:T(8,128)S(1)}, s32[136,128]{1,0:T(8,128)S(1)}, s32[136,128]{1,0:T(8,128)S(1)}, s32[136,128]{1,0:T(8,128)S(1)}) custom-call(s32[1,3,52]{2,1,0:T(4,128)S(1)} %get-tuple-element.32.refs_0_, s32[1]{0:T(128)} %get-tuple-element.33.refs_1_, bf16[1536,128]{1,0:T(8,128)(2,1)S(1)} %collective-permute-done.7.refs_2_, ...), custom_call_target="tpu_custom_call" | custom-call | flops 25165824 | bytes 1703936 | tf_op jit(solution)/shard_map/peer_products_1/pallas_call | solution.py:354
  29.5 1.1 %collective-permute-start.8 = (s32[136,128]{1,0:T(8,128)S(1)}, s32[136,128]{1,0:T(8,128)S(1)}, u32[]{:S(2)}, u32[]{:S(2)}) collective-permute-start(s32[136,128]{1,0:T(8,128)S(1)} %get-tuple-element.36), channel_id=1, source_target_pairs={{3,0},{0,1},{1,2},{2,3},{7,4},{4,5},{5,6},{6,7},{11,8},{8,9},{9,10... | collective-permute-start | bytes 208904 | tf_op jit(solution)/shard_map/ppermute | solution.py:31
  30.6 2.8 %collective-permute-start.9 = (s32[136,128]{1,0:T(8,128)S(1)}, s32[136,128]{1,0:T(8,128)S(1)}, u32[]{:S(2)}, u32[]{:S(2)}) collective-permute-start(s32[136,128]{1,0:T(8,128)S(1)} %get-tuple-element.37), channel_id=1, source_target_pairs={{2,0},{3,1},{0,2},{1,3},{6,4},{7,5},{4,6},{5,7},{10,8},{11,9},{8,1... | collective-permute-start | bytes 208904 | tf_op jit(solution)/shard_map/ppermute | solution.py:31
  33.4 0.0 collective-permute-done.4.refs_1_
  33.4 1.4 %collective-permute-start.10 = (s32[136,128]{1,0:T(8,128)S(1)}, s32[136,128]{1,0:T(8,128)S(1)}, u32[]{:S(2)}, u32[]{:S(2)}) collective-permute-start(s32[136,128]{1,0:T(8,128)S(1)} %get-tuple-element.38), channel_id=1, source_target_pairs={{1,0},{2,1},{3,2},{0,3},{5,4},{6,5},{7,6},{4,7},{9,8},{10,9},{11,1... | collective-permute-start | bytes 208904 | tf_op jit(solution)/shard_map/ppermute | solution.py:31
  34.7 0.0 collective-permute-done.5.refs_2_
  34.7 0.0 collective-permute-done.6.refs_3_
  34.7 1.7 %collective-permute-done.8.refs_5_ = s32[136,128]{1,0:T(8,128)S(1)} collective-permute-done((s32[136,128]{1,0:T(8,128)S(1)}, s32[136,128]{1,0:T(8,128)S(1)}, u32[]{:S(2)}, u32[]{:S(2)}) %collective-permute-start.8) | collective-permute-done | bytes 69664 | tf_op jit(solution)/shard_map/ppermute | solution.py:31
  36.4 1.8 %collective-permute-done.9.refs_6_ = s32[136,128]{1,0:T(8,128)S(1)} collective-permute-done((s32[136,128]{1,0:T(8,128)S(1)}, s32[136,128]{1,0:T(8,128)S(1)}, u32[]{:S(2)}, u32[]{:S(2)}) %collective-permute-start.9) | collective-permute-done | bytes 69664 | tf_op jit(solution)/shard_map/ppermute | solution.py:31
  38.2 0.0 collective-permute-done.10.refs_7_
  38.2 0.8 %finish.1 = bf16[2,2,128,128]{3,2,1,0:T(8,128)(2,1)} custom-call(f32[4,64,128]{2,1,0:T(8,128)S(1)} %get-tuple-element.28.refs_0_, s32[136,128]{1,0:T(8,128)S(1)} %collective-permute-done.4.refs_1_, s32[136,128]{1,0:T(8,128)S(1)} %collective-permute-done.5.refs_2_, s32[136,128]{1,0:T(8,128)S(1)} %collective-permute-done.6.refs_3_, ...), custom_call_target="tpu_custom_call" | custom-call | tf_op jit(solution)/shard_map/finish/pallas_call | solution.py:376
  (5 shorter events, 0.1 us)
Async XLA Ops:
  0.0 9.0 %copy-start = (bf16[24,128,128]{2,1,0:T(8,128)(2,1)S(1)}, bf16[24,128,128]{2,1,0:T(8,128)(2,1)}, u32[]{:S(2)}) copy-start(bf16[24,128,128]{2,1,0:T(8,128)(2,1)} %refs_4_.1) | copy-start | bytes 2359300
  0.9 8.8 %copy-start.3 = (s32[24]{0:T(128)S(1)}, s32[24]{0:T(128)}, u32[]{:S(2)}) copy-start(s32[24]{0:T(128)} %param.7) | copy-start | bytes 292
  0.9 8.8 %copy-start.4 = (s32[24]{0:T(128)S(1)}, s32[24]{0:T(128)}, u32[]{:S(2)}) copy-start(s32[24]{0:T(128)} %param.8) | copy-start | bytes 292
  0.9 8.9 %copy-start.5 = (s32[8,2]{0,1:T(2,128)S(1)}, s32[8,2]{0,1:T(2,128)}, u32[]{:S(2)}) copy-start(s32[8,2]{0,1:T(2,128)} %param.11) | copy-start | bytes 196
  0.9 10.2 %copy-start.1 = (bf16[2,2,128,128]{3,2,1,0:T(8,128)(2,1)S(1)}, bf16[2,2,128,128]{3,2,1,0:T(8,128)(2,1)}, u32[]{:S(2)}) copy-start(bf16[2,2,128,128]{3,2,1,0:T(8,128)(2,1)} %param.9) | copy-start | bytes 393220
  0.9 10.2 %copy-start.2 = (s32[2,2]{1,0:T(2,128)S(1)}, s32[2,2]{1,0:T(2,128)}, u32[]{:S(2)}) copy-start(s32[2,2]{1,0:T(2,128)} %refs_2_.1) | copy-start | bytes 52
  1.9 8.0 %collective-permute-start = (bf16[528,128]{1,0:T(8,128)(2,1)S(1)}, bf16[528,128]{1,0:T(8,128)(2,1)S(1)}, u32[]{:S(2)}, u32[]{:S(2)}) collective-permute-start(bf16[528,128]{1,0:T(8,128)(2,1)S(1)} %pad_maximum_fusion), channel_id=1, source_target_pairs={{0,8},{8,0},{16,24},{24,16},{1,9},{9,1},{17,25},{25,17},{2,10},{10... | collective-permute-start | bytes 405512 | tf_op jit(solution)/shard_map/ppermute | solution.py:17
  2.4 7.2 %collective-permute-start.1 = (bf16[528,128]{1,0:T(8,128)(2,1)S(1)}, bf16[528,128]{1,0:T(8,128)(2,1)S(1)}, u32[]{:S(2)}, u32[]{:S(2)}) collective-permute-start(bf16[528,128]{1,0:T(8,128)(2,1)S(1)} %pad_maximum_fusion), channel_id=1, source_target_pairs={{0,16},{8,24},{16,0},{24,8},{1,17},{9,25},{17,1},{25,9},{2,18},{10... | collective-permute-start | bytes 405512 | tf_op jit(solution)/shard_map/ppermute | solution.py:17
  7.4 12.3 %collective-permute-start.3 = (bf16[1552,128]{1,0:T(8,128)(2,1)}, bf16[1552,128]{1,0:T(8,128)(2,1)S(1)}, u32[]{:S(2)}, u32[]{:S(2)}) collective-permute-start(bf16[1552,128]{1,0:T(8,128)(2,1)} %pack.1), channel_id=1, source_target_pairs={{4,0},{0,4},{5,1},{1,5},{6,2},{2,6},{7,3},{3,7},{12,8},{8,12},{13,... | collective-permute-start | bytes 1191944 | tf_op jit(solution)/shard_map/ppermute | solution.py:31
  9.0 18.8 %collective-permute-start.7 = (bf16[1536,128]{1,0:T(8,128)(2,1)S(1)}, bf16[1536,128]{1,0:T(8,128)(2,1)S(1)}, u32[]{:S(2)}, u32[]{:S(2)}) collective-permute-start(bf16[1536,128]{1,0:T(8,128)(2,1)S(1)} %bitcast.17), channel_id=1, source_target_pairs={{4,0},{0,4},{5,1},{1,5},{6,2},{2,6},{7,3},{3,7},{12,8},{8,12},{13,... | collective-permute-start | bytes 1179656 | tf_op jit(solution)/shard_map/ppermute | solution.py:31
  9.7 1.4 %collective-permute-start.2 = (bf16[528,128]{1,0:T(8,128)(2,1)S(1)}, bf16[528,128]{1,0:T(8,128)(2,1)S(1)}, u32[]{:S(2)}, u32[]{:S(2)}) collective-permute-start(bf16[528,128]{1,0:T(8,128)(2,1)S(1)} %collective-permute-done.1.refs_7_), channel_id=1, source_target_pairs={{0,8},{8,0},{16,24},{24,16},{1,9},{9,1},{17,25},{25,17},{2,10},{10... | collective-permute-start | bytes 405512 | tf_op jit(solution)/shard_map/ppermute | solution.py:17
  22.2 11.1 %collective-permute-start.4 = (s32[136,128]{1,0:T(8,128)S(1)}, s32[136,128]{1,0:T(8,128)S(1)}, u32[]{:S(2)}, u32[]{:S(2)}) collective-permute-start(s32[136,128]{1,0:T(8,128)S(1)} %get-tuple-element.29), channel_id=1, source_target_pairs={{3,0},{0,1},{1,2},{2,3},{7,4},{4,5},{5,6},{6,7},{11,8},{8,9},{9,10... | collective-permute-start | bytes 208904 | tf_op jit(solution)/shard_map/ppermute | solution.py:31
  23.7 11.0 %collective-permute-start.5 = (s32[136,128]{1,0:T(8,128)S(1)}, s32[136,128]{1,0:T(8,128)S(1)}, u32[]{:S(2)}, u32[]{:S(2)}) collective-permute-start(s32[136,128]{1,0:T(8,128)S(1)} %get-tuple-element.30), channel_id=1, source_target_pairs={{2,0},{3,1},{0,2},{1,3},{6,4},{7,5},{4,6},{5,7},{10,8},{11,9},{8,1... | collective-permute-start | bytes 208904 | tf_op jit(solution)/shard_map/ppermute | solution.py:31
  26.4 8.3 %collective-permute-start.6 = (s32[136,128]{1,0:T(8,128)S(1)}, s32[136,128]{1,0:T(8,128)S(1)}, u32[]{:S(2)}, u32[]{:S(2)}) collective-permute-start(s32[136,128]{1,0:T(8,128)S(1)} %get-tuple-element.31), channel_id=1, source_target_pairs={{1,0},{2,1},{3,2},{0,3},{5,4},{6,5},{7,6},{4,7},{9,8},{10,9},{11,1... | collective-permute-start | bytes 208904 | tf_op jit(solution)/shard_map/ppermute | solution.py:31
  29.5 6.9 %collective-permute-start.8 = (s32[136,128]{1,0:T(8,128)S(1)}, s32[136,128]{1,0:T(8,128)S(1)}, u32[]{:S(2)}, u32[]{:S(2)}) collective-permute-start(s32[136,128]{1,0:T(8,128)S(1)} %get-tuple-element.36), channel_id=1, source_target_pairs={{3,0},{0,1},{1,2},{2,3},{7,4},{4,5},{5,6},{6,7},{11,8},{8,9},{9,10... | collective-permute-start | bytes 208904 | tf_op jit(solution)/shard_map/ppermute | solution.py:31
  30.6 7.6 %collective-permute-start.9 = (s32[136,128]{1,0:T(8,128)S(1)}, s32[136,128]{1,0:T(8,128)S(1)}, u32[]{:S(2)}, u32[]{:S(2)}) collective-permute-start(s32[136,128]{1,0:T(8,128)S(1)} %get-tuple-element.37), channel_id=1, source_target_pairs={{2,0},{3,1},{0,2},{1,3},{6,4},{7,5},{4,6},{5,7},{10,8},{11,9},{8,1... | collective-permute-start | bytes 208904 | tf_op jit(solution)/shard_map/ppermute | solution.py:31
  33.4 4.8 %collective-permute-start.10 = (s32[136,128]{1,0:T(8,128)S(1)}, s32[136,128]{1,0:T(8,128)S(1)}, u32[]{:S(2)}, u32[]{:S(2)}) collective-permute-start(s32[136,128]{1,0:T(8,128)S(1)} %get-tuple-element.38), channel_id=1, source_target_pairs={{1,0},{2,1},{3,2},{0,3},{5,4},{6,5},{7,6},{4,7},{9,8},{10,9},{11,1... | collective-permute-start | bytes 208904 | tf_op jit(solution)/shard_map/ppermute | solution.py:31

commit v8 on v7

--- a/solution.py
+++ b/solution.py
@@ -72,21 +72,19 @@
     owner = quotient(a_cols, piece_rows * layers)
     rights = ((owner ^ row_at) * piece_rows + remainder(a_cols, piece_rows)) * width
     local = a_rows - row_at * local_rows
-    goals = remainder(quotient(local, own_rows) - layer_at + layers, layers) * own_rows
+    goals = (quotient(local, own_rows) ^ layer_at) * own_rows
     return rights, (goals + remainder(local, own_rows)) * kept
 
 
-def pack_kernel(sizes, a_rows, a_cols, x_in, x_out, tile, sem):
+def pack_kernel(sizes, a_rows, a_cols, x_in, x_out, tile):
     count, height = sizes
-    spot = x_out.at[pl.ds(0, count * height)].reshape(count, height, x_out.shape[1])
-    load = pltpu.make_async_copy(x_in.at[:, pl.ds(0, height), :], spot, sem)
-    load.start()
+    x_out[:count] = x_in[:, :height]
     tile[...] = jnp.zeros_like(tile)
     for p, value in enumerate((a_rows[...], a_cols[...])):
         tile[2 * p : 2 * p + 1, :count] = remainder(value, LANES)
         tile[2 * p + 1 : 2 * p + 2, :count] = quotient(value, LANES)
-    x_out[count * height :] = tile[...].astype(jnp.float32).astype(jnp.bfloat16)
-    load.wait()
+    x_out[count, :16] = tile[...].astype(jnp.float32).astype(jnp.bfloat16)
+    x_out[count, 16:] = jnp.zeros((height - 16, LANES), jnp.bfloat16)
 
 
 def list_pairs(sizes, index, row, panel_cols, kept_cols, pairs, tally, j):
@@ -135,28 +133,20 @@
     place, index, s_cols, c_cols, x_in, s_in = refs[:6]
     s_other, refs = refs[6 : 5 + rows], refs[5 + rows :]
     totals, panel, panel_cols, kept_cols = refs[:4]
-    pairs, tally, whole, notes, s_sem, note_sem = refs[4:]
+    pairs, tally, whole, notes, note_sem = refs[4:]
     piece = piece_rows * width
-    loads = [pltpu.make_async_copy(s_in, panel.at[pl.ds(0, piece)], s_sem.at[0])]
-    for d in range(1, rows):
-        loads += [
-            pltpu.make_async_copy(
-                s_other[d - 1].at[pl.ds(q * order, order)],
-                panel.at[d * piece + q],
-                s_sem.at[d * piece + q],
-            )
-            for q in range(piece)
-        ]
     reads = [
         read_notes(s_other[d], piece * order, piece, whole.at[d], notes.at[d], note_sem.at[d])
         for d in range(rows - 1)
     ]
-    for load in loads:
-        load.start()
     totals[...] = jnp.zeros_like(totals)
+    panel[:piece] = s_in[...]
+    for d in range(1, rows):
+        for q in range(piece):
+            panel[d * piece + q] = s_other[d - 1][q * order : (q + 1) * order]
     own_rows = local_rows // layers
     for g in range(layers):
-        base = remainder(place[1] + g, layers) * own_rows
+        base = (place[1] ^ g) * own_rows
         for i in range(own_rows):
             for t in range(kept):
                 kept_cols[(g * own_rows + i) * kept + t] = c_cols[base + i, t]
@@ -168,8 +158,6 @@
             panel_cols[d * piece + q] = note(notes.at[d - 1], piece, q)
     sizes = (count, width, kept, local_rows * kept)
     list_pairs(sizes, index, 0, panel_cols, kept_cols, pairs, tally, 0)
-    for load in loads:
-        load.wait()
     add_products(lambda n: x_in[n], panel, totals, pairs, tally, 0)
 
 
@@ -186,7 +174,7 @@
         pairs, tally, totals, whole, index, note_sem = refs
         copies = []
         for j in range(cols - 1):
-            digits = x_in[j][pl.ds(count * height, 16)].astype(jnp.float32).astype(jnp.int32)
+            digits = x_in[j][count, :16].astype(jnp.float32).astype(jnp.int32)
             rights, goals = positions(
                 (layers, piece_rows, width, local_rows, kept),
                 digits[0:1] + digits[1:2] * LANES,
@@ -216,11 +204,7 @@
             )
 
     for j in range(cols - 1):
-
-        def left(n):
-            return x_in[j][pl.ds(pl.multiple_of(n * height, height), height)]
-
-        add_products(left, panel, totals, pairs, tally, j)
+        add_products(lambda n: x_in[j][n], panel, totals, pairs, tally, j)
 
     own[...] = totals[:slots]
     half = height // 2
@@ -278,22 +262,24 @@
 
     x_first = pl.pallas_call(
         functools.partial(pack_kernel, (count, height)),
-        out_shape=jax.ShapeDtypeStruct((count * height + 16, order), jnp.bfloat16),
-        in_specs=[vector] * 2 + [anywhere],
+        out_shape=jax.ShapeDtypeStruct((count + 1, height, order), jnp.bfloat16),
+        in_specs=[vector] * 3,
         out_specs=vector,
-        scratch_shapes=[pltpu.VMEM((16, LANES), jnp.int32), pltpu.SemaphoreType.DMA],
+        scratch_shapes=[pltpu.VMEM((16, LANES), jnp.int32)],
+        compiler_params=pltpu.CompilerParams(
+            vmem_limit_bytes=2 * block_size * (2 * count + 1) + 4 * MIB
+        ),
         name="pack",
     )(a_rows.reshape(1, count), a_cols.reshape(1, count), a_blocks)
     x_pieces = [[shifted(x_first, "col", j) for j in range(1, cols)]]
-    s_sent = with_notes(flat_s.reshape(piece * order, order), s_cols.reshape(-1))
-    s_pieces = gathered(s_sent, "row")[1:]
-    later_blocks, later_rows, later_cols, _ = lax.optimization_barrier(
-        (a_blocks, a_rows, a_cols, x_first)
+    later_s, later_blocks, later_rows, later_cols, _ = lax.optimization_barrier(
+        (flat_s, a_blocks, a_rows, a_cols, x_first)
     )
     for c in range(1, CHUNKS):
         part = lax.slice_in_dim(later_blocks, c * height, (c + 1) * height, axis=1)
-        part = part.reshape(count * height, order)
         x_pieces.append([shifted(part, "col", j) for j in range(1, cols)])
+    s_sent = with_notes(later_s.reshape(piece * order, order), s_cols.reshape(-1))
+    s_pieces = gathered(s_sent, "row")[1:]
 
     place = jnp.stack([lax.axis_index("row"), lax.axis_index("layer")])
     index = jnp.stack(
@@ -323,7 +309,6 @@
             pltpu.SMEM((1,), jnp.int32),
             pltpu.VMEM((rows - 1, note_height, LANES), jnp.int32),
             pltpu.SMEM((rows - 1, note_height, LANES), jnp.int32),
-            pltpu.SemaphoreType.DMA((panel_size,)),
             pltpu.SemaphoreType.DMA((rows - 1,)),
         ],
         compiler_params=pltpu.CompilerParams(vmem_limit_bytes=moved + 4 * MIB),
@@ -337,6 +322,7 @@
     moved = block_size * (8 * all_slots + 2 * panel_size + 2 * count * (cols - 1))
     pair_shapes = [(cols - 1, 3, count * width + GROUP), (cols - 1,)]
     final, plan = [], []
+    order_out = sorted(range(1, layers), key=lambda d: (1 - d % 2, d))
     for c in range(CHUNKS):
         out_shape = [jax.ShapeDtypeStruct((slots, height, order), jnp.float32)]
         out_shape += [jax.ShapeDtypeStruct((code_rows, order), jnp.int32)] * (layers - 1)
@@ -371,7 +357,7 @@
         )(*given, *x_pieces[c], panel, totals)
         plan = plan or out[layers:]
         final.append(out[0])
-        final += [shifted(out[d], "layer", layers - d) for d in range(1, layers)]
+        final += [flipped(out[d], "layer", d) for d in order_out]
 
     return pl.pallas_call(
         functools.partial(finish_kernel, (layers, CHUNKS, slots, height)),

time: 39.2 us -> 39.8 us (1.015)
  waiting for transfers between devices: 10.4 us -> 14.3 us
  Pallas kernels: 10.3 us -> 7.67 us
  local copies, waits for them, and re-layouts: 0.97 us -> 3.39 us
  starting transfers between devices: 16.1 us -> 14 us
  other arithmetic: 1.08 us -> 0.12 us
    ppermute x8 -> x2, starting transfers between devices: 12.9 us -> 2.09 us  [shifted(): lax.ppermute(value, axis, [((i + offset) % size, i) for i in range(size)])]
    ppermute x3 -> x9, starting transfers between devices: 3.18 us -> 11.9 us  [flipped(): lax.ppermute(value, axis, [(i, i ^ bits) for i in range(lax.axis_size(axi...]
    ppermute x3 -> x9, waiting for transfers between devices: 1.17 us -> 9.56 us  [flipped(): lax.ppermute(value, axis, [(i, i ^ bits) for i in range(lax.axis_size(axi...]
    ppermute x8 -> x2, waiting for transfers between devices: 9.26 us -> 4.72 us  [shifted(): lax.ppermute(value, axis, [((i + offset) % size, i) for i in range(size)])]
    unnamed x13 -> x19, local copies, waits for them, and re-layouts: 0.11 us -> 3.28 us
    pallas_call x1, Pallas kernels: 2.43 us -> 0.04 us  [per_device(): pl.pallas_call(functools.partial(pack_kernel, (count, height)), out_shape...]
    concatenate x1, other arithmetic: 0.97 us -> 0.01 us  [with_notes(): return jnp.concatenate([payload, tile.astype(payload.dtype)])]
    reshape x1, local copies, waits for them, and re-layouts: 0.83 us -> 0.08 us  [per_device(): s_cols.reshape(-1)]
  transfers between devices with their start and end apart: 11 -> 11, of which waited for: 4 -> 6; matrix products, arithmetic and copies ran while one was open for 1% -> 0% of each run, Pallas kernels for 24% -> 17%
where the time goes in v8:
time: 39.8 us; the launch traced here: 39.6 us
  waiting for transfers between devices  14.3 us (36%)
  starting transfers between devices  14 us (35%)
  Pallas kernels  7.67 us (19%)
  local copies, waits for them, and re-layouts  3.39 us (9%)
    ppermute x9, starting transfers between devices, flipped(): lax.ppermute(value, axis, [(i, i ^ bits) for i in range(lax.axis_size(axi...  11.9 us
    ppermute x9, waiting for transfers between devices, flipped(): lax.ppermute(value, axis, [(i, i ^ bits) for i in range(lax.axis_size(axi...  9.56 us
    ppermute x2, waiting for transfers between devices, shifted(): lax.ppermute(value, axis, [((i + offset) % size, i) for i in range(size)])  4.72 us
    pallas_call x2, Pallas kernels, per_device(): pl.pallas_call(functools.partial(peer_kernel, (cols, layers, count, piece...  3.83 us
    unnamed x19, local copies, waits for them, and re-layouts  3.28 us
    pallas_call x1, Pallas kernels, per_device(): pl.pallas_call(functools.partial(own_kernel, (rows, layers, count, piece_...  3.01 us
    ppermute x2, starting transfers between devices, shifted(): lax.ppermute(value, axis, [((i + offset) % size, i) for i in range(size)])  2.09 us
    pallas_call x1, Pallas kernels, per_device(): pl.pallas_call(functools.partial(finish_kernel, (layers, CHUNKS, slots, h...  0.8 us
  transfers between devices with their start and end apart: 11, of which 6 were waited for; matrix products, arithmetic and copies ran while one was open for 0% of the time, Pallas kernels for 17%

profile of v8, /device:TPU:0, one launch (start us, length us, event | category | flops | bytes accessed | tf_op | source)
XLA Modules:
  0.0 39.6 jit_solution(15826851621678855023)
XLA Ops:
  0.0 0.0 copy-start.7
  0.0 0.0 copy-start
  0.0 1.1 %copy-done = bf16[24,128,128]{2,1,0:T(8,128)(2,1)S(1)} copy-done((bf16[24,128,128]{2,1,0:T(8,128)(2,1)S(1)}, bf16[24,128,128]{2,1,0:T(8,128)(2,1)}, u32[]{:S(2)}) %copy-start) | copy-done | bytes 786456
  1.1 0.0 copy-start.3
  1.2 0.7 %copy-done.3 = s32[24]{0:T(128)S(1)} copy-done((s32[24]{0:T(128)S(1)}, s32[24]{0:T(128)}, u32[]{:S(2)}) %copy-start.3) | copy-done | bytes 120
  1.8 0.0 copy-start.5
  1.8 0.7 %copy-done.5 = s32[24]{0:T(128)S(1)} copy-done((s32[24]{0:T(128)S(1)}, s32[24]{0:T(128)}, u32[]{:S(2)}) %copy-start.5) | copy-done | bytes 120
  2.5 0.0 copy-start.2
  2.5 0.0 copy-start.1
  2.5 0.0 copy-start.4
  2.5 0.0 copy-start.6
  2.5 0.0 copy-start.8
  2.5 0.0 copy-done.7
  2.5 0.1 reshape.24
  2.6 0.7 %copy-done.2 = bf16[2,2,128,128]{3,2,1,0:T(8,128)(2,1)S(1)} copy-done((bf16[2,2,128,128]{3,2,1,0:T(8,128)(2,1)S(1)}, bf16[2,2,128,128]{3,2,1,0:T(8,128)(2,1)}, u32[]{:S(2)}) %copy-start.2) | copy-done | bytes 131096
  3.4 0.5 %collective-permute-start = (bf16[528,128]{1,0:T(8,128)(2,1)S(1)}, bf16[528,128]{1,0:T(8,128)(2,1)S(1)}, u32[]{:S(2)}, u32[]{:S(2)}) collective-permute-start(bf16[528,128]{1,0:T(8,128)(2,1)S(1)} %pad_maximum_fusion), channel_id=1, source_target_pairs={{0,8},{8,0},{16,24},{24,16},{1,9},{9,1},{17,25},{25,17},{2,10},{10... | collective-permute-start | bytes 405512 | tf_op jit(solution)/shard_map/ppermute | solution.py:17
  3.9 2.6 %collective-permute-start.1 = (bf16[528,128]{1,0:T(8,128)(2,1)S(1)}, bf16[528,128]{1,0:T(8,128)(2,1)S(1)}, u32[]{:S(2)}, u32[]{:S(2)}) collective-permute-start(bf16[528,128]{1,0:T(8,128)(2,1)S(1)} %pad_maximum_fusion), channel_id=1, source_target_pairs={{0,16},{8,24},{16,0},{24,8},{1,17},{9,25},{17,1},{25,9},{2,18},{10... | collective-permute-start | bytes 405512 | tf_op jit(solution)/shard_map/ppermute | solution.py:17
  6.5 1.5 %collective-permute-start.3 = (bf16[25,64,128]{2,1,0:T(8,128)(2,1)S(1)}, bf16[25,64,128]{2,1,0:T(8,128)(2,1)S(1)}, u32[]{:S(2)}, u32[]{:S(2)}) collective-permute-start(bf16[25,64,128]{2,1,0:T(8,128)(2,1)S(1)} %pack.1), channel_id=1, source_target_pairs={{4,0},{0,4},{5,1},{1,5},{6,2},{2,6},{7,3},{3,7},{12,8},{8,12},{13,... | collective-permute-start | bytes 1228808 | tf_op jit(solution)/shard_map/ppermute | solution.py:31
  8.0 0.0 copy-done.1
  8.0 0.6 %collective-permute-start.7 = (bf16[24,64,128]{2,1,0:T(8,128)(2,1)S(1)}, bf16[24,64,128]{2,1,0:T(8,128)(2,1)S(1)}, u32[]{:S(2)}, u32[]{:S(2)}) collective-permute-start(bf16[24,64,128]{2,1,0:T(8,128)(2,1)S(1)} %slice.3), channel_id=1, source_target_pairs={{4,0},{0,4},{5,1},{1,5},{6,2},{2,6},{7,3},{3,7},{12,8},{8,12},{13,... | collective-permute-start | bytes 1179656 | tf_op jit(solution)/shard_map/ppermute | solution.py:31
  8.6 0.0 copy-done.4
  8.6 0.0 copy-done.6
  8.6 2.0 %collective-permute-done.1.refs_7_ = bf16[528,128]{1,0:T(8,128)(2,1)S(1)} collective-permute-done((bf16[528,128]{1,0:T(8,128)(2,1)S(1)}, bf16[528,128]{1,0:T(8,128)(2,1)S(1)}, u32[]{:S(2)}, u32[]{:S(2)}) %collective-permute-start.1) | collective-permute-done | bytes 135200 | tf_op jit(solution)/shard_map/ppermute | solution.py:17
  10.7 0.0 collective-permute-start.2
  10.7 0.1 pad_add_fusion.1.refs_0_
  10.7 0.0 copy-done.8
  10.8 0.1 copy.7.refs_3_
  10.8 0.0 collective-permute-done.refs_6_
  10.8 1.2 %collective-permute-done.2.refs_8_ = bf16[528,128]{1,0:T(8,128)(2,1)S(1)} collective-permute-done((bf16[528,128]{1,0:T(8,128)(2,1)S(1)}, bf16[528,128]{1,0:T(8,128)(2,1)S(1)}, u32[]{:S(2)}, u32[]{:S(2)}) %collective-permute-start.2) | collective-permute-done | bytes 135200 | tf_op jit(solution)/shard_map/ppermute | solution.py:17
  12.0 3.0 %own_products.1 = (f32[17,128,128]{2,1,0:T(8,128)S(1)}, bf16[16,128,128]{2,1,0:T(8,128)(2,1)S(1)}, s32[16]{0:T(128)S(1)}, s32[16]{0:T(128)S(1)}) custom-call(s32[2]{0:T(128)S(1)} %pad_add_fusion.1.refs_0_, s32[2,24]{1,0:T(2,128)S(1)} %pad_add_fusion.refs_1_, s32[2,2]{1,0:T(2,128)S(1)} %copy-done.7, s32[8,2]{1,0:T(8,128)S(1)} %copy.7.refs_3_, ...), custom_call_target="tpu_custom_call" | custom-call | flops 50331648 | bytes 2883584 | tf_op jit(solution)/shard_map/own_products/pallas_call | solution.py:295
  15.0 3.8 %collective-permute-done.3.refs_3_ = bf16[25,64,128]{2,1,0:T(8,128)(2,1)S(1)} collective-permute-done((bf16[25,64,128]{2,1,0:T(8,128)(2,1)S(1)}, bf16[25,64,128]{2,1,0:T(8,128)(2,1)S(1)}, u32[]{:S(2)}, u32[]{:S(2)}) %collective-permute-start.3) | collective-permute-done | bytes 409632 | tf_op jit(solution)/shard_map/ppermute | solution.py:31
  18.8 2.3 %peer_products_0.1 = (f32[4,64,128]{2,1,0:T(8,128)S(1)}, s32[136,128]{1,0:T(8,128)S(1)}, s32[136,128]{1,0:T(8,128)S(1)}, s32[136,128]{1,0:T(8,128)S(1)}, s32[1,3,52]{2,1,0:T(4,128)S(1)}, /*index=5*/s32[1]{0:T(128)}) custom-call(s32[2]{0:T(128)S(1)} %pad_add_fusion.1.refs_0_, s32[16]{0:T(128)S(1)} %get-tuple-element.26.refs_1_, ...), custom_call_target="tpu_custom_call" | custom-call | flops 25165824 | bytes 1703936 | tf_op jit(solution)/shard_map/peer_products_0/pallas_call | solution.py:340
  21.1 1.8 %collective-permute-start.4 = (s32[136,128]{1,0:T(8,128)S(1)}, s32[136,128]{1,0:T(8,128)S(1)}, u32[]{:S(2)}, u32[]{:S(2)}) collective-permute-start(s32[136,128]{1,0:T(8,128)S(1)} %get-tuple-element.31), channel_id=1, source_target_pairs={{0,1},{1,0},{2,3},{3,2},{4,5},{5,4},{6,7},{7,6},{8,9},{9,8},{10,11... | collective-permute-start | bytes 208904 | tf_op jit(solution)/shard_map/ppermute | solution.py:17
  22.9 2.5 %collective-permute-start.5 = (s32[136,128]{1,0:T(8,128)S(1)}, s32[136,128]{1,0:T(8,128)S(1)}, u32[]{:S(2)}, u32[]{:S(2)}) collective-permute-start(s32[136,128]{1,0:T(8,128)S(1)} %get-tuple-element.32), channel_id=1, source_target_pairs={{0,3},{1,2},{2,1},{3,0},{4,7},{5,6},{6,5},{7,4},{8,11},{9,10},{10,... | collective-permute-start | bytes 208904 | tf_op jit(solution)/shard_map/ppermute | solution.py:17
  25.4 0.1 collective-permute-start.6
  25.5 1.0 %collective-permute-done.7.refs_2_ = bf16[24,64,128]{2,1,0:T(8,128)(2,1)S(1)} collective-permute-done((bf16[24,64,128]{2,1,0:T(8,128)(2,1)S(1)}, bf16[24,64,128]{2,1,0:T(8,128)(2,1)S(1)}, u32[]{:S(2)}, u32[]{:S(2)}) %collective-permute-start.7) | collective-permute-done | bytes 393248 | tf_op jit(solution)/shard_map/ppermute | solution.py:31
  26.5 1.6 %peer_products_1.1 = (f32[4,64,128]{2,1,0:T(8,128)S(1)}, s32[136,128]{1,0:T(8,128)S(1)}, s32[136,128]{1,0:T(8,128)S(1)}, s32[136,128]{1,0:T(8,128)S(1)}) custom-call(s32[1,3,52]{2,1,0:T(4,128)S(1)} %get-tuple-element.34.refs_0_, s32[1]{0:T(128)} %get-tuple-element.35.refs_1_, bf16[24,64,128]{2,1,0:T(8,128)(2,1)S(1)} %collective-permute-done.7.refs_2_, ...), custom_call_target="tpu_custom_call" | custom-call | flops 25165824 | bytes 1703936 | tf_op jit(solution)/shard_map/peer_products_1/pallas_call | solution.py:340
  28.0 1.8 %collective-permute-start.8 = (s32[136,128]{1,0:T(8,128)S(1)}, s32[136,128]{1,0:T(8,128)S(1)}, u32[]{:S(2)}, u32[]{:S(2)}) collective-permute-start(s32[136,128]{1,0:T(8,128)S(1)} %get-tuple-element.38), channel_id=1, source_target_pairs={{0,1},{1,0},{2,3},{3,2},{4,5},{5,4},{6,7},{7,6},{8,9},{9,8},{10,11... | collective-permute-start | bytes 208904 | tf_op jit(solution)/shard_map/ppermute | solution.py:17
  29.8 2.5 %collective-permute-start.9 = (s32[136,128]{1,0:T(8,128)S(1)}, s32[136,128]{1,0:T(8,128)S(1)}, u32[]{:S(2)}, u32[]{:S(2)}) collective-permute-start(s32[136,128]{1,0:T(8,128)S(1)} %get-tuple-element.39), channel_id=1, source_target_pairs={{0,3},{1,2},{2,1},{3,0},{4,7},{5,6},{6,5},{7,4},{8,11},{9,10},{10,... | collective-permute-start | bytes 208904 | tf_op jit(solution)/shard_map/ppermute | solution.py:17
  32.3 0.0 collective-permute-done.4.refs_1_
  32.3 0.1 collective-permute-start.10
  32.4 0.0 collective-permute-done.5.refs_2_
  32.4 0.0 collective-permute-done.6.refs_3_
  32.4 0.0 collective-permute-done.8.refs_5_
  32.4 4.1 %collective-permute-done.9.refs_6_ = s32[136,128]{1,0:T(8,128)S(1)} collective-permute-done((s32[136,128]{1,0:T(8,128)S(1)}, s32[136,128]{1,0:T(8,128)S(1)}, u32[]{:S(2)}, u32[]{:S(2)}) %collective-permute-start.9) | collective-permute-done | bytes 69664 | tf_op jit(solution)/shard_map/ppermute | solution.py:17
  36.5 2.2 %collective-permute-done.10.refs_7_ = s32[136,128]{1,0:T(8,128)S(1)} collective-permute-done((s32[136,128]{1,0:T(8,128)S(1)}, s32[136,128]{1,0:T(8,128)S(1)}, u32[]{:S(2)}, u32[]{:S(2)}) %collective-permute-start.10) | collective-permute-done | bytes 69664 | tf_op jit(solution)/shard_map/ppermute | solution.py:17
  38.8 0.8 %finish.1 = bf16[2,2,128,128]{3,2,1,0:T(8,128)(2,1)} custom-call(f32[4,64,128]{2,1,0:T(8,128)S(1)} %get-tuple-element.30.refs_0_, s32[136,128]{1,0:T(8,128)S(1)} %collective-permute-done.4.refs_1_, s32[136,128]{1,0:T(8,128)S(1)} %collective-permute-done.5.refs_2_, s32[136,128]{1,0:T(8,128)S(1)} %collective-permute-done.6.refs_3_, ...), custom_call_target="tpu_custom_call" | custom-call | tf_op jit(solution)/shard_map/finish/pallas_call | solution.py:362
  (7 shorter events, 0.1 us)
Async XLA Ops:
  0.0 2.5 %copy-start.7 = (s32[2,2]{1,0:T(2,128)S(1)}, s32[2,2]{1,0:T(2,128)}, u32[]{:S(2)}) copy-start(s32[2,2]{1,0:T(2,128)} %refs_2_.1) | copy-start | bytes 52
  0.0 1.1 %copy-start = (bf16[24,128,128]{2,1,0:T(8,128)(2,1)S(1)}, bf16[24,128,128]{2,1,0:T(8,128)(2,1)}, u32[]{:S(2)}) copy-start(bf16[24,128,128]{2,1,0:T(8,128)(2,1)} %refs_4_.1) | copy-start | bytes 2359300
  1.1 0.7 %copy-start.3 = (s32[24]{0:T(128)S(1)}, s32[24]{0:T(128)}, u32[]{:S(2)}) copy-start(s32[24]{0:T(128)} %param.7) | copy-start | bytes 292
  1.8 0.7 %copy-start.5 = (s32[24]{0:T(128)S(1)}, s32[24]{0:T(128)}, u32[]{:S(2)}) copy-start(s32[24]{0:T(128)} %param.8) | copy-start | bytes 292
  2.5 0.9 %copy-start.2 = (bf16[2,2,128,128]{3,2,1,0:T(8,128)(2,1)S(1)}, bf16[2,2,128,128]{3,2,1,0:T(8,128)(2,1)}, u32[]{:S(2)}) copy-start(bf16[2,2,128,128]{3,2,1,0:T(8,128)(2,1)} %param.9) | copy-start | bytes 393220
  2.5 5.5 %copy-start.1 = (bf16[24,128,128]{2,1,0:T(8,128)(2,1)S(1)}, bf16[24,128,128]{2,1,0:T(8,128)(2,1)}, u32[]{:S(2)}) copy-start(bf16[24,128,128]{2,1,0:T(8,128)(2,1)} %refs_4_.1) | copy-start | bytes 2359300
  2.5 6.2 %copy-start.4 = (s32[24]{0:T(128)S(1)}, s32[24]{0:T(128)}, u32[]{:S(2)}) copy-start(s32[24]{0:T(128)} %param.7) | copy-start | bytes 292
  2.5 6.2 %copy-start.6 = (s32[24]{0:T(128)S(1)}, s32[24]{0:T(128)}, u32[]{:S(2)}) copy-start(s32[24]{0:T(128)} %param.8) | copy-start | bytes 292
  2.5 8.3 %copy-start.8 = (s32[8,2]{0,1:T(2,128)S(1)}, s32[8,2]{0,1:T(2,128)}, u32[]{:S(2)}) copy-start(s32[8,2]{0,1:T(2,128)} %param.11) | copy-start | bytes 196
  3.4 7.5 %collective-permute-start = (bf16[528,128]{1,0:T(8,128)(2,1)S(1)}, bf16[528,128]{1,0:T(8,128)(2,1)S(1)}, u32[]{:S(2)}, u32[]{:S(2)}) collective-permute-start(bf16[528,128]{1,0:T(8,128)(2,1)S(1)} %pad_maximum_fusion), channel_id=1, source_target_pairs={{0,8},{8,0},{16,24},{24,16},{1,9},{9,1},{17,25},{25,17},{2,10},{10... | collective-permute-start | bytes 405512 | tf_op jit(solution)/shard_map/ppermute | solution.py:17
  3.9 6.8 %collective-permute-start.1 = (bf16[528,128]{1,0:T(8,128)(2,1)S(1)}, bf16[528,128]{1,0:T(8,128)(2,1)S(1)}, u32[]{:S(2)}, u32[]{:S(2)}) collective-permute-start(bf16[528,128]{1,0:T(8,128)(2,1)S(1)} %pad_maximum_fusion), channel_id=1, source_target_pairs={{0,16},{8,24},{16,0},{24,8},{1,17},{9,25},{17,1},{25,9},{2,18},{10... | collective-permute-start | bytes 405512 | tf_op jit(solution)/shard_map/ppermute | solution.py:17
  6.5 12.3 %collective-permute-start.3 = (bf16[25,64,128]{2,1,0:T(8,128)(2,1)S(1)}, bf16[25,64,128]{2,1,0:T(8,128)(2,1)S(1)}, u32[]{:S(2)}, u32[]{:S(2)}) collective-permute-start(bf16[25,64,128]{2,1,0:T(8,128)(2,1)S(1)} %pack.1), channel_id=1, source_target_pairs={{4,0},{0,4},{5,1},{1,5},{6,2},{2,6},{7,3},{3,7},{12,8},{8,12},{13,... | collective-permute-start | bytes 1228808 | tf_op jit(solution)/shard_map/ppermute | solution.py:31
  8.0 18.4 %collective-permute-start.7 = (bf16[24,64,128]{2,1,0:T(8,128)(2,1)S(1)}, bf16[24,64,128]{2,1,0:T(8,128)(2,1)S(1)}, u32[]{:S(2)}, u32[]{:S(2)}) collective-permute-start(bf16[24,64,128]{2,1,0:T(8,128)(2,1)S(1)} %slice.3), channel_id=1, source_target_pairs={{4,0},{0,4},{5,1},{1,5},{6,2},{2,6},{7,3},{3,7},{12,8},{8,12},{13,... | collective-permute-start | bytes 1179656 | tf_op jit(solution)/shard_map/ppermute | solution.py:31
  10.7 1.4 %collective-permute-start.2 = (bf16[528,128]{1,0:T(8,128)(2,1)S(1)}, bf16[528,128]{1,0:T(8,128)(2,1)S(1)}, u32[]{:S(2)}, u32[]{:S(2)}) collective-permute-start(bf16[528,128]{1,0:T(8,128)(2,1)S(1)} %collective-permute-done.1.refs_7_), channel_id=1, source_target_pairs={{0,8},{8,0},{16,24},{24,16},{1,9},{9,1},{17,25},{25,17},{2,10},{10... | collective-permute-start | bytes 405512 | tf_op jit(solution)/shard_map/ppermute | solution.py:17
  21.1 11.2 %collective-permute-start.4 = (s32[136,128]{1,0:T(8,128)S(1)}, s32[136,128]{1,0:T(8,128)S(1)}, u32[]{:S(2)}, u32[]{:S(2)}) collective-permute-start(s32[136,128]{1,0:T(8,128)S(1)} %get-tuple-element.31), channel_id=1, source_target_pairs={{0,1},{1,0},{2,3},{3,2},{4,5},{5,4},{6,7},{7,6},{8,9},{9,8},{10,11... | collective-permute-start | bytes 208904 | tf_op jit(solution)/shard_map/ppermute | solution.py:17
  22.9 9.5 %collective-permute-start.5 = (s32[136,128]{1,0:T(8,128)S(1)}, s32[136,128]{1,0:T(8,128)S(1)}, u32[]{:S(2)}, u32[]{:S(2)}) collective-permute-start(s32[136,128]{1,0:T(8,128)S(1)} %get-tuple-element.32), channel_id=1, source_target_pairs={{0,3},{1,2},{2,1},{3,0},{4,7},{5,6},{6,5},{7,4},{8,11},{9,10},{10,... | collective-permute-start | bytes 208904 | tf_op jit(solution)/shard_map/ppermute | solution.py:17
  25.4 7.1 %collective-permute-start.6 = (s32[136,128]{1,0:T(8,128)S(1)}, s32[136,128]{1,0:T(8,128)S(1)}, u32[]{:S(2)}, u32[]{:S(2)}) collective-permute-start(s32[136,128]{1,0:T(8,128)S(1)} %get-tuple-element.33), channel_id=1, source_target_pairs={{0,2},{1,3},{2,0},{3,1},{4,6},{5,7},{6,4},{7,5},{8,10},{9,11},{10,... | collective-permute-start | bytes 208904 | tf_op jit(solution)/shard_map/ppermute | solution.py:17
  28.0 4.4 %collective-permute-start.8 = (s32[136,128]{1,0:T(8,128)S(1)}, s32[136,128]{1,0:T(8,128)S(1)}, u32[]{:S(2)}, u32[]{:S(2)}) collective-permute-start(s32[136,128]{1,0:T(8,128)S(1)} %get-tuple-element.38), channel_id=1, source_target_pairs={{0,1},{1,0},{2,3},{3,2},{4,5},{5,4},{6,7},{7,6},{8,9},{9,8},{10,11... | collective-permute-start | bytes 208904 | tf_op jit(solution)/shard_map/ppermute | solution.py:17
  29.8 6.7 %collective-permute-start.9 = (s32[136,128]{1,0:T(8,128)S(1)}, s32[136,128]{1,0:T(8,128)S(1)}, u32[]{:S(2)}, u32[]{:S(2)}) collective-permute-start(s32[136,128]{1,0:T(8,128)S(1)} %get-tuple-element.39), channel_id=1, source_target_pairs={{0,3},{1,2},{2,1},{3,0},{4,7},{5,6},{6,5},{7,4},{8,11},{9,10},{10,... | collective-permute-start | bytes 208904 | tf_op jit(solution)/shard_map/ppermute | solution.py:17
  32.3 6.5 %collective-permute-start.10 = (s32[136,128]{1,0:T(8,128)S(1)}, s32[136,128]{1,0:T(8,128)S(1)}, u32[]{:S(2)}, u32[]{:S(2)}) collective-permute-start(s32[136,128]{1,0:T(8,128)S(1)} %get-tuple-element.40), channel_id=1, source_target_pairs={{0,2},{1,3},{2,0},{3,1},{4,6},{5,7},{6,4},{7,5},{8,10},{9,11},{10,... | collective-permute-start | bytes 208904 | tf_op jit(solution)/shard_map/ppermute | solution.py:17

commit v9 on v8

v9 whole, which is shorter than its diff:
```python
import functools

import jax
import jax.numpy as jnp
from jax import lax
from jax.experimental import pallas as pl
from jax.experimental.pallas import tpu as pltpu
from jax.sharding import PartitionSpec as P

GROUP = 4
LANES = 128
MIB = 2**20
HBM = pltpu.MemorySpace.HBM


def row_ranges(order):
    first = order * 5 // 8
    return [(0, first), (first, order - first)]


def in_hbm(*values):
    return [pltpu.with_memory_space_constraint(value, HBM) for value in values]


def flipped(value, axis, bits):
    return lax.ppermute(value, axis, [(i, i ^ bits) for i in range(lax.axis_size(axis))])


def gathered(value, axis):
    values = {0: value}
    bit = lax.axis_size(axis) // 2
    while bit:
        values |= {d ^ bit: flipped(held, axis, bit) for d, held in values.items()}
        bit //= 2
    return [values[d] for d in range(len(values))]


def shifted(value, axis, offset):
    size = lax.axis_size(axis)
    return lax.ppermute(value, axis, [((i + offset) % size, i) for i in range(size)])


def quotient(value, by):
    return value >> (by.bit_length() - 1) if by & (by - 1) == 0 else lax.div(value, by)


def remainder(value, by):
    return value & (by - 1) if by & (by - 1) == 0 else lax.rem(value, by)


def write_digits(tile, at, value):
    height, width = value.shape
    tile[at : at + height, :width] = remainder(value, LANES)
    tile[at + height : at + 2 * height, :width] = quotient(value, LANES)


def positions(sizes, a_rows, a_cols, row_at, layer_at):
    layers, piece_rows, width, local_rows, kept = sizes
    own_rows = local_rows // layers
    owner = quotient(a_cols, piece_rows * layers)
    rights = ((owner ^ row_at) * piece_rows + remainder(a_cols, piece_rows)) * width
    local = a_rows - row_at * local_rows
    goals = remainder(quotient(local, own_rows) - layer_at + layers, layers) * own_rows
    return rights, (goals + remainder(local, own_rows)) * kept


def pack_kernel(sizes, a_rows, a_cols, x_in, s_cols, s_in, *refs):
    count, piece, order, ranges = sizes
    s_out, x_out, refs = refs[0], refs[1 : 1 + len(ranges)], refs[1 + len(ranges) :]
    rows, cols, s_held, x_tile, s_tile, sem = refs
    small = [(a_rows, rows), (a_cols, cols), (s_cols, s_held)]
    large = [(x_in.at[:, pl.ds(*span)], out.at[pl.ds(0, count)]) for span, out in zip(ranges, x_out)]
    large += [(s_in.at[q], s_out.at[pl.ds(q * order, order)]) for q in range(piece)]
    loads = [
        pltpu.make_async_copy(source, goal, sem.at[p])
        for p, (source, goal) in enumerate(small + large)
    ]
    for load in loads:
        load.start()
    x_tile[...] = jnp.zeros_like(x_tile)
    s_tile[...] = jnp.zeros_like(s_tile)
    height = ranges[0][1]
    x_out[0][count, 16:] = jnp.zeros((height - 16, LANES), jnp.bfloat16)
    for load in loads[:3]:
        load.wait()
    write_digits(x_tile, 0, rows[...])
    write_digits(x_tile, 2, cols[...])
    write_digits(s_tile, 0, s_held[...])
    x_out[0][count, :16] = x_tile[...].astype(jnp.float32).astype(jnp.bfloat16)
    s_out[piece * order :] = s_tile[...].astype(jnp.float32).astype(jnp.bfloat16)
    for load in loads[3:]:
        load.wait()


def place_kernel(sizes, place, a_rows, a_cols, c_cols, index, kept_cols, rows, cols, held, sem):
    layers, count, piece_rows, width, local_rows, kept = sizes
    loads = [
        pltpu.make_async_copy(source, goal, sem.at[p])
        for p, (source, goal) in enumerate(((a_rows, rows), (a_cols, cols), (c_cols, held)))
    ]
    for load in loads:
        load.start()
    for load in loads:
        load.wait()
    own_rows = local_rows // layers
    for n in range(count):
        index[0, n], index[1, n] = positions(
            (layers, piece_rows, width, local_rows, kept), rows[0, n], cols[0, n], place[0], place[1]
        )
    for g in range(layers):
        base = remainder(place[1] + g, layers) * own_rows
        for i in range(own_rows):
            for t in range(kept):
                kept_cols[(g * own_rows + i) * kept + t] = held[t, base + i]


def list_pairs(sizes, index, panel_cols, kept_cols, pairs):
    count, width, kept, trash = sizes
    total = jnp.int32(0)
    for n in range(count):
        right, goal = index[0, n], index[1, n]
        for s in range(width):
            wanted = panel_cols[right + s]
            hit, slot = jnp.int32(0), goal
            for t in range(kept):
                same = (kept_cols[goal + t] == wanted).astype(jnp.int32)
                hit += same
                slot += t * same
            pairs[0, total] = n
            pairs[1, total] = right + s
            pairs[2, total] = slot
            total += hit
    for g in range(GROUP):
        pairs[0, total + g] = 0
        pairs[1, total + g] = 0
        pairs[2, total + g] = trash
    pairs[0, count * width + GROUP] = total


def add_products(left, panel, totals, pairs):
    def one_group(group, carry):
        base = group * GROUP
        products = [
            jnp.dot(
                left[pairs[0, base + g]],
                panel[pairs[1, base + g]],
                preferred_element_type=jnp.float32,
            )
            for g in range(GROUP)
        ]
        for g in range(GROUP):
            totals[pairs[2, base + g]] += products[g]
        return carry

    total = pairs[0, pairs.shape[1] - 1]
    lax.fori_loop(0, quotient(total + GROUP - 1, GROUP), one_group, 0)


def own_kernel(sizes, ranges, *refs):
    rows, count, piece_rows, width, kept, order = sizes
    index, kept_cols, refs = refs[0], refs[1], refs[2:]
    x_in, s_in, refs = refs[: len(ranges)], refs[len(ranges) :][:rows], refs[len(ranges) + rows :]
    totals, panel, panel_cols, pairs, whole, notes, sem = refs
    piece = piece_rows * width
    for d in range(rows):
        tile = s_in[d][piece * order :].astype(jnp.float32).astype(jnp.int32)
        whole[d] = tile[:piece_rows] + tile[piece_rows : 2 * piece_rows] * LANES
    copy = pltpu.make_async_copy(whole, notes, sem)
    copy.start()
    totals[...] = jnp.zeros_like(totals)
    for d in range(rows):
        for q in range(piece):
            panel[d * piece + q] = s_in[d][q * order : (q + 1) * order]
    copy.wait()
    for d in range(rows):
        for q in range(piece):
            panel_cols[d * piece + q] = notes[d, q // width, q % width]
    list_pairs((count, width, kept, totals.shape[0] - 1), index, panel_cols, kept_cols, pairs)
    for (first, height), blocks in zip(ranges, x_in):
        add_products(blocks, panel, totals.at[:, pl.ds(first, height)], pairs)


def peer_kernel(sizes, span, *refs):
    cols, layers, count, piece_rows, width, local_rows, kept = sizes
    first, height = span
    slots = local_rows * kept // layers
    if first == 0:
        place, panel_cols, kept_cols, *refs = refs
    else:
        pairs, *refs = refs
    x_in, refs = refs[: cols - 1], refs[cols - 1 :]
    panel, before, own, sent, refs = refs[0], refs[1], refs[2], refs[3 : 2 + layers], refs[2 + layers :]
    if first == 0:
        pairs, totals, whole, index, sem = refs
        copies = []
        for j in range(cols - 1):
            digits = x_in[j][count, :16].astype(jnp.float32).astype(jnp.int32)
            whole[j, 0:1], whole[j, 1:2] = positions(
                (layers, piece_rows, width, local_rows, kept),
                digits[0:1] + digits[1:2] * LANES,
                digits[2:3] + digits[3:4] * LANES,
                place[0],
                place[1],
            )
            copies.append(pltpu.make_async_copy(whole.at[j], index.at[j], sem.at[j]))
            copies[j].start()
    else:
        (totals,) = refs
    totals[...] = before[:, first : first + height]
    if first == 0:
        for j in range(cols - 1):
            copies[j].wait()
            list_pairs(
                (count, width, kept, layers * slots),
                index.at[j],
                panel_cols,
                kept_cols,
                pairs.at[j],
            )
    for j in range(cols - 1):
        add_products(x_in[j], panel, totals, pairs.at[j])

    own[...] = totals[:slots]
    half = height // 2
    for d in range(1, layers):
        code = sent[d - 1]
        spare = code.shape[0] - slots * half
        code[slots * half :] = jnp.zeros((spare, code.shape[1]), jnp.int32)
        for u in range(slots):
            value = totals[d * slots + u]
            peak = jnp.max(jnp.abs(value), axis=0, keepdims=True)
            power = jnp.floor(jnp.log2(jnp.maximum(peak, 1e-30)) + 1e-3) + 1.0
            word = jnp.floor(value * jnp.exp2(15.0 - power) + 0.5).astype(jnp.int32)
            code[pl.ds(u * half, half)] = (word[:half] << 16) | (word[half:] & 0xFFFF)
            code[pl.ds(slots * half + u, 1)] = power.astype(jnp.int32)


def finish_kernel(sizes, span, *refs):
    layers, slots = sizes
    first, height = span
    half = height // 2
    before, own, codes, result = refs[: first > 0], refs[-layers - 1], refs[-layers:-1], refs[-1]
    kept = result.shape[1]
    for done in before:
        result[:, :, :first] = done[...]
    for u in range(slots):
        high, low = own[u, :half], own[u, half:]
        for code in codes:
            word = code[pl.ds(u * half, half)]
            power = code[pl.ds(slots * half + u, 1)].astype(jnp.float32)
            scale = jnp.exp2(power - 15.0)
            high += (word >> 16).astype(jnp.float32) * scale
            low += ((word << 16) >> 16).astype(jnp.float32) * scale
        result[u // kept, u % kept, first : first + half] = high.astype(jnp.bfloat16)
        result[u // kept, u % kept, first + half : first + height] = low.astype(jnp.bfloat16)


def per_device(a_blocks, a_rows, a_cols, s_blocks, s_cols, c_cols):
    rows, cols, layers = (lax.axis_size(axis) for axis in ("row", "col", "layer"))
    count, order = a_blocks.shape[:2]
    piece_rows, width = s_cols.shape
    local_rows, kept = c_cols.shape
    own_rows = local_rows // layers
    slots = own_rows * kept
    all_slots = layers * slots
    ranges = row_ranges(order)
    piece = piece_rows * width
    panel_size = rows * piece
    block_size = order * order
    flat_s = s_blocks.reshape(piece, order, order)
    note_height = (2 * piece_rows + 15) // 16 * 16
    first_height = ranges[0][1]

    scalars = pl.BlockSpec(memory_space=pltpu.SMEM)
    vector = pl.BlockSpec(memory_space=pltpu.VMEM)
    far = pl.BlockSpec(memory_space=HBM)

    s_sent, *x_sent = pl.pallas_call(
        functools.partial(pack_kernel, (count, piece, order, ranges)),
        out_shape=[jax.ShapeDtypeStruct((piece * order + note_height, order), jnp.bfloat16)]
        + [
            jax.ShapeDtypeStruct((count + (at == 0), height, order), jnp.bfloat16)
            for at, height in ranges
        ],
        in_specs=[far] * 5,
        out_specs=[vector] * (1 + len(ranges)),
        scratch_shapes=[
            pltpu.VMEM((1, count), jnp.int32),
            pltpu.VMEM((1, count), jnp.int32),
            pltpu.VMEM((piece_rows, width), jnp.int32),
            pltpu.VMEM((16, LANES), jnp.int32),
            pltpu.VMEM((note_height, LANES), jnp.int32),
            pltpu.SemaphoreType.DMA((3 + piece + len(ranges),)),
        ],
        compiler_params=pltpu.CompilerParams(
            vmem_limit_bytes=2 * block_size * (2 * count + piece) + 4 * MIB
        ),
        name="pack",
    )(*in_hbm(a_rows.reshape(1, count), a_cols.reshape(1, count), a_blocks, s_cols, flat_s))
    x_pieces = [[shifted(part, "col", j) for j in range(1, cols)] for part in x_sent]
    s_pieces = gathered(s_sent, "row")

    place = jnp.stack([lax.axis_index("row"), lax.axis_index("layer")])
    index, kept_cols = pl.pallas_call(
        functools.partial(place_kernel, (layers, count, piece_rows, width, local_rows, kept)),
        out_shape=[
            jax.ShapeDtypeStruct((2, count), jnp.int32),
            jax.ShapeDtypeStruct((all_slots,), jnp.int32),
        ],
        in_specs=[scalars] + [far] * 3,
        out_specs=[scalars] * 2,
        scratch_shapes=[
            pltpu.SMEM((1, count), jnp.int32),
            pltpu.SMEM((1, count), jnp.int32),
            pltpu.SMEM((kept, local_rows), jnp.int32),
            pltpu.SemaphoreType.DMA((3,)),
        ],
        cost_estimate=pl.CostEstimate(flops=0, bytes_accessed=16 * MIB, transcendentals=0),
        name="place",
    )(place, *in_hbm(a_rows.reshape(1, count), a_cols.reshape(1, count), c_cols.T))

    moved = block_size * (4 * all_slots + 4 * panel_size + 2 * count)
    totals, panel, panel_cols = pl.pallas_call(
        functools.partial(own_kernel, (rows, count, piece_rows, width, kept, order), ranges),
        out_shape=[
            jax.ShapeDtypeStruct((all_slots + 1, order, order), jnp.float32),
            jax.ShapeDtypeStruct((panel_size, order, order), jnp.bfloat16),
            jax.ShapeDtypeStruct((panel_size,), jnp.int32),
        ],
        in_specs=[scalars] * 2 + [vector] * (len(ranges) + rows),
        out_specs=[vector] * 2 + [scalars],
        scratch_shapes=[
            pltpu.SMEM((3, count * width + GROUP + 1), jnp.int32),
            pltpu.VMEM((rows, piece_rows, LANES), jnp.int32),
            pltpu.SMEM((rows, piece_rows, LANES), jnp.int32),
            pltpu.SemaphoreType.DMA,
        ],
        compiler_params=pltpu.CompilerParams(vmem_limit_bytes=moved + 4 * MIB),
        cost_estimate=pl.CostEstimate(
            flops=2 * order**3 * count * width // 4, bytes_accessed=moved, transcendentals=0
        ),
        name="own_products",
    )(index, kept_cols, *x_sent, *s_pieces)

    moved = block_size * (8 * all_slots + 2 * panel_size + 2 * count * (cols - 1))
    finished, plan = [], []
    for (at, height), pieces in zip(ranges, x_pieces):
        code_rows = slots * (height // 2) + (slots + 7) // 8 * 8
        out_shape = [jax.ShapeDtypeStruct((slots, height, order), jnp.float32)]
        out_shape += [jax.ShapeDtypeStruct((code_rows, order), jnp.int32)] * (layers - 1)
        out_specs = [vector] * layers
        scratch = [pltpu.VMEM((all_slots + 1, height, order), jnp.float32)]
        if at == 0:
            out_shape.append(
                jax.ShapeDtypeStruct((cols - 1, 3, count * width + GROUP + 1), jnp.int32)
            )
            out_specs.append(scalars)
            scratch += [
                pltpu.VMEM((cols - 1, 2, LANES), jnp.int32),
                pltpu.SMEM((cols - 1, 2, LANES), jnp.int32),
                pltpu.SemaphoreType.DMA((cols - 1,)),
            ]
        given = plan or (place, panel_cols, kept_cols)
        out = pl.pallas_call(
            functools.partial(
                peer_kernel,
                (cols, layers, count, piece_rows, width, local_rows, kept),
                (at, height),
            ),
            out_shape=out_shape,
            in_specs=[scalars] * len(given) + [vector] * (cols + 1),
            out_specs=out_specs,
            scratch_shapes=scratch,
            compiler_params=pltpu.CompilerParams(vmem_limit_bytes=moved + 4 * MIB),
            cost_estimate=pl.CostEstimate(
                flops=2 * order**2 * height * count * width // 4 * (cols - 1),
                bytes_accessed=moved // 2,
                transcendentals=0,
            ),
            name=f"peer_products_{at}",
        )(*given, *pieces, panel, totals)
        plan = plan or out[layers:]
        codes = [shifted(out[d], "layer", layers - d) for d in range(1, layers)]
        finished = [
            pl.pallas_call(
                functools.partial(finish_kernel, (layers, slots), (at, height)),
                out_shape=jax.ShapeDtypeStruct((own_rows, kept, at + height, order), jnp.bfloat16),
                in_specs=[vector] * (len(finished) + layers),
                out_specs=vector,
                compiler_params=pltpu.CompilerParams(
                    vmem_limit_bytes=16 * slots * block_size + 4 * MIB
                ),
                name=f"finish_{at}",
            )(*finished, out[0], *codes)
        ]
    return finished[0]


def solution(mesh):
    placed = (
        P(("row", "col", "layer"), None, None),
        P(("row", "col", "layer")),
        P(("row", "col", "layer")),
        P(("row", "layer"), "col", None, None),
        P(("row", "layer"), "col"),
        P("row", "col"),
    )
    return jax.shard_map(
        per_device,
        mesh=mesh,
        in_specs=placed,
        out_specs=P(("row", "layer"), "col", None, None),
        check_vma=False,
    )
```

time: 39.8 us -> 37.1 us (0.932)
  waiting for transfers between devices: 14.3 us -> 11.5 us
  Pallas kernels: 7.67 us -> 10 us
  local copies, waits for them, and re-layouts: 3.39 us -> 1.33 us
  other arithmetic: 0.12 us -> 0.66 us
  starting transfers between devices: 14 us -> 13.6 us
    ppermute x9 -> x3, starting transfers between devices: 11.9 us -> 1.52 us  [flipped(): lax.ppermute(value, axis, [(i, i ^ bits) for i in range(lax.axis_size(axi...]
    ppermute x2 -> x8, starting transfers between devices: 2.09 us -> 12.1 us  [shifted(): lax.ppermute(value, axis, [((i + offset) % size, i) for i in range(size)])]
    ppermute x9 -> x3, waiting for transfers between devices: 9.56 us -> 2.99 us  [flipped(): lax.ppermute(value, axis, [(i, i ^ bits) for i in range(lax.axis_size(axi...]
    ppermute x2 -> x8, waiting for transfers between devices: 4.72 us -> 8.49 us  [shifted(): lax.ppermute(value, axis, [((i + offset) % size, i) for i in range(size)])]
    pallas_call x3 -> x5, Pallas kernels: 3.84 us -> 6.83 us  [the longest x1 2.56 us: per_device(): pl.pallas_call(functools.partial(own_kernel, (rows, count, piece_rows, wi...]
    unnamed x19 -> x8, local copies, waits for them, and re-layouts: 3.28 us -> 1.33 us
    pallas_call x2, Pallas kernels: 3.83 us -> 3.18 us  [per_device(): pl.pallas_call(functools.partial(peer_kernel, (cols, layers, count, piece...]
    another operation x1, other arithmetic: 0.07 us -> 0.66 us  [per_device(): place = jnp.stack([lax.axis_index('row'), lax.axis_index('layer')])]
  transfers between devices with their start and end apart: 11 -> 11, of which waited for: 6 -> 7; matrix products, arithmetic and copies ran while one was open for 0% -> 2% of each run, Pallas kernels for 17% -> 22%
where the time goes in v9:
time: 37.1 us
  starting transfers between devices  13.6 us (37%)
  waiting for transfers between devices  11.5 us (31%)
  Pallas kernels  10 us (27%)
  local copies, waits for them, and re-layouts  1.33 us (4%)
  other arithmetic  0.66 us (2%)
    ppermute x8, starting transfers between devices, shifted(): lax.ppermute(value, axis, [((i + offset) % size, i) for i in range(size)])  12.1 us
    ppermute x8, waiting for transfers between devices, shifted(): lax.ppermute(value, axis, [((i + offset) % size, i) for i in range(size)])  8.49 us
    pallas_call x2, Pallas kernels, per_device(): pl.pallas_call(functools.partial(peer_kernel, (cols, layers, count, piece...  3.18 us
    ppermute x3, waiting for transfers between devices, flipped(): lax.ppermute(value, axis, [(i, i ^ bits) for i in range(lax.axis_size(axi...  2.99 us
    pallas_call x1, Pallas kernels, per_device(): pl.pallas_call(functools.partial(own_kernel, (rows, count, piece_rows, wi...  2.56 us
    pallas_call x1, Pallas kernels, per_device(): pl.pallas_call(functools.partial(place_kernel, (layers, count, piece_rows...  2.22 us
    ppermute x3, starting transfers between devices, flipped(): lax.ppermute(value, axis, [(i, i ^ bits) for i in range(lax.axis_size(axi...  1.52 us
    unnamed x8, local copies, waits for them, and re-layouts  1.33 us
  transfers between devices with their start and end apart: 11, of which 7 were waited for; matrix products, arithmetic and copies ran while one was open for 2% of the time, Pallas kernels for 22%

profile of v9, /device:TPU:0, one launch (start us, length us, event | category | flops | bytes accessed | tf_op | source)
XLA Modules:
  0.0 37.1 jit_solution(14851083155319554971)
XLA Ops:
  0.0 1.2 %pack.1 = (bf16[528,128]{1,0:T(8,128)(2,1)S(1)}, bf16[25,80,128]{2,1,0:T(8,128)(2,1)S(1)}, bf16[24,48,128]{2,1,0:T(8,128)(2,1)S(1)}) custom-call(s32[1,24]{1,0:T(1,128)} %bitcast.7, s32[1,24]{1,0:T(1,128)} %bitcast.9, bf16[24,128,128]{2,1,0:T(8,128)(2,1)} %x_in.1, s32[2,2]{1,0:T(2,128)} %s_cols.1, bf16[4,128,128]{2,1,0:T(8,128)(2,1)} %bitcast.6), custom_call_target="tpu_custom_call" | custom-call | tf_op jit(solution)/shard_map/pack/pallas_call | solution.py:278
  1.3 3.0 %collective-permute-start.3 = (bf16[25,80,128]{2,1,0:T(8,128)(2,1)S(1)}, bf16[25,80,128]{2,1,0:T(8,128)(2,1)S(1)}, u32[]{:S(2)}, u32[]{:S(2)}) collective-permute-start(bf16[25,80,128]{2,1,0:T(8,128)(2,1)S(1)} %get-tuple-element.24.refs_2_), channel_id=1, source_target_pairs={{4,0},{0,4},{5,1},{1,5},{6,2},{2,6},{7,3},{3,7},{12,8},{8,12},{13,... | collective-permute-start | bytes 1536008 | tf_op jit(solution)/shard_map/ppermute | solution.py:40
  4.3 1.5 %collective-permute-start.1 = (bf16[528,128]{1,0:T(8,128)(2,1)S(1)}, bf16[528,128]{1,0:T(8,128)(2,1)S(1)}, u32[]{:S(2)}, u32[]{:S(2)}) collective-permute-start(bf16[528,128]{1,0:T(8,128)(2,1)S(1)} %get-tuple-element.26.refs_4_), channel_id=1, source_target_pairs={{0,16},{8,24},{16,0},{24,8},{1,17},{9,25},{17,1},{25,9},{2,18},{10... | collective-permute-start | bytes 405512 | tf_op jit(solution)/shard_map/ppermute | solution.py:26
  5.8 0.5 %collective-permute-start.7 = (bf16[24,48,128]{2,1,0:T(8,128)(2,1)S(1)}, bf16[24,48,128]{2,1,0:T(8,128)(2,1)S(1)}, u32[]{:S(2)}, u32[]{:S(2)}) collective-permute-start(bf16[24,48,128]{2,1,0:T(8,128)(2,1)S(1)} %get-tuple-element.25.refs_3_), channel_id=1, source_target_pairs={{4,0},{0,4},{5,1},{1,5},{6,2},{2,6},{7,3},{3,7},{12,8},{8,12},{13,... | collective-permute-start | bytes 884744 | tf_op jit(solution)/shard_map/ppermute | solution.py:40
  6.3 0.0 collective-permute-start
  6.3 3.0 %collective-permute-done.1.refs_6_ = bf16[528,128]{1,0:T(8,128)(2,1)S(1)} collective-permute-done((bf16[528,128]{1,0:T(8,128)(2,1)S(1)}, bf16[528,128]{1,0:T(8,128)(2,1)S(1)}, u32[]{:S(2)}, u32[]{:S(2)}) %collective-permute-start.1) | collective-permute-done | bytes 135200 | tf_op jit(solution)/shard_map/ppermute | solution.py:26
  9.3 0.0 collective-permute-start.2
  9.3 0.7 %pad_add_fusion.place.refs_0_ = s32[2]{0:T(128)} fusion(s32[1]{0:T(128)} %bitcast.1, s32[1]{0:T(128)} %bitcast), kind=kLoop, calls=%fused_computation | loop fusion | flops 2 | bytes 16 | tf_op jit(solution)/shard_map/stack | solution.py:303
  10.0 0.0 copy-start.2
  10.0 2.2 %place.1 = (s32[2,24]{1,0:T(2,128)}, s32[16]{0:T(128)}) custom-call(s32[2]{0:T(128)} %pad_add_fusion.place.refs_0_, s32[1,24]{1,0:T(1,128)} %bitcast.8, s32[1,24]{1,0:T(1,128)} %bitcast.10, s32[2,8]{1,0:T(2,128)} %bitcast.11), custom_call_target="tpu_custom_call" | custom-call | bytes 16777216 | tf_op jit(solution)/shard_map/place/pallas_call | solution.py:304
  12.2 0.0 copy-start.1
  12.2 0.0 collective-permute-done.refs_5_
  12.2 0.0 collective-permute-done.2.refs_7_
  12.2 0.0 copy-start
  12.2 0.6 %copy-done = s32[16]{0:T(128)S(1)} copy-done((s32[16]{0:T(128)S(1)}, s32[16]{0:T(128)}, u32[]{:S(2)}) %copy-start) | copy-done | bytes 88
  12.9 0.0 copy-start.3
  12.9 0.7 %copy-done.3 = s32[2,24]{1,0:T(2,128)S(1)} copy-done((s32[2,24]{1,0:T(2,128)S(1)}, s32[2,24]{1,0:T(2,128)}, u32[]{:S(2)}) %copy-start.3) | copy-done | bytes 216
  13.6 2.6 %own_products.1 = (f32[17,128,128]{2,1,0:T(8,128)S(1)}, bf16[16,128,128]{2,1,0:T(8,128)(2,1)S(1)}, s32[16]{0:T(128)S(1)}) custom-call(s32[2,24]{1,0:T(2,128)S(1)} %copy-done.3, s32[16]{0:T(128)S(1)} %copy-done, bf16[25,80,128]{2,1,0:T(8,128)(2,1)S(1)} %get-tuple-element.24.refs_2_, bf16[24,48,128]{2,1,0:T(8,128)(2,1)S(1)} %get-tuple-element.25.refs_3_, ...), custom_call_target="tpu_custom_call" | custom-call | flops 50331648 | bytes 2883584 | tf_op jit(solution)/shard_map/own_products/pallas_call | solution.py:323
  16.1 0.6 %collective-permute-done.3.refs_3_ = bf16[25,80,128]{2,1,0:T(8,128)(2,1)S(1)} collective-permute-done((bf16[25,80,128]{2,1,0:T(8,128)(2,1)S(1)}, bf16[25,80,128]{2,1,0:T(8,128)(2,1)S(1)}, u32[]{:S(2)}, u32[]{:S(2)}) %collective-permute-start.3) | collective-permute-done | bytes 512032 | tf_op jit(solution)/shard_map/ppermute | solution.py:40
  16.7 0.0 copy-done.2
  16.7 0.0 copy-done.1
  16.7 2.3 %peer_products_0.1 = (f32[4,80,128]{2,1,0:T(8,128)S(1)}, s32[168,128]{1,0:T(8,128)S(1)}, s32[168,128]{1,0:T(8,128)S(1)}, s32[168,128]{1,0:T(8,128)S(1)}, s32[1,3,53]{2,1,0:T(4,128)S(1)}) custom-call(s32[2]{0:T(128)S(1)} %copy-done.2, s32[16]{0:T(128)S(1)} %get-tuple-element.27.refs_1_, s32[16]{0:T(128)S(1)} %copy-done.1, ...), custom_call_target="tpu_custom_call" | custom-call | flops 31457280 | bytes 1703936 | tf_op jit(solution)/shard_map/peer_products_0/pallas_call | solution.py:364
  19.1 2.4 %collective-permute-start.4 = (s32[168,128]{1,0:T(8,128)S(1)}, s32[168,128]{1,0:T(8,128)S(1)}, u32[]{:S(2)}, u32[]{:S(2)}) collective-permute-start(s32[168,128]{1,0:T(8,128)S(1)} %get-tuple-element.31), channel_id=1, source_target_pairs={{3,0},{0,1},{1,2},{2,3},{7,4},{4,5},{5,6},{6,7},{11,8},{8,9},{9,10... | collective-permute-start | bytes 258056 | tf_op jit(solution)/shard_map/ppermute | solution.py:40
  21.5 2.4 %collective-permute-start.5 = (s32[168,128]{1,0:T(8,128)S(1)}, s32[168,128]{1,0:T(8,128)S(1)}, u32[]{:S(2)}, u32[]{:S(2)}) collective-permute-start(s32[168,128]{1,0:T(8,128)S(1)} %get-tuple-element.32), channel_id=1, source_target_pairs={{2,0},{3,1},{0,2},{1,3},{6,4},{7,5},{4,6},{5,7},{10,8},{11,9},{8,1... | collective-permute-start | bytes 258056 | tf_op jit(solution)/shard_map/ppermute | solution.py:40
  23.8 1.3 %collective-permute-start.6 = (s32[168,128]{1,0:T(8,128)S(1)}, s32[168,128]{1,0:T(8,128)S(1)}, u32[]{:S(2)}, u32[]{:S(2)}) collective-permute-start(s32[168,128]{1,0:T(8,128)S(1)} %get-tuple-element.33), channel_id=1, source_target_pairs={{1,0},{2,1},{3,2},{0,3},{5,4},{6,5},{7,6},{4,7},{9,8},{10,9},{11,1... | collective-permute-start | bytes 258056 | tf_op jit(solution)/shard_map/ppermute | solution.py:40
  25.2 0.0 collective-permute-done.7.refs_1_
  25.2 0.9 %peer_products_80.1 = (f32[4,48,128]{2,1,0:T(8,128)S(1)}, s32[104,128]{1,0:T(8,128)S(1)}, s32[104,128]{1,0:T(8,128)S(1)}, s32[104,128]{1,0:T(8,128)S(1)}) custom-call(s32[1,3,53]{2,1,0:T(4,128)S(1)} %get-tuple-element.34.refs_0_, bf16[24,48,128]{2,1,0:T(8,128)(2,1)S(1)} %collective-permute-done.7.refs_1_, ...), custom_call_target="tpu_custom_call" | custom-call | flops 18874368 | bytes 1703936 | tf_op jit(solution)/shard_map/peer_products_80/pallas_call | solution.py:364
  26.1 0.9 %collective-permute-start.10 = (s32[104,128]{1,0:T(8,128)S(1)}, s32[104,128]{1,0:T(8,128)S(1)}, u32[]{:S(2)}, u32[]{:S(2)}) collective-permute-start(s32[104,128]{1,0:T(8,128)S(1)} %get-tuple-element.38), channel_id=1, source_target_pairs={{1,0},{2,1},{3,2},{0,3},{5,4},{6,5},{7,6},{4,7},{9,8},{10,9},{11,1... | collective-permute-start | bytes 159752 | tf_op jit(solution)/shard_map/ppermute | solution.py:40
  27.0 1.1 %collective-permute-start.8 = (s32[104,128]{1,0:T(8,128)S(1)}, s32[104,128]{1,0:T(8,128)S(1)}, u32[]{:S(2)}, u32[]{:S(2)}) collective-permute-start(s32[104,128]{1,0:T(8,128)S(1)} %get-tuple-element.36), channel_id=1, source_target_pairs={{3,0},{0,1},{1,2},{2,3},{7,4},{4,5},{5,6},{6,7},{11,8},{8,9},{9,10... | collective-permute-start | bytes 159752 | tf_op jit(solution)/shard_map/ppermute | solution.py:40
  28.2 0.0 collective-permute-done.4.refs_1_
  28.2 0.3 collective-permute-start.9
  28.5 1.6 %collective-permute-done.5.refs_2_ = s32[168,128]{1,0:T(8,128)S(1)} collective-permute-done((s32[168,128]{1,0:T(8,128)S(1)}, s32[168,128]{1,0:T(8,128)S(1)}, u32[]{:S(2)}, u32[]{:S(2)}) %collective-permute-start.5) | collective-permute-done | bytes 86048 | tf_op jit(solution)/shard_map/ppermute | solution.py:40
  30.1 0.4 %collective-permute-done.6.refs_3_ = s32[168,128]{1,0:T(8,128)S(1)} collective-permute-done((s32[168,128]{1,0:T(8,128)S(1)}, s32[168,128]{1,0:T(8,128)S(1)}, u32[]{:S(2)}, u32[]{:S(2)}) %collective-permute-start.6) | collective-permute-done | bytes 86048 | tf_op jit(solution)/shard_map/ppermute | solution.py:40
  30.6 0.1 finish_0.1.refs_0_
  30.7 1.0 %collective-permute-done.10.refs_4_ = s32[104,128]{1,0:T(8,128)S(1)} collective-permute-done((s32[104,128]{1,0:T(8,128)S(1)}, s32[104,128]{1,0:T(8,128)S(1)}, u32[]{:S(2)}, u32[]{:S(2)}) %collective-permute-start.10) | collective-permute-done | bytes 53280 | tf_op jit(solution)/shard_map/ppermute | solution.py:40
  31.7 1.3 %collective-permute-done.8.refs_2_ = s32[104,128]{1,0:T(8,128)S(1)} collective-permute-done((s32[104,128]{1,0:T(8,128)S(1)}, s32[104,128]{1,0:T(8,128)S(1)}, u32[]{:S(2)}, u32[]{:S(2)}) %collective-permute-start.8) | collective-permute-done | bytes 53280 | tf_op jit(solution)/shard_map/ppermute | solution.py:40
  33.0 3.4 %collective-permute-done.9.refs_3_ = s32[104,128]{1,0:T(8,128)S(1)} collective-permute-done((s32[104,128]{1,0:T(8,128)S(1)}, s32[104,128]{1,0:T(8,128)S(1)}, u32[]{:S(2)}, u32[]{:S(2)}) %collective-permute-start.9) | collective-permute-done | bytes 53280 | tf_op jit(solution)/shard_map/ppermute | solution.py:40
  36.4 0.7 %finish_80.1 = bf16[2,2,128,128]{3,2,1,0:T(8,128)(2,1)} custom-call(bf16[2,2,80,128]{3,2,1,0:T(8,128)(2,1)S(1)} %finish_0.1.refs_0_, f32[4,48,128]{2,1,0:T(8,128)S(1)} %get-tuple-element.35.refs_1_, s32[104,128]{1,0:T(8,128)S(1)} %collective-permute-done.8.refs_2_, s32[104,128]{1,0:T(8,128)S(1)} %collective-permute-done.9.refs_3_, ...), custom_call_target="tpu_custom_call" | custom-call | tf_op jit(solution)/shard_map/finish_80/pallas_call | solution.py:385
Async XLA Ops:
  1.3 15.5 %collective-permute-start.3 = (bf16[25,80,128]{2,1,0:T(8,128)(2,1)S(1)}, bf16[25,80,128]{2,1,0:T(8,128)(2,1)S(1)}, u32[]{:S(2)}, u32[]{:S(2)}) collective-permute-start(bf16[25,80,128]{2,1,0:T(8,128)(2,1)S(1)} %get-tuple-element.24.refs_2_), channel_id=1, source_target_pairs={{4,0},{0,4},{5,1},{1,5},{6,2},{2,6},{7,3},{3,7},{12,8},{8,12},{13,... | collective-permute-start | bytes 1536008 | tf_op jit(solution)/shard_map/ppermute | solution.py:40
  4.3 5.0 %collective-permute-start.1 = (bf16[528,128]{1,0:T(8,128)(2,1)S(1)}, bf16[528,128]{1,0:T(8,128)(2,1)S(1)}, u32[]{:S(2)}, u32[]{:S(2)}) collective-permute-start(bf16[528,128]{1,0:T(8,128)(2,1)S(1)} %get-tuple-element.26.refs_4_), channel_id=1, source_target_pairs={{0,16},{8,24},{16,0},{24,8},{1,17},{9,25},{17,1},{25,9},{2,18},{10... | collective-permute-start | bytes 405512 | tf_op jit(solution)/shard_map/ppermute | solution.py:26
  5.8 19.4 %collective-permute-start.7 = (bf16[24,48,128]{2,1,0:T(8,128)(2,1)S(1)}, bf16[24,48,128]{2,1,0:T(8,128)(2,1)S(1)}, u32[]{:S(2)}, u32[]{:S(2)}) collective-permute-start(bf16[24,48,128]{2,1,0:T(8,128)(2,1)S(1)} %get-tuple-element.25.refs_3_), channel_id=1, source_target_pairs={{4,0},{0,4},{5,1},{1,5},{6,2},{2,6},{7,3},{3,7},{12,8},{8,12},{13,... | collective-permute-start | bytes 884744 | tf_op jit(solution)/shard_map/ppermute | solution.py:40
  6.3 5.9 %collective-permute-start = (bf16[528,128]{1,0:T(8,128)(2,1)S(1)}, bf16[528,128]{1,0:T(8,128)(2,1)S(1)}, u32[]{:S(2)}, u32[]{:S(2)}) collective-permute-start(bf16[528,128]{1,0:T(8,128)(2,1)S(1)} %get-tuple-element.26.refs_4_), channel_id=1, source_target_pairs={{0,8},{8,0},{16,24},{24,16},{1,9},{9,1},{17,25},{25,17},{2,10},{10... | collective-permute-start | bytes 405512 | tf_op jit(solution)/shard_map/ppermute | solution.py:26
  9.3 2.9 %collective-permute-start.2 = (bf16[528,128]{1,0:T(8,128)(2,1)S(1)}, bf16[528,128]{1,0:T(8,128)(2,1)S(1)}, u32[]{:S(2)}, u32[]{:S(2)}) collective-permute-start(bf16[528,128]{1,0:T(8,128)(2,1)S(1)} %collective-permute-done.1.refs_6_), channel_id=1, source_target_pairs={{0,8},{8,0},{16,24},{24,16},{1,9},{9,1},{17,25},{25,17},{2,10},{10... | collective-permute-start | bytes 405512 | tf_op jit(solution)/shard_map/ppermute | solution.py:26
  10.0 6.8 %copy-start.2 = (s32[2]{0:T(128)S(1)}, s32[2]{0:T(128)}, u32[]{:S(2)}) copy-start(s32[2]{0:T(128)} %pad_add_fusion.place.refs_0_) | copy-start | bytes 28
  12.2 4.5 %copy-start.1 = (s32[16]{0:T(128)S(1)}, s32[16]{0:T(128)}, u32[]{:S(2)}) copy-start(s32[16]{0:T(128)} %get-tuple-element.23.refs_1_.refs_2_) | copy-start | bytes 196
  12.2 0.6 %copy-start = (s32[16]{0:T(128)S(1)}, s32[16]{0:T(128)}, u32[]{:S(2)}) copy-start(s32[16]{0:T(128)} %get-tuple-element.23.refs_1_.refs_2_) | copy-start | bytes 196
  12.9 0.7 %copy-start.3 = (s32[2,24]{1,0:T(2,128)S(1)}, s32[2,24]{1,0:T(2,128)}, u32[]{:S(2)}) copy-start(s32[2,24]{1,0:T(2,128)} %get-tuple-element.22.refs_0_) | copy-start | bytes 580
  19.1 9.1 %collective-permute-start.4 = (s32[168,128]{1,0:T(8,128)S(1)}, s32[168,128]{1,0:T(8,128)S(1)}, u32[]{:S(2)}, u32[]{:S(2)}) collective-permute-start(s32[168,128]{1,0:T(8,128)S(1)} %get-tuple-element.31), channel_id=1, source_target_pairs={{3,0},{0,1},{1,2},{2,3},{7,4},{4,5},{5,6},{6,7},{11,8},{8,9},{9,10... | collective-permute-start | bytes 258056 | tf_op jit(solution)/shard_map/ppermute | solution.py:40
  21.5 8.7 %collective-permute-start.5 = (s32[168,128]{1,0:T(8,128)S(1)}, s32[168,128]{1,0:T(8,128)S(1)}, u32[]{:S(2)}, u32[]{:S(2)}) collective-permute-start(s32[168,128]{1,0:T(8,128)S(1)} %get-tuple-element.32), channel_id=1, source_target_pairs={{2,0},{3,1},{0,2},{1,3},{6,4},{7,5},{4,6},{5,7},{10,8},{11,9},{8,1... | collective-permute-start | bytes 258056 | tf_op jit(solution)/shard_map/ppermute | solution.py:40
  23.8 6.7 %collective-permute-start.6 = (s32[168,128]{1,0:T(8,128)S(1)}, s32[168,128]{1,0:T(8,128)S(1)}, u32[]{:S(2)}, u32[]{:S(2)}) collective-permute-start(s32[168,128]{1,0:T(8,128)S(1)} %get-tuple-element.33), channel_id=1, source_target_pairs={{1,0},{2,1},{3,2},{0,3},{5,4},{6,5},{7,6},{4,7},{9,8},{10,9},{11,1... | collective-permute-start | bytes 258056 | tf_op jit(solution)/shard_map/ppermute | solution.py:40
  26.1 5.6 %collective-permute-start.10 = (s32[104,128]{1,0:T(8,128)S(1)}, s32[104,128]{1,0:T(8,128)S(1)}, u32[]{:S(2)}, u32[]{:S(2)}) collective-permute-start(s32[104,128]{1,0:T(8,128)S(1)} %get-tuple-element.38), channel_id=1, source_target_pairs={{1,0},{2,1},{3,2},{0,3},{5,4},{6,5},{7,6},{4,7},{9,8},{10,9},{11,1... | collective-permute-start | bytes 159752 | tf_op jit(solution)/shard_map/ppermute | solution.py:40
  27.0 6.0 %collective-permute-start.8 = (s32[104,128]{1,0:T(8,128)S(1)}, s32[104,128]{1,0:T(8,128)S(1)}, u32[]{:S(2)}, u32[]{:S(2)}) collective-permute-start(s32[104,128]{1,0:T(8,128)S(1)} %get-tuple-element.36), channel_id=1, source_target_pairs={{3,0},{0,1},{1,2},{2,3},{7,4},{4,5},{5,6},{6,7},{11,8},{8,9},{9,10... | collective-permute-start | bytes 159752 | tf_op jit(solution)/shard_map/ppermute | solution.py:40
  28.2 8.3 %collective-permute-start.9 = (s32[104,128]{1,0:T(8,128)S(1)}, s32[104,128]{1,0:T(8,128)S(1)}, u32[]{:S(2)}, u32[]{:S(2)}) collective-permute-start(s32[104,128]{1,0:T(8,128)S(1)} %get-tuple-element.37), channel_id=1, source_target_pairs={{2,0},{3,1},{0,2},{1,3},{6,4},{7,5},{4,6},{5,7},{10,8},{11,9},{8,1... | collective-permute-start | bytes 159752 | tf_op jit(solution)/shard_map/ppermute | solution.py:40

commit v10 on v9

v10 whole, which is shorter than its diff:
```python
import functools

import jax
import jax.numpy as jnp
from jax import lax
from jax.experimental import pallas as pl
from jax.experimental.pallas import tpu as pltpu
from jax.sharding import PartitionSpec as P

GROUP = 4
LANES = 128
MIB = 2**20
HBM = pltpu.MemorySpace.HBM


def row_ranges(order):
    first = order * 5 // 8
    return [(0, first), (first, order - first)]


def in_hbm(*values):
    return [pltpu.with_memory_space_constraint(value, HBM) for value in values]


def flipped(value, axis, bits):
    return lax.ppermute(value, axis, [(i, i ^ bits) for i in range(lax.axis_size(axis))])


def gathered(value, axis):
    values = {0: value}
    bit = lax.axis_size(axis) // 2
    while bit:
        values |= {d ^ bit: flipped(held, axis, bit) for d, held in values.items()}
        bit //= 2
    return [values[d] for d in range(len(values))]


def shifted(value, axis, offset):
    size = lax.axis_size(axis)
    return lax.ppermute(value, axis, [((i + offset) % size, i) for i in range(size)])


def quotient(value, by):
    return value >> (by.bit_length() - 1) if by & (by - 1) == 0 else lax.div(value, by)


def remainder(value, by):
    return value & (by - 1) if by & (by - 1) == 0 else lax.rem(value, by)


def write_digits(tile, at, value):
    height, width = value.shape
    tile[at : at + height, :width] = remainder(value, LANES)
    tile[at + height : at + 2 * height, :width] = quotient(value, LANES)


def pack_kernel(sizes, a_rows, a_cols, c_cols, x_in, s_cols, s_in, *refs):
    layers, count, piece_rows, width, local_rows, kept, order, ranges = sizes
    known, s_out, x_out, refs = refs[0], refs[1], refs[2 : 2 + len(ranges)], refs[2 + len(ranges) :]
    rows, cols, kept_held, s_held, x_tile, s_tile, sem = refs
    piece = piece_rows * width
    small = [(a_rows, rows), (a_cols, cols), (c_cols, kept_held), (s_cols, s_held)]
    large = [(x_in.at[:, pl.ds(*span)], out.at[pl.ds(0, count)]) for span, out in zip(ranges, x_out)]
    large += [(s_in.at[q], s_out.at[pl.ds(q * order, order)]) for q in range(piece)]
    loads = [
        pltpu.make_async_copy(source, goal, sem.at[p])
        for p, (source, goal) in enumerate(small + large)
    ]
    for load in loads:
        load.start()
    known[...] = jnp.zeros_like(known)
    x_tile[...] = jnp.zeros_like(x_tile)
    s_tile[...] = jnp.zeros_like(s_tile)
    x_out[0][count, 16:] = jnp.zeros((ranges[0][1] - 16, LANES), jnp.bfloat16)
    for load in loads[: len(small)]:
        load.wait()
    own_rows = local_rows // layers
    row, col = rows[...], cols[...]
    here = quotient(row[:, :1], local_rows)
    layer = remainder(quotient(col[:, :1], piece_rows), layers)
    owner = quotient(col, piece_rows * layers)
    local = row - here * local_rows
    goal = remainder(quotient(local, own_rows) - layer + layers, layers) * own_rows
    place = (
        ((owner ^ here) * piece_rows + remainder(col, piece_rows)) * width,
        (goal + remainder(local, own_rows)) * kept,
        local,
    )
    for p, value in enumerate(place):
        known[p : p + 1, :count] = value
        write_digits(x_tile, 2 * p, value)
    known[8 : 8 + kept, :local_rows] = kept_held[...]
    write_digits(s_tile, 0, s_held[...])
    x_out[0][count, :16] = x_tile[...].astype(jnp.float32).astype(jnp.bfloat16)
    s_out[piece * order :] = s_tile[...].astype(jnp.float32).astype(jnp.bfloat16)
    for load in loads[len(small) :]:
        load.wait()


def match(sizes, place, panel_cols, kept_cols, codes):
    width, local_rows, kept = sizes
    right, goal, local = place
    wanted, held = [jnp.zeros_like(right)] * width, [jnp.zeros_like(right)] * kept
    for p in range(panel_cols.shape[0]):
        for s in range(width):
            wanted[s] = jnp.where(right == p * width, panel_cols[p : p + 1, s : s + 1], wanted[s])
    for i in range(local_rows):
        for t in range(kept):
            held[t] = jnp.where(local == i, kept_cols[t : t + 1, i : i + 1], held[t])
    codes[0:1] = right
    for s in range(width):
        slot = jnp.full_like(right, -1)
        for t in range(kept):
            slot = jnp.where(held[t] == wanted[s], goal + t, slot)
        codes[1 + s : 2 + s] = slot


def list_pairs(sizes, codes, pairs):
    count, width, trash = sizes
    total = jnp.int32(0)
    for n in range(count):
        right = codes[0, n]
        for s in range(width):
            slot = codes[1 + s, n]
            pairs[0, total] = n
            pairs[1, total] = right + s
            pairs[2, total] = slot
            total += (slot >= 0).astype(jnp.int32)
    for g in range(GROUP):
        pairs[0, total + g] = 0
        pairs[1, total + g] = 0
        pairs[2, total + g] = trash
    return total


def add_products(left, panel, totals, pairs, total):
    def one_group(group, carry):
        base = group * GROUP
        products = [
            jnp.dot(
                left[pairs[0, base + g]],
                panel[pairs[1, base + g]],
                preferred_element_type=jnp.float32,
            )
            for g in range(GROUP)
        ]
        for g in range(GROUP):
            totals[pairs[2, base + g]] += products[g]
        return carry

    lax.fori_loop(0, quotient(total + GROUP - 1, GROUP), one_group, 0)


def own_kernel(sizes, ranges, known, *refs):
    rows, count, piece_rows, width, local_rows, kept, order = sizes
    x_in, s_in, refs = refs[: len(ranges)], refs[len(ranges) :][:rows], refs[len(ranges) + rows :]
    totals, panel, panel_cols, codes, numbers, pairs, sem = refs
    piece = piece_rows * width
    for d in range(rows):
        tile = s_in[d][piece * order :].astype(jnp.float32).astype(jnp.int32)
        panel_cols[d * piece_rows : (d + 1) * piece_rows] = (
            tile[:piece_rows] + tile[piece_rows : 2 * piece_rows] * LANES
        )
    place = known[0:1], known[1:2], known[2:3]
    match((width, local_rows, kept), place, panel_cols[...], known[8 : 8 + kept], codes)
    copy = pltpu.make_async_copy(codes, numbers, sem)
    copy.start()
    totals[...] = jnp.zeros_like(totals)
    for d in range(rows):
        for q in range(piece):
            panel[d * piece + q] = s_in[d][q * order : (q + 1) * order]
    copy.wait()
    total = list_pairs((count, width, totals.shape[0] - 1), numbers, pairs)
    for (first, height), blocks in zip(ranges, x_in):
        add_products(blocks, panel, totals.at[:, pl.ds(first, height)], pairs, total)


def peer_kernel(sizes, span, *refs):
    cols, layers, count, width, local_rows, kept = sizes
    first, height = span
    slots = local_rows * kept // layers
    if first == 0:
        known, panel_cols, *refs = refs
    else:
        codes, *refs = refs
    x_in, refs = refs[: cols - 1], refs[cols - 1 :]
    panel, before, own, sent, refs = refs[0], refs[1], refs[2], refs[3 : 2 + layers], refs[2 + layers :]
    if first == 0:
        codes, *refs = refs
        for j in range(cols - 1):
            digits = x_in[j][count, :16].astype(jnp.float32).astype(jnp.int32)
            place = [digits[p : p + 1] + digits[p + 1 : p + 2] * LANES for p in (0, 2, 4)]
            match(
                (width, local_rows, kept), place, panel_cols[...], known[8 : 8 + kept], codes.at[j]
            )
    totals, numbers, pairs, sem = refs
    copy = pltpu.make_async_copy(codes, numbers, sem)
    copy.start()
    totals[...] = before[:, first : first + height]
    copy.wait()
    for j in range(cols - 1):
        total = list_pairs((count, width, layers * slots), numbers.at[j], pairs)
        add_products(x_in[j], panel, totals, pairs, total)

    own[...] = totals[:slots]
    half = height // 2
    for d in range(1, layers):
        code = sent[d - 1]
        spare = code.shape[0] - slots * half
        code[slots * half :] = jnp.zeros((spare, code.shape[1]), jnp.int32)
        for u in range(slots):
            value = totals[d * slots + u]
            peak = jnp.max(jnp.abs(value), axis=0, keepdims=True)
            power = jnp.floor(jnp.log2(jnp.maximum(peak, 1e-30)) + 1e-3) + 1.0
            word = jnp.floor(value * jnp.exp2(15.0 - power) + 0.5).astype(jnp.int32)
            code[pl.ds(u * half, half)] = (word[:half] << 16) | (word[half:] & 0xFFFF)
            code[pl.ds(slots * half + u, 1)] = power.astype(jnp.int32)


def finish_kernel(sizes, span, *refs):
    layers, slots = sizes
    first, height = span
    half = height // 2
    before, own, codes, result = refs[: first > 0], refs[-layers - 1], refs[-layers:-1], refs[-1]
    kept = result.shape[1]
    for done in before:
        result[:, :, :first] = done[...]
    for u in range(slots):
        high, low = own[u, :half], own[u, half:]
        for code in codes:
            word = code[pl.ds(u * half, half)]
            power = code[pl.ds(slots * half + u, 1)].astype(jnp.float32)
            scale = jnp.exp2(power - 15.0)
            high += (word >> 16).astype(jnp.float32) * scale
            low += ((word << 16) >> 16).astype(jnp.float32) * scale
        result[u // kept, u % kept, first : first + half] = high.astype(jnp.bfloat16)
        result[u // kept, u % kept, first + half : first + height] = low.astype(jnp.bfloat16)


def per_device(a_blocks, a_rows, a_cols, s_blocks, s_cols, c_cols):
    rows, cols, layers = (lax.axis_size(axis) for axis in ("row", "col", "layer"))
    count, order = a_blocks.shape[:2]
    piece_rows, width = s_cols.shape
    local_rows, kept = c_cols.shape
    own_rows = local_rows // layers
    slots = own_rows * kept
    all_slots = layers * slots
    ranges = row_ranges(order)
    piece = piece_rows * width
    panel_size = rows * piece
    block_size = order * order
    flat_s = s_blocks.reshape(piece, order, order)
    note_height = (2 * piece_rows + 15) // 16 * 16
    code_height = (1 + width + 7) // 8 * 8

    vector = pl.BlockSpec(memory_space=pltpu.VMEM)
    far = pl.BlockSpec(memory_space=HBM)

    known, s_sent, *x_sent = pl.pallas_call(
        functools.partial(
            pack_kernel, (layers, count, piece_rows, width, local_rows, kept, order, ranges)
        ),
        out_shape=[
            jax.ShapeDtypeStruct((16, LANES), jnp.int32),
            jax.ShapeDtypeStruct((piece * order + note_height, order), jnp.bfloat16),
        ]
        + [
            jax.ShapeDtypeStruct((count + (at == 0), height, order), jnp.bfloat16)
            for at, height in ranges
        ],
        in_specs=[far] * 6,
        out_specs=[vector] * (2 + len(ranges)),
        scratch_shapes=[
            pltpu.VMEM((1, count), jnp.int32),
            pltpu.VMEM((1, count), jnp.int32),
            pltpu.VMEM((kept, local_rows), jnp.int32),
            pltpu.VMEM((piece_rows, width), jnp.int32),
            pltpu.VMEM((16, LANES), jnp.int32),
            pltpu.VMEM((note_height, LANES), jnp.int32),
            pltpu.SemaphoreType.DMA((4 + piece + len(ranges),)),
        ],
        compiler_params=pltpu.CompilerParams(
            vmem_limit_bytes=2 * block_size * (2 * count + piece) + 4 * MIB
        ),
        name="pack",
    )(
        *in_hbm(
            a_rows.reshape(1, count), a_cols.reshape(1, count), c_cols.T, a_blocks, s_cols, flat_s
        )
    )
    x_pieces = [[shifted(part, "col", j) for j in range(1, cols)] for part in x_sent]
    s_pieces = gathered(s_sent, "row")

    moved = block_size * (4 * all_slots + 4 * panel_size + 2 * count)
    totals, panel, panel_cols = pl.pallas_call(
        functools.partial(
            own_kernel, (rows, count, piece_rows, width, local_rows, kept, order), ranges
        ),
        out_shape=[
            jax.ShapeDtypeStruct((all_slots + 1, order, order), jnp.float32),
            jax.ShapeDtypeStruct((panel_size, order, order), jnp.bfloat16),
            jax.ShapeDtypeStruct((rows * piece_rows, LANES), jnp.int32),
        ],
        in_specs=[vector] * (1 + len(ranges) + rows),
        out_specs=[vector] * 3,
        scratch_shapes=[
            pltpu.VMEM((code_height, LANES), jnp.int32),
            pltpu.SMEM((code_height, LANES), jnp.int32),
            pltpu.SMEM((3, count * width + GROUP), jnp.int32),
            pltpu.SemaphoreType.DMA,
        ],
        compiler_params=pltpu.CompilerParams(vmem_limit_bytes=moved + 4 * MIB),
        cost_estimate=pl.CostEstimate(
            flops=2 * order**3 * count * width // 4, bytes_accessed=moved, transcendentals=0
        ),
        name="own_products",
    )(known, *x_sent, *s_pieces)

    moved = block_size * (8 * all_slots + 2 * panel_size + 2 * count * (cols - 1))
    code_shape = (cols - 1, code_height, LANES)
    finished, plan = [], []
    for (at, height), pieces in zip(ranges, x_pieces):
        code_rows = slots * (height // 2) + (slots + 7) // 8 * 8
        out_shape = [jax.ShapeDtypeStruct((slots, height, order), jnp.float32)]
        out_shape += [jax.ShapeDtypeStruct((code_rows, order), jnp.int32)] * (layers - 1)
        if at == 0:
            out_shape.append(jax.ShapeDtypeStruct(code_shape, jnp.int32))
        given = plan or (known, panel_cols)
        out = pl.pallas_call(
            functools.partial(
                peer_kernel, (cols, layers, count, width, local_rows, kept), (at, height)
            ),
            out_shape=out_shape,
            in_specs=[vector] * (len(given) + cols + 1),
            out_specs=[vector] * len(out_shape),
            scratch_shapes=[
                pltpu.VMEM((all_slots + 1, height, order), jnp.float32),
                pltpu.SMEM(code_shape, jnp.int32),
                pltpu.SMEM((3, count * width + GROUP), jnp.int32),
                pltpu.SemaphoreType.DMA,
            ],
            compiler_params=pltpu.CompilerParams(vmem_limit_bytes=moved + 4 * MIB),
            cost_estimate=pl.CostEstimate(
                flops=2 * order**2 * height * count * width // 4 * (cols - 1),
                bytes_accessed=moved // 2,
                transcendentals=0,
            ),
            name=f"peer_products_{at}",
        )(*given, *pieces, panel, totals)
        plan = plan or out[layers:]
        codes = [shifted(out[d], "layer", layers - d) for d in range(1, layers)]
        finished = [
            pl.pallas_call(
                functools.partial(finish_kernel, (layers, slots), (at, height)),
                out_shape=jax.ShapeDtypeStruct((own_rows, kept, at + height, order), jnp.bfloat16),
                in_specs=[vector] * (len(finished) + layers),
                out_specs=vector,
                compiler_params=pltpu.CompilerParams(
                    vmem_limit_bytes=16 * slots * block_size + 4 * MIB
                ),
                name=f"finish_{at}",
            )(*finished, out[0], *codes)
        ]
    return finished[0]


def solution(mesh):
    placed = (
        P(("row", "col", "layer"), None, None),
        P(("row", "col", "layer")),
        P(("row", "col", "layer")),
        P(("row", "layer"), "col", None, None),
        P(("row", "layer"), "col"),
        P("row", "col"),
    )
    return jax.shard_map(
        per_device,
        mesh=mesh,
        in_specs=placed,
        out_specs=P(("row", "layer"), "col", None, None),
        check_vma=False,
    )
```

time: 37.1 us -> 34.2 us (0.922)
  Pallas kernels: 10 us -> 6.24 us
  waiting for transfers between devices: 11.5 us -> 13.4 us
  local copies, waits for them, and re-layouts: 1.33 us -> 0 us
  starting transfers between devices: 13.6 us -> 14.5 us
  other arithmetic: 0.66 us -> 0 us
    pallas_call x4 -> x3, Pallas kernels: 6.64 us -> 3.71 us  [the longest x2 2.44 us: per_device(): pl.pallas_call(functools.partial(peer_kernel, (cols, layers, count, width...]
    ppermute x3, waiting for transfers between devices: 2.99 us -> 4.34 us  [flipped(): lax.ppermute(value, axis, [(i, i ^ bits) for i in range(lax.axis_size(axi...]
    unnamed x8 -> x0, local copies, waits for them, and re-layouts: 1.33 us -> none
    ppermute x8, starting transfers between devices: 12.1 us -> 13 us  [shifted(): lax.ppermute(value, axis, [((i + offset) % size, i) for i in range(size)])]
    pallas_call x1, Pallas kernels: 2.56 us -> 1.72 us  [per_device(): pl.pallas_call(functools.partial(own_kernel, (rows, count, piece_rows, wi...]
    another operation x1 -> x0, other arithmetic: 0.66 us -> none  [per_device(): place = jnp.stack([lax.axis_index('row'), lax.axis_index('layer')])]
    ppermute x8, waiting for transfers between devices: 8.49 us -> 9.04 us  [shifted(): lax.ppermute(value, axis, [((i + offset) % size, i) for i in range(size)])]
  transfers between devices with their start and end apart: 11 -> 11, of which waited for: 7 -> 5; matrix products, arithmetic and copies ran while one was open for 2% -> 0% of each run, Pallas kernels for 22% -> 12%
where the time goes in v10:
time: 34.2 us
  starting transfers between devices  14.5 us (42%)
  waiting for transfers between devices  13.4 us (39%)
  Pallas kernels  6.24 us (18%)
    ppermute x8, starting transfers between devices, shifted(): lax.ppermute(value, axis, [((i + offset) % size, i) for i in range(size)])  13 us
    ppermute x8, waiting for transfers between devices, shifted(): lax.ppermute(value, axis, [((i + offset) % size, i) for i in range(size)])  9.04 us
    ppermute x3, waiting for transfers between devices, flipped(): lax.ppermute(value, axis, [(i, i ^ bits) for i in range(lax.axis_size(axi...  4.34 us
    pallas_call x2, Pallas kernels, per_device(): pl.pallas_call(functools.partial(peer_kernel, (cols, layers, count, width...  2.44 us
    pallas_call x1, Pallas kernels, per_device(): pl.pallas_call(functools.partial(own_kernel, (rows, count, piece_rows, wi...  1.72 us
    ppermute x3, starting transfers between devices, flipped(): lax.ppermute(value, axis, [(i, i ^ bits) for i in range(lax.axis_size(axi...  1.52 us
    pallas_call x1, Pallas kernels, per_device(): pl.pallas_call(functools.partial(pack_kernel, (layers, count, piece_rows,...  1.27 us
    pallas_call x2, Pallas kernels, per_device(): pl.pallas_call(functools.partial(finish_kernel, (layers, slots), (at, hei...  0.81 us
  transfers between devices with their start and end apart: 11, of which 5 were waited for; matrix products, arithmetic and copies ran while one was open for 0% of the time, Pallas kernels for 12%

profile of v10, /device:TPU:0, one launch (start us, length us, event | category | flops | bytes accessed | tf_op | source)
XLA Modules:
  0.0 34.2 jit_solution(6127410220427820677)
XLA Ops:
  0.0 1.3 %pack.1 = (s32[16,128]{1,0:T(8,128)S(1)}, bf16[528,128]{1,0:T(8,128)(2,1)S(1)}, bf16[25,80,128]{2,1,0:T(8,128)(2,1)S(1)}, bf16[24,48,128]{2,1,0:T(8,128)(2,1)S(1)}) custom-call(s32[1,24]{1,0:T(1,128)} %bitcast.6, s32[1,24]{1,0:T(1,128)} %bitcast.7, s32[2,8]{1,0:T(2,128)} %bitcast.5, bf16[24,128,128]{2,1,0:T(8,128)(2,1)} %x_in.1, s32[2,2]{1,0:T(2,128)} %s_cols.1, ...), custom_call_target="tpu_custom_call" | custom-call | tf_op jit(solution)/shard_map/pack/pallas_call | solution.py:259
  1.3 3.0 %collective-permute-start.3 = (bf16[25,80,128]{2,1,0:T(8,128)(2,1)S(1)}, bf16[25,80,128]{2,1,0:T(8,128)(2,1)S(1)}, u32[]{:S(2)}, u32[]{:S(2)}) collective-permute-start(bf16[25,80,128]{2,1,0:T(8,128)(2,1)S(1)} %get-tuple-element.22.refs_0_), channel_id=1, source_target_pairs={{4,0},{0,4},{5,1},{1,5},{6,2},{2,6},{7,3},{3,7},{12,8},{8,12},{13,... | collective-permute-start | bytes 1536008 | tf_op jit(solution)/shard_map/ppermute | solution.py:40
  4.3 1.5 %collective-permute-start.1 = (bf16[528,128]{1,0:T(8,128)(2,1)S(1)}, bf16[528,128]{1,0:T(8,128)(2,1)S(1)}, u32[]{:S(2)}, u32[]{:S(2)}) collective-permute-start(bf16[528,128]{1,0:T(8,128)(2,1)S(1)} %get-tuple-element.24.refs_2_), channel_id=1, source_target_pairs={{0,16},{8,24},{16,0},{24,8},{1,17},{9,25},{17,1},{25,9},{2,18},{10... | collective-permute-start | bytes 405512 | tf_op jit(solution)/shard_map/ppermute | solution.py:26
  5.8 0.5 %collective-permute-start.7 = (bf16[24,48,128]{2,1,0:T(8,128)(2,1)S(1)}, bf16[24,48,128]{2,1,0:T(8,128)(2,1)S(1)}, u32[]{:S(2)}, u32[]{:S(2)}) collective-permute-start(bf16[24,48,128]{2,1,0:T(8,128)(2,1)S(1)} %get-tuple-element.23.refs_1_), channel_id=1, source_target_pairs={{4,0},{0,4},{5,1},{1,5},{6,2},{2,6},{7,3},{3,7},{12,8},{8,12},{13,... | collective-permute-start | bytes 884744 | tf_op jit(solution)/shard_map/ppermute | solution.py:40
  6.3 0.0 collective-permute-start
  6.3 3.0 %collective-permute-done.1.refs_4_ = bf16[528,128]{1,0:T(8,128)(2,1)S(1)} collective-permute-done((bf16[528,128]{1,0:T(8,128)(2,1)S(1)}, bf16[528,128]{1,0:T(8,128)(2,1)S(1)}, u32[]{:S(2)}, u32[]{:S(2)}) %collective-permute-start.1) | collective-permute-done | bytes 135200 | tf_op jit(solution)/shard_map/ppermute | solution.py:26
  9.3 0.0 collective-permute-start.2
  9.3 0.0 collective-permute-done.refs_3_
  9.3 1.3 %collective-permute-done.2.refs_5_ = bf16[528,128]{1,0:T(8,128)(2,1)S(1)} collective-permute-done((bf16[528,128]{1,0:T(8,128)(2,1)S(1)}, bf16[528,128]{1,0:T(8,128)(2,1)S(1)}, u32[]{:S(2)}, u32[]{:S(2)}) %collective-permute-start.2) | collective-permute-done | bytes 135200 | tf_op jit(solution)/shard_map/ppermute | solution.py:26
  10.7 1.7 %own_products.1 = (f32[17,128,128]{2,1,0:T(8,128)S(1)}, bf16[16,128,128]{2,1,0:T(8,128)(2,1)S(1)}, s32[8,128]{1,0:T(8,128)S(1)}) custom-call(s32[16,128]{1,0:T(8,128)S(1)} %get-tuple-element.21.known.refs_0_, bf16[25,80,128]{2,1,0:T(8,128)(2,1)S(1)} %get-tuple-element.22.refs_0_, bf16[24,48,128]{2,1,0:T(8,128)(2,1)S(1)} %get-tuple-element.23.refs_1_, ...), custom_call_target="tpu_custom_call" | custom-call | flops 50331648 | bytes 2883584 | tf_op jit(solution)/shard_map/own_products/pallas_call | solution.py:295
  12.4 4.4 %collective-permute-done.3.refs_2_ = bf16[25,80,128]{2,1,0:T(8,128)(2,1)S(1)} collective-permute-done((bf16[25,80,128]{2,1,0:T(8,128)(2,1)S(1)}, bf16[25,80,128]{2,1,0:T(8,128)(2,1)S(1)}, u32[]{:S(2)}, u32[]{:S(2)}) %collective-permute-start.3) | collective-permute-done | bytes 512032 | tf_op jit(solution)/shard_map/ppermute | solution.py:40
  16.8 1.3 %peer_products_0.1 = (f32[4,80,128]{2,1,0:T(8,128)S(1)}, s32[168,128]{1,0:T(8,128)S(1)}, s32[168,128]{1,0:T(8,128)S(1)}, s32[168,128]{1,0:T(8,128)S(1)}, s32[1,8,128]{2,1,0:T(8,128)S(1)}) custom-call(s32[16,128]{1,0:T(8,128)S(1)} %get-tuple-element.21.known.refs_0_, s32[8,128]{1,0:T(8,128)S(1)} %get-tuple-element.25.refs_1_, ...), custom_call_target="tpu_custom_call" | custom-call | flops 31457280 | bytes 1703936 | tf_op jit(solution)/shard_map/peer_products_0/pallas_call | solution.py:329
  18.1 2.4 %collective-permute-start.4 = (s32[168,128]{1,0:T(8,128)S(1)}, s32[168,128]{1,0:T(8,128)S(1)}, u32[]{:S(2)}, u32[]{:S(2)}) collective-permute-start(s32[168,128]{1,0:T(8,128)S(1)} %get-tuple-element.29), channel_id=1, source_target_pairs={{3,0},{0,1},{1,2},{2,3},{7,4},{4,5},{5,6},{6,7},{11,8},{8,9},{9,10... | collective-permute-start | bytes 258056 | tf_op jit(solution)/shard_map/ppermute | solution.py:40
  20.5 2.6 %collective-permute-start.5 = (s32[168,128]{1,0:T(8,128)S(1)}, s32[168,128]{1,0:T(8,128)S(1)}, u32[]{:S(2)}, u32[]{:S(2)}) collective-permute-start(s32[168,128]{1,0:T(8,128)S(1)} %get-tuple-element.30), channel_id=1, source_target_pairs={{2,0},{3,1},{0,2},{1,3},{6,4},{7,5},{4,6},{5,7},{10,8},{11,9},{8,1... | collective-permute-start | bytes 258056 | tf_op jit(solution)/shard_map/ppermute | solution.py:40
  23.1 1.5 %collective-permute-start.6 = (s32[168,128]{1,0:T(8,128)S(1)}, s32[168,128]{1,0:T(8,128)S(1)}, u32[]{:S(2)}, u32[]{:S(2)}) collective-permute-start(s32[168,128]{1,0:T(8,128)S(1)} %get-tuple-element.31), channel_id=1, source_target_pairs={{1,0},{2,1},{3,2},{0,3},{5,4},{6,5},{7,6},{4,7},{9,8},{10,9},{11,1... | collective-permute-start | bytes 258056 | tf_op jit(solution)/shard_map/ppermute | solution.py:40
  24.6 0.0 collective-permute-done.7.refs_1_
  24.6 1.1 %peer_products_80.1 = (f32[4,48,128]{2,1,0:T(8,128)S(1)}, s32[104,128]{1,0:T(8,128)S(1)}, s32[104,128]{1,0:T(8,128)S(1)}, s32[104,128]{1,0:T(8,128)S(1)}) custom-call(s32[1,8,128]{2,1,0:T(8,128)S(1)} %get-tuple-element.32.refs_0_, bf16[24,48,128]{2,1,0:T(8,128)(2,1)S(1)} %collective-permute-done.7.refs_1_, ...), custom_call_target="tpu_custom_call" | custom-call | flops 18874368 | bytes 1703936 | tf_op jit(solution)/shard_map/peer_products_80/pallas_call | solution.py:329
  25.8 1.7 %collective-permute-start.10 = (s32[104,128]{1,0:T(8,128)S(1)}, s32[104,128]{1,0:T(8,128)S(1)}, u32[]{:S(2)}, u32[]{:S(2)}) collective-permute-start(s32[104,128]{1,0:T(8,128)S(1)} %get-tuple-element.36), channel_id=1, source_target_pairs={{1,0},{2,1},{3,2},{0,3},{5,4},{6,5},{7,6},{4,7},{9,8},{10,9},{11,1... | collective-permute-start | bytes 159752 | tf_op jit(solution)/shard_map/ppermute | solution.py:40
  27.5 0.3 %collective-permute-start.8 = (s32[104,128]{1,0:T(8,128)S(1)}, s32[104,128]{1,0:T(8,128)S(1)}, u32[]{:S(2)}, u32[]{:S(2)}) collective-permute-start(s32[104,128]{1,0:T(8,128)S(1)} %get-tuple-element.34), channel_id=1, source_target_pairs={{3,0},{0,1},{1,2},{2,3},{7,4},{4,5},{5,6},{6,7},{11,8},{8,9},{9,10... | collective-permute-start | bytes 159752 | tf_op jit(solution)/shard_map/ppermute | solution.py:40
  27.8 0.0 collective-permute-done.4.refs_1_
  27.8 0.8 %collective-permute-start.9 = (s32[104,128]{1,0:T(8,128)S(1)}, s32[104,128]{1,0:T(8,128)S(1)}, u32[]{:S(2)}, u32[]{:S(2)}) collective-permute-start(s32[104,128]{1,0:T(8,128)S(1)} %get-tuple-element.35), channel_id=1, source_target_pairs={{2,0},{3,1},{0,2},{1,3},{6,4},{7,5},{4,6},{5,7},{10,8},{11,9},{8,1... | collective-permute-start | bytes 159752 | tf_op jit(solution)/shard_map/ppermute | solution.py:40
  28.7 0.0 collective-permute-done.5.refs_2_
  28.7 0.0 collective-permute-done.6.refs_3_
  28.7 0.1 finish_0.1.refs_0_
  28.8 1.4 %collective-permute-done.10.refs_4_ = s32[104,128]{1,0:T(8,128)S(1)} collective-permute-done((s32[104,128]{1,0:T(8,128)S(1)}, s32[104,128]{1,0:T(8,128)S(1)}, u32[]{:S(2)}, u32[]{:S(2)}) %collective-permute-start.10) | collective-permute-done | bytes 53280 | tf_op jit(solution)/shard_map/ppermute | solution.py:40
  30.2 3.2 %collective-permute-done.8.refs_2_ = s32[104,128]{1,0:T(8,128)S(1)} collective-permute-done((s32[104,128]{1,0:T(8,128)S(1)}, s32[104,128]{1,0:T(8,128)S(1)}, u32[]{:S(2)}, u32[]{:S(2)}) %collective-permute-start.8) | collective-permute-done | bytes 53280 | tf_op jit(solution)/shard_map/ppermute | solution.py:40
  33.4 0.0 collective-permute-done.9.refs_3_
  33.5 0.7 %finish_80.1 = bf16[2,2,128,128]{3,2,1,0:T(8,128)(2,1)} custom-call(bf16[2,2,80,128]{3,2,1,0:T(8,128)(2,1)S(1)} %finish_0.1.refs_0_, f32[4,48,128]{2,1,0:T(8,128)S(1)} %get-tuple-element.33.refs_1_, s32[104,128]{1,0:T(8,128)S(1)} %collective-permute-done.8.refs_2_, s32[104,128]{1,0:T(8,128)S(1)} %collective-permute-done.9.refs_3_, ...), custom_call_target="tpu_custom_call" | custom-call | tf_op jit(solution)/shard_map/finish_80/pallas_call | solution.py:353
Async XLA Ops:
  1.3 15.5 %collective-permute-start.3 = (bf16[25,80,128]{2,1,0:T(8,128)(2,1)S(1)}, bf16[25,80,128]{2,1,0:T(8,128)(2,1)S(1)}, u32[]{:S(2)}, u32[]{:S(2)}) collective-permute-start(bf16[25,80,128]{2,1,0:T(8,128)(2,1)S(1)} %get-tuple-element.22.refs_0_), channel_id=1, source_target_pairs={{4,0},{0,4},{5,1},{1,5},{6,2},{2,6},{7,3},{3,7},{12,8},{8,12},{13,... | collective-permute-start | bytes 1536008 | tf_op jit(solution)/shard_map/ppermute | solution.py:40
  4.3 5.0 %collective-permute-start.1 = (bf16[528,128]{1,0:T(8,128)(2,1)S(1)}, bf16[528,128]{1,0:T(8,128)(2,1)S(1)}, u32[]{:S(2)}, u32[]{:S(2)}) collective-permute-start(bf16[528,128]{1,0:T(8,128)(2,1)S(1)} %get-tuple-element.24.refs_2_), channel_id=1, source_target_pairs={{0,16},{8,24},{16,0},{24,8},{1,17},{9,25},{17,1},{25,9},{2,18},{10... | collective-permute-start | bytes 405512 | tf_op jit(solution)/shard_map/ppermute | solution.py:26
  5.8 18.8 %collective-permute-start.7 = (bf16[24,48,128]{2,1,0:T(8,128)(2,1)S(1)}, bf16[24,48,128]{2,1,0:T(8,128)(2,1)S(1)}, u32[]{:S(2)}, u32[]{:S(2)}) collective-permute-start(bf16[24,48,128]{2,1,0:T(8,128)(2,1)S(1)} %get-tuple-element.23.refs_1_), channel_id=1, source_target_pairs={{4,0},{0,4},{5,1},{1,5},{6,2},{2,6},{7,3},{3,7},{12,8},{8,12},{13,... | collective-permute-start | bytes 884744 | tf_op jit(solution)/shard_map/ppermute | solution.py:40
  6.3 3.0 %collective-permute-start = (bf16[528,128]{1,0:T(8,128)(2,1)S(1)}, bf16[528,128]{1,0:T(8,128)(2,1)S(1)}, u32[]{:S(2)}, u32[]{:S(2)}) collective-permute-start(bf16[528,128]{1,0:T(8,128)(2,1)S(1)} %get-tuple-element.24.refs_2_), channel_id=1, source_target_pairs={{0,8},{8,0},{16,24},{24,16},{1,9},{9,1},{17,25},{25,17},{2,10},{10... | collective-permute-start | bytes 405512 | tf_op jit(solution)/shard_map/ppermute | solution.py:26
  9.3 1.4 %collective-permute-start.2 = (bf16[528,128]{1,0:T(8,128)(2,1)S(1)}, bf16[528,128]{1,0:T(8,128)(2,1)S(1)}, u32[]{:S(2)}, u32[]{:S(2)}) collective-permute-start(bf16[528,128]{1,0:T(8,128)(2,1)S(1)} %collective-permute-done.1.refs_4_), channel_id=1, source_target_pairs={{0,8},{8,0},{16,24},{24,16},{1,9},{9,1},{17,25},{25,17},{2,10},{10... | collective-permute-start | bytes 405512 | tf_op jit(solution)/shard_map/ppermute | solution.py:26
  18.1 9.8 %collective-permute-start.4 = (s32[168,128]{1,0:T(8,128)S(1)}, s32[168,128]{1,0:T(8,128)S(1)}, u32[]{:S(2)}, u32[]{:S(2)}) collective-permute-start(s32[168,128]{1,0:T(8,128)S(1)} %get-tuple-element.29), channel_id=1, source_target_pairs={{3,0},{0,1},{1,2},{2,3},{7,4},{4,5},{5,6},{6,7},{11,8},{8,9},{9,10... | collective-permute-start | bytes 258056 | tf_op jit(solution)/shard_map/ppermute | solution.py:40
  20.5 8.2 %collective-permute-start.5 = (s32[168,128]{1,0:T(8,128)S(1)}, s32[168,128]{1,0:T(8,128)S(1)}, u32[]{:S(2)}, u32[]{:S(2)}) collective-permute-start(s32[168,128]{1,0:T(8,128)S(1)} %get-tuple-element.30), channel_id=1, source_target_pairs={{2,0},{3,1},{0,2},{1,3},{6,4},{7,5},{4,6},{5,7},{10,8},{11,9},{8,1... | collective-permute-start | bytes 258056 | tf_op jit(solution)/shard_map/ppermute | solution.py:40
  23.1 5.6 %collective-permute-start.6 = (s32[168,128]{1,0:T(8,128)S(1)}, s32[168,128]{1,0:T(8,128)S(1)}, u32[]{:S(2)}, u32[]{:S(2)}) collective-permute-start(s32[168,128]{1,0:T(8,128)S(1)} %get-tuple-element.31), channel_id=1, source_target_pairs={{1,0},{2,1},{3,2},{0,3},{5,4},{6,5},{7,6},{4,7},{9,8},{10,9},{11,1... | collective-permute-start | bytes 258056 | tf_op jit(solution)/shard_map/ppermute | solution.py:40
  25.8 4.5 %collective-permute-start.10 = (s32[104,128]{1,0:T(8,128)S(1)}, s32[104,128]{1,0:T(8,128)S(1)}, u32[]{:S(2)}, u32[]{:S(2)}) collective-permute-start(s32[104,128]{1,0:T(8,128)S(1)} %get-tuple-element.36), channel_id=1, source_target_pairs={{1,0},{2,1},{3,2},{0,3},{5,4},{6,5},{7,6},{4,7},{9,8},{10,9},{11,1... | collective-permute-start | bytes 159752 | tf_op jit(solution)/shard_map/ppermute | solution.py:40
  27.5 6.0 %collective-permute-start.8 = (s32[104,128]{1,0:T(8,128)S(1)}, s32[104,128]{1,0:T(8,128)S(1)}, u32[]{:S(2)}, u32[]{:S(2)}) collective-permute-start(s32[104,128]{1,0:T(8,128)S(1)} %get-tuple-element.34), channel_id=1, source_target_pairs={{3,0},{0,1},{1,2},{2,3},{7,4},{4,5},{5,6},{6,7},{11,8},{8,9},{9,10... | collective-permute-start | bytes 159752 | tf_op jit(solution)/shard_map/ppermute | solution.py:40
  27.8 5.6 %collective-permute-start.9 = (s32[104,128]{1,0:T(8,128)S(1)}, s32[104,128]{1,0:T(8,128)S(1)}, u32[]{:S(2)}, u32[]{:S(2)}) collective-permute-start(s32[104,128]{1,0:T(8,128)S(1)} %get-tuple-element.35), channel_id=1, source_target_pairs={{2,0},{3,1},{0,2},{1,3},{6,4},{7,5},{4,6},{5,7},{10,8},{11,9},{8,1... | collective-permute-start | bytes 159752 | tf_op jit(solution)/shard_map/ppermute | solution.py:40

commit v11 on v10

--- a/solution.py
+++ b/solution.py
@@ -60,7 +60,13 @@
     rows, cols, kept_held, s_held, x_tile, s_tile, sem = refs
     piece = piece_rows * width
     small = [(a_rows, rows), (a_cols, cols), (c_cols, kept_held), (s_cols, s_held)]
-    large = [(x_in.at[:, pl.ds(*span)], out.at[pl.ds(0, count)]) for span, out in zip(ranges, x_out)]
+    large = [
+        (
+            x_in.at[:, pl.ds(first, height)],
+            out.at[pl.ds(0, count * height)].reshape(count, height, order),
+        )
+        for (first, height), out in zip(ranges, x_out)
+    ]
     large += [(s_in.at[q], s_out.at[pl.ds(q * order, order)]) for q in range(piece)]
     loads = [
         pltpu.make_async_copy(source, goal, sem.at[p])
@@ -71,7 +77,6 @@
     known[...] = jnp.zeros_like(known)
     x_tile[...] = jnp.zeros_like(x_tile)
     s_tile[...] = jnp.zeros_like(s_tile)
-    x_out[0][count, 16:] = jnp.zeros((ranges[0][1] - 16, LANES), jnp.bfloat16)
     for load in loads[: len(small)]:
         load.wait()
     own_rows = local_rows // layers
@@ -91,7 +96,7 @@
         write_digits(x_tile, 2 * p, value)
     known[8 : 8 + kept, :local_rows] = kept_held[...]
     write_digits(s_tile, 0, s_held[...])
-    x_out[0][count, :16] = x_tile[...].astype(jnp.float32).astype(jnp.bfloat16)
+    x_out[0][count * ranges[0][1] :] = x_tile[...].astype(jnp.float32).astype(jnp.bfloat16)
     s_out[piece * order :] = s_tile[...].astype(jnp.float32).astype(jnp.bfloat16)
     for load in loads[len(small) :]:
         load.wait()
@@ -134,11 +139,16 @@
 
 
 def add_products(left, panel, totals, pairs, total):
+    height = totals.shape[1]
+
+    def block(n):
+        return left[pl.ds(pl.multiple_of(n * height, height), height)]
+
     def one_group(group, carry):
         base = group * GROUP
         products = [
             jnp.dot(
-                left[pairs[0, base + g]],
+                block(pairs[0, base + g]),
                 panel[pairs[1, base + g]],
                 preferred_element_type=jnp.float32,
             )
@@ -188,7 +198,7 @@
     if first == 0:
         codes, *refs = refs
         for j in range(cols - 1):
-            digits = x_in[j][count, :16].astype(jnp.float32).astype(jnp.int32)
+            digits = x_in[j][count * height :].astype(jnp.float32).astype(jnp.int32)
             place = [digits[p : p + 1] + digits[p + 1 : p + 2] * LANES for p in (0, 2, 4)]
             match(
                 (width, local_rows, kept), place, panel_cols[...], known[8 : 8 + kept], codes.at[j]
@@ -265,7 +275,7 @@
             jax.ShapeDtypeStruct((piece * order + note_height, order), jnp.bfloat16),
         ]
         + [
-            jax.ShapeDtypeStruct((count + (at == 0), height, order), jnp.bfloat16)
+            jax.ShapeDtypeStruct((count * height + 16 * (at == 0), order), jnp.bfloat16)
             for at, height in ranges
         ],
         in_specs=[far] * 6,
@@ -348,7 +358,8 @@
             name=f"peer_products_{at}",
         )(*given, *pieces, panel, totals)
         plan = plan or out[layers:]
-        codes = [shifted(out[d], "layer", layers - d) for d in range(1, layers)]
+        turn = range(layers - 1, 0, -1) if at == 0 else [*range(layers - 2, 0, -1), layers - 1]
+        codes = [shifted(out[d], "layer", layers - d) for d in turn]
         finished = [
             pl.pallas_call(
                 functools.partial(finish_kernel, (layers, slots), (at, height)),

time: 34.2 us -> 35.2 us (1.029)
  waiting for transfers between devices: 13.4 us -> 14.4 us
    ppermute x8, waiting for transfers between devices: 9.04 us -> 10 us  [shifted(): lax.ppermute(value, axis, [((i + offset) % size, i) for i in range(size)])]
    pallas_call x1, Pallas kernels: 1.72 us -> 1.34 us  [per_device(): pl.pallas_call(functools.partial(own_kernel, (rows, count, piece_rows, wi...]
    pallas_call x2, Pallas kernels: 2.44 us -> 2.82 us  [per_device(): pl.pallas_call(functools.partial(peer_kernel, (cols, layers, count, width...]
  transfers between devices with their start and end apart: 11 -> 11, of which waited for: 5 -> 7; matrix products, arithmetic and copies ran while one was open for 0% -> 0% of each run, Pallas kernels for 12% -> 12%
where the time goes in v11:
time: 35.2 us; the launch traced here: 35 us
  waiting for transfers between devices  14.4 us (41%)
  starting transfers between devices  14.3 us (41%)
  Pallas kernels  6.23 us (18%)
    ppermute x8, starting transfers between devices, shifted(): lax.ppermute(value, axis, [((i + offset) % size, i) for i in range(size)])  12.8 us
    ppermute x8, waiting for transfers between devices, shifted(): lax.ppermute(value, axis, [((i + offset) % size, i) for i in range(size)])  10 us
    ppermute x3, waiting for transfers between devices, flipped(): lax.ppermute(value, axis, [(i, i ^ bits) for i in range(lax.axis_size(axi...  4.34 us
    pallas_call x2, Pallas kernels, per_device(): pl.pallas_call(functools.partial(peer_kernel, (cols, layers, count, width...  2.82 us
    ppermute x3, starting transfers between devices, flipped(): lax.ppermute(value, axis, [(i, i ^ bits) for i in range(lax.axis_size(axi...  1.52 us
    pallas_call x1, Pallas kernels, per_device(): pl.pallas_call(functools.partial(own_kernel, (rows, count, piece_rows, wi...  1.34 us
    pallas_call x1, Pallas kernels, per_device(): pl.pallas_call(functools.partial(pack_kernel, (layers, count, piece_rows,...  1.27 us
    pallas_call x2, Pallas kernels, per_device(): pl.pallas_call(functools.partial(finish_kernel, (layers, slots), (at, hei...  0.81 us
  transfers between devices with their start and end apart: 11, of which 7 were waited for; matrix products, arithmetic and copies ran while one was open for 0% of the time, Pallas kernels for 12%

profile of v11, /device:TPU:0, one launch (start us, length us, event | category | flops | bytes accessed | tf_op | source)
XLA Modules:
  0.0 35.0 jit_solution(16338058160264976187)
XLA Ops:
  0.0 1.3 %pack.1 = (s32[16,128]{1,0:T(8,128)S(1)}, bf16[528,128]{1,0:T(8,128)(2,1)S(1)}, bf16[1936,128]{1,0:T(8,128)(2,1)S(1)}, bf16[1152,128]{1,0:T(8,128)(2,1)S(1)}) custom-call(s32[1,24]{1,0:T(1,128)} %bitcast.6, s32[1,24]{1,0:T(1,128)} %bitcast.7, s32[2,8]{1,0:T(2,128)} %bitcast.5, bf16[24,128,128]{2,1,0:T(8,128)(2,1)} %x_in.1, s32[2,2]{1,0:T(2,128)} %s_cols.1, ...), custom_call_target="tpu_custom_call" | custom-call | tf_op jit(solution)/shard_map/pack/pallas_call | solution.py:269
  1.3 3.0 %collective-permute-start.3 = (bf16[1936,128]{1,0:T(8,128)(2,1)S(1)}, bf16[1936,128]{1,0:T(8,128)(2,1)S(1)}, u32[]{:S(2)}, u32[]{:S(2)}) collective-permute-start(bf16[1936,128]{1,0:T(8,128)(2,1)S(1)} %get-tuple-element.22.refs_0_), channel_id=1, source_target_pairs={{4,0},{0,4},{5,1},{1,5},{6,2},{2,6},{7,3},{3,7},{12,8},{8,12},{13,... | collective-permute-start | bytes 1486856 | tf_op jit(solution)/shard_map/ppermute | solution.py:40
  4.3 1.5 %collective-permute-start.1 = (bf16[528,128]{1,0:T(8,128)(2,1)S(1)}, bf16[528,128]{1,0:T(8,128)(2,1)S(1)}, u32[]{:S(2)}, u32[]{:S(2)}) collective-permute-start(bf16[528,128]{1,0:T(8,128)(2,1)S(1)} %get-tuple-element.24.refs_2_), channel_id=1, source_target_pairs={{0,16},{8,24},{16,0},{24,8},{1,17},{9,25},{17,1},{25,9},{2,18},{10... | collective-permute-start | bytes 405512 | tf_op jit(solution)/shard_map/ppermute | solution.py:26
  5.8 0.5 %collective-permute-start.7 = (bf16[1152,128]{1,0:T(8,128)(2,1)S(1)}, bf16[1152,128]{1,0:T(8,128)(2,1)S(1)}, u32[]{:S(2)}, u32[]{:S(2)}) collective-permute-start(bf16[1152,128]{1,0:T(8,128)(2,1)S(1)} %get-tuple-element.23.refs_1_), channel_id=1, source_target_pairs={{4,0},{0,4},{5,1},{1,5},{6,2},{2,6},{7,3},{3,7},{12,8},{8,12},{13,... | collective-permute-start | bytes 884744 | tf_op jit(solution)/shard_map/ppermute | solution.py:40
  6.3 0.0 collective-permute-start
  6.3 3.0 %collective-permute-done.1.refs_4_ = bf16[528,128]{1,0:T(8,128)(2,1)S(1)} collective-permute-done((bf16[528,128]{1,0:T(8,128)(2,1)S(1)}, bf16[528,128]{1,0:T(8,128)(2,1)S(1)}, u32[]{:S(2)}, u32[]{:S(2)}) %collective-permute-start.1) | collective-permute-done | bytes 135200 | tf_op jit(solution)/shard_map/ppermute | solution.py:26
  9.3 0.0 collective-permute-start.2
  9.3 0.0 collective-permute-done.refs_3_
  9.3 1.3 %collective-permute-done.2.refs_5_ = bf16[528,128]{1,0:T(8,128)(2,1)S(1)} collective-permute-done((bf16[528,128]{1,0:T(8,128)(2,1)S(1)}, bf16[528,128]{1,0:T(8,128)(2,1)S(1)}, u32[]{:S(2)}, u32[]{:S(2)}) %collective-permute-start.2) | collective-permute-done | bytes 135200 | tf_op jit(solution)/shard_map/ppermute | solution.py:26
  10.7 1.3 %own_products.1 = (f32[17,128,128]{2,1,0:T(8,128)S(1)}, bf16[16,128,128]{2,1,0:T(8,128)(2,1)S(1)}, s32[8,128]{1,0:T(8,128)S(1)}) custom-call(s32[16,128]{1,0:T(8,128)S(1)} %get-tuple-element.21.known.refs_0_, bf16[1936,128]{1,0:T(8,128)(2,1)S(1)} %get-tuple-element.22.refs_0_, bf16[1152,128]{1,0:T(8,128)(2,1)S(1)} %get-tuple-element.23.refs_1_, ...), custom_call_target="tpu_custom_call" | custom-call | flops 50331648 | bytes 2883584 | tf_op jit(solution)/shard_map/own_products/pallas_call | solution.py:305
  12.0 4.4 %collective-permute-done.3.refs_2_ = bf16[1936,128]{1,0:T(8,128)(2,1)S(1)} collective-permute-done((bf16[1936,128]{1,0:T(8,128)(2,1)S(1)}, bf16[1936,128]{1,0:T(8,128)(2,1)S(1)}, u32[]{:S(2)}, u32[]{:S(2)}) %collective-permute-start.3) | collective-permute-done | bytes 495648 | tf_op jit(solution)/shard_map/ppermute | solution.py:40
  16.4 1.5 %peer_products_0.1 = (f32[4,80,128]{2,1,0:T(8,128)S(1)}, s32[168,128]{1,0:T(8,128)S(1)}, s32[168,128]{1,0:T(8,128)S(1)}, s32[168,128]{1,0:T(8,128)S(1)}, s32[1,8,128]{2,1,0:T(8,128)S(1)}) custom-call(s32[16,128]{1,0:T(8,128)S(1)} %get-tuple-element.21.known.refs_0_, s32[8,128]{1,0:T(8,128)S(1)} %get-tuple-element.25.refs_1_, ...), custom_call_target="tpu_custom_call" | custom-call | flops 31457280 | bytes 1703936 | tf_op jit(solution)/shard_map/peer_products_0/pallas_call | solution.py:339
  17.9 4.2 %collective-permute-start.4 = (s32[168,128]{1,0:T(8,128)S(1)}, s32[168,128]{1,0:T(8,128)S(1)}, u32[]{:S(2)}, u32[]{:S(2)}) collective-permute-start(s32[168,128]{1,0:T(8,128)S(1)} %get-tuple-element.29), channel_id=1, source_target_pairs={{1,0},{2,1},{3,2},{0,3},{5,4},{6,5},{7,6},{4,7},{9,8},{10,9},{11,1... | collective-permute-start | bytes 258056 | tf_op jit(solution)/shard_map/ppermute | solution.py:40
  22.1 0.0 collective-permute-start.5
  22.2 1.0 %collective-permute-start.6 = (s32[168,128]{1,0:T(8,128)S(1)}, s32[168,128]{1,0:T(8,128)S(1)}, u32[]{:S(2)}, u32[]{:S(2)}) collective-permute-start(s32[168,128]{1,0:T(8,128)S(1)} %get-tuple-element.31), channel_id=1, source_target_pairs={{3,0},{0,1},{1,2},{2,3},{7,4},{4,5},{5,6},{6,7},{11,8},{8,9},{9,10... | collective-permute-start | bytes 258056 | tf_op jit(solution)/shard_map/ppermute | solution.py:40
  23.2 0.0 collective-permute-done.7.refs_1_
  23.2 1.3 %peer_products_80.1 = (f32[4,48,128]{2,1,0:T(8,128)S(1)}, s32[104,128]{1,0:T(8,128)S(1)}, s32[104,128]{1,0:T(8,128)S(1)}, s32[104,128]{1,0:T(8,128)S(1)}) custom-call(s32[1,8,128]{2,1,0:T(8,128)S(1)} %get-tuple-element.32.refs_0_, bf16[1152,128]{1,0:T(8,128)(2,1)S(1)} %collective-permute-done.7.refs_1_, ...), custom_call_target="tpu_custom_call" | custom-call | flops 18874368 | bytes 1703936 | tf_op jit(solution)/shard_map/peer_products_80/pallas_call | solution.py:339
  24.5 2.9 %collective-permute-start.10 = (s32[104,128]{1,0:T(8,128)S(1)}, s32[104,128]{1,0:T(8,128)S(1)}, u32[]{:S(2)}, u32[]{:S(2)}) collective-permute-start(s32[104,128]{1,0:T(8,128)S(1)} %get-tuple-element.36), channel_id=1, source_target_pairs={{1,0},{2,1},{3,2},{0,3},{5,4},{6,5},{7,6},{4,7},{9,8},{10,9},{11,1... | collective-permute-start | bytes 159752 | tf_op jit(solution)/shard_map/ppermute | solution.py:40
  27.4 0.9 %collective-permute-start.8 = (s32[104,128]{1,0:T(8,128)S(1)}, s32[104,128]{1,0:T(8,128)S(1)}, u32[]{:S(2)}, u32[]{:S(2)}) collective-permute-start(s32[104,128]{1,0:T(8,128)S(1)} %get-tuple-element.34), channel_id=1, source_target_pairs={{2,0},{3,1},{0,2},{1,3},{6,4},{7,5},{4,6},{5,7},{10,8},{11,9},{8,1... | collective-permute-start | bytes 159752 | tf_op jit(solution)/shard_map/ppermute | solution.py:40
  28.3 0.0 collective-permute-done.4.refs_1_
  28.3 0.2 collective-permute-start.9
  28.5 1.6 %collective-permute-done.5.refs_2_ = s32[168,128]{1,0:T(8,128)S(1)} collective-permute-done((s32[168,128]{1,0:T(8,128)S(1)}, s32[168,128]{1,0:T(8,128)S(1)}, u32[]{:S(2)}, u32[]{:S(2)}) %collective-permute-start.5) | collective-permute-done | bytes 86048 | tf_op jit(solution)/shard_map/ppermute | solution.py:40
  30.1 0.0 collective-permute-done.6.refs_3_
  30.1 0.1 finish_0.1.refs_0_
  30.2 0.7 %collective-permute-done.10.refs_4_ = s32[104,128]{1,0:T(8,128)S(1)} collective-permute-done((s32[104,128]{1,0:T(8,128)S(1)}, s32[104,128]{1,0:T(8,128)S(1)}, u32[]{:S(2)}, u32[]{:S(2)}) %collective-permute-start.10) | collective-permute-done | bytes 53280 | tf_op jit(solution)/shard_map/ppermute | solution.py:40
  30.9 1.6 %collective-permute-done.8.refs_2_ = s32[104,128]{1,0:T(8,128)S(1)} collective-permute-done((s32[104,128]{1,0:T(8,128)S(1)}, s32[104,128]{1,0:T(8,128)S(1)}, u32[]{:S(2)}, u32[]{:S(2)}) %collective-permute-start.8) | collective-permute-done | bytes 53280 | tf_op jit(solution)/shard_map/ppermute | solution.py:40
  32.5 1.8 %collective-permute-done.9.refs_3_ = s32[104,128]{1,0:T(8,128)S(1)} collective-permute-done((s32[104,128]{1,0:T(8,128)S(1)}, s32[104,128]{1,0:T(8,128)S(1)}, u32[]{:S(2)}, u32[]{:S(2)}) %collective-permute-start.9) | collective-permute-done | bytes 53280 | tf_op jit(solution)/shard_map/ppermute | solution.py:40
  34.2 0.7 %finish_80.1 = bf16[2,2,128,128]{3,2,1,0:T(8,128)(2,1)} custom-call(bf16[2,2,80,128]{3,2,1,0:T(8,128)(2,1)S(1)} %finish_0.1.refs_0_, f32[4,48,128]{2,1,0:T(8,128)S(1)} %get-tuple-element.33.refs_1_, s32[104,128]{1,0:T(8,128)S(1)} %collective-permute-done.8.refs_2_, s32[104,128]{1,0:T(8,128)S(1)} %collective-permute-done.9.refs_3_, ...), custom_call_target="tpu_custom_call" | custom-call | tf_op jit(solution)/shard_map/finish_80/pallas_call | solution.py:364
Async XLA Ops:
  1.3 15.1 %collective-permute-start.3 = (bf16[1936,128]{1,0:T(8,128)(2,1)S(1)}, bf16[1936,128]{1,0:T(8,128)(2,1)S(1)}, u32[]{:S(2)}, u32[]{:S(2)}) collective-permute-start(bf16[1936,128]{1,0:T(8,128)(2,1)S(1)} %get-tuple-element.22.refs_0_), channel_id=1, source_target_pairs={{4,0},{0,4},{5,1},{1,5},{6,2},{2,6},{7,3},{3,7},{12,8},{8,12},{13,... | collective-permute-start | bytes 1486856 | tf_op jit(solution)/shard_map/ppermute | solution.py:40
  4.3 5.0 %collective-permute-start.1 = (bf16[528,128]{1,0:T(8,128)(2,1)S(1)}, bf16[528,128]{1,0:T(8,128)(2,1)S(1)}, u32[]{:S(2)}, u32[]{:S(2)}) collective-permute-start(bf16[528,128]{1,0:T(8,128)(2,1)S(1)} %get-tuple-element.24.refs_2_), channel_id=1, source_target_pairs={{0,16},{8,24},{16,0},{24,8},{1,17},{9,25},{17,1},{25,9},{2,18},{10... | collective-permute-start | bytes 405512 | tf_op jit(solution)/shard_map/ppermute | solution.py:26
  5.8 17.4 %collective-permute-start.7 = (bf16[1152,128]{1,0:T(8,128)(2,1)S(1)}, bf16[1152,128]{1,0:T(8,128)(2,1)S(1)}, u32[]{:S(2)}, u32[]{:S(2)}) collective-permute-start(bf16[1152,128]{1,0:T(8,128)(2,1)S(1)} %get-tuple-element.23.refs_1_), channel_id=1, source_target_pairs={{4,0},{0,4},{5,1},{1,5},{6,2},{2,6},{7,3},{3,7},{12,8},{8,12},{13,... | collective-permute-start | bytes 884744 | tf_op jit(solution)/shard_map/ppermute | solution.py:40
  6.3 3.0 %collective-permute-start = (bf16[528,128]{1,0:T(8,128)(2,1)S(1)}, bf16[528,128]{1,0:T(8,128)(2,1)S(1)}, u32[]{:S(2)}, u32[]{:S(2)}) collective-permute-start(bf16[528,128]{1,0:T(8,128)(2,1)S(1)} %get-tuple-element.24.refs_2_), channel_id=1, source_target_pairs={{0,8},{8,0},{16,24},{24,16},{1,9},{9,1},{17,25},{25,17},{2,10},{10... | collective-permute-start | bytes 405512 | tf_op jit(solution)/shard_map/ppermute | solution.py:26
  9.3 1.4 %collective-permute-start.2 = (bf16[528,128]{1,0:T(8,128)(2,1)S(1)}, bf16[528,128]{1,0:T(8,128)(2,1)S(1)}, u32[]{:S(2)}, u32[]{:S(2)}) collective-permute-start(bf16[528,128]{1,0:T(8,128)(2,1)S(1)} %collective-permute-done.1.refs_4_), channel_id=1, source_target_pairs={{0,8},{8,0},{16,24},{24,16},{1,9},{9,1},{17,25},{25,17},{2,10},{10... | collective-permute-start | bytes 405512 | tf_op jit(solution)/shard_map/ppermute | solution.py:26
  17.9 10.4 %collective-permute-start.4 = (s32[168,128]{1,0:T(8,128)S(1)}, s32[168,128]{1,0:T(8,128)S(1)}, u32[]{:S(2)}, u32[]{:S(2)}) collective-permute-start(s32[168,128]{1,0:T(8,128)S(1)} %get-tuple-element.29), channel_id=1, source_target_pairs={{1,0},{2,1},{3,2},{0,3},{5,4},{6,5},{7,6},{4,7},{9,8},{10,9},{11,1... | collective-permute-start | bytes 258056 | tf_op jit(solution)/shard_map/ppermute | solution.py:40
  22.1 8.0 %collective-permute-start.5 = (s32[168,128]{1,0:T(8,128)S(1)}, s32[168,128]{1,0:T(8,128)S(1)}, u32[]{:S(2)}, u32[]{:S(2)}) collective-permute-start(s32[168,128]{1,0:T(8,128)S(1)} %get-tuple-element.30), channel_id=1, source_target_pairs={{2,0},{3,1},{0,2},{1,3},{6,4},{7,5},{4,6},{5,7},{10,8},{11,9},{8,1... | collective-permute-start | bytes 258056 | tf_op jit(solution)/shard_map/ppermute | solution.py:40
  22.2 8.0 %collective-permute-start.6 = (s32[168,128]{1,0:T(8,128)S(1)}, s32[168,128]{1,0:T(8,128)S(1)}, u32[]{:S(2)}, u32[]{:S(2)}) collective-permute-start(s32[168,128]{1,0:T(8,128)S(1)} %get-tuple-element.31), channel_id=1, source_target_pairs={{3,0},{0,1},{1,2},{2,3},{7,4},{4,5},{5,6},{6,7},{11,8},{8,9},{9,10... | collective-permute-start | bytes 258056 | tf_op jit(solution)/shard_map/ppermute | solution.py:40
  24.5 6.4 %collective-permute-start.10 = (s32[104,128]{1,0:T(8,128)S(1)}, s32[104,128]{1,0:T(8,128)S(1)}, u32[]{:S(2)}, u32[]{:S(2)}) collective-permute-start(s32[104,128]{1,0:T(8,128)S(1)} %get-tuple-element.36), channel_id=1, source_target_pairs={{1,0},{2,1},{3,2},{0,3},{5,4},{6,5},{7,6},{4,7},{9,8},{10,9},{11,1... | collective-permute-start | bytes 159752 | tf_op jit(solution)/shard_map/ppermute | solution.py:40
  27.4 5.1 %collective-permute-start.8 = (s32[104,128]{1,0:T(8,128)S(1)}, s32[104,128]{1,0:T(8,128)S(1)}, u32[]{:S(2)}, u32[]{:S(2)}) collective-permute-start(s32[104,128]{1,0:T(8,128)S(1)} %get-tuple-element.34), channel_id=1, source_target_pairs={{2,0},{3,1},{0,2},{1,3},{6,4},{7,5},{4,6},{5,7},{10,8},{11,9},{8,1... | collective-permute-start | bytes 159752 | tf_op jit(solution)/shard_map/ppermute | solution.py:40
  28.3 5.9 %collective-permute-start.9 = (s32[104,128]{1,0:T(8,128)S(1)}, s32[104,128]{1,0:T(8,128)S(1)}, u32[]{:S(2)}, u32[]{:S(2)}) collective-permute-start(s32[104,128]{1,0:T(8,128)S(1)} %get-tuple-element.35), channel_id=1, source_target_pairs={{3,0},{0,1},{1,2},{2,3},{7,4},{4,5},{5,6},{6,7},{11,8},{8,9},{9,10... | collective-permute-start | bytes 159752 | tf_op jit(solution)/shard_map/ppermute | solution.py:40

commit v12 on v11

--- a/solution.py
+++ b/solution.py
@@ -298,8 +298,11 @@
             a_rows.reshape(1, count), a_cols.reshape(1, count), c_cols.T, a_blocks, s_cols, flat_s
         )
     )
-    x_pieces = [[shifted(part, "col", j) for j in range(1, cols)] for part in x_sent]
     s_pieces = gathered(s_sent, "row")
+    later, _ = lax.optimization_barrier((x_sent[1:], s_pieces))
+    x_pieces = [
+        [shifted(part, "col", j) for j in range(1, cols)] for part in (x_sent[0], *later)
+    ]
 
     moved = block_size * (4 * all_slots + 4 * panel_size + 2 * count)
     totals, panel, panel_cols = pl.pallas_call(
@@ -358,8 +361,7 @@
             name=f"peer_products_{at}",
         )(*given, *pieces, panel, totals)
         plan = plan or out[layers:]
-        turn = range(layers - 1, 0, -1) if at == 0 else [*range(layers - 2, 0, -1), layers - 1]
-        codes = [shifted(out[d], "layer", layers - d) for d in turn]
+        codes = [shifted(out[d], "layer", layers - d) for d in range(1, layers)]
         finished = [
             pl.pallas_call(
                 functools.partial(finish_kernel, (layers, slots), (at, height)),

time: 35.2 us -> 33.9 us (0.963)
  waiting for transfers between devices: 14.4 us -> 13.4 us
  starting transfers between devices: 14.3 us -> 13.8 us
  Pallas kernels: 6.23 us -> 6.61 us
    ppermute x8, waiting for transfers between devices: 10 us -> 8.48 us  [shifted(): lax.ppermute(value, axis, [((i + offset) % size, i) for i in range(size)])]
    ppermute x3, waiting for transfers between devices: 4.34 us -> 4.87 us  [flipped(): lax.ppermute(value, axis, [(i, i ^ bits) for i in range(lax.axis_size(axi...]
    ppermute x8, starting transfers between devices: 12.8 us -> 12.3 us  [shifted(): lax.ppermute(value, axis, [((i + offset) % size, i) for i in range(size)])]
    pallas_call x1, Pallas kernels: 1.34 us -> 1.72 us  [per_device(): pl.pallas_call(functools.partial(own_kernel, (rows, count, piece_rows, wi...]
  transfers between devices with their start and end apart: 11 -> 11, of which waited for: 7 -> 5; matrix products, arithmetic and copies ran while one was open for 0% -> 0% of each run, Pallas kernels for 12% -> 14%
where the time goes in v12:
time: 33.9 us; the launch traced here: 33.8 us
  starting transfers between devices  13.8 us (41%)
  waiting for transfers between devices  13.4 us (40%)
  Pallas kernels  6.61 us (19%)
    ppermute x8, starting transfers between devices, shifted(): lax.ppermute(value, axis, [((i + offset) % size, i) for i in range(size)])  12.3 us
    ppermute x8, waiting for transfers between devices, shifted(): lax.ppermute(value, axis, [((i + offset) % size, i) for i in range(size)])  8.48 us
    ppermute x3, waiting for transfers between devices, flipped(): lax.ppermute(value, axis, [(i, i ^ bits) for i in range(lax.axis_size(axi...  4.87 us
    pallas_call x2, Pallas kernels, per_device(): pl.pallas_call(functools.partial(peer_kernel, (cols, layers, count, width...  2.82 us
    pallas_call x1, Pallas kernels, per_device(): pl.pallas_call(functools.partial(own_kernel, (rows, count, piece_rows, wi...  1.72 us
    ppermute x3, starting transfers between devices, flipped(): lax.ppermute(value, axis, [(i, i ^ bits) for i in range(lax.axis_size(axi...  1.52 us
    pallas_call x1, Pallas kernels, per_device(): pl.pallas_call(functools.partial(pack_kernel, (layers, count, piece_rows,...  1.27 us
    pallas_call x2, Pallas kernels, per_device(): pl.pallas_call(functools.partial(finish_kernel, (layers, slots), (at, hei...  0.81 us
  transfers between devices with their start and end apart: 11, of which 5 were waited for; matrix products, arithmetic and copies ran while one was open for 0% of the time, Pallas kernels for 14%

profile of v12, /device:TPU:0, one launch (start us, length us, event | category | flops | bytes accessed | tf_op | source)
XLA Modules:
  0.0 33.8 jit_solution(14616943863114814447)
XLA Ops:
  0.0 1.3 %pack.1 = (s32[16,128]{1,0:T(8,128)S(1)}, bf16[528,128]{1,0:T(8,128)(2,1)S(1)}, bf16[1936,128]{1,0:T(8,128)(2,1)S(1)}, bf16[1152,128]{1,0:T(8,128)(2,1)S(1)}) custom-call(s32[1,24]{1,0:T(1,128)} %bitcast.6, s32[1,24]{1,0:T(1,128)} %bitcast.7, s32[2,8]{1,0:T(2,128)} %bitcast.5, bf16[24,128,128]{2,1,0:T(8,128)(2,1)} %x_in.1, s32[2,2]{1,0:T(2,128)} %s_cols.1, ...), custom_call_target="tpu_custom_call" | custom-call | tf_op jit(solution)/shard_map/pack/pallas_call | solution.py:269
  1.3 3.0 %collective-permute-start.3 = (bf16[1936,128]{1,0:T(8,128)(2,1)S(1)}, bf16[1936,128]{1,0:T(8,128)(2,1)S(1)}, u32[]{:S(2)}, u32[]{:S(2)}) collective-permute-start(bf16[1936,128]{1,0:T(8,128)(2,1)S(1)} %get-tuple-element.23.refs_0_), channel_id=1, source_target_pairs={{4,0},{0,4},{5,1},{1,5},{6,2},{2,6},{7,3},{3,7},{12,8},{8,12},{13,... | collective-permute-start | bytes 1486856 | tf_op jit(solution)/shard_map/ppermute | solution.py:40
  4.3 1.5 %collective-permute-start.1 = (bf16[528,128]{1,0:T(8,128)(2,1)S(1)}, bf16[528,128]{1,0:T(8,128)(2,1)S(1)}, u32[]{:S(2)}, u32[]{:S(2)}) collective-permute-start(bf16[528,128]{1,0:T(8,128)(2,1)S(1)} %get-tuple-element.25.refs_2_), channel_id=1, source_target_pairs={{0,16},{8,24},{16,0},{24,8},{1,17},{9,25},{17,1},{25,9},{2,18},{10... | collective-permute-start | bytes 405512 | tf_op jit(solution)/shard_map/ppermute | solution.py:26
  5.8 0.0 collective-permute-start
  5.8 3.5 %collective-permute-done.1.refs_4_ = bf16[528,128]{1,0:T(8,128)(2,1)S(1)} collective-permute-done((bf16[528,128]{1,0:T(8,128)(2,1)S(1)}, bf16[528,128]{1,0:T(8,128)(2,1)S(1)}, u32[]{:S(2)}, u32[]{:S(2)}) %collective-permute-start.1) | collective-permute-done | bytes 135200 | tf_op jit(solution)/shard_map/ppermute | solution.py:26
  9.3 0.0 collective-permute-start.2
  9.3 0.0 collective-permute-done.refs_3_
  9.3 1.3 %collective-permute-done.2.refs_5_ = bf16[528,128]{1,0:T(8,128)(2,1)S(1)} collective-permute-done((bf16[528,128]{1,0:T(8,128)(2,1)S(1)}, bf16[528,128]{1,0:T(8,128)(2,1)S(1)}, u32[]{:S(2)}, u32[]{:S(2)}) %collective-permute-start.2) | collective-permute-done | bytes 135200 | tf_op jit(solution)/shard_map/ppermute | solution.py:26
  10.7 0.4 %collective-permute-start.7 = (bf16[1152,128]{1,0:T(8,128)(2,1)S(1)}, bf16[1152,128]{1,0:T(8,128)(2,1)S(1)}, u32[]{:S(2)}, u32[]{:S(2)}) collective-permute-start(bf16[1152,128]{1,0:T(8,128)(2,1)S(1)} %get-tuple-element.34.refs_1_), channel_id=1, source_target_pairs={{4,0},{0,4},{5,1},{1,5},{6,2},{2,6},{7,3},{3,7},{12,8},{8,12},{13,... | collective-permute-start | bytes 884744 | tf_op jit(solution)/shard_map/ppermute | solution.py:40
  11.0 1.7 %own_products.1 = (f32[17,128,128]{2,1,0:T(8,128)S(1)}, bf16[16,128,128]{2,1,0:T(8,128)(2,1)S(1)}, s32[8,128]{1,0:T(8,128)S(1)}) custom-call(s32[16,128]{1,0:T(8,128)S(1)} %get-tuple-element.22.known.refs_0_, bf16[1936,128]{1,0:T(8,128)(2,1)S(1)} %get-tuple-element.23.refs_0_, bf16[1152,128]{1,0:T(8,128)(2,1)S(1)} %get-tuple-element.34.refs_1_, ...), custom_call_target="tpu_custom_call" | custom-call | flops 50331648 | bytes 2883584 | tf_op jit(solution)/shard_map/own_products/pallas_call | solution.py:308
  12.8 3.6 %collective-permute-done.3.refs_2_ = bf16[1936,128]{1,0:T(8,128)(2,1)S(1)} collective-permute-done((bf16[1936,128]{1,0:T(8,128)(2,1)S(1)}, bf16[1936,128]{1,0:T(8,128)(2,1)S(1)}, u32[]{:S(2)}, u32[]{:S(2)}) %collective-permute-start.3) | collective-permute-done | bytes 495648 | tf_op jit(solution)/shard_map/ppermute | solution.py:40
  16.4 1.5 %peer_products_0.1 = (f32[4,80,128]{2,1,0:T(8,128)S(1)}, s32[168,128]{1,0:T(8,128)S(1)}, s32[168,128]{1,0:T(8,128)S(1)}, s32[168,128]{1,0:T(8,128)S(1)}, s32[1,8,128]{2,1,0:T(8,128)S(1)}) custom-call(s32[16,128]{1,0:T(8,128)S(1)} %get-tuple-element.22.known.refs_0_, s32[8,128]{1,0:T(8,128)S(1)} %get-tuple-element.26.refs_1_, ...), custom_call_target="tpu_custom_call" | custom-call | flops 31457280 | bytes 1703936 | tf_op jit(solution)/shard_map/peer_products_0/pallas_call | solution.py:342
  17.9 2.2 %collective-permute-start.4 = (s32[168,128]{1,0:T(8,128)S(1)}, s32[168,128]{1,0:T(8,128)S(1)}, u32[]{:S(2)}, u32[]{:S(2)}) collective-permute-start(s32[168,128]{1,0:T(8,128)S(1)} %get-tuple-element.30), channel_id=1, source_target_pairs={{3,0},{0,1},{1,2},{2,3},{7,4},{4,5},{5,6},{6,7},{11,8},{8,9},{9,10... | collective-permute-start | bytes 258056 | tf_op jit(solution)/shard_map/ppermute | solution.py:40
  20.1 2.6 %collective-permute-start.5 = (s32[168,128]{1,0:T(8,128)S(1)}, s32[168,128]{1,0:T(8,128)S(1)}, u32[]{:S(2)}, u32[]{:S(2)}) collective-permute-start(s32[168,128]{1,0:T(8,128)S(1)} %get-tuple-element.31), channel_id=1, source_target_pairs={{2,0},{3,1},{0,2},{1,3},{6,4},{7,5},{4,6},{5,7},{10,8},{11,9},{8,1... | collective-permute-start | bytes 258056 | tf_op jit(solution)/shard_map/ppermute | solution.py:40
  22.7 1.3 %collective-permute-start.6 = (s32[168,128]{1,0:T(8,128)S(1)}, s32[168,128]{1,0:T(8,128)S(1)}, u32[]{:S(2)}, u32[]{:S(2)}) collective-permute-start(s32[168,128]{1,0:T(8,128)S(1)} %get-tuple-element.32), channel_id=1, source_target_pairs={{1,0},{2,1},{3,2},{0,3},{5,4},{6,5},{7,6},{4,7},{9,8},{10,9},{11,1... | collective-permute-start | bytes 258056 | tf_op jit(solution)/shard_map/ppermute | solution.py:40
  24.1 0.0 collective-permute-done.7.refs_1_
  24.1 1.3 %peer_products_80.1 = (f32[4,48,128]{2,1,0:T(8,128)S(1)}, s32[104,128]{1,0:T(8,128)S(1)}, s32[104,128]{1,0:T(8,128)S(1)}, s32[104,128]{1,0:T(8,128)S(1)}) custom-call(s32[1,8,128]{2,1,0:T(8,128)S(1)} %get-tuple-element.33.refs_0_, bf16[1152,128]{1,0:T(8,128)(2,1)S(1)} %collective-permute-done.7.refs_1_, ...), custom_call_target="tpu_custom_call" | custom-call | flops 18874368 | bytes 1703936 | tf_op jit(solution)/shard_map/peer_products_80/pallas_call | solution.py:342
  25.4 1.8 %collective-permute-start.10 = (s32[104,128]{1,0:T(8,128)S(1)}, s32[104,128]{1,0:T(8,128)S(1)}, u32[]{:S(2)}, u32[]{:S(2)}) collective-permute-start(s32[104,128]{1,0:T(8,128)S(1)} %get-tuple-element.38), channel_id=1, source_target_pairs={{1,0},{2,1},{3,2},{0,3},{5,4},{6,5},{7,6},{4,7},{9,8},{10,9},{11,1... | collective-permute-start | bytes 159752 | tf_op jit(solution)/shard_map/ppermute | solution.py:40
  27.1 0.3 collective-permute-start.8
  27.5 0.0 collective-permute-done.4.refs_1_
  27.5 0.7 %collective-permute-start.9 = (s32[104,128]{1,0:T(8,128)S(1)}, s32[104,128]{1,0:T(8,128)S(1)}, u32[]{:S(2)}, u32[]{:S(2)}) collective-permute-start(s32[104,128]{1,0:T(8,128)S(1)} %get-tuple-element.37), channel_id=1, source_target_pairs={{2,0},{3,1},{0,2},{1,3},{6,4},{7,5},{4,6},{5,7},{10,8},{11,9},{8,1... | collective-permute-start | bytes 159752 | tf_op jit(solution)/shard_map/ppermute | solution.py:40
  28.2 0.0 collective-permute-done.5.refs_2_
  28.2 0.0 collective-permute-done.6.refs_3_
  28.2 0.1 finish_0.1.refs_0_
  28.3 1.6 %collective-permute-done.10.refs_4_ = s32[104,128]{1,0:T(8,128)S(1)} collective-permute-done((s32[104,128]{1,0:T(8,128)S(1)}, s32[104,128]{1,0:T(8,128)S(1)}, u32[]{:S(2)}, u32[]{:S(2)}) %collective-permute-start.10) | collective-permute-done | bytes 53280 | tf_op jit(solution)/shard_map/ppermute | solution.py:40
  29.8 3.2 %collective-permute-done.8.refs_2_ = s32[104,128]{1,0:T(8,128)S(1)} collective-permute-done((s32[104,128]{1,0:T(8,128)S(1)}, s32[104,128]{1,0:T(8,128)S(1)}, u32[]{:S(2)}, u32[]{:S(2)}) %collective-permute-start.8) | collective-permute-done | bytes 53280 | tf_op jit(solution)/shard_map/ppermute | solution.py:40
  33.1 0.0 collective-permute-done.9.refs_3_
  33.1 0.7 %finish_80.1 = bf16[2,2,128,128]{3,2,1,0:T(8,128)(2,1)} custom-call(bf16[2,2,80,128]{3,2,1,0:T(8,128)(2,1)S(1)} %finish_0.1.refs_0_, f32[4,48,128]{2,1,0:T(8,128)S(1)} %get-tuple-element.35.refs_1_, s32[104,128]{1,0:T(8,128)S(1)} %collective-permute-done.8.refs_2_, s32[104,128]{1,0:T(8,128)S(1)} %collective-permute-done.9.refs_3_, ...), custom_call_target="tpu_custom_call" | custom-call | tf_op jit(solution)/shard_map/finish_80/pallas_call | solution.py:366
Async XLA Ops:
  1.3 15.1 %collective-permute-start.3 = (bf16[1936,128]{1,0:T(8,128)(2,1)S(1)}, bf16[1936,128]{1,0:T(8,128)(2,1)S(1)}, u32[]{:S(2)}, u32[]{:S(2)}) collective-permute-start(bf16[1936,128]{1,0:T(8,128)(2,1)S(1)} %get-tuple-element.23.refs_0_), channel_id=1, source_target_pairs={{4,0},{0,4},{5,1},{1,5},{6,2},{2,6},{7,3},{3,7},{12,8},{8,12},{13,... | collective-permute-start | bytes 1486856 | tf_op jit(solution)/shard_map/ppermute | solution.py:40
  4.3 5.0 %collective-permute-start.1 = (bf16[528,128]{1,0:T(8,128)(2,1)S(1)}, bf16[528,128]{1,0:T(8,128)(2,1)S(1)}, u32[]{:S(2)}, u32[]{:S(2)}) collective-permute-start(bf16[528,128]{1,0:T(8,128)(2,1)S(1)} %get-tuple-element.25.refs_2_), channel_id=1, source_target_pairs={{0,16},{8,24},{16,0},{24,8},{1,17},{9,25},{17,1},{25,9},{2,18},{10... | collective-permute-start | bytes 405512 | tf_op jit(solution)/shard_map/ppermute | solution.py:26
  5.8 3.5 %collective-permute-start = (bf16[528,128]{1,0:T(8,128)(2,1)S(1)}, bf16[528,128]{1,0:T(8,128)(2,1)S(1)}, u32[]{:S(2)}, u32[]{:S(2)}) collective-permute-start(bf16[528,128]{1,0:T(8,128)(2,1)S(1)} %get-tuple-element.25.refs_2_), channel_id=1, source_target_pairs={{0,8},{8,0},{16,24},{24,16},{1,9},{9,1},{17,25},{25,17},{2,10},{10... | collective-permute-start | bytes 405512 | tf_op jit(solution)/shard_map/ppermute | solution.py:26
  9.3 1.4 %collective-permute-start.2 = (bf16[528,128]{1,0:T(8,128)(2,1)S(1)}, bf16[528,128]{1,0:T(8,128)(2,1)S(1)}, u32[]{:S(2)}, u32[]{:S(2)}) collective-permute-start(bf16[528,128]{1,0:T(8,128)(2,1)S(1)} %collective-permute-done.1.refs_4_), channel_id=1, source_target_pairs={{0,8},{8,0},{16,24},{24,16},{1,9},{9,1},{17,25},{25,17},{2,10},{10... | collective-permute-start | bytes 405512 | tf_op jit(solution)/shard_map/ppermute | solution.py:26
  10.7 13.4 %collective-permute-start.7 = (bf16[1152,128]{1,0:T(8,128)(2,1)S(1)}, bf16[1152,128]{1,0:T(8,128)(2,1)S(1)}, u32[]{:S(2)}, u32[]{:S(2)}) collective-permute-start(bf16[1152,128]{1,0:T(8,128)(2,1)S(1)} %get-tuple-element.34.refs_1_), channel_id=1, source_target_pairs={{4,0},{0,4},{5,1},{1,5},{6,2},{2,6},{7,3},{3,7},{12,8},{8,12},{13,... | collective-permute-start | bytes 884744 | tf_op jit(solution)/shard_map/ppermute | solution.py:40
  17.9 9.5 %collective-permute-start.4 = (s32[168,128]{1,0:T(8,128)S(1)}, s32[168,128]{1,0:T(8,128)S(1)}, u32[]{:S(2)}, u32[]{:S(2)}) collective-permute-start(s32[168,128]{1,0:T(8,128)S(1)} %get-tuple-element.30), channel_id=1, source_target_pairs={{3,0},{0,1},{1,2},{2,3},{7,4},{4,5},{5,6},{6,7},{11,8},{8,9},{9,10... | collective-permute-start | bytes 258056 | tf_op jit(solution)/shard_map/ppermute | solution.py:40
  20.1 8.0 %collective-permute-start.5 = (s32[168,128]{1,0:T(8,128)S(1)}, s32[168,128]{1,0:T(8,128)S(1)}, u32[]{:S(2)}, u32[]{:S(2)}) collective-permute-start(s32[168,128]{1,0:T(8,128)S(1)} %get-tuple-element.31), channel_id=1, source_target_pairs={{2,0},{3,1},{0,2},{1,3},{6,4},{7,5},{4,6},{5,7},{10,8},{11,9},{8,1... | collective-permute-start | bytes 258056 | tf_op jit(solution)/shard_map/ppermute | solution.py:40
  22.7 5.4 %collective-permute-start.6 = (s32[168,128]{1,0:T(8,128)S(1)}, s32[168,128]{1,0:T(8,128)S(1)}, u32[]{:S(2)}, u32[]{:S(2)}) collective-permute-start(s32[168,128]{1,0:T(8,128)S(1)} %get-tuple-element.32), channel_id=1, source_target_pairs={{1,0},{2,1},{3,2},{0,3},{5,4},{6,5},{7,6},{4,7},{9,8},{10,9},{11,1... | collective-permute-start | bytes 258056 | tf_op jit(solution)/shard_map/ppermute | solution.py:40
  25.4 4.4 %collective-permute-start.10 = (s32[104,128]{1,0:T(8,128)S(1)}, s32[104,128]{1,0:T(8,128)S(1)}, u32[]{:S(2)}, u32[]{:S(2)}) collective-permute-start(s32[104,128]{1,0:T(8,128)S(1)} %get-tuple-element.38), channel_id=1, source_target_pairs={{1,0},{2,1},{3,2},{0,3},{5,4},{6,5},{7,6},{4,7},{9,8},{10,9},{11,1... | collective-permute-start | bytes 159752 | tf_op jit(solution)/shard_map/ppermute | solution.py:40
  27.1 5.9 %collective-permute-start.8 = (s32[104,128]{1,0:T(8,128)S(1)}, s32[104,128]{1,0:T(8,128)S(1)}, u32[]{:S(2)}, u32[]{:S(2)}) collective-permute-start(s32[104,128]{1,0:T(8,128)S(1)} %get-tuple-element.36), channel_id=1, source_target_pairs={{3,0},{0,1},{1,2},{2,3},{7,4},{4,5},{5,6},{6,7},{11,8},{8,9},{9,10... | collective-permute-start | bytes 159752 | tf_op jit(solution)/shard_map/ppermute | solution.py:40
  27.5 5.6 %collective-permute-start.9 = (s32[104,128]{1,0:T(8,128)S(1)}, s32[104,128]{1,0:T(8,128)S(1)}, u32[]{:S(2)}, u32[]{:S(2)}) collective-permute-start(s32[104,128]{1,0:T(8,128)S(1)} %get-tuple-element.37), channel_id=1, source_target_pairs={{2,0},{3,1},{0,2},{1,3},{6,4},{7,5},{4,6},{5,7},{10,8},{11,9},{8,1... | collective-permute-start | bytes 159752 | tf_op jit(solution)/shard_map/ppermute | solution.py:40

commit v13 on v12

--- a/solution.py
+++ b/solution.py
@@ -7,7 +7,7 @@
 from jax.experimental.pallas import tpu as pltpu
 from jax.sharding import PartitionSpec as P
 
-GROUP = 4
+GROUP = 8
 LANES = 128
 MIB = 2**20
 HBM = pltpu.MemorySpace.HBM
@@ -214,23 +214,25 @@
 
     own[...] = totals[:slots]
     half = height // 2
+    sublane = lax.broadcasted_iota(jnp.int32, (8, totals.shape[2]), 0)
     for d in range(1, layers):
         code = sent[d - 1]
-        spare = code.shape[0] - slots * half
-        code[slots * half :] = jnp.zeros((spare, code.shape[1]), jnp.int32)
         for u in range(slots):
             value = totals[d * slots + u]
             peak = jnp.max(jnp.abs(value), axis=0, keepdims=True)
             power = jnp.floor(jnp.log2(jnp.maximum(peak, 1e-30)) + 1e-3) + 1.0
-            word = jnp.floor(value * jnp.exp2(15.0 - power) + 0.5).astype(jnp.int32)
-            code[pl.ds(u * half, half)] = (word[:half] << 16) | (word[half:] & 0xFFFF)
-            code[pl.ds(slots * half + u, 1)] = power.astype(jnp.int32)
+            whole = jnp.floor(value * jnp.exp2(15.0 - power) + 0.5).astype(jnp.int32)
+            word = (whole[:half] << 16) | (whole[half:] & 0xFFFF)
+            bits = ((power.astype(jnp.int32) + 128) >> sublane) & 1
+            code[pl.ds(u * half, 8)] = (word[:8] & ~1) | bits
+            code[pl.ds(u * half + 8, half - 8)] = word[8:]
 
 
 def finish_kernel(sizes, span, *refs):
     layers, slots = sizes
     first, height = span
     half = height // 2
+    sublane = lax.broadcasted_iota(jnp.int32, (8, refs[-1].shape[3]), 0)
     before, own, codes, result = refs[: first > 0], refs[-layers - 1], refs[-layers:-1], refs[-1]
     kept = result.shape[1]
     for done in before:
@@ -239,8 +241,8 @@
         high, low = own[u, :half], own[u, half:]
         for code in codes:
             word = code[pl.ds(u * half, half)]
-            power = code[pl.ds(slots * half + u, 1)].astype(jnp.float32)
-            scale = jnp.exp2(power - 15.0)
+            power = jnp.sum((word[:8] & 1) << sublane, axis=0, keepdims=True).astype(jnp.float32)
+            scale = jnp.exp2(power - (128.0 + 15.0))
             high += (word >> 16).astype(jnp.float32) * scale
             low += ((word << 16) >> 16).astype(jnp.float32) * scale
         result[u // kept, u % kept, first : first + half] = high.astype(jnp.bfloat16)
@@ -333,7 +335,7 @@
     code_shape = (cols - 1, code_height, LANES)
     finished, plan = [], []
     for (at, height), pieces in zip(ranges, x_pieces):
-        code_rows = slots * (height // 2) + (slots + 7) // 8 * 8
+        code_rows = slots * (height // 2)
         out_shape = [jax.ShapeDtypeStruct((slots, height, order), jnp.float32)]
         out_shape += [jax.ShapeDtypeStruct((code_rows, order), jnp.int32)] * (layers - 1)
         if at == 0:

time: 33.9 us -> 33.8 us (level)
  Pallas kernels: 6.61 us -> 6.12 us
  transfers between devices with their start and end apart: 11 -> 11, of which waited for: 5 -> 5; matrix products, arithmetic and copies ran while one was open for 0% -> 0% of each run, Pallas kernels for 14% -> 12%
where the time goes in v13:
time: 33.8 us; the launch traced here: 33.6 us
  starting transfers between devices  13.9 us (41%)
  waiting for transfers between devices  13.6 us (40%)
  Pallas kernels  6.12 us (18%)
    ppermute x8, starting transfers between devices, shifted(): lax.ppermute(value, axis, [((i + offset) % size, i) for i in range(size)])  12.4 us
    ppermute x8, waiting for transfers between devices, shifted(): lax.ppermute(value, axis, [((i + offset) % size, i) for i in range(size)])  8.7 us
    ppermute x3, waiting for transfers between devices, flipped(): lax.ppermute(value, axis, [(i, i ^ bits) for i in range(lax.axis_size(axi...  4.87 us
    pallas_call x2, Pallas kernels, per_device(): pl.pallas_call(functools.partial(peer_kernel, (cols, layers, count, width...  2.58 us
    ppermute x3, starting transfers between devices, flipped(): lax.ppermute(value, axis, [(i, i ^ bits) for i in range(lax.axis_size(axi...  1.52 us
    pallas_call x1, Pallas kernels, per_device(): pl.pallas_call(functools.partial(own_kernel, (rows, count, piece_rows, wi...  1.45 us
    pallas_call x1, Pallas kernels, per_device(): pl.pallas_call(functools.partial(pack_kernel, (layers, count, piece_rows,...  1.27 us
    pallas_call x2, Pallas kernels, per_device(): pl.pallas_call(functools.partial(finish_kernel, (layers, slots), (at, hei...  0.83 us
  transfers between devices with their start and end apart: 11, of which 5 were waited for; matrix products, arithmetic and copies ran while one was open for 0% of the time, Pallas kernels for 12%

profile of v13, /device:TPU:0, one launch (start us, length us, event | category | flops | bytes accessed | tf_op | source)
XLA Modules:
  0.0 33.6 jit_solution(1651558791198622093)
XLA Ops:
  0.0 1.3 %pack.1 = (s32[16,128]{1,0:T(8,128)S(1)}, bf16[528,128]{1,0:T(8,128)(2,1)S(1)}, bf16[1936,128]{1,0:T(8,128)(2,1)S(1)}, bf16[1152,128]{1,0:T(8,128)(2,1)S(1)}) custom-call(s32[1,24]{1,0:T(1,128)} %bitcast.6, s32[1,24]{1,0:T(1,128)} %bitcast.7, s32[2,8]{1,0:T(2,128)} %bitcast.5, bf16[24,128,128]{2,1,0:T(8,128)(2,1)} %x_in.1, s32[2,2]{1,0:T(2,128)} %s_cols.1, ...), custom_call_target="tpu_custom_call" | custom-call | tf_op jit(solution)/shard_map/pack/pallas_call | solution.py:271
  1.3 3.0 %collective-permute-start.3 = (bf16[1936,128]{1,0:T(8,128)(2,1)S(1)}, bf16[1936,128]{1,0:T(8,128)(2,1)S(1)}, u32[]{:S(2)}, u32[]{:S(2)}) collective-permute-start(bf16[1936,128]{1,0:T(8,128)(2,1)S(1)} %get-tuple-element.23.refs_0_), channel_id=1, source_target_pairs={{4,0},{0,4},{5,1},{1,5},{6,2},{2,6},{7,3},{3,7},{12,8},{8,12},{13,... | collective-permute-start | bytes 1486856 | tf_op jit(solution)/shard_map/ppermute | solution.py:40
  4.3 1.5 %collective-permute-start.1 = (bf16[528,128]{1,0:T(8,128)(2,1)S(1)}, bf16[528,128]{1,0:T(8,128)(2,1)S(1)}, u32[]{:S(2)}, u32[]{:S(2)}) collective-permute-start(bf16[528,128]{1,0:T(8,128)(2,1)S(1)} %get-tuple-element.25.refs_2_), channel_id=1, source_target_pairs={{0,16},{8,24},{16,0},{24,8},{1,17},{9,25},{17,1},{25,9},{2,18},{10... | collective-permute-start | bytes 405512 | tf_op jit(solution)/shard_map/ppermute | solution.py:26
  5.8 0.0 collective-permute-start
  5.8 3.5 %collective-permute-done.1.refs_4_ = bf16[528,128]{1,0:T(8,128)(2,1)S(1)} collective-permute-done((bf16[528,128]{1,0:T(8,128)(2,1)S(1)}, bf16[528,128]{1,0:T(8,128)(2,1)S(1)}, u32[]{:S(2)}, u32[]{:S(2)}) %collective-permute-start.1) | collective-permute-done | bytes 135200 | tf_op jit(solution)/shard_map/ppermute | solution.py:26
  9.3 0.0 collective-permute-start.2
  9.3 0.0 collective-permute-done.refs_3_
  9.3 1.3 %collective-permute-done.2.refs_5_ = bf16[528,128]{1,0:T(8,128)(2,1)S(1)} collective-permute-done((bf16[528,128]{1,0:T(8,128)(2,1)S(1)}, bf16[528,128]{1,0:T(8,128)(2,1)S(1)}, u32[]{:S(2)}, u32[]{:S(2)}) %collective-permute-start.2) | collective-permute-done | bytes 135200 | tf_op jit(solution)/shard_map/ppermute | solution.py:26
  10.7 0.4 %collective-permute-start.7 = (bf16[1152,128]{1,0:T(8,128)(2,1)S(1)}, bf16[1152,128]{1,0:T(8,128)(2,1)S(1)}, u32[]{:S(2)}, u32[]{:S(2)}) collective-permute-start(bf16[1152,128]{1,0:T(8,128)(2,1)S(1)} %get-tuple-element.34.refs_1_), channel_id=1, source_target_pairs={{4,0},{0,4},{5,1},{1,5},{6,2},{2,6},{7,3},{3,7},{12,8},{8,12},{13,... | collective-permute-start | bytes 884744 | tf_op jit(solution)/shard_map/ppermute | solution.py:40
  11.0 1.4 %own_products.1 = (f32[17,128,128]{2,1,0:T(8,128)S(1)}, bf16[16,128,128]{2,1,0:T(8,128)(2,1)S(1)}, s32[8,128]{1,0:T(8,128)S(1)}) custom-call(s32[16,128]{1,0:T(8,128)S(1)} %get-tuple-element.22.known.refs_0_, bf16[1936,128]{1,0:T(8,128)(2,1)S(1)} %get-tuple-element.23.refs_0_, bf16[1152,128]{1,0:T(8,128)(2,1)S(1)} %get-tuple-element.34.refs_1_, ...), custom_call_target="tpu_custom_call" | custom-call | flops 50331648 | bytes 2883584 | tf_op jit(solution)/shard_map/own_products/pallas_call | solution.py:310
  12.5 3.9 %collective-permute-done.3.refs_2_ = bf16[1936,128]{1,0:T(8,128)(2,1)S(1)} collective-permute-done((bf16[1936,128]{1,0:T(8,128)(2,1)S(1)}, bf16[1936,128]{1,0:T(8,128)(2,1)S(1)}, u32[]{:S(2)}, u32[]{:S(2)}) %collective-permute-start.3) | collective-permute-done | bytes 495648 | tf_op jit(solution)/shard_map/ppermute | solution.py:40
  16.4 1.4 %peer_products_0.1 = (f32[4,80,128]{2,1,0:T(8,128)S(1)}, s32[160,128]{1,0:T(8,128)S(1)}, s32[160,128]{1,0:T(8,128)S(1)}, s32[160,128]{1,0:T(8,128)S(1)}, s32[1,8,128]{2,1,0:T(8,128)S(1)}) custom-call(s32[16,128]{1,0:T(8,128)S(1)} %get-tuple-element.22.known.refs_0_, s32[8,128]{1,0:T(8,128)S(1)} %get-tuple-element.26.refs_1_, ...), custom_call_target="tpu_custom_call" | custom-call | flops 31457280 | bytes 1703936 | tf_op jit(solution)/shard_map/peer_products_0/pallas_call | solution.py:344
  17.8 2.2 %collective-permute-start.4 = (s32[160,128]{1,0:T(8,128)S(1)}, s32[160,128]{1,0:T(8,128)S(1)}, u32[]{:S(2)}, u32[]{:S(2)}) collective-permute-start(s32[160,128]{1,0:T(8,128)S(1)} %get-tuple-element.30), channel_id=1, source_target_pairs={{3,0},{0,1},{1,2},{2,3},{7,4},{4,5},{5,6},{6,7},{11,8},{8,9},{9,10... | collective-permute-start | bytes 245768 | tf_op jit(solution)/shard_map/ppermute | solution.py:40
  20.0 2.6 %collective-permute-start.5 = (s32[160,128]{1,0:T(8,128)S(1)}, s32[160,128]{1,0:T(8,128)S(1)}, u32[]{:S(2)}, u32[]{:S(2)}) collective-permute-start(s32[160,128]{1,0:T(8,128)S(1)} %get-tuple-element.31), channel_id=1, source_target_pairs={{2,0},{3,1},{0,2},{1,3},{6,4},{7,5},{4,6},{5,7},{10,8},{11,9},{8,1... | collective-permute-start | bytes 245768 | tf_op jit(solution)/shard_map/ppermute | solution.py:40
  22.6 1.3 %collective-permute-start.6 = (s32[160,128]{1,0:T(8,128)S(1)}, s32[160,128]{1,0:T(8,128)S(1)}, u32[]{:S(2)}, u32[]{:S(2)}) collective-permute-start(s32[160,128]{1,0:T(8,128)S(1)} %get-tuple-element.32), channel_id=1, source_target_pairs={{1,0},{2,1},{3,2},{0,3},{5,4},{6,5},{7,6},{4,7},{9,8},{10,9},{11,1... | collective-permute-start | bytes 245768 | tf_op jit(solution)/shard_map/ppermute | solution.py:40
  23.9 0.0 collective-permute-done.7.refs_1_
  23.9 1.2 %peer_products_80.1 = (f32[4,48,128]{2,1,0:T(8,128)S(1)}, s32[96,128]{1,0:T(8,128)S(1)}, s32[96,128]{1,0:T(8,128)S(1)}, s32[96,128]{1,0:T(8,128)S(1)}) custom-call(s32[1,8,128]{2,1,0:T(8,128)S(1)} %get-tuple-element.33.refs_0_, bf16[1152,128]{1,0:T(8,128)(2,1)S(1)} %collective-permute-done.7.refs_1_, ...), custom_call_target="tpu_custom_call" | custom-call | flops 18874368 | bytes 1703936 | tf_op jit(solution)/shard_map/peer_products_80/pallas_call | solution.py:344
  25.1 1.9 %collective-permute-start.10 = (s32[96,128]{1,0:T(8,128)S(1)}, s32[96,128]{1,0:T(8,128)S(1)}, u32[]{:S(2)}, u32[]{:S(2)}) collective-permute-start(s32[96,128]{1,0:T(8,128)S(1)} %get-tuple-element.38), channel_id=1, source_target_pairs={{1,0},{2,1},{3,2},{0,3},{5,4},{6,5},{7,6},{4,7},{9,8},{10,9},{11,1... | collective-permute-start | bytes 147464 | tf_op jit(solution)/shard_map/ppermute | solution.py:40
  27.0 0.2 collective-permute-start.8
  27.2 0.0 collective-permute-done.4.refs_1_
  27.2 0.8 %collective-permute-start.9 = (s32[96,128]{1,0:T(8,128)S(1)}, s32[96,128]{1,0:T(8,128)S(1)}, u32[]{:S(2)}, u32[]{:S(2)}) collective-permute-start(s32[96,128]{1,0:T(8,128)S(1)} %get-tuple-element.37), channel_id=1, source_target_pairs={{2,0},{3,1},{0,2},{1,3},{6,4},{7,5},{4,6},{5,7},{10,8},{11,9},{8,1... | collective-permute-start | bytes 147464 | tf_op jit(solution)/shard_map/ppermute | solution.py:40
  28.0 0.0 collective-permute-done.5.refs_2_
  28.0 0.0 collective-permute-done.6.refs_3_
  28.0 0.1 finish_0.1.refs_0_
  28.1 1.2 %collective-permute-done.10.refs_4_ = s32[96,128]{1,0:T(8,128)S(1)} collective-permute-done((s32[96,128]{1,0:T(8,128)S(1)}, s32[96,128]{1,0:T(8,128)S(1)}, u32[]{:S(2)}, u32[]{:S(2)}) %collective-permute-start.10) | collective-permute-done | bytes 49184 | tf_op jit(solution)/shard_map/ppermute | solution.py:40
  29.4 3.5 %collective-permute-done.8.refs_2_ = s32[96,128]{1,0:T(8,128)S(1)} collective-permute-done((s32[96,128]{1,0:T(8,128)S(1)}, s32[96,128]{1,0:T(8,128)S(1)}, u32[]{:S(2)}, u32[]{:S(2)}) %collective-permute-start.8) | collective-permute-done | bytes 49184 | tf_op jit(solution)/shard_map/ppermute | solution.py:40
  32.9 0.0 collective-permute-done.9.refs_3_
  32.9 0.7 %finish_80.1 = bf16[2,2,128,128]{3,2,1,0:T(8,128)(2,1)} custom-call(bf16[2,2,80,128]{3,2,1,0:T(8,128)(2,1)S(1)} %finish_0.1.refs_0_, f32[4,48,128]{2,1,0:T(8,128)S(1)} %get-tuple-element.35.refs_1_, s32[96,128]{1,0:T(8,128)S(1)} %collective-permute-done.8.refs_2_, s32[96,128]{1,0:T(8,128)S(1)} %collective-permute-done.9.refs_3_, ...), custom_call_target="tpu_custom_call" | custom-call | tf_op jit(solution)/shard_map/finish_80/pallas_call | solution.py:368
Async XLA Ops:
  1.3 15.1 %collective-permute-start.3 = (bf16[1936,128]{1,0:T(8,128)(2,1)S(1)}, bf16[1936,128]{1,0:T(8,128)(2,1)S(1)}, u32[]{:S(2)}, u32[]{:S(2)}) collective-permute-start(bf16[1936,128]{1,0:T(8,128)(2,1)S(1)} %get-tuple-element.23.refs_0_), channel_id=1, source_target_pairs={{4,0},{0,4},{5,1},{1,5},{6,2},{2,6},{7,3},{3,7},{12,8},{8,12},{13,... | collective-permute-start | bytes 1486856 | tf_op jit(solution)/shard_map/ppermute | solution.py:40
  4.3 5.0 %collective-permute-start.1 = (bf16[528,128]{1,0:T(8,128)(2,1)S(1)}, bf16[528,128]{1,0:T(8,128)(2,1)S(1)}, u32[]{:S(2)}, u32[]{:S(2)}) collective-permute-start(bf16[528,128]{1,0:T(8,128)(2,1)S(1)} %get-tuple-element.25.refs_2_), channel_id=1, source_target_pairs={{0,16},{8,24},{16,0},{24,8},{1,17},{9,25},{17,1},{25,9},{2,18},{10... | collective-permute-start | bytes 405512 | tf_op jit(solution)/shard_map/ppermute | solution.py:26
  5.8 3.5 %collective-permute-start = (bf16[528,128]{1,0:T(8,128)(2,1)S(1)}, bf16[528,128]{1,0:T(8,128)(2,1)S(1)}, u32[]{:S(2)}, u32[]{:S(2)}) collective-permute-start(bf16[528,128]{1,0:T(8,128)(2,1)S(1)} %get-tuple-element.25.refs_2_), channel_id=1, source_target_pairs={{0,8},{8,0},{16,24},{24,16},{1,9},{9,1},{17,25},{25,17},{2,10},{10... | collective-permute-start | bytes 405512 | tf_op jit(solution)/shard_map/ppermute | solution.py:26
  9.3 1.4 %collective-permute-start.2 = (bf16[528,128]{1,0:T(8,128)(2,1)S(1)}, bf16[528,128]{1,0:T(8,128)(2,1)S(1)}, u32[]{:S(2)}, u32[]{:S(2)}) collective-permute-start(bf16[528,128]{1,0:T(8,128)(2,1)S(1)} %collective-permute-done.1.refs_4_), channel_id=1, source_target_pairs={{0,8},{8,0},{16,24},{24,16},{1,9},{9,1},{17,25},{25,17},{2,10},{10... | collective-permute-start | bytes 405512 | tf_op jit(solution)/shard_map/ppermute | solution.py:26
  10.7 13.3 %collective-permute-start.7 = (bf16[1152,128]{1,0:T(8,128)(2,1)S(1)}, bf16[1152,128]{1,0:T(8,128)(2,1)S(1)}, u32[]{:S(2)}, u32[]{:S(2)}) collective-permute-start(bf16[1152,128]{1,0:T(8,128)(2,1)S(1)} %get-tuple-element.34.refs_1_), channel_id=1, source_target_pairs={{4,0},{0,4},{5,1},{1,5},{6,2},{2,6},{7,3},{3,7},{12,8},{8,12},{13,... | collective-permute-start | bytes 884744 | tf_op jit(solution)/shard_map/ppermute | solution.py:40
  17.8 9.4 %collective-permute-start.4 = (s32[160,128]{1,0:T(8,128)S(1)}, s32[160,128]{1,0:T(8,128)S(1)}, u32[]{:S(2)}, u32[]{:S(2)}) collective-permute-start(s32[160,128]{1,0:T(8,128)S(1)} %get-tuple-element.30), channel_id=1, source_target_pairs={{3,0},{0,1},{1,2},{2,3},{7,4},{4,5},{5,6},{6,7},{11,8},{8,9},{9,10... | collective-permute-start | bytes 245768 | tf_op jit(solution)/shard_map/ppermute | solution.py:40
  20.0 8.0 %collective-permute-start.5 = (s32[160,128]{1,0:T(8,128)S(1)}, s32[160,128]{1,0:T(8,128)S(1)}, u32[]{:S(2)}, u32[]{:S(2)}) collective-permute-start(s32[160,128]{1,0:T(8,128)S(1)} %get-tuple-element.31), channel_id=1, source_target_pairs={{2,0},{3,1},{0,2},{1,3},{6,4},{7,5},{4,6},{5,7},{10,8},{11,9},{8,1... | collective-permute-start | bytes 245768 | tf_op jit(solution)/shard_map/ppermute | solution.py:40
  22.6 5.5 %collective-permute-start.6 = (s32[160,128]{1,0:T(8,128)S(1)}, s32[160,128]{1,0:T(8,128)S(1)}, u32[]{:S(2)}, u32[]{:S(2)}) collective-permute-start(s32[160,128]{1,0:T(8,128)S(1)} %get-tuple-element.32), channel_id=1, source_target_pairs={{1,0},{2,1},{3,2},{0,3},{5,4},{6,5},{7,6},{4,7},{9,8},{10,9},{11,1... | collective-permute-start | bytes 245768 | tf_op jit(solution)/shard_map/ppermute | solution.py:40
  25.1 4.2 %collective-permute-start.10 = (s32[96,128]{1,0:T(8,128)S(1)}, s32[96,128]{1,0:T(8,128)S(1)}, u32[]{:S(2)}, u32[]{:S(2)}) collective-permute-start(s32[96,128]{1,0:T(8,128)S(1)} %get-tuple-element.38), channel_id=1, source_target_pairs={{1,0},{2,1},{3,2},{0,3},{5,4},{6,5},{7,6},{4,7},{9,8},{10,9},{11,1... | collective-permute-start | bytes 147464 | tf_op jit(solution)/shard_map/ppermute | solution.py:40
  27.0 5.9 %collective-permute-start.8 = (s32[96,128]{1,0:T(8,128)S(1)}, s32[96,128]{1,0:T(8,128)S(1)}, u32[]{:S(2)}, u32[]{:S(2)}) collective-permute-start(s32[96,128]{1,0:T(8,128)S(1)} %get-tuple-element.36), channel_id=1, source_target_pairs={{3,0},{0,1},{1,2},{2,3},{7,4},{4,5},{5,6},{6,7},{11,8},{8,9},{9,10... | collective-permute-start | bytes 147464 | tf_op jit(solution)/shard_map/ppermute | solution.py:40
  27.2 5.7 %collective-permute-start.9 = (s32[96,128]{1,0:T(8,128)S(1)}, s32[96,128]{1,0:T(8,128)S(1)}, u32[]{:S(2)}, u32[]{:S(2)}) collective-permute-start(s32[96,128]{1,0:T(8,128)S(1)} %get-tuple-element.37), channel_id=1, source_target_pairs={{2,0},{3,1},{0,2},{1,3},{6,4},{7,5},{4,6},{5,7},{10,8},{11,9},{8,1... | collective-permute-start | bytes 147464 | tf_op jit(solution)/shard_map/ppermute | solution.py:40

commit v14 on v13

--- a/solution.py
+++ b/solution.py
@@ -85,7 +85,7 @@
     layer = remainder(quotient(col[:, :1], piece_rows), layers)
     owner = quotient(col, piece_rows * layers)
     local = row - here * local_rows
-    goal = remainder(quotient(local, own_rows) - layer + layers, layers) * own_rows
+    goal = (quotient(local, own_rows) ^ layer) * own_rows
     place = (
         ((owner ^ here) * piece_rows + remainder(col, piece_rows)) * width,
         (goal + remainder(local, own_rows)) * kept,
@@ -363,7 +363,8 @@
             name=f"peer_products_{at}",
         )(*given, *pieces, panel, totals)
         plan = plan or out[layers:]
-        codes = [shifted(out[d], "layer", layers - d) for d in range(1, layers)]
+        turn = range(layers - 1, 0, -1) if at == 0 else [*range(layers - 2, 0, -1), layers - 1]
+        codes = [flipped(out[d], "layer", d) for d in turn]
         finished = [
             pl.pallas_call(
                 functools.partial(finish_kernel, (layers, slots), (at, height)),

time: 33.8 us -> 33.6 us (level)
  waiting for transfers between devices: 13.6 us -> 13 us
    ppermute x3 -> x9, starting transfers between devices: 1.52 us -> 10.9 us  [flipped(): lax.ppermute(value, axis, [(i, i ^ bits) for i in range(lax.axis_size(axi...]
    ppermute x8 -> x2, starting transfers between devices: 12.4 us -> 3.36 us  [shifted(): lax.ppermute(value, axis, [((i + offset) % size, i) for i in range(size)])]
    ppermute x8 -> x2, waiting for transfers between devices: 8.7 us -> 3.93 us  [shifted(): lax.ppermute(value, axis, [((i + offset) % size, i) for i in range(size)])]
    ppermute x3 -> x9, waiting for transfers between devices: 4.87 us -> 9.11 us  [flipped(): lax.ppermute(value, axis, [(i, i ^ bits) for i in range(lax.axis_size(axi...]
  transfers between devices with their start and end apart: 11 -> 11, of which waited for: 5 -> 6; matrix products, arithmetic and copies ran while one was open for 0% -> 0% of each run, Pallas kernels for 12% -> 12%
where the time goes in v14:
time: 33.6 us; the launch traced here: 33.4 us
  starting transfers between devices  14.2 us (42%)
  waiting for transfers between devices  13 us (39%)
  Pallas kernels  6.11 us (18%)
    ppermute x9, starting transfers between devices, flipped(): lax.ppermute(value, axis, [(i, i ^ bits) for i in range(lax.axis_size(axi...  10.9 us
    ppermute x9, waiting for transfers between devices, flipped(): lax.ppermute(value, axis, [(i, i ^ bits) for i in range(lax.axis_size(axi...  9.11 us
    ppermute x2, waiting for transfers between devices, shifted(): lax.ppermute(value, axis, [((i + offset) % size, i) for i in range(size)])  3.93 us
    ppermute x2, starting transfers between devices, shifted(): lax.ppermute(value, axis, [((i + offset) % size, i) for i in range(size)])  3.36 us
    pallas_call x2, Pallas kernels, per_device(): pl.pallas_call(functools.partial(peer_kernel, (cols, layers, count, width...  2.58 us
    pallas_call x1, Pallas kernels, per_device(): pl.pallas_call(functools.partial(own_kernel, (rows, count, piece_rows, wi...  1.44 us
    pallas_call x1, Pallas kernels, per_device(): pl.pallas_call(functools.partial(pack_kernel, (layers, count, piece_rows,...  1.27 us
    pallas_call x2, Pallas kernels, per_device(): pl.pallas_call(functools.partial(finish_kernel, (layers, slots), (at, hei...  0.83 us
  transfers between devices with their start and end apart: 11, of which 6 were waited for; matrix products, arithmetic and copies ran while one was open for 0% of the time, Pallas kernels for 12%

profile of v14, /device:TPU:0, one launch (start us, length us, event | category | flops | bytes accessed | tf_op | source)
XLA Modules:
  0.0 33.4 jit_solution(17732636902854522557)
XLA Ops:
  0.0 1.3 %pack.1 = (s32[16,128]{1,0:T(8,128)S(1)}, bf16[528,128]{1,0:T(8,128)(2,1)S(1)}, bf16[1936,128]{1,0:T(8,128)(2,1)S(1)}, bf16[1152,128]{1,0:T(8,128)(2,1)S(1)}) custom-call(s32[1,24]{1,0:T(1,128)} %bitcast.6, s32[1,24]{1,0:T(1,128)} %bitcast.7, s32[2,8]{1,0:T(2,128)} %bitcast.5, bf16[24,128,128]{2,1,0:T(8,128)(2,1)} %x_in.1, s32[2,2]{1,0:T(2,128)} %s_cols.1, ...), custom_call_target="tpu_custom_call" | custom-call | tf_op jit(solution)/shard_map/pack/pallas_call | solution.py:271
  1.3 3.0 %collective-permute-start.3 = (bf16[1936,128]{1,0:T(8,128)(2,1)S(1)}, bf16[1936,128]{1,0:T(8,128)(2,1)S(1)}, u32[]{:S(2)}, u32[]{:S(2)}) collective-permute-start(bf16[1936,128]{1,0:T(8,128)(2,1)S(1)} %get-tuple-element.23.refs_0_), channel_id=1, source_target_pairs={{4,0},{0,4},{5,1},{1,5},{6,2},{2,6},{7,3},{3,7},{12,8},{8,12},{13,... | collective-permute-start | bytes 1486856 | tf_op jit(solution)/shard_map/ppermute | solution.py:40
  4.3 1.5 %collective-permute-start.1 = (bf16[528,128]{1,0:T(8,128)(2,1)S(1)}, bf16[528,128]{1,0:T(8,128)(2,1)S(1)}, u32[]{:S(2)}, u32[]{:S(2)}) collective-permute-start(bf16[528,128]{1,0:T(8,128)(2,1)S(1)} %get-tuple-element.25.refs_2_), channel_id=1, source_target_pairs={{0,16},{8,24},{16,0},{24,8},{1,17},{9,25},{17,1},{25,9},{2,18},{10... | collective-permute-start | bytes 405512 | tf_op jit(solution)/shard_map/ppermute | solution.py:26
  5.8 0.0 collective-permute-start
  5.8 3.5 %collective-permute-done.1.refs_4_ = bf16[528,128]{1,0:T(8,128)(2,1)S(1)} collective-permute-done((bf16[528,128]{1,0:T(8,128)(2,1)S(1)}, bf16[528,128]{1,0:T(8,128)(2,1)S(1)}, u32[]{:S(2)}, u32[]{:S(2)}) %collective-permute-start.1) | collective-permute-done | bytes 135200 | tf_op jit(solution)/shard_map/ppermute | solution.py:26
  9.3 0.0 collective-permute-start.2
  9.3 0.0 collective-permute-done.refs_3_
  9.3 1.3 %collective-permute-done.2.refs_5_ = bf16[528,128]{1,0:T(8,128)(2,1)S(1)} collective-permute-done((bf16[528,128]{1,0:T(8,128)(2,1)S(1)}, bf16[528,128]{1,0:T(8,128)(2,1)S(1)}, u32[]{:S(2)}, u32[]{:S(2)}) %collective-permute-start.2) | collective-permute-done | bytes 135200 | tf_op jit(solution)/shard_map/ppermute | solution.py:26
  10.7 0.4 %collective-permute-start.7 = (bf16[1152,128]{1,0:T(8,128)(2,1)S(1)}, bf16[1152,128]{1,0:T(8,128)(2,1)S(1)}, u32[]{:S(2)}, u32[]{:S(2)}) collective-permute-start(bf16[1152,128]{1,0:T(8,128)(2,1)S(1)} %get-tuple-element.34.refs_1_), channel_id=1, source_target_pairs={{4,0},{0,4},{5,1},{1,5},{6,2},{2,6},{7,3},{3,7},{12,8},{8,12},{13,... | collective-permute-start | bytes 884744 | tf_op jit(solution)/shard_map/ppermute | solution.py:40
  11.0 1.4 %own_products.1 = (f32[17,128,128]{2,1,0:T(8,128)S(1)}, bf16[16,128,128]{2,1,0:T(8,128)(2,1)S(1)}, s32[8,128]{1,0:T(8,128)S(1)}) custom-call(s32[16,128]{1,0:T(8,128)S(1)} %get-tuple-element.22.known.refs_0_, bf16[1936,128]{1,0:T(8,128)(2,1)S(1)} %get-tuple-element.23.refs_0_, bf16[1152,128]{1,0:T(8,128)(2,1)S(1)} %get-tuple-element.34.refs_1_, ...), custom_call_target="tpu_custom_call" | custom-call | flops 50331648 | bytes 2883584 | tf_op jit(solution)/shard_map/own_products/pallas_call | solution.py:310
  12.5 3.9 %collective-permute-done.3.refs_2_ = bf16[1936,128]{1,0:T(8,128)(2,1)S(1)} collective-permute-done((bf16[1936,128]{1,0:T(8,128)(2,1)S(1)}, bf16[1936,128]{1,0:T(8,128)(2,1)S(1)}, u32[]{:S(2)}, u32[]{:S(2)}) %collective-permute-start.3) | collective-permute-done | bytes 495648 | tf_op jit(solution)/shard_map/ppermute | solution.py:40
  16.4 1.4 %peer_products_0.1 = (f32[4,80,128]{2,1,0:T(8,128)S(1)}, s32[160,128]{1,0:T(8,128)S(1)}, s32[160,128]{1,0:T(8,128)S(1)}, s32[160,128]{1,0:T(8,128)S(1)}, s32[1,8,128]{2,1,0:T(8,128)S(1)}) custom-call(s32[16,128]{1,0:T(8,128)S(1)} %get-tuple-element.22.known.refs_0_, s32[8,128]{1,0:T(8,128)S(1)} %get-tuple-element.26.refs_1_, ...), custom_call_target="tpu_custom_call" | custom-call | flops 31457280 | bytes 1703936 | tf_op jit(solution)/shard_map/peer_products_0/pallas_call | solution.py:344
  17.8 4.2 %collective-permute-start.4 = (s32[160,128]{1,0:T(8,128)S(1)}, s32[160,128]{1,0:T(8,128)S(1)}, u32[]{:S(2)}, u32[]{:S(2)}) collective-permute-start(s32[160,128]{1,0:T(8,128)S(1)} %get-tuple-element.30), channel_id=1, source_target_pairs={{0,3},{1,2},{2,1},{3,0},{4,7},{5,6},{6,5},{7,4},{8,11},{9,10},{10,... | collective-permute-start | bytes 245768 | tf_op jit(solution)/shard_map/ppermute | solution.py:26
  22.0 0.0 collective-permute-start.5
  22.0 0.6 %collective-permute-start.6 = (s32[160,128]{1,0:T(8,128)S(1)}, s32[160,128]{1,0:T(8,128)S(1)}, u32[]{:S(2)}, u32[]{:S(2)}) collective-permute-start(s32[160,128]{1,0:T(8,128)S(1)} %get-tuple-element.32), channel_id=1, source_target_pairs={{0,1},{1,0},{2,3},{3,2},{4,5},{5,4},{6,7},{7,6},{8,9},{9,8},{10,11... | collective-permute-start | bytes 245768 | tf_op jit(solution)/shard_map/ppermute | solution.py:26
  22.7 0.0 collective-permute-done.7.refs_1_
  22.7 1.2 %peer_products_80.1 = (f32[4,48,128]{2,1,0:T(8,128)S(1)}, s32[96,128]{1,0:T(8,128)S(1)}, s32[96,128]{1,0:T(8,128)S(1)}, s32[96,128]{1,0:T(8,128)S(1)}) custom-call(s32[1,8,128]{2,1,0:T(8,128)S(1)} %get-tuple-element.33.refs_0_, bf16[1152,128]{1,0:T(8,128)(2,1)S(1)} %collective-permute-done.7.refs_1_, ...), custom_call_target="tpu_custom_call" | custom-call | flops 18874368 | bytes 1703936 | tf_op jit(solution)/shard_map/peer_products_80/pallas_call | solution.py:344
  23.9 3.8 %collective-permute-start.10 = (s32[96,128]{1,0:T(8,128)S(1)}, s32[96,128]{1,0:T(8,128)S(1)}, u32[]{:S(2)}, u32[]{:S(2)}) collective-permute-start(s32[96,128]{1,0:T(8,128)S(1)} %get-tuple-element.38), channel_id=1, source_target_pairs={{0,3},{1,2},{2,1},{3,0},{4,7},{5,6},{6,5},{7,4},{8,11},{9,10},{10,... | collective-permute-start | bytes 147464 | tf_op jit(solution)/shard_map/ppermute | solution.py:26
  27.7 0.0 collective-permute-start.8
  27.7 0.0 collective-permute-done.4.refs_1_
  27.7 0.6 %collective-permute-start.9 = (s32[96,128]{1,0:T(8,128)S(1)}, s32[96,128]{1,0:T(8,128)S(1)}, u32[]{:S(2)}, u32[]{:S(2)}) collective-permute-start(s32[96,128]{1,0:T(8,128)S(1)} %get-tuple-element.37), channel_id=1, source_target_pairs={{0,1},{1,0},{2,3},{3,2},{4,5},{5,4},{6,7},{7,6},{8,9},{9,8},{10,11... | collective-permute-start | bytes 147464 | tf_op jit(solution)/shard_map/ppermute | solution.py:26
  28.3 0.5 %collective-permute-done.5.refs_2_ = s32[160,128]{1,0:T(8,128)S(1)} collective-permute-done((s32[160,128]{1,0:T(8,128)S(1)}, s32[160,128]{1,0:T(8,128)S(1)}, u32[]{:S(2)}, u32[]{:S(2)}) %collective-permute-start.5) | collective-permute-done | bytes 81952 | tf_op jit(solution)/shard_map/ppermute | solution.py:26
  28.9 0.0 collective-permute-done.6.refs_3_
  28.9 0.1 finish_0.1.refs_0_
  29.0 1.0 %collective-permute-done.10.refs_4_ = s32[96,128]{1,0:T(8,128)S(1)} collective-permute-done((s32[96,128]{1,0:T(8,128)S(1)}, s32[96,128]{1,0:T(8,128)S(1)}, u32[]{:S(2)}, u32[]{:S(2)}) %collective-permute-start.10) | collective-permute-done | bytes 49184 | tf_op jit(solution)/shard_map/ppermute | solution.py:26
  30.0 2.7 %collective-permute-done.8.refs_2_ = s32[96,128]{1,0:T(8,128)S(1)} collective-permute-done((s32[96,128]{1,0:T(8,128)S(1)}, s32[96,128]{1,0:T(8,128)S(1)}, u32[]{:S(2)}, u32[]{:S(2)}) %collective-permute-start.8) | collective-permute-done | bytes 49184 | tf_op jit(solution)/shard_map/ppermute | solution.py:26
  32.7 0.0 collective-permute-done.9.refs_3_
  32.7 0.7 %finish_80.1 = bf16[2,2,128,128]{3,2,1,0:T(8,128)(2,1)} custom-call(bf16[2,2,80,128]{3,2,1,0:T(8,128)(2,1)S(1)} %finish_0.1.refs_0_, f32[4,48,128]{2,1,0:T(8,128)S(1)} %get-tuple-element.35.refs_1_, s32[96,128]{1,0:T(8,128)S(1)} %collective-permute-done.8.refs_2_, s32[96,128]{1,0:T(8,128)S(1)} %collective-permute-done.9.refs_3_, ...), custom_call_target="tpu_custom_call" | custom-call | tf_op jit(solution)/shard_map/finish_80/pallas_call | solution.py:369
Async XLA Ops:
  1.3 15.1 %collective-permute-start.3 = (bf16[1936,128]{1,0:T(8,128)(2,1)S(1)}, bf16[1936,128]{1,0:T(8,128)(2,1)S(1)}, u32[]{:S(2)}, u32[]{:S(2)}) collective-permute-start(bf16[1936,128]{1,0:T(8,128)(2,1)S(1)} %get-tuple-element.23.refs_0_), channel_id=1, source_target_pairs={{4,0},{0,4},{5,1},{1,5},{6,2},{2,6},{7,3},{3,7},{12,8},{8,12},{13,... | collective-permute-start | bytes 1486856 | tf_op jit(solution)/shard_map/ppermute | solution.py:40
  4.3 5.0 %collective-permute-start.1 = (bf16[528,128]{1,0:T(8,128)(2,1)S(1)}, bf16[528,128]{1,0:T(8,128)(2,1)S(1)}, u32[]{:S(2)}, u32[]{:S(2)}) collective-permute-start(bf16[528,128]{1,0:T(8,128)(2,1)S(1)} %get-tuple-element.25.refs_2_), channel_id=1, source_target_pairs={{0,16},{8,24},{16,0},{24,8},{1,17},{9,25},{17,1},{25,9},{2,18},{10... | collective-permute-start | bytes 405512 | tf_op jit(solution)/shard_map/ppermute | solution.py:26
  5.8 3.5 %collective-permute-start = (bf16[528,128]{1,0:T(8,128)(2,1)S(1)}, bf16[528,128]{1,0:T(8,128)(2,1)S(1)}, u32[]{:S(2)}, u32[]{:S(2)}) collective-permute-start(bf16[528,128]{1,0:T(8,128)(2,1)S(1)} %get-tuple-element.25.refs_2_), channel_id=1, source_target_pairs={{0,8},{8,0},{16,24},{24,16},{1,9},{9,1},{17,25},{25,17},{2,10},{10... | collective-permute-start | bytes 405512 | tf_op jit(solution)/shard_map/ppermute | solution.py:26
  9.3 1.4 %collective-permute-start.2 = (bf16[528,128]{1,0:T(8,128)(2,1)S(1)}, bf16[528,128]{1,0:T(8,128)(2,1)S(1)}, u32[]{:S(2)}, u32[]{:S(2)}) collective-permute-start(bf16[528,128]{1,0:T(8,128)(2,1)S(1)} %collective-permute-done.1.refs_4_), channel_id=1, source_target_pairs={{0,8},{8,0},{16,24},{24,16},{1,9},{9,1},{17,25},{25,17},{2,10},{10... | collective-permute-start | bytes 405512 | tf_op jit(solution)/shard_map/ppermute | solution.py:26
  10.7 12.0 %collective-permute-start.7 = (bf16[1152,128]{1,0:T(8,128)(2,1)S(1)}, bf16[1152,128]{1,0:T(8,128)(2,1)S(1)}, u32[]{:S(2)}, u32[]{:S(2)}) collective-permute-start(bf16[1152,128]{1,0:T(8,128)(2,1)S(1)} %get-tuple-element.34.refs_1_), channel_id=1, source_target_pairs={{4,0},{0,4},{5,1},{1,5},{6,2},{2,6},{7,3},{3,7},{12,8},{8,12},{13,... | collective-permute-start | bytes 884744 | tf_op jit(solution)/shard_map/ppermute | solution.py:40
  17.8 9.9 %collective-permute-start.4 = (s32[160,128]{1,0:T(8,128)S(1)}, s32[160,128]{1,0:T(8,128)S(1)}, u32[]{:S(2)}, u32[]{:S(2)}) collective-permute-start(s32[160,128]{1,0:T(8,128)S(1)} %get-tuple-element.30), channel_id=1, source_target_pairs={{0,3},{1,2},{2,1},{3,0},{4,7},{5,6},{6,5},{7,4},{8,11},{9,10},{10,... | collective-permute-start | bytes 245768 | tf_op jit(solution)/shard_map/ppermute | solution.py:26
  22.0 6.9 %collective-permute-start.5 = (s32[160,128]{1,0:T(8,128)S(1)}, s32[160,128]{1,0:T(8,128)S(1)}, u32[]{:S(2)}, u32[]{:S(2)}) collective-permute-start(s32[160,128]{1,0:T(8,128)S(1)} %get-tuple-element.31), channel_id=1, source_target_pairs={{0,2},{1,3},{2,0},{3,1},{4,6},{5,7},{6,4},{7,5},{8,10},{9,11},{10,... | collective-permute-start | bytes 245768 | tf_op jit(solution)/shard_map/ppermute | solution.py:26
  22.0 6.9 %collective-permute-start.6 = (s32[160,128]{1,0:T(8,128)S(1)}, s32[160,128]{1,0:T(8,128)S(1)}, u32[]{:S(2)}, u32[]{:S(2)}) collective-permute-start(s32[160,128]{1,0:T(8,128)S(1)} %get-tuple-element.32), channel_id=1, source_target_pairs={{0,1},{1,0},{2,3},{3,2},{4,5},{5,4},{6,7},{7,6},{8,9},{9,8},{10,11... | collective-permute-start | bytes 245768 | tf_op jit(solution)/shard_map/ppermute | solution.py:26
  23.9 6.1 %collective-permute-start.10 = (s32[96,128]{1,0:T(8,128)S(1)}, s32[96,128]{1,0:T(8,128)S(1)}, u32[]{:S(2)}, u32[]{:S(2)}) collective-permute-start(s32[96,128]{1,0:T(8,128)S(1)} %get-tuple-element.38), channel_id=1, source_target_pairs={{0,3},{1,2},{2,1},{3,0},{4,7},{5,6},{6,5},{7,4},{8,11},{9,10},{10,... | collective-permute-start | bytes 147464 | tf_op jit(solution)/shard_map/ppermute | solution.py:26
  27.7 5.0 %collective-permute-start.8 = (s32[96,128]{1,0:T(8,128)S(1)}, s32[96,128]{1,0:T(8,128)S(1)}, u32[]{:S(2)}, u32[]{:S(2)}) collective-permute-start(s32[96,128]{1,0:T(8,128)S(1)} %get-tuple-element.36), channel_id=1, source_target_pairs={{0,2},{1,3},{2,0},{3,1},{4,6},{5,7},{6,4},{7,5},{8,10},{9,11},{10,... | collective-permute-start | bytes 147464 | tf_op jit(solution)/shard_map/ppermute | solution.py:26
  27.7 5.0 %collective-permute-start.9 = (s32[96,128]{1,0:T(8,128)S(1)}, s32[96,128]{1,0:T(8,128)S(1)}, u32[]{:S(2)}, u32[]{:S(2)}) collective-permute-start(s32[96,128]{1,0:T(8,128)S(1)} %get-tuple-element.37), channel_id=1, source_target_pairs={{0,1},{1,0},{2,3},{3,2},{4,5},{5,4},{6,7},{7,6},{8,9},{9,8},{10,11... | collective-permute-start | bytes 147464 | tf_op jit(solution)/shard_map/ppermute | solution.py:26

commit v15 on v14

--- a/solution.py
+++ b/solution.py
@@ -9,6 +9,7 @@
 
 GROUP = 8
 LANES = 128
+FIELD = 10
 MIB = 2**20
 HBM = pltpu.MemorySpace.HBM
 
@@ -112,50 +113,46 @@
     for i in range(local_rows):
         for t in range(kept):
             held[t] = jnp.where(local == i, kept_cols[t : t + 1, i : i + 1], held[t])
-    codes[0:1] = right
+    block = lax.broadcasted_iota(jnp.int32, right.shape, 1)
     for s in range(width):
-        slot = jnp.full_like(right, -1)
+        word = jnp.full_like(right, -1)
         for t in range(kept):
-            slot = jnp.where(held[t] == wanted[s], goal + t, slot)
-        codes[1 + s : 2 + s] = slot
+            pair = ((block << FIELD) | (right + s)) << FIELD | (goal + t)
+            word = jnp.where(held[t] == wanted[s], pair, word)
+        codes[s : s + 1] = word
 
 
 def list_pairs(sizes, codes, pairs):
     count, width, trash = sizes
     total = jnp.int32(0)
     for n in range(count):
-        right = codes[0, n]
         for s in range(width):
-            slot = codes[1 + s, n]
-            pairs[0, total] = n
-            pairs[1, total] = right + s
-            pairs[2, total] = slot
-            total += (slot >= 0).astype(jnp.int32)
+            word = codes[s, n]
+            pairs[total] = word
+            total += (word >= 0).astype(jnp.int32)
     for g in range(GROUP):
-        pairs[0, total + g] = 0
-        pairs[1, total + g] = 0
-        pairs[2, total + g] = trash
+        pairs[total + g] = trash
     return total
 
 
 def add_products(left, panel, totals, pairs, total):
     height = totals.shape[1]
-
-    def block(n):
-        return left[pl.ds(pl.multiple_of(n * height, height), height)]
+    mask = (1 << FIELD) - 1
 
     def one_group(group, carry):
-        base = group * GROUP
-        products = [
-            jnp.dot(
-                block(pairs[0, base + g]),
-                panel[pairs[1, base + g]],
-                preferred_element_type=jnp.float32,
+        words = [pairs[group * GROUP + g] for g in range(GROUP)]
+        products = []
+        for word in words:
+            at = pl.multiple_of((word >> (2 * FIELD)) * height, height)
+            products.append(
+                jnp.dot(
+                    left[pl.ds(at, height)],
+                    panel[(word >> FIELD) & mask],
+                    preferred_element_type=jnp.float32,
+                )
             )
-            for g in range(GROUP)
-        ]
-        for g in range(GROUP):
-            totals[pairs[2, base + g]] += products[g]
+        for word, product in zip(words, products):
+            totals[word & mask] += product
         return carry
 
     lax.fori_loop(0, quotient(total + GROUP - 1, GROUP), one_group, 0)
@@ -263,7 +260,7 @@
     block_size = order * order
     flat_s = s_blocks.reshape(piece, order, order)
     note_height = (2 * piece_rows + 15) // 16 * 16
-    code_height = (1 + width + 7) // 8 * 8
+    code_height = (width + 7) // 8 * 8
 
     vector = pl.BlockSpec(memory_space=pltpu.VMEM)
     far = pl.BlockSpec(memory_space=HBM)
@@ -321,7 +318,7 @@
         scratch_shapes=[
             pltpu.VMEM((code_height, LANES), jnp.int32),
             pltpu.SMEM((code_height, LANES), jnp.int32),
-            pltpu.SMEM((3, count * width + GROUP), jnp.int32),
+            pltpu.SMEM((count * width + GROUP,), jnp.int32),
             pltpu.SemaphoreType.DMA,
         ],
         compiler_params=pltpu.CompilerParams(vmem_limit_bytes=moved + 4 * MIB),
@@ -351,7 +348,7 @@
             scratch_shapes=[
                 pltpu.VMEM((all_slots + 1, height, order), jnp.float32),
                 pltpu.SMEM(code_shape, jnp.int32),
-                pltpu.SMEM((3, count * width + GROUP), jnp.int32),
+                pltpu.SMEM((count * width + GROUP,), jnp.int32),
                 pltpu.SemaphoreType.DMA,
             ],
             compiler_params=pltpu.CompilerParams(vmem_limit_bytes=moved + 4 * MIB),

time: 33.6 us -> 33.2 us (0.988)
  Pallas kernels: 6.11 us -> 5.64 us
  transfers between devices with their start and end apart: 11 -> 11, of which waited for: 6 -> 6; matrix products, arithmetic and copies ran while one was open for 0% -> 0% of each run, Pallas kernels for 12% -> 11%
where the time goes in v15:
time: 33.2 us; the launch traced here: 33.1 us
  starting transfers between devices  14.2 us (43%)
  waiting for transfers between devices  13.2 us (40%)
  Pallas kernels  5.64 us (17%)
    ppermute x9, starting transfers between devices, flipped(): lax.ppermute(value, axis, [(i, i ^ bits) for i in range(lax.axis_size(axi...  10.9 us
    ppermute x9, waiting for transfers between devices, flipped(): lax.ppermute(value, axis, [(i, i ^ bits) for i in range(lax.axis_size(axi...  9.11 us
    ppermute x2, waiting for transfers between devices, shifted(): lax.ppermute(value, axis, [((i + offset) % size, i) for i in range(size)])  4.08 us
    ppermute x2, starting transfers between devices, shifted(): lax.ppermute(value, axis, [((i + offset) % size, i) for i in range(size)])  3.36 us
    pallas_call x2, Pallas kernels, per_device(): pl.pallas_call(functools.partial(peer_kernel, (cols, layers, count, width...  2.25 us
    pallas_call x1, Pallas kernels, per_device(): pl.pallas_call(functools.partial(own_kernel, (rows, count, piece_rows, wi...  1.29 us
    pallas_call x1, Pallas kernels, per_device(): pl.pallas_call(functools.partial(pack_kernel, (layers, count, piece_rows,...  1.27 us
    pallas_call x2, Pallas kernels, per_device(): pl.pallas_call(functools.partial(finish_kernel, (layers, slots), (at, hei...  0.83 us
  transfers between devices with their start and end apart: 11, of which 6 were waited for; matrix products, arithmetic and copies ran while one was open for 0% of the time, Pallas kernels for 11%

profile of v15, /device:TPU:0, one launch (start us, length us, event | category | flops | bytes accessed | tf_op | source)
XLA Modules:
  0.0 33.1 jit_solution(6049533736119622857)
XLA Ops:
  0.0 1.3 %pack.1 = (s32[16,128]{1,0:T(8,128)S(1)}, bf16[528,128]{1,0:T(8,128)(2,1)S(1)}, bf16[1936,128]{1,0:T(8,128)(2,1)S(1)}, bf16[1152,128]{1,0:T(8,128)(2,1)S(1)}) custom-call(s32[1,24]{1,0:T(1,128)} %bitcast.6, s32[1,24]{1,0:T(1,128)} %bitcast.7, s32[2,8]{1,0:T(2,128)} %bitcast.5, bf16[24,128,128]{2,1,0:T(8,128)(2,1)} %x_in.1, s32[2,2]{1,0:T(2,128)} %s_cols.1, ...), custom_call_target="tpu_custom_call" | custom-call | tf_op jit(solution)/shard_map/pack/pallas_call | solution.py:268
  1.3 3.0 %collective-permute-start.3 = (bf16[1936,128]{1,0:T(8,128)(2,1)S(1)}, bf16[1936,128]{1,0:T(8,128)(2,1)S(1)}, u32[]{:S(2)}, u32[]{:S(2)}) collective-permute-start(bf16[1936,128]{1,0:T(8,128)(2,1)S(1)} %get-tuple-element.23.refs_0_), channel_id=1, source_target_pairs={{4,0},{0,4},{5,1},{1,5},{6,2},{2,6},{7,3},{3,7},{12,8},{8,12},{13,... | collective-permute-start | bytes 1486856 | tf_op jit(solution)/shard_map/ppermute | solution.py:41
  4.3 1.5 %collective-permute-start.1 = (bf16[528,128]{1,0:T(8,128)(2,1)S(1)}, bf16[528,128]{1,0:T(8,128)(2,1)S(1)}, u32[]{:S(2)}, u32[]{:S(2)}) collective-permute-start(bf16[528,128]{1,0:T(8,128)(2,1)S(1)} %get-tuple-element.25.refs_2_), channel_id=1, source_target_pairs={{0,16},{8,24},{16,0},{24,8},{1,17},{9,25},{17,1},{25,9},{2,18},{10... | collective-permute-start | bytes 405512 | tf_op jit(solution)/shard_map/ppermute | solution.py:27
  5.8 0.0 collective-permute-start
  5.8 3.5 %collective-permute-done.1.refs_4_ = bf16[528,128]{1,0:T(8,128)(2,1)S(1)} collective-permute-done((bf16[528,128]{1,0:T(8,128)(2,1)S(1)}, bf16[528,128]{1,0:T(8,128)(2,1)S(1)}, u32[]{:S(2)}, u32[]{:S(2)}) %collective-permute-start.1) | collective-permute-done | bytes 135200 | tf_op jit(solution)/shard_map/ppermute | solution.py:27
  9.3 0.0 collective-permute-start.2
  9.3 0.0 collective-permute-done.refs_3_
  9.3 1.3 %collective-permute-done.2.refs_5_ = bf16[528,128]{1,0:T(8,128)(2,1)S(1)} collective-permute-done((bf16[528,128]{1,0:T(8,128)(2,1)S(1)}, bf16[528,128]{1,0:T(8,128)(2,1)S(1)}, u32[]{:S(2)}, u32[]{:S(2)}) %collective-permute-start.2) | collective-permute-done | bytes 135200 | tf_op jit(solution)/shard_map/ppermute | solution.py:27
  10.7 0.4 %collective-permute-start.7 = (bf16[1152,128]{1,0:T(8,128)(2,1)S(1)}, bf16[1152,128]{1,0:T(8,128)(2,1)S(1)}, u32[]{:S(2)}, u32[]{:S(2)}) collective-permute-start(bf16[1152,128]{1,0:T(8,128)(2,1)S(1)} %get-tuple-element.34.refs_1_), channel_id=1, source_target_pairs={{4,0},{0,4},{5,1},{1,5},{6,2},{2,6},{7,3},{3,7},{12,8},{8,12},{13,... | collective-permute-start | bytes 884744 | tf_op jit(solution)/shard_map/ppermute | solution.py:41
  11.0 1.3 %own_products.1 = (f32[17,128,128]{2,1,0:T(8,128)S(1)}, bf16[16,128,128]{2,1,0:T(8,128)(2,1)S(1)}, s32[8,128]{1,0:T(8,128)S(1)}) custom-call(s32[16,128]{1,0:T(8,128)S(1)} %get-tuple-element.22.known.refs_0_, bf16[1936,128]{1,0:T(8,128)(2,1)S(1)} %get-tuple-element.23.refs_0_, bf16[1152,128]{1,0:T(8,128)(2,1)S(1)} %get-tuple-element.34.refs_1_, ...), custom_call_target="tpu_custom_call" | custom-call | flops 50331648 | bytes 2883584 | tf_op jit(solution)/shard_map/own_products/pallas_call | solution.py:307
  12.3 4.1 %collective-permute-done.3.refs_2_ = bf16[1936,128]{1,0:T(8,128)(2,1)S(1)} collective-permute-done((bf16[1936,128]{1,0:T(8,128)(2,1)S(1)}, bf16[1936,128]{1,0:T(8,128)(2,1)S(1)}, u32[]{:S(2)}, u32[]{:S(2)}) %collective-permute-start.3) | collective-permute-done | bytes 495648 | tf_op jit(solution)/shard_map/ppermute | solution.py:41
  16.4 1.2 %peer_products_0.1 = (f32[4,80,128]{2,1,0:T(8,128)S(1)}, s32[160,128]{1,0:T(8,128)S(1)}, s32[160,128]{1,0:T(8,128)S(1)}, s32[160,128]{1,0:T(8,128)S(1)}, s32[1,8,128]{2,1,0:T(8,128)S(1)}) custom-call(s32[16,128]{1,0:T(8,128)S(1)} %get-tuple-element.22.known.refs_0_, s32[8,128]{1,0:T(8,128)S(1)} %get-tuple-element.26.refs_1_, ...), custom_call_target="tpu_custom_call" | custom-call | flops 31457280 | bytes 1703936 | tf_op jit(solution)/shard_map/peer_products_0/pallas_call | solution.py:341
  17.6 4.2 %collective-permute-start.4 = (s32[160,128]{1,0:T(8,128)S(1)}, s32[160,128]{1,0:T(8,128)S(1)}, u32[]{:S(2)}, u32[]{:S(2)}) collective-permute-start(s32[160,128]{1,0:T(8,128)S(1)} %get-tuple-element.30), channel_id=1, source_target_pairs={{0,3},{1,2},{2,1},{3,0},{4,7},{5,6},{6,5},{7,4},{8,11},{9,10},{10,... | collective-permute-start | bytes 245768 | tf_op jit(solution)/shard_map/ppermute | solution.py:27
  21.9 0.0 collective-permute-start.5
  21.9 0.6 %collective-permute-start.6 = (s32[160,128]{1,0:T(8,128)S(1)}, s32[160,128]{1,0:T(8,128)S(1)}, u32[]{:S(2)}, u32[]{:S(2)}) collective-permute-start(s32[160,128]{1,0:T(8,128)S(1)} %get-tuple-element.32), channel_id=1, source_target_pairs={{0,1},{1,0},{2,3},{3,2},{4,5},{5,4},{6,7},{7,6},{8,9},{9,8},{10,11... | collective-permute-start | bytes 245768 | tf_op jit(solution)/shard_map/ppermute | solution.py:27
  22.5 0.0 collective-permute-done.7.refs_1_
  22.5 1.0 %peer_products_80.1 = (f32[4,48,128]{2,1,0:T(8,128)S(1)}, s32[96,128]{1,0:T(8,128)S(1)}, s32[96,128]{1,0:T(8,128)S(1)}, s32[96,128]{1,0:T(8,128)S(1)}) custom-call(s32[1,8,128]{2,1,0:T(8,128)S(1)} %get-tuple-element.33.refs_0_, bf16[1152,128]{1,0:T(8,128)(2,1)S(1)} %collective-permute-done.7.refs_1_, ...), custom_call_target="tpu_custom_call" | custom-call | flops 18874368 | bytes 1703936 | tf_op jit(solution)/shard_map/peer_products_80/pallas_call | solution.py:341
  23.6 3.8 %collective-permute-start.10 = (s32[96,128]{1,0:T(8,128)S(1)}, s32[96,128]{1,0:T(8,128)S(1)}, u32[]{:S(2)}, u32[]{:S(2)}) collective-permute-start(s32[96,128]{1,0:T(8,128)S(1)} %get-tuple-element.38), channel_id=1, source_target_pairs={{0,3},{1,2},{2,1},{3,0},{4,7},{5,6},{6,5},{7,4},{8,11},{9,10},{10,... | collective-permute-start | bytes 147464 | tf_op jit(solution)/shard_map/ppermute | solution.py:27
  27.4 0.0 collective-permute-start.8
  27.4 0.0 collective-permute-done.4.refs_1_
  27.4 0.6 %collective-permute-start.9 = (s32[96,128]{1,0:T(8,128)S(1)}, s32[96,128]{1,0:T(8,128)S(1)}, u32[]{:S(2)}, u32[]{:S(2)}) collective-permute-start(s32[96,128]{1,0:T(8,128)S(1)} %get-tuple-element.37), channel_id=1, source_target_pairs={{0,1},{1,0},{2,3},{3,2},{4,5},{5,4},{6,7},{7,6},{8,9},{9,8},{10,11... | collective-permute-start | bytes 147464 | tf_op jit(solution)/shard_map/ppermute | solution.py:27
  28.0 0.7 %collective-permute-done.5.refs_2_ = s32[160,128]{1,0:T(8,128)S(1)} collective-permute-done((s32[160,128]{1,0:T(8,128)S(1)}, s32[160,128]{1,0:T(8,128)S(1)}, u32[]{:S(2)}, u32[]{:S(2)}) %collective-permute-start.5) | collective-permute-done | bytes 81952 | tf_op jit(solution)/shard_map/ppermute | solution.py:27
  28.7 0.0 collective-permute-done.6.refs_3_
  28.7 0.1 finish_0.1.refs_0_
  28.8 1.0 %collective-permute-done.10.refs_4_ = s32[96,128]{1,0:T(8,128)S(1)} collective-permute-done((s32[96,128]{1,0:T(8,128)S(1)}, s32[96,128]{1,0:T(8,128)S(1)}, u32[]{:S(2)}, u32[]{:S(2)}) %collective-permute-start.10) | collective-permute-done | bytes 49184 | tf_op jit(solution)/shard_map/ppermute | solution.py:27
  29.8 2.5 %collective-permute-done.8.refs_2_ = s32[96,128]{1,0:T(8,128)S(1)} collective-permute-done((s32[96,128]{1,0:T(8,128)S(1)}, s32[96,128]{1,0:T(8,128)S(1)}, u32[]{:S(2)}, u32[]{:S(2)}) %collective-permute-start.8) | collective-permute-done | bytes 49184 | tf_op jit(solution)/shard_map/ppermute | solution.py:27
  32.4 0.0 collective-permute-done.9.refs_3_
  32.4 0.7 %finish_80.1 = bf16[2,2,128,128]{3,2,1,0:T(8,128)(2,1)} custom-call(bf16[2,2,80,128]{3,2,1,0:T(8,128)(2,1)S(1)} %finish_0.1.refs_0_, f32[4,48,128]{2,1,0:T(8,128)S(1)} %get-tuple-element.35.refs_1_, s32[96,128]{1,0:T(8,128)S(1)} %collective-permute-done.8.refs_2_, s32[96,128]{1,0:T(8,128)S(1)} %collective-permute-done.9.refs_3_, ...), custom_call_target="tpu_custom_call" | custom-call | tf_op jit(solution)/shard_map/finish_80/pallas_call | solution.py:366
Async XLA Ops:
  1.3 15.1 %collective-permute-start.3 = (bf16[1936,128]{1,0:T(8,128)(2,1)S(1)}, bf16[1936,128]{1,0:T(8,128)(2,1)S(1)}, u32[]{:S(2)}, u32[]{:S(2)}) collective-permute-start(bf16[1936,128]{1,0:T(8,128)(2,1)S(1)} %get-tuple-element.23.refs_0_), channel_id=1, source_target_pairs={{4,0},{0,4},{5,1},{1,5},{6,2},{2,6},{7,3},{3,7},{12,8},{8,12},{13,... | collective-permute-start | bytes 1486856 | tf_op jit(solution)/shard_map/ppermute | solution.py:41
  4.3 5.0 %collective-permute-start.1 = (bf16[528,128]{1,0:T(8,128)(2,1)S(1)}, bf16[528,128]{1,0:T(8,128)(2,1)S(1)}, u32[]{:S(2)}, u32[]{:S(2)}) collective-permute-start(bf16[528,128]{1,0:T(8,128)(2,1)S(1)} %get-tuple-element.25.refs_2_), channel_id=1, source_target_pairs={{0,16},{8,24},{16,0},{24,8},{1,17},{9,25},{17,1},{25,9},{2,18},{10... | collective-permute-start | bytes 405512 | tf_op jit(solution)/shard_map/ppermute | solution.py:27
  5.8 3.5 %collective-permute-start = (bf16[528,128]{1,0:T(8,128)(2,1)S(1)}, bf16[528,128]{1,0:T(8,128)(2,1)S(1)}, u32[]{:S(2)}, u32[]{:S(2)}) collective-permute-start(bf16[528,128]{1,0:T(8,128)(2,1)S(1)} %get-tuple-element.25.refs_2_), channel_id=1, source_target_pairs={{0,8},{8,0},{16,24},{24,16},{1,9},{9,1},{17,25},{25,17},{2,10},{10... | collective-permute-start | bytes 405512 | tf_op jit(solution)/shard_map/ppermute | solution.py:27
  9.3 1.4 %collective-permute-start.2 = (bf16[528,128]{1,0:T(8,128)(2,1)S(1)}, bf16[528,128]{1,0:T(8,128)(2,1)S(1)}, u32[]{:S(2)}, u32[]{:S(2)}) collective-permute-start(bf16[528,128]{1,0:T(8,128)(2,1)S(1)} %collective-permute-done.1.refs_4_), channel_id=1, source_target_pairs={{0,8},{8,0},{16,24},{24,16},{1,9},{9,1},{17,25},{25,17},{2,10},{10... | collective-permute-start | bytes 405512 | tf_op jit(solution)/shard_map/ppermute | solution.py:27
  10.7 11.8 %collective-permute-start.7 = (bf16[1152,128]{1,0:T(8,128)(2,1)S(1)}, bf16[1152,128]{1,0:T(8,128)(2,1)S(1)}, u32[]{:S(2)}, u32[]{:S(2)}) collective-permute-start(bf16[1152,128]{1,0:T(8,128)(2,1)S(1)} %get-tuple-element.34.refs_1_), channel_id=1, source_target_pairs={{4,0},{0,4},{5,1},{1,5},{6,2},{2,6},{7,3},{3,7},{12,8},{8,12},{13,... | collective-permute-start | bytes 884744 | tf_op jit(solution)/shard_map/ppermute | solution.py:41
  17.6 9.8 %collective-permute-start.4 = (s32[160,128]{1,0:T(8,128)S(1)}, s32[160,128]{1,0:T(8,128)S(1)}, u32[]{:S(2)}, u32[]{:S(2)}) collective-permute-start(s32[160,128]{1,0:T(8,128)S(1)} %get-tuple-element.30), channel_id=1, source_target_pairs={{0,3},{1,2},{2,1},{3,0},{4,7},{5,6},{6,5},{7,4},{8,11},{9,10},{10,... | collective-permute-start | bytes 245768 | tf_op jit(solution)/shard_map/ppermute | solution.py:27
  21.9 6.8 %collective-permute-start.5 = (s32[160,128]{1,0:T(8,128)S(1)}, s32[160,128]{1,0:T(8,128)S(1)}, u32[]{:S(2)}, u32[]{:S(2)}) collective-permute-start(s32[160,128]{1,0:T(8,128)S(1)} %get-tuple-element.31), channel_id=1, source_target_pairs={{0,2},{1,3},{2,0},{3,1},{4,6},{5,7},{6,4},{7,5},{8,10},{9,11},{10,... | collective-permute-start | bytes 245768 | tf_op jit(solution)/shard_map/ppermute | solution.py:27
  21.9 6.8 %collective-permute-start.6 = (s32[160,128]{1,0:T(8,128)S(1)}, s32[160,128]{1,0:T(8,128)S(1)}, u32[]{:S(2)}, u32[]{:S(2)}) collective-permute-start(s32[160,128]{1,0:T(8,128)S(1)} %get-tuple-element.32), channel_id=1, source_target_pairs={{0,1},{1,0},{2,3},{3,2},{4,5},{5,4},{6,7},{7,6},{8,9},{9,8},{10,11... | collective-permute-start | bytes 245768 | tf_op jit(solution)/shard_map/ppermute | solution.py:27
  23.6 6.3 %collective-permute-start.10 = (s32[96,128]{1,0:T(8,128)S(1)}, s32[96,128]{1,0:T(8,128)S(1)}, u32[]{:S(2)}, u32[]{:S(2)}) collective-permute-start(s32[96,128]{1,0:T(8,128)S(1)} %get-tuple-element.38), channel_id=1, source_target_pairs={{0,3},{1,2},{2,1},{3,0},{4,7},{5,6},{6,5},{7,4},{8,11},{9,10},{10,... | collective-permute-start | bytes 147464 | tf_op jit(solution)/shard_map/ppermute | solution.py:27
  27.4 5.0 %collective-permute-start.8 = (s32[96,128]{1,0:T(8,128)S(1)}, s32[96,128]{1,0:T(8,128)S(1)}, u32[]{:S(2)}, u32[]{:S(2)}) collective-permute-start(s32[96,128]{1,0:T(8,128)S(1)} %get-tuple-element.36), channel_id=1, source_target_pairs={{0,2},{1,3},{2,0},{3,1},{4,6},{5,7},{6,4},{7,5},{8,10},{9,11},{10,... | collective-permute-start | bytes 147464 | tf_op jit(solution)/shard_map/ppermute | solution.py:27
  27.4 5.0 %collective-permute-start.9 = (s32[96,128]{1,0:T(8,128)S(1)}, s32[96,128]{1,0:T(8,128)S(1)}, u32[]{:S(2)}, u32[]{:S(2)}) collective-permute-start(s32[96,128]{1,0:T(8,128)S(1)} %get-tuple-element.37), channel_id=1, source_target_pairs={{0,1},{1,0},{2,3},{3,2},{4,5},{5,4},{6,7},{7,6},{8,9},{9,8},{10,11... | collective-permute-start | bytes 147464 | tf_op jit(solution)/shard_map/ppermute | solution.py:27

commit v16 on v15

--- a/solution.py
+++ b/solution.py
@@ -360,7 +360,10 @@
             name=f"peer_products_{at}",
         )(*given, *pieces, panel, totals)
         plan = plan or out[layers:]
-        turn = range(layers - 1, 0, -1) if at == 0 else [*range(layers - 2, 0, -1), layers - 1]
+        far = [d for d in range(layers // 2, layers)]
+        turn = far + [d for d in range(1, layers) if d not in far]
+        if at > 0:
+            turn = turn[1:] + turn[:1]
         codes = [flipped(out[d], "layer", d) for d in turn]
         finished = [
             pl.pallas_call(

time: 33.2 us -> 33.7 us (1.015)
  no operation moved by 1% of the time
where the time goes in v16:
time: 33.7 us; the launch traced here: 33.5 us
  starting transfers between devices  14.4 us (43%)
  waiting for transfers between devices  13.4 us (40%)
  Pallas kernels  5.65 us (17%)
    ppermute x9, starting transfers between devices, flipped(): lax.ppermute(value, axis, [(i, i ^ bits) for i in range(lax.axis_size(axi...  11 us
    ppermute x9, waiting for transfers between devices, flipped(): lax.ppermute(value, axis, [(i, i ^ bits) for i in range(lax.axis_size(axi...  9.36 us
    ppermute x2, waiting for transfers between devices, shifted(): lax.ppermute(value, axis, [((i + offset) % size, i) for i in range(size)])  4.07 us
    ppermute x2, starting transfers between devices, shifted(): lax.ppermute(value, axis, [((i + offset) % size, i) for i in range(size)])  3.36 us
    pallas_call x2, Pallas kernels, per_device(): pl.pallas_call(functools.partial(peer_kernel, (cols, layers, count, width...  2.25 us
    pallas_call x1, Pallas kernels, per_device(): pl.pallas_call(functools.partial(own_kernel, (rows, count, piece_rows, wi...  1.3 us
    pallas_call x1, Pallas kernels, per_device(): pl.pallas_call(functools.partial(pack_kernel, (layers, count, piece_rows,...  1.27 us
    pallas_call x2, Pallas kernels, per_device(): pl.pallas_call(functools.partial(finish_kernel, (layers, slots), (at, hei...  0.83 us
  transfers between devices with their start and end apart: 11, of which 6 were waited for; matrix products, arithmetic and copies ran while one was open for 0% of the time, Pallas kernels for 11%

profile of v16, /device:TPU:0, one launch (start us, length us, event | category | flops | bytes accessed | tf_op | source)
XLA Modules:
  0.0 33.5 jit_solution(13716825395893440685)
XLA Ops:
  0.0 1.3 %pack.1 = (s32[16,128]{1,0:T(8,128)S(1)}, bf16[528,128]{1,0:T(8,128)(2,1)S(1)}, bf16[1936,128]{1,0:T(8,128)(2,1)S(1)}, bf16[1152,128]{1,0:T(8,128)(2,1)S(1)}) custom-call(s32[1,24]{1,0:T(1,128)} %bitcast.6, s32[1,24]{1,0:T(1,128)} %bitcast.7, s32[2,8]{1,0:T(2,128)} %bitcast.5, bf16[24,128,128]{2,1,0:T(8,128)(2,1)} %x_in.1, s32[2,2]{1,0:T(2,128)} %s_cols.1, ...), custom_call_target="tpu_custom_call" | custom-call | tf_op jit(solution)/shard_map/pack/pallas_call | solution.py:268
  1.3 3.0 %collective-permute-start.3 = (bf16[1936,128]{1,0:T(8,128)(2,1)S(1)}, bf16[1936,128]{1,0:T(8,128)(2,1)S(1)}, u32[]{:S(2)}, u32[]{:S(2)}) collective-permute-start(bf16[1936,128]{1,0:T(8,128)(2,1)S(1)} %get-tuple-element.23.refs_0_), channel_id=1, source_target_pairs={{4,0},{0,4},{5,1},{1,5},{6,2},{2,6},{7,3},{3,7},{12,8},{8,12},{13,... | collective-permute-start | bytes 1486856 | tf_op jit(solution)/shard_map/ppermute | solution.py:41
  4.3 1.5 %collective-permute-start.1 = (bf16[528,128]{1,0:T(8,128)(2,1)S(1)}, bf16[528,128]{1,0:T(8,128)(2,1)S(1)}, u32[]{:S(2)}, u32[]{:S(2)}) collective-permute-start(bf16[528,128]{1,0:T(8,128)(2,1)S(1)} %get-tuple-element.25.refs_2_), channel_id=1, source_target_pairs={{0,16},{8,24},{16,0},{24,8},{1,17},{9,25},{17,1},{25,9},{2,18},{10... | collective-permute-start | bytes 405512 | tf_op jit(solution)/shard_map/ppermute | solution.py:27
  5.8 0.0 collective-permute-start
  5.8 3.5 %collective-permute-done.1.refs_4_ = bf16[528,128]{1,0:T(8,128)(2,1)S(1)} collective-permute-done((bf16[528,128]{1,0:T(8,128)(2,1)S(1)}, bf16[528,128]{1,0:T(8,128)(2,1)S(1)}, u32[]{:S(2)}, u32[]{:S(2)}) %collective-permute-start.1) | collective-permute-done | bytes 135200 | tf_op jit(solution)/shard_map/ppermute | solution.py:27
  9.3 0.0 collective-permute-start.2
  9.3 0.0 collective-permute-done.refs_3_
  9.3 1.3 %collective-permute-done.2.refs_5_ = bf16[528,128]{1,0:T(8,128)(2,1)S(1)} collective-permute-done((bf16[528,128]{1,0:T(8,128)(2,1)S(1)}, bf16[528,128]{1,0:T(8,128)(2,1)S(1)}, u32[]{:S(2)}, u32[]{:S(2)}) %collective-permute-start.2) | collective-permute-done | bytes 135200 | tf_op jit(solution)/shard_map/ppermute | solution.py:27
  10.7 0.4 %collective-permute-start.7 = (bf16[1152,128]{1,0:T(8,128)(2,1)S(1)}, bf16[1152,128]{1,0:T(8,128)(2,1)S(1)}, u32[]{:S(2)}, u32[]{:S(2)}) collective-permute-start(bf16[1152,128]{1,0:T(8,128)(2,1)S(1)} %get-tuple-element.34.refs_1_), channel_id=1, source_target_pairs={{4,0},{0,4},{5,1},{1,5},{6,2},{2,6},{7,3},{3,7},{12,8},{8,12},{13,... | collective-permute-start | bytes 884744 | tf_op jit(solution)/shard_map/ppermute | solution.py:41
  11.0 1.3 %own_products.1 = (f32[17,128,128]{2,1,0:T(8,128)S(1)}, bf16[16,128,128]{2,1,0:T(8,128)(2,1)S(1)}, s32[8,128]{1,0:T(8,128)S(1)}) custom-call(s32[16,128]{1,0:T(8,128)S(1)} %get-tuple-element.22.known.refs_0_, bf16[1936,128]{1,0:T(8,128)(2,1)S(1)} %get-tuple-element.23.refs_0_, bf16[1152,128]{1,0:T(8,128)(2,1)S(1)} %get-tuple-element.34.refs_1_, ...), custom_call_target="tpu_custom_call" | custom-call | flops 50331648 | bytes 2883584 | tf_op jit(solution)/shard_map/own_products/pallas_call | solution.py:307
  12.3 4.1 %collective-permute-done.3.refs_2_ = bf16[1936,128]{1,0:T(8,128)(2,1)S(1)} collective-permute-done((bf16[1936,128]{1,0:T(8,128)(2,1)S(1)}, bf16[1936,128]{1,0:T(8,128)(2,1)S(1)}, u32[]{:S(2)}, u32[]{:S(2)}) %collective-permute-start.3) | collective-permute-done | bytes 495648 | tf_op jit(solution)/shard_map/ppermute | solution.py:41
  16.4 1.2 %peer_products_0.1 = (f32[4,80,128]{2,1,0:T(8,128)S(1)}, s32[160,128]{1,0:T(8,128)S(1)}, s32[160,128]{1,0:T(8,128)S(1)}, s32[160,128]{1,0:T(8,128)S(1)}, s32[1,8,128]{2,1,0:T(8,128)S(1)}) custom-call(s32[16,128]{1,0:T(8,128)S(1)} %get-tuple-element.22.known.refs_0_, s32[8,128]{1,0:T(8,128)S(1)} %get-tuple-element.26.refs_1_, ...), custom_call_target="tpu_custom_call" | custom-call | flops 31457280 | bytes 1703936 | tf_op jit(solution)/shard_map/peer_products_0/pallas_call | solution.py:341
  17.6 3.2 %collective-permute-start.4 = (s32[160,128]{1,0:T(8,128)S(1)}, s32[160,128]{1,0:T(8,128)S(1)}, u32[]{:S(2)}, u32[]{:S(2)}) collective-permute-start(s32[160,128]{1,0:T(8,128)S(1)} %get-tuple-element.30), channel_id=1, source_target_pairs={{0,2},{1,3},{2,0},{3,1},{4,6},{5,7},{6,4},{7,5},{8,10},{9,11},{10,... | collective-permute-start | bytes 245768 | tf_op jit(solution)/shard_map/ppermute | solution.py:27
  20.9 1.6 %collective-permute-start.5 = (s32[160,128]{1,0:T(8,128)S(1)}, s32[160,128]{1,0:T(8,128)S(1)}, u32[]{:S(2)}, u32[]{:S(2)}) collective-permute-start(s32[160,128]{1,0:T(8,128)S(1)} %get-tuple-element.31), channel_id=1, source_target_pairs={{0,3},{1,2},{2,1},{3,0},{4,7},{5,6},{6,5},{7,4},{8,11},{9,10},{10,... | collective-permute-start | bytes 245768 | tf_op jit(solution)/shard_map/ppermute | solution.py:27
  22.5 0.0 collective-permute-start.6
  22.5 0.0 collective-permute-done.7.refs_1_
  22.5 1.0 %peer_products_80.1 = (f32[4,48,128]{2,1,0:T(8,128)S(1)}, s32[96,128]{1,0:T(8,128)S(1)}, s32[96,128]{1,0:T(8,128)S(1)}, s32[96,128]{1,0:T(8,128)S(1)}) custom-call(s32[1,8,128]{2,1,0:T(8,128)S(1)} %get-tuple-element.33.refs_0_, bf16[1152,128]{1,0:T(8,128)(2,1)S(1)} %collective-permute-done.7.refs_1_, ...), custom_call_target="tpu_custom_call" | custom-call | flops 18874368 | bytes 1703936 | tf_op jit(solution)/shard_map/peer_products_80/pallas_call | solution.py:341
  23.5 2.9 %collective-permute-start.10 = (s32[96,128]{1,0:T(8,128)S(1)}, s32[96,128]{1,0:T(8,128)S(1)}, u32[]{:S(2)}, u32[]{:S(2)}) collective-permute-start(s32[96,128]{1,0:T(8,128)S(1)} %get-tuple-element.38), channel_id=1, source_target_pairs={{0,2},{1,3},{2,0},{3,1},{4,6},{5,7},{6,4},{7,5},{8,10},{9,11},{10,... | collective-permute-start | bytes 147464 | tf_op jit(solution)/shard_map/ppermute | solution.py:27
  26.4 1.8 %collective-permute-start.8 = (s32[96,128]{1,0:T(8,128)S(1)}, s32[96,128]{1,0:T(8,128)S(1)}, u32[]{:S(2)}, u32[]{:S(2)}) collective-permute-start(s32[96,128]{1,0:T(8,128)S(1)} %get-tuple-element.36), channel_id=1, source_target_pairs={{0,3},{1,2},{2,1},{3,0},{4,7},{5,6},{6,5},{7,4},{8,11},{9,10},{10,... | collective-permute-start | bytes 147464 | tf_op jit(solution)/shard_map/ppermute | solution.py:27
  28.2 0.0 collective-permute-done.4.refs_1_
  28.2 0.0 collective-permute-start.9
  28.2 0.0 collective-permute-done.5.refs_2_
  28.2 0.0 collective-permute-done.6.refs_3_
  28.2 0.1 finish_0.1.refs_0_
  28.3 1.8 %collective-permute-done.10.refs_4_ = s32[96,128]{1,0:T(8,128)S(1)} collective-permute-done((s32[96,128]{1,0:T(8,128)S(1)}, s32[96,128]{1,0:T(8,128)S(1)}, u32[]{:S(2)}, u32[]{:S(2)}) %collective-permute-start.10) | collective-permute-done | bytes 49184 | tf_op jit(solution)/shard_map/ppermute | solution.py:27
  30.1 2.2 %collective-permute-done.8.refs_2_ = s32[96,128]{1,0:T(8,128)S(1)} collective-permute-done((s32[96,128]{1,0:T(8,128)S(1)}, s32[96,128]{1,0:T(8,128)S(1)}, u32[]{:S(2)}, u32[]{:S(2)}) %collective-permute-start.8) | collective-permute-done | bytes 49184 | tf_op jit(solution)/shard_map/ppermute | solution.py:27
  32.3 0.5 %collective-permute-done.9.refs_3_ = s32[96,128]{1,0:T(8,128)S(1)} collective-permute-done((s32[96,128]{1,0:T(8,128)S(1)}, s32[96,128]{1,0:T(8,128)S(1)}, u32[]{:S(2)}, u32[]{:S(2)}) %collective-permute-start.9) | collective-permute-done | bytes 49184 | tf_op jit(solution)/shard_map/ppermute | solution.py:27
  32.8 0.7 %finish_80.1 = bf16[2,2,128,128]{3,2,1,0:T(8,128)(2,1)} custom-call(bf16[2,2,80,128]{3,2,1,0:T(8,128)(2,1)S(1)} %finish_0.1.refs_0_, f32[4,48,128]{2,1,0:T(8,128)S(1)} %get-tuple-element.35.refs_1_, s32[96,128]{1,0:T(8,128)S(1)} %collective-permute-done.8.refs_2_, s32[96,128]{1,0:T(8,128)S(1)} %collective-permute-done.9.refs_3_, ...), custom_call_target="tpu_custom_call" | custom-call | tf_op jit(solution)/shard_map/finish_80/pallas_call | solution.py:369
Async XLA Ops:
  1.3 15.1 %collective-permute-start.3 = (bf16[1936,128]{1,0:T(8,128)(2,1)S(1)}, bf16[1936,128]{1,0:T(8,128)(2,1)S(1)}, u32[]{:S(2)}, u32[]{:S(2)}) collective-permute-start(bf16[1936,128]{1,0:T(8,128)(2,1)S(1)} %get-tuple-element.23.refs_0_), channel_id=1, source_target_pairs={{4,0},{0,4},{5,1},{1,5},{6,2},{2,6},{7,3},{3,7},{12,8},{8,12},{13,... | collective-permute-start | bytes 1486856 | tf_op jit(solution)/shard_map/ppermute | solution.py:41
  4.3 5.0 %collective-permute-start.1 = (bf16[528,128]{1,0:T(8,128)(2,1)S(1)}, bf16[528,128]{1,0:T(8,128)(2,1)S(1)}, u32[]{:S(2)}, u32[]{:S(2)}) collective-permute-start(bf16[528,128]{1,0:T(8,128)(2,1)S(1)} %get-tuple-element.25.refs_2_), channel_id=1, source_target_pairs={{0,16},{8,24},{16,0},{24,8},{1,17},{9,25},{17,1},{25,9},{2,18},{10... | collective-permute-start | bytes 405512 | tf_op jit(solution)/shard_map/ppermute | solution.py:27
  5.8 3.5 %collective-permute-start = (bf16[528,128]{1,0:T(8,128)(2,1)S(1)}, bf16[528,128]{1,0:T(8,128)(2,1)S(1)}, u32[]{:S(2)}, u32[]{:S(2)}) collective-permute-start(bf16[528,128]{1,0:T(8,128)(2,1)S(1)} %get-tuple-element.25.refs_2_), channel_id=1, source_target_pairs={{0,8},{8,0},{16,24},{24,16},{1,9},{9,1},{17,25},{25,17},{2,10},{10... | collective-permute-start | bytes 405512 | tf_op jit(solution)/shard_map/ppermute | solution.py:27
  9.3 1.4 %collective-permute-start.2 = (bf16[528,128]{1,0:T(8,128)(2,1)S(1)}, bf16[528,128]{1,0:T(8,128)(2,1)S(1)}, u32[]{:S(2)}, u32[]{:S(2)}) collective-permute-start(bf16[528,128]{1,0:T(8,128)(2,1)S(1)} %collective-permute-done.1.refs_4_), channel_id=1, source_target_pairs={{0,8},{8,0},{16,24},{24,16},{1,9},{9,1},{17,25},{25,17},{2,10},{10... | collective-permute-start | bytes 405512 | tf_op jit(solution)/shard_map/ppermute | solution.py:27
  10.7 11.8 %collective-permute-start.7 = (bf16[1152,128]{1,0:T(8,128)(2,1)S(1)}, bf16[1152,128]{1,0:T(8,128)(2,1)S(1)}, u32[]{:S(2)}, u32[]{:S(2)}) collective-permute-start(bf16[1152,128]{1,0:T(8,128)(2,1)S(1)} %get-tuple-element.34.refs_1_), channel_id=1, source_target_pairs={{4,0},{0,4},{5,1},{1,5},{6,2},{2,6},{7,3},{3,7},{12,8},{8,12},{13,... | collective-permute-start | bytes 884744 | tf_op jit(solution)/shard_map/ppermute | solution.py:41
  17.6 10.5 %collective-permute-start.4 = (s32[160,128]{1,0:T(8,128)S(1)}, s32[160,128]{1,0:T(8,128)S(1)}, u32[]{:S(2)}, u32[]{:S(2)}) collective-permute-start(s32[160,128]{1,0:T(8,128)S(1)} %get-tuple-element.30), channel_id=1, source_target_pairs={{0,2},{1,3},{2,0},{3,1},{4,6},{5,7},{6,4},{7,5},{8,10},{9,11},{10,... | collective-permute-start | bytes 245768 | tf_op jit(solution)/shard_map/ppermute | solution.py:27
  20.9 7.3 %collective-permute-start.5 = (s32[160,128]{1,0:T(8,128)S(1)}, s32[160,128]{1,0:T(8,128)S(1)}, u32[]{:S(2)}, u32[]{:S(2)}) collective-permute-start(s32[160,128]{1,0:T(8,128)S(1)} %get-tuple-element.31), channel_id=1, source_target_pairs={{0,3},{1,2},{2,1},{3,0},{4,7},{5,6},{6,5},{7,4},{8,11},{9,10},{10,... | collective-permute-start | bytes 245768 | tf_op jit(solution)/shard_map/ppermute | solution.py:27
  22.5 5.7 %collective-permute-start.6 = (s32[160,128]{1,0:T(8,128)S(1)}, s32[160,128]{1,0:T(8,128)S(1)}, u32[]{:S(2)}, u32[]{:S(2)}) collective-permute-start(s32[160,128]{1,0:T(8,128)S(1)} %get-tuple-element.32), channel_id=1, source_target_pairs={{0,1},{1,0},{2,3},{3,2},{4,5},{5,4},{6,7},{7,6},{8,9},{9,8},{10,11... | collective-permute-start | bytes 245768 | tf_op jit(solution)/shard_map/ppermute | solution.py:27
  23.5 6.6 %collective-permute-start.10 = (s32[96,128]{1,0:T(8,128)S(1)}, s32[96,128]{1,0:T(8,128)S(1)}, u32[]{:S(2)}, u32[]{:S(2)}) collective-permute-start(s32[96,128]{1,0:T(8,128)S(1)} %get-tuple-element.38), channel_id=1, source_target_pairs={{0,2},{1,3},{2,0},{3,1},{4,6},{5,7},{6,4},{7,5},{8,10},{9,11},{10,... | collective-permute-start | bytes 147464 | tf_op jit(solution)/shard_map/ppermute | solution.py:27
  26.4 5.9 %collective-permute-start.8 = (s32[96,128]{1,0:T(8,128)S(1)}, s32[96,128]{1,0:T(8,128)S(1)}, u32[]{:S(2)}, u32[]{:S(2)}) collective-permute-start(s32[96,128]{1,0:T(8,128)S(1)} %get-tuple-element.36), channel_id=1, source_target_pairs={{0,3},{1,2},{2,1},{3,0},{4,7},{5,6},{6,5},{7,4},{8,11},{9,10},{10,... | collective-permute-start | bytes 147464 | tf_op jit(solution)/shard_map/ppermute | solution.py:27
  28.2 4.6 %collective-permute-start.9 = (s32[96,128]{1,0:T(8,128)S(1)}, s32[96,128]{1,0:T(8,128)S(1)}, u32[]{:S(2)}, u32[]{:S(2)}) collective-permute-start(s32[96,128]{1,0:T(8,128)S(1)} %get-tuple-element.37), channel_id=1, source_target_pairs={{0,1},{1,0},{2,3},{3,2},{4,5},{5,4},{6,7},{7,6},{8,9},{9,8},{10,11... | collective-permute-start | bytes 147464 | tf_op jit(solution)/shard_map/ppermute | solution.py:27

commit v17 on v16

--- a/solution.py
+++ b/solution.py
@@ -55,30 +55,20 @@
     tile[at + height : at + 2 * height, :width] = quotient(value, LANES)
 
 
-def pack_kernel(sizes, a_rows, a_cols, c_cols, x_in, s_cols, s_in, *refs):
-    layers, count, piece_rows, width, local_rows, kept, order, ranges = sizes
-    known, s_out, x_out, refs = refs[0], refs[1], refs[2 : 2 + len(ranges)], refs[2 + len(ranges) :]
-    rows, cols, kept_held, s_held, x_tile, s_tile, sem = refs
-    piece = piece_rows * width
-    small = [(a_rows, rows), (a_cols, cols), (c_cols, kept_held), (s_cols, s_held)]
-    large = [
-        (
-            x_in.at[:, pl.ds(first, height)],
-            out.at[pl.ds(0, count * height)].reshape(count, height, order),
-        )
-        for (first, height), out in zip(ranges, x_out)
-    ]
-    large += [(s_in.at[q], s_out.at[pl.ds(q * order, order)]) for q in range(piece)]
+def pack_first_kernel(sizes, a_rows, a_cols, c_cols, x_in, known, x_out, rows, cols, held, tile, sem):
+    layers, count, piece_rows, width, local_rows, kept, order, height = sizes
+    spot = x_out.at[pl.ds(0, count * height)].reshape(count, height, order)
     loads = [
         pltpu.make_async_copy(source, goal, sem.at[p])
-        for p, (source, goal) in enumerate(small + large)
+        for p, (source, goal) in enumerate(
+            ((a_rows, rows), (a_cols, cols), (c_cols, held), (x_in.at[:, pl.ds(0, height)], spot))
+        )
     ]
     for load in loads:
         load.start()
     known[...] = jnp.zeros_like(known)
-    x_tile[...] = jnp.zeros_like(x_tile)
-    s_tile[...] = jnp.zeros_like(s_tile)
-    for load in loads[: len(small)]:
+    tile[...] = jnp.zeros_like(tile)
+    for load in loads[:3]:
         load.wait()
     own_rows = local_rows // layers
     row, col = rows[...], cols[...]
@@ -94,12 +84,29 @@
     )
     for p, value in enumerate(place):
         known[p : p + 1, :count] = value
-        write_digits(x_tile, 2 * p, value)
-    known[8 : 8 + kept, :local_rows] = kept_held[...]
-    write_digits(s_tile, 0, s_held[...])
-    x_out[0][count * ranges[0][1] :] = x_tile[...].astype(jnp.float32).astype(jnp.bfloat16)
-    s_out[piece * order :] = s_tile[...].astype(jnp.float32).astype(jnp.bfloat16)
-    for load in loads[len(small) :]:
+        write_digits(tile, 2 * p, value)
+    known[8 : 8 + kept, :local_rows] = held[...]
+    x_out[count * height :] = tile[...].astype(jnp.float32).astype(jnp.bfloat16)
+    loads[3].wait()
+
+
+def pack_later_kernel(sizes, x_in, s_cols, s_in, s_out, *refs):
+    count, piece, order, ranges = sizes
+    x_out, (held, tile, sem) = refs[: len(ranges)], refs[len(ranges) :]
+    sources = [(s_cols, held)]
+    sources += [(s_in.at[q], s_out.at[pl.ds(q * order, order)]) for q in range(piece)]
+    sources += [
+        (x_in.at[:, pl.ds(first, height)], out.reshape(count, height, order))
+        for (first, height), out in zip(ranges, x_out)
+    ]
+    loads = [pltpu.make_async_copy(*pair, sem.at[p]) for p, pair in enumerate(sources)]
+    for load in loads:
+        load.start()
+    tile[...] = jnp.zeros_like(tile)
+    loads[0].wait()
+    write_digits(tile, 0, held[...])
+    s_out[piece * order :] = tile[...].astype(jnp.float32).astype(jnp.bfloat16)
+    for load in loads[1:]:
         load.wait()
 
 
@@ -240,6 +247,7 @@
             word = code[pl.ds(u * half, half)]
             power = jnp.sum((word[:8] & 1) << sublane, axis=0, keepdims=True).astype(jnp.float32)
             scale = jnp.exp2(power - (128.0 + 15.0))
+            word = jnp.concatenate([word[:8] & ~1, word[8:]])
             high += (word >> 16).astype(jnp.float32) * scale
             low += ((word << 16) >> 16).astype(jnp.float32) * scale
         result[u // kept, u % kept, first : first + half] = high.astype(jnp.bfloat16)
@@ -265,43 +273,57 @@
     vector = pl.BlockSpec(memory_space=pltpu.VMEM)
     far = pl.BlockSpec(memory_space=HBM)
 
-    known, s_sent, *x_sent = pl.pallas_call(
+    first_height = ranges[0][1]
+    known, x_first = pl.pallas_call(
         functools.partial(
-            pack_kernel, (layers, count, piece_rows, width, local_rows, kept, order, ranges)
+            pack_first_kernel,
+            (layers, count, piece_rows, width, local_rows, kept, order, first_height),
         ),
         out_shape=[
             jax.ShapeDtypeStruct((16, LANES), jnp.int32),
-            jax.ShapeDtypeStruct((piece * order + note_height, order), jnp.bfloat16),
-        ]
-        + [
-            jax.ShapeDtypeStruct((count * height + 16 * (at == 0), order), jnp.bfloat16)
-            for at, height in ranges
-        ],
-        in_specs=[far] * 6,
-        out_specs=[vector] * (2 + len(ranges)),
+            jax.ShapeDtypeStruct((count * first_height + 16, order), jnp.bfloat16),
+        ],
+        in_specs=[far] * 4,
+        out_specs=[vector] * 2,
         scratch_shapes=[
             pltpu.VMEM((1, count), jnp.int32),
             pltpu.VMEM((1, count), jnp.int32),
             pltpu.VMEM((kept, local_rows), jnp.int32),
+            pltpu.VMEM((16, LANES), jnp.int32),
+            pltpu.SemaphoreType.DMA((4,)),
+        ],
+        compiler_params=pltpu.CompilerParams(
+            vmem_limit_bytes=2 * block_size * (count + 1) + 4 * MIB
+        ),
+        name="pack_first",
+    )(*in_hbm(a_rows.reshape(1, count), a_cols.reshape(1, count), c_cols.T, a_blocks))
+    first_piece = [shifted(x_first, "col", j) for j in range(1, cols)]
+    later_blocks, later_s_cols, later_s, _ = lax.optimization_barrier(
+        (a_blocks, s_cols, flat_s, known)
+    )
+    s_sent, *x_later = pl.pallas_call(
+        functools.partial(pack_later_kernel, (count, piece, order, ranges[1:])),
+        out_shape=[jax.ShapeDtypeStruct((piece * order + note_height, order), jnp.bfloat16)]
+        + [
+            jax.ShapeDtypeStruct((count * height, order), jnp.bfloat16) for _, height in ranges[1:]
+        ],
+        in_specs=[far] * 3,
+        out_specs=[vector] * len(ranges),
+        scratch_shapes=[
             pltpu.VMEM((piece_rows, width), jnp.int32),
-            pltpu.VMEM((16, LANES), jnp.int32),
             pltpu.VMEM((note_height, LANES), jnp.int32),
-            pltpu.SemaphoreType.DMA((4 + piece + len(ranges),)),
+            pltpu.SemaphoreType.DMA((piece + len(ranges),)),
         ],
         compiler_params=pltpu.CompilerParams(
-            vmem_limit_bytes=2 * block_size * (2 * count + piece) + 4 * MIB
+            vmem_limit_bytes=2 * block_size * (count + piece + 1) + 4 * MIB
         ),
-        name="pack",
-    )(
-        *in_hbm(
-            a_rows.reshape(1, count), a_cols.reshape(1, count), c_cols.T, a_blocks, s_cols, flat_s
-        )
-    )
+        name="pack_later",
+    )(*in_hbm(later_blocks, later_s_cols, later_s))
+    x_sent = [x_first, *x_later]
     s_pieces = gathered(s_sent, "row")
     later, _ = lax.optimization_barrier((x_sent[1:], s_pieces))
-    x_pieces = [
-        [shifted(part, "col", j) for j in range(1, cols)] for part in (x_sent[0], *later)
-    ]
+    x_pieces = [first_piece]
+    x_pieces += [[shifted(part, "col", j) for j in range(1, cols)] for part in later]
 
     moved = block_size * (4 * all_slots + 4 * panel_size + 2 * count)
     totals, panel, panel_cols = pl.pallas_call(

time: 33.7 us -> 33.1 us (0.982)
  waiting for transfers between devices: 13.4 us -> 12.3 us
  Pallas kernels: 5.65 us -> 6.62 us
  starting transfers between devices: 14.4 us -> 13.9 us
    ppermute x2, waiting for transfers between devices: 4.07 us -> 2.93 us  [shifted(): lax.ppermute(value, axis, [((i + offset) % size, i) for i in range(size)])]
    pallas_call x1 -> x2, Pallas kernels: 1.27 us -> 2.22 us  [the longest x1 1.11 us: per_device(): pl.pallas_call(functools.partial(pack_first_kernel, (layers, count, piece...]
    ppermute x9, starting transfers between devices: 11 us -> 10.6 us  [flipped(): lax.ppermute(value, axis, [(i, i ^ bits) for i in range(lax.axis_size(axi...]
  transfers between devices with their start and end apart: 11 -> 11, of which waited for: 6 -> 5; matrix products, arithmetic and copies ran while one was open for 0% -> 0% of each run, Pallas kernels for 11% -> 15%
where the time goes in v17:
time: 33.1 us; the launch traced here: 32.9 us
  starting transfers between devices  13.9 us (42%)
  waiting for transfers between devices  12.3 us (37%)
  Pallas kernels  6.62 us (20%)
    ppermute x9, starting transfers between devices, flipped(): lax.ppermute(value, axis, [(i, i ^ bits) for i in range(lax.axis_size(axi...  10.6 us
    ppermute x9, waiting for transfers between devices, flipped(): lax.ppermute(value, axis, [(i, i ^ bits) for i in range(lax.axis_size(axi...  9.38 us
    ppermute x2, starting transfers between devices, shifted(): lax.ppermute(value, axis, [((i + offset) % size, i) for i in range(size)])  3.32 us
    ppermute x2, waiting for transfers between devices, shifted(): lax.ppermute(value, axis, [((i + offset) % size, i) for i in range(size)])  2.93 us
    pallas_call x2, Pallas kernels, per_device(): pl.pallas_call(functools.partial(peer_kernel, (cols, layers, count, width...  2.26 us
    pallas_call x1, Pallas kernels, per_device(): pl.pallas_call(functools.partial(own_kernel, (rows, count, piece_rows, wi...  1.3 us
    pallas_call x1, Pallas kernels, per_device(): pl.pallas_call(functools.partial(pack_first_kernel, (layers, count, piece...  1.11 us
    pallas_call x1, Pallas kernels, per_device(): pl.pallas_call(functools.partial(pack_later_kernel, (count, piece, order,...  1.11 us
  transfers between devices with their start and end apart: 11, of which 5 were waited for; matrix products, arithmetic and copies ran while one was open for 0% of the time, Pallas kernels for 15%

profile of v17, /device:TPU:0, one launch (start us, length us, event | category | flops | bytes accessed | tf_op | source)
XLA Modules:
  0.0 32.9 jit_solution(4647684237641615127)
XLA Ops:
  0.0 1.1 %pack_first.1 = (s32[16,128]{1,0:T(8,128)S(1)}, bf16[1936,128]{1,0:T(8,128)(2,1)S(1)}) custom-call(s32[1,24]{1,0:T(1,128)} %bitcast.6, s32[1,24]{1,0:T(1,128)} %bitcast.7, s32[2,8]{1,0:T(2,128)} %bitcast.5, bf16[24,128,128]{2,1,0:T(8,128)(2,1)} %x_in.2), custom_call_target="tpu_custom_call" | custom-call | tf_op jit(solution)/shard_map/pack_first/pallas_call | solution.py:277
  1.1 3.0 %collective-permute-start.3 = (bf16[1936,128]{1,0:T(8,128)(2,1)S(1)}, bf16[1936,128]{1,0:T(8,128)(2,1)S(1)}, u32[]{:S(2)}, u32[]{:S(2)}) collective-permute-start(bf16[1936,128]{1,0:T(8,128)(2,1)S(1)} %get-tuple-element.26.refs_0_), channel_id=1, source_target_pairs={{4,0},{0,4},{5,1},{1,5},{6,2},{2,6},{7,3},{3,7},{12,8},{8,12},{13,... | collective-permute-start | bytes 1486856 | tf_op jit(solution)/shard_map/ppermute | solution.py:41
  4.1 1.1 %pack_later.1 = (bf16[528,128]{1,0:T(8,128)(2,1)S(1)}, bf16[1152,128]{1,0:T(8,128)(2,1)S(1)}) custom-call(bf16[24,128,128]{2,1,0:T(8,128)(2,1)} %x_in.2, s32[2,2]{1,0:T(2,128)} %s_cols, bf16[4,128,128]{2,1,0:T(8,128)(2,1)} %bitcast.4), custom_call_target="tpu_custom_call" | custom-call | tf_op jit(solution)/shard_map/pack_later/pallas_call | solution.py:304
  5.2 1.6 %collective-permute-start.1 = (bf16[528,128]{1,0:T(8,128)(2,1)S(1)}, bf16[528,128]{1,0:T(8,128)(2,1)S(1)}, u32[]{:S(2)}, u32[]{:S(2)}) collective-permute-start(bf16[528,128]{1,0:T(8,128)(2,1)S(1)} %get-tuple-element.31.refs_2_), channel_id=1, source_target_pairs={{0,16},{8,24},{16,0},{24,8},{1,17},{9,25},{17,1},{25,9},{2,18},{10... | collective-permute-start | bytes 405512 | tf_op jit(solution)/shard_map/ppermute | solution.py:27
  6.8 0.0 collective-permute-start
  6.8 3.5 %collective-permute-done.1.refs_4_ = bf16[528,128]{1,0:T(8,128)(2,1)S(1)} collective-permute-done((bf16[528,128]{1,0:T(8,128)(2,1)S(1)}, bf16[528,128]{1,0:T(8,128)(2,1)S(1)}, u32[]{:S(2)}, u32[]{:S(2)}) %collective-permute-start.1) | collective-permute-done | bytes 135200 | tf_op jit(solution)/shard_map/ppermute | solution.py:27
  10.4 0.0 collective-permute-start.2
  10.4 0.0 collective-permute-done.refs_3_
  10.4 1.3 %collective-permute-done.2.refs_5_ = bf16[528,128]{1,0:T(8,128)(2,1)S(1)} collective-permute-done((bf16[528,128]{1,0:T(8,128)(2,1)S(1)}, bf16[528,128]{1,0:T(8,128)(2,1)S(1)}, u32[]{:S(2)}, u32[]{:S(2)}) %collective-permute-start.2) | collective-permute-done | bytes 135200 | tf_op jit(solution)/shard_map/ppermute | solution.py:27
  11.7 0.3 collective-permute-start.7
  12.0 1.3 %own_products.1 = (f32[17,128,128]{2,1,0:T(8,128)S(1)}, bf16[16,128,128]{2,1,0:T(8,128)(2,1)S(1)}, s32[8,128]{1,0:T(8,128)S(1)}) custom-call(s32[16,128]{1,0:T(8,128)S(1)} %get-tuple-element.25.known.refs_0_, bf16[1936,128]{1,0:T(8,128)(2,1)S(1)} %get-tuple-element.26.refs_0_, bf16[1152,128]{1,0:T(8,128)(2,1)S(1)} %get-tuple-element.40.refs_1_, ...), custom_call_target="tpu_custom_call" | custom-call | flops 50331648 | bytes 2883584 | tf_op jit(solution)/shard_map/own_products/pallas_call | solution.py:329
  13.3 2.9 %collective-permute-done.3.refs_2_ = bf16[1936,128]{1,0:T(8,128)(2,1)S(1)} collective-permute-done((bf16[1936,128]{1,0:T(8,128)(2,1)S(1)}, bf16[1936,128]{1,0:T(8,128)(2,1)S(1)}, u32[]{:S(2)}, u32[]{:S(2)}) %collective-permute-start.3) | collective-permute-done | bytes 495648 | tf_op jit(solution)/shard_map/ppermute | solution.py:41
  16.3 1.2 %peer_products_0.1 = (f32[4,80,128]{2,1,0:T(8,128)S(1)}, s32[160,128]{1,0:T(8,128)S(1)}, s32[160,128]{1,0:T(8,128)S(1)}, s32[160,128]{1,0:T(8,128)S(1)}, s32[1,8,128]{2,1,0:T(8,128)S(1)}) custom-call(s32[16,128]{1,0:T(8,128)S(1)} %get-tuple-element.25.known.refs_0_, s32[8,128]{1,0:T(8,128)S(1)} %get-tuple-element.32.refs_1_, ...), custom_call_target="tpu_custom_call" | custom-call | flops 31457280 | bytes 1703936 | tf_op jit(solution)/shard_map/peer_products_0/pallas_call | solution.py:363
  17.5 3.2 %collective-permute-start.4 = (s32[160,128]{1,0:T(8,128)S(1)}, s32[160,128]{1,0:T(8,128)S(1)}, u32[]{:S(2)}, u32[]{:S(2)}) collective-permute-start(s32[160,128]{1,0:T(8,128)S(1)} %get-tuple-element.36), channel_id=1, source_target_pairs={{0,2},{1,3},{2,0},{3,1},{4,6},{5,7},{6,4},{7,5},{8,10},{9,11},{10,... | collective-permute-start | bytes 245768 | tf_op jit(solution)/shard_map/ppermute | solution.py:27
  20.7 1.3 %collective-permute-start.5 = (s32[160,128]{1,0:T(8,128)S(1)}, s32[160,128]{1,0:T(8,128)S(1)}, u32[]{:S(2)}, u32[]{:S(2)}) collective-permute-start(s32[160,128]{1,0:T(8,128)S(1)} %get-tuple-element.37), channel_id=1, source_target_pairs={{0,3},{1,2},{2,1},{3,0},{4,7},{5,6},{6,5},{7,4},{8,11},{9,10},{10,... | collective-permute-start | bytes 245768 | tf_op jit(solution)/shard_map/ppermute | solution.py:27
  22.1 0.2 collective-permute-start.6
  22.3 0.0 collective-permute-done.7.refs_1_
  22.3 1.0 %peer_products_80.1 = (f32[4,48,128]{2,1,0:T(8,128)S(1)}, s32[96,128]{1,0:T(8,128)S(1)}, s32[96,128]{1,0:T(8,128)S(1)}, s32[96,128]{1,0:T(8,128)S(1)}) custom-call(s32[1,8,128]{2,1,0:T(8,128)S(1)} %get-tuple-element.39.refs_0_, bf16[1152,128]{1,0:T(8,128)(2,1)S(1)} %collective-permute-done.7.refs_1_, ...), custom_call_target="tpu_custom_call" | custom-call | flops 18874368 | bytes 1703936 | tf_op jit(solution)/shard_map/peer_products_80/pallas_call | solution.py:363
  23.3 2.9 %collective-permute-start.10 = (s32[96,128]{1,0:T(8,128)S(1)}, s32[96,128]{1,0:T(8,128)S(1)}, u32[]{:S(2)}, u32[]{:S(2)}) collective-permute-start(s32[96,128]{1,0:T(8,128)S(1)} %get-tuple-element.44), channel_id=1, source_target_pairs={{0,2},{1,3},{2,0},{3,1},{4,6},{5,7},{6,4},{7,5},{8,10},{9,11},{10,... | collective-permute-start | bytes 147464 | tf_op jit(solution)/shard_map/ppermute | solution.py:27
  26.2 1.3 %collective-permute-start.8 = (s32[96,128]{1,0:T(8,128)S(1)}, s32[96,128]{1,0:T(8,128)S(1)}, u32[]{:S(2)}, u32[]{:S(2)}) collective-permute-start(s32[96,128]{1,0:T(8,128)S(1)} %get-tuple-element.42), channel_id=1, source_target_pairs={{0,3},{1,2},{2,1},{3,0},{4,7},{5,6},{6,5},{7,4},{8,11},{9,10},{10,... | collective-permute-start | bytes 147464 | tf_op jit(solution)/shard_map/ppermute | solution.py:27
  27.6 0.0 collective-permute-done.4.refs_1_
  27.6 0.0 collective-permute-start.9
  27.6 0.0 collective-permute-done.5.refs_2_
  27.6 0.0 collective-permute-done.6.refs_3_
  27.6 0.1 finish_0.1.refs_0_
  27.7 2.5 %collective-permute-done.10.refs_4_ = s32[96,128]{1,0:T(8,128)S(1)} collective-permute-done((s32[96,128]{1,0:T(8,128)S(1)}, s32[96,128]{1,0:T(8,128)S(1)}, u32[]{:S(2)}, u32[]{:S(2)}) %collective-permute-start.10) | collective-permute-done | bytes 49184 | tf_op jit(solution)/shard_map/ppermute | solution.py:27
  30.3 1.9 %collective-permute-done.8.refs_2_ = s32[96,128]{1,0:T(8,128)S(1)} collective-permute-done((s32[96,128]{1,0:T(8,128)S(1)}, s32[96,128]{1,0:T(8,128)S(1)}, u32[]{:S(2)}, u32[]{:S(2)}) %collective-permute-start.8) | collective-permute-done | bytes 49184 | tf_op jit(solution)/shard_map/ppermute | solution.py:27
  32.2 0.0 collective-permute-done.9.refs_3_
  32.2 0.7 %finish_80.1 = bf16[2,2,128,128]{3,2,1,0:T(8,128)(2,1)} custom-call(bf16[2,2,80,128]{3,2,1,0:T(8,128)(2,1)S(1)} %finish_0.1.refs_0_, f32[4,48,128]{2,1,0:T(8,128)S(1)} %get-tuple-element.41.refs_1_, s32[96,128]{1,0:T(8,128)S(1)} %collective-permute-done.8.refs_2_, s32[96,128]{1,0:T(8,128)S(1)} %collective-permute-done.9.refs_3_, ...), custom_call_target="tpu_custom_call" | custom-call | tf_op jit(solution)/shard_map/finish_80/pallas_call | solution.py:391
Async XLA Ops:
  1.1 15.1 %collective-permute-start.3 = (bf16[1936,128]{1,0:T(8,128)(2,1)S(1)}, bf16[1936,128]{1,0:T(8,128)(2,1)S(1)}, u32[]{:S(2)}, u32[]{:S(2)}) collective-permute-start(bf16[1936,128]{1,0:T(8,128)(2,1)S(1)} %get-tuple-element.26.refs_0_), channel_id=1, source_target_pairs={{4,0},{0,4},{5,1},{1,5},{6,2},{2,6},{7,3},{3,7},{12,8},{8,12},{13,... | collective-permute-start | bytes 1486856 | tf_op jit(solution)/shard_map/ppermute | solution.py:41
  5.2 5.1 %collective-permute-start.1 = (bf16[528,128]{1,0:T(8,128)(2,1)S(1)}, bf16[528,128]{1,0:T(8,128)(2,1)S(1)}, u32[]{:S(2)}, u32[]{:S(2)}) collective-permute-start(bf16[528,128]{1,0:T(8,128)(2,1)S(1)} %get-tuple-element.31.refs_2_), channel_id=1, source_target_pairs={{0,16},{8,24},{16,0},{24,8},{1,17},{9,25},{17,1},{25,9},{2,18},{10... | collective-permute-start | bytes 405512 | tf_op jit(solution)/shard_map/ppermute | solution.py:27
  6.8 3.5 %collective-permute-start = (bf16[528,128]{1,0:T(8,128)(2,1)S(1)}, bf16[528,128]{1,0:T(8,128)(2,1)S(1)}, u32[]{:S(2)}, u32[]{:S(2)}) collective-permute-start(bf16[528,128]{1,0:T(8,128)(2,1)S(1)} %get-tuple-element.31.refs_2_), channel_id=1, source_target_pairs={{0,8},{8,0},{16,24},{24,16},{1,9},{9,1},{17,25},{25,17},{2,10},{10... | collective-permute-start | bytes 405512 | tf_op jit(solution)/shard_map/ppermute | solution.py:27
  10.4 1.4 %collective-permute-start.2 = (bf16[528,128]{1,0:T(8,128)(2,1)S(1)}, bf16[528,128]{1,0:T(8,128)(2,1)S(1)}, u32[]{:S(2)}, u32[]{:S(2)}) collective-permute-start(bf16[528,128]{1,0:T(8,128)(2,1)S(1)} %collective-permute-done.1.refs_4_), channel_id=1, source_target_pairs={{0,8},{8,0},{16,24},{24,16},{1,9},{9,1},{17,25},{25,17},{2,10},{10... | collective-permute-start | bytes 405512 | tf_op jit(solution)/shard_map/ppermute | solution.py:27
  11.7 10.6 %collective-permute-start.7 = (bf16[1152,128]{1,0:T(8,128)(2,1)S(1)}, bf16[1152,128]{1,0:T(8,128)(2,1)S(1)}, u32[]{:S(2)}, u32[]{:S(2)}) collective-permute-start(bf16[1152,128]{1,0:T(8,128)(2,1)S(1)} %get-tuple-element.40.refs_1_), channel_id=1, source_target_pairs={{4,0},{0,4},{5,1},{1,5},{6,2},{2,6},{7,3},{3,7},{12,8},{8,12},{13,... | collective-permute-start | bytes 884744 | tf_op jit(solution)/shard_map/ppermute | solution.py:41
  17.5 10.1 %collective-permute-start.4 = (s32[160,128]{1,0:T(8,128)S(1)}, s32[160,128]{1,0:T(8,128)S(1)}, u32[]{:S(2)}, u32[]{:S(2)}) collective-permute-start(s32[160,128]{1,0:T(8,128)S(1)} %get-tuple-element.36), channel_id=1, source_target_pairs={{0,2},{1,3},{2,0},{3,1},{4,6},{5,7},{6,4},{7,5},{8,10},{9,11},{10,... | collective-permute-start | bytes 245768 | tf_op jit(solution)/shard_map/ppermute | solution.py:27
  20.7 6.9 %collective-permute-start.5 = (s32[160,128]{1,0:T(8,128)S(1)}, s32[160,128]{1,0:T(8,128)S(1)}, u32[]{:S(2)}, u32[]{:S(2)}) collective-permute-start(s32[160,128]{1,0:T(8,128)S(1)} %get-tuple-element.37), channel_id=1, source_target_pairs={{0,3},{1,2},{2,1},{3,0},{4,7},{5,6},{6,5},{7,4},{8,11},{9,10},{10,... | collective-permute-start | bytes 245768 | tf_op jit(solution)/shard_map/ppermute | solution.py:27
  22.1 5.6 %collective-permute-start.6 = (s32[160,128]{1,0:T(8,128)S(1)}, s32[160,128]{1,0:T(8,128)S(1)}, u32[]{:S(2)}, u32[]{:S(2)}) collective-permute-start(s32[160,128]{1,0:T(8,128)S(1)} %get-tuple-element.38), channel_id=1, source_target_pairs={{0,1},{1,0},{2,3},{3,2},{4,5},{5,4},{6,7},{7,6},{8,9},{9,8},{10,11... | collective-permute-start | bytes 245768 | tf_op jit(solution)/shard_map/ppermute | solution.py:27
  23.3 6.9 %collective-permute-start.10 = (s32[96,128]{1,0:T(8,128)S(1)}, s32[96,128]{1,0:T(8,128)S(1)}, u32[]{:S(2)}, u32[]{:S(2)}) collective-permute-start(s32[96,128]{1,0:T(8,128)S(1)} %get-tuple-element.44), channel_id=1, source_target_pairs={{0,2},{1,3},{2,0},{3,1},{4,6},{5,7},{6,4},{7,5},{8,10},{9,11},{10,... | collective-permute-start | bytes 147464 | tf_op jit(solution)/shard_map/ppermute | solution.py:27
  26.2 6.0 %collective-permute-start.8 = (s32[96,128]{1,0:T(8,128)S(1)}, s32[96,128]{1,0:T(8,128)S(1)}, u32[]{:S(2)}, u32[]{:S(2)}) collective-permute-start(s32[96,128]{1,0:T(8,128)S(1)} %get-tuple-element.42), channel_id=1, source_target_pairs={{0,3},{1,2},{2,1},{3,0},{4,7},{5,6},{6,5},{7,4},{8,11},{9,10},{10,... | collective-permute-start | bytes 147464 | tf_op jit(solution)/shard_map/ppermute | solution.py:27
  27.6 4.6 %collective-permute-start.9 = (s32[96,128]{1,0:T(8,128)S(1)}, s32[96,128]{1,0:T(8,128)S(1)}, u32[]{:S(2)}, u32[]{:S(2)}) collective-permute-start(s32[96,128]{1,0:T(8,128)S(1)} %get-tuple-element.43), channel_id=1, source_target_pairs={{0,1},{1,0},{2,3},{3,2},{4,5},{5,4},{6,7},{7,6},{8,9},{9,8},{10,11... | collective-permute-start | bytes 147464 | tf_op jit(solution)/shard_map/ppermute | solution.py:27

commit v18 on v17

--- a/solution.py
+++ b/solution.py
@@ -321,10 +321,6 @@
     )(*in_hbm(later_blocks, later_s_cols, later_s))
     x_sent = [x_first, *x_later]
     s_pieces = gathered(s_sent, "row")
-    later, _ = lax.optimization_barrier((x_sent[1:], s_pieces))
-    x_pieces = [first_piece]
-    x_pieces += [[shifted(part, "col", j) for j in range(1, cols)] for part in later]
-
     moved = block_size * (4 * all_slots + 4 * panel_size + 2 * count)
     totals, panel, panel_cols = pl.pallas_call(
         functools.partial(
@@ -351,6 +347,10 @@
     )(known, *x_sent, *s_pieces)
 
     moved = block_size * (8 * all_slots + 2 * panel_size + 2 * count * (cols - 1))
+    later, panel_cols = lax.optimization_barrier((x_sent[1:], panel_cols))
+    x_pieces = [first_piece]
+    x_pieces += [[shifted(part, "col", j) for j in range(1, cols)] for part in later]
+
     code_shape = (cols - 1, code_height, LANES)
     finished, plan = [], []
     for (at, height), pieces in zip(ranges, x_pieces):

time: 33.1 us -> 33 us (level)
  Pallas kernels: 6.62 us -> 7.55 us
  starting transfers between devices: 13.9 us -> 13 us
    ppermute x9, starting transfers between devices: 10.6 us -> 9.61 us  [flipped(): lax.ppermute(value, axis, [(i, i ^ bits) for i in range(lax.axis_size(axi...]
    pallas_call x1, Pallas kernels: 1.3 us -> 1.77 us  [per_device(): pl.pallas_call(functools.partial(own_kernel, (rows, count, piece_rows, wi...]
    pallas_call x2, Pallas kernels: 2.26 us -> 2.73 us  [per_device(): pl.pallas_call(functools.partial(peer_kernel, (cols, layers, count, width...]
  transfers between devices with their start and end apart: 11 -> 11, of which waited for: 5 -> 7; matrix products, arithmetic and copies ran while one was open for 0% -> 0% of each run, Pallas kernels for 15% -> 17%
where the time goes in v18:
time: 33 us; the launch traced here: 32.8 us
  starting transfers between devices  13 us (39%)
  waiting for transfers between devices  12.2 us (37%)
  Pallas kernels  7.55 us (23%)
    ppermute x9, starting transfers between devices, flipped(): lax.ppermute(value, axis, [(i, i ^ bits) for i in range(lax.axis_size(axi...  9.61 us
    ppermute x9, waiting for transfers between devices, flipped(): lax.ppermute(value, axis, [(i, i ^ bits) for i in range(lax.axis_size(axi...  9.37 us
    ppermute x2, starting transfers between devices, shifted(): lax.ppermute(value, axis, [((i + offset) % size, i) for i in range(size)])  3.37 us
    ppermute x2, waiting for transfers between devices, shifted(): lax.ppermute(value, axis, [((i + offset) % size, i) for i in range(size)])  2.8 us
    pallas_call x2, Pallas kernels, per_device(): pl.pallas_call(functools.partial(peer_kernel, (cols, layers, count, width...  2.73 us
    pallas_call x1, Pallas kernels, per_device(): pl.pallas_call(functools.partial(own_kernel, (rows, count, piece_rows, wi...  1.77 us
    pallas_call x1, Pallas kernels, per_device(): pl.pallas_call(functools.partial(pack_first_kernel, (layers, count, piece...  1.11 us
    pallas_call x1, Pallas kernels, per_device(): pl.pallas_call(functools.partial(pack_later_kernel, (count, piece, order,...  1.11 us
  transfers between devices with their start and end apart: 11, of which 7 were waited for; matrix products, arithmetic and copies ran while one was open for 0% of the time, Pallas kernels for 17%

profile of v18, /device:TPU:0, one launch (start us, length us, event | category | flops | bytes accessed | tf_op | source)
XLA Modules:
  0.0 32.8 jit_solution(1626666252963324185)
XLA Ops:
  0.0 1.1 %pack_first.1 = (s32[16,128]{1,0:T(8,128)S(1)}, bf16[1936,128]{1,0:T(8,128)(2,1)S(1)}) custom-call(s32[1,24]{1,0:T(1,128)} %bitcast.6, s32[1,24]{1,0:T(1,128)} %bitcast.7, s32[2,8]{1,0:T(2,128)} %bitcast.5, bf16[24,128,128]{2,1,0:T(8,128)(2,1)} %x_in.2), custom_call_target="tpu_custom_call" | custom-call | tf_op jit(solution)/shard_map/pack_first/pallas_call | solution.py:277
  1.1 3.0 %collective-permute-start.3 = (bf16[1936,128]{1,0:T(8,128)(2,1)S(1)}, bf16[1936,128]{1,0:T(8,128)(2,1)S(1)}, u32[]{:S(2)}, u32[]{:S(2)}) collective-permute-start(bf16[1936,128]{1,0:T(8,128)(2,1)S(1)} %get-tuple-element.31.refs_0_), channel_id=1, source_target_pairs={{4,0},{0,4},{5,1},{1,5},{6,2},{2,6},{7,3},{3,7},{12,8},{8,12},{13,... | collective-permute-start | bytes 1486856 | tf_op jit(solution)/shard_map/ppermute | solution.py:41
  4.1 1.1 %pack_later.1 = (bf16[528,128]{1,0:T(8,128)(2,1)S(1)}, bf16[1152,128]{1,0:T(8,128)(2,1)S(1)}) custom-call(bf16[24,128,128]{2,1,0:T(8,128)(2,1)} %x_in.2, s32[2,2]{1,0:T(2,128)} %s_cols, bf16[4,128,128]{2,1,0:T(8,128)(2,1)} %bitcast.4), custom_call_target="tpu_custom_call" | custom-call | tf_op jit(solution)/shard_map/pack_later/pallas_call | solution.py:304
  5.2 1.6 %collective-permute-start.1 = (bf16[528,128]{1,0:T(8,128)(2,1)S(1)}, bf16[528,128]{1,0:T(8,128)(2,1)S(1)}, u32[]{:S(2)}, u32[]{:S(2)}) collective-permute-start(bf16[528,128]{1,0:T(8,128)(2,1)S(1)} %get-tuple-element.32.refs_2_), channel_id=1, source_target_pairs={{0,16},{8,24},{16,0},{24,8},{1,17},{9,25},{17,1},{25,9},{2,18},{10... | collective-permute-start | bytes 405512 | tf_op jit(solution)/shard_map/ppermute | solution.py:27
  6.8 0.0 collective-permute-start
  6.8 3.5 %collective-permute-done.1.refs_4_ = bf16[528,128]{1,0:T(8,128)(2,1)S(1)} collective-permute-done((bf16[528,128]{1,0:T(8,128)(2,1)S(1)}, bf16[528,128]{1,0:T(8,128)(2,1)S(1)}, u32[]{:S(2)}, u32[]{:S(2)}) %collective-permute-start.1) | collective-permute-done | bytes 135200 | tf_op jit(solution)/shard_map/ppermute | solution.py:27
  10.4 0.0 collective-permute-start.2
  10.4 0.0 collective-permute-done.refs_3_
  10.4 1.3 %collective-permute-done.2.refs_5_ = bf16[528,128]{1,0:T(8,128)(2,1)S(1)} collective-permute-done((bf16[528,128]{1,0:T(8,128)(2,1)S(1)}, bf16[528,128]{1,0:T(8,128)(2,1)S(1)}, u32[]{:S(2)}, u32[]{:S(2)}) %collective-permute-start.2) | collective-permute-done | bytes 135200 | tf_op jit(solution)/shard_map/ppermute | solution.py:27
  11.7 1.8 %own_products.1 = (f32[17,128,128]{2,1,0:T(8,128)S(1)}, bf16[16,128,128]{2,1,0:T(8,128)(2,1)S(1)}, s32[8,128]{1,0:T(8,128)S(1)}) custom-call(s32[16,128]{1,0:T(8,128)S(1)} %get-tuple-element.26.known.refs_0_, bf16[1936,128]{1,0:T(8,128)(2,1)S(1)} %get-tuple-element.31.refs_0_, bf16[1152,128]{1,0:T(8,128)(2,1)S(1)} %get-tuple-element.42.refs_1_, ...), custom_call_target="tpu_custom_call" | custom-call | flops 50331648 | bytes 2883584 | tf_op jit(solution)/shard_map/own_products/pallas_call | solution.py:325
  13.5 0.4 %collective-permute-start.7 = (bf16[1152,128]{1,0:T(8,128)(2,1)S(1)}, bf16[1152,128]{1,0:T(8,128)(2,1)S(1)}, u32[]{:S(2)}, u32[]{:S(2)}) collective-permute-start(bf16[1152,128]{1,0:T(8,128)(2,1)S(1)} %get-tuple-element.42.refs_1_), channel_id=1, source_target_pairs={{4,0},{0,4},{5,1},{1,5},{6,2},{2,6},{7,3},{3,7},{12,8},{8,12},{13,... | collective-permute-start | bytes 884744 | tf_op jit(solution)/shard_map/ppermute | solution.py:41
  13.9 1.8 %collective-permute-done.3.refs_2_ = bf16[1936,128]{1,0:T(8,128)(2,1)S(1)} collective-permute-done((bf16[1936,128]{1,0:T(8,128)(2,1)S(1)}, bf16[1936,128]{1,0:T(8,128)(2,1)S(1)}, u32[]{:S(2)}, u32[]{:S(2)}) %collective-permute-start.3) | collective-permute-done | bytes 495648 | tf_op jit(solution)/shard_map/ppermute | solution.py:41
  15.7 1.5 %peer_products_0.1 = (f32[4,80,128]{2,1,0:T(8,128)S(1)}, s32[160,128]{1,0:T(8,128)S(1)}, s32[160,128]{1,0:T(8,128)S(1)}, s32[160,128]{1,0:T(8,128)S(1)}, s32[1,8,128]{2,1,0:T(8,128)S(1)}) custom-call(s32[16,128]{1,0:T(8,128)S(1)} %get-tuple-element.26.known.refs_0_, s32[8,128]{1,0:T(8,128)S(1)} %get-tuple-element.34.refs_1_, ...), custom_call_target="tpu_custom_call" | custom-call | flops 31457280 | bytes 1703936 | tf_op jit(solution)/shard_map/peer_products_0/pallas_call | solution.py:363
  17.1 2.4 %collective-permute-start.4 = (s32[160,128]{1,0:T(8,128)S(1)}, s32[160,128]{1,0:T(8,128)S(1)}, u32[]{:S(2)}, u32[]{:S(2)}) collective-permute-start(s32[160,128]{1,0:T(8,128)S(1)} %get-tuple-element.38), channel_id=1, source_target_pairs={{0,2},{1,3},{2,0},{3,1},{4,6},{5,7},{6,4},{7,5},{8,10},{9,11},{10,... | collective-permute-start | bytes 245768 | tf_op jit(solution)/shard_map/ppermute | solution.py:27
  19.6 1.6 %collective-permute-start.5 = (s32[160,128]{1,0:T(8,128)S(1)}, s32[160,128]{1,0:T(8,128)S(1)}, u32[]{:S(2)}, u32[]{:S(2)}) collective-permute-start(s32[160,128]{1,0:T(8,128)S(1)} %get-tuple-element.39), channel_id=1, source_target_pairs={{0,3},{1,2},{2,1},{3,0},{4,7},{5,6},{6,5},{7,4},{8,11},{9,10},{10,... | collective-permute-start | bytes 245768 | tf_op jit(solution)/shard_map/ppermute | solution.py:27
  21.2 0.0 collective-permute-start.6
  21.2 1.0 %collective-permute-done.7.refs_1_ = bf16[1152,128]{1,0:T(8,128)(2,1)S(1)} collective-permute-done((bf16[1152,128]{1,0:T(8,128)(2,1)S(1)}, bf16[1152,128]{1,0:T(8,128)(2,1)S(1)}, u32[]{:S(2)}, u32[]{:S(2)}) %collective-permute-start.7) | collective-permute-done | bytes 294944 | tf_op jit(solution)/shard_map/ppermute | solution.py:41
  22.1 1.3 %peer_products_80.1 = (f32[4,48,128]{2,1,0:T(8,128)S(1)}, s32[96,128]{1,0:T(8,128)S(1)}, s32[96,128]{1,0:T(8,128)S(1)}, s32[96,128]{1,0:T(8,128)S(1)}) custom-call(s32[1,8,128]{2,1,0:T(8,128)S(1)} %get-tuple-element.41.refs_0_, bf16[1152,128]{1,0:T(8,128)(2,1)S(1)} %collective-permute-done.7.refs_1_, ...), custom_call_target="tpu_custom_call" | custom-call | flops 18874368 | bytes 1703936 | tf_op jit(solution)/shard_map/peer_products_80/pallas_call | solution.py:363
  23.4 2.4 %collective-permute-start.10 = (s32[96,128]{1,0:T(8,128)S(1)}, s32[96,128]{1,0:T(8,128)S(1)}, u32[]{:S(2)}, u32[]{:S(2)}) collective-permute-start(s32[96,128]{1,0:T(8,128)S(1)} %get-tuple-element.46), channel_id=1, source_target_pairs={{0,2},{1,3},{2,0},{3,1},{4,6},{5,7},{6,4},{7,5},{8,10},{9,11},{10,... | collective-permute-start | bytes 147464 | tf_op jit(solution)/shard_map/ppermute | solution.py:27
  25.9 1.6 %collective-permute-start.8 = (s32[96,128]{1,0:T(8,128)S(1)}, s32[96,128]{1,0:T(8,128)S(1)}, u32[]{:S(2)}, u32[]{:S(2)}) collective-permute-start(s32[96,128]{1,0:T(8,128)S(1)} %get-tuple-element.44), channel_id=1, source_target_pairs={{0,3},{1,2},{2,1},{3,0},{4,7},{5,6},{6,5},{7,4},{8,11},{9,10},{10,... | collective-permute-start | bytes 147464 | tf_op jit(solution)/shard_map/ppermute | solution.py:27
  27.4 0.0 collective-permute-done.4.refs_1_
  27.4 0.0 collective-permute-start.9
  27.4 0.0 collective-permute-done.5.refs_2_
  27.4 0.0 collective-permute-done.6.refs_3_
  27.4 0.1 finish_0.1.refs_0_
  27.5 1.0 %collective-permute-done.10.refs_4_ = s32[96,128]{1,0:T(8,128)S(1)} collective-permute-done((s32[96,128]{1,0:T(8,128)S(1)}, s32[96,128]{1,0:T(8,128)S(1)}, u32[]{:S(2)}, u32[]{:S(2)}) %collective-permute-start.10) | collective-permute-done | bytes 49184 | tf_op jit(solution)/shard_map/ppermute | solution.py:27
  28.5 3.3 %collective-permute-done.8.refs_2_ = s32[96,128]{1,0:T(8,128)S(1)} collective-permute-done((s32[96,128]{1,0:T(8,128)S(1)}, s32[96,128]{1,0:T(8,128)S(1)}, u32[]{:S(2)}, u32[]{:S(2)}) %collective-permute-start.8) | collective-permute-done | bytes 49184 | tf_op jit(solution)/shard_map/ppermute | solution.py:27
  31.8 0.2 collective-permute-done.9.refs_3_
  32.0 0.7 %finish_80.1 = bf16[2,2,128,128]{3,2,1,0:T(8,128)(2,1)} custom-call(bf16[2,2,80,128]{3,2,1,0:T(8,128)(2,1)S(1)} %finish_0.1.refs_0_, f32[4,48,128]{2,1,0:T(8,128)S(1)} %get-tuple-element.43.refs_1_, s32[96,128]{1,0:T(8,128)S(1)} %collective-permute-done.8.refs_2_, s32[96,128]{1,0:T(8,128)S(1)} %collective-permute-done.9.refs_3_, ...), custom_call_target="tpu_custom_call" | custom-call | tf_op jit(solution)/shard_map/finish_80/pallas_call | solution.py:391
Async XLA Ops:
  1.1 14.5 %collective-permute-start.3 = (bf16[1936,128]{1,0:T(8,128)(2,1)S(1)}, bf16[1936,128]{1,0:T(8,128)(2,1)S(1)}, u32[]{:S(2)}, u32[]{:S(2)}) collective-permute-start(bf16[1936,128]{1,0:T(8,128)(2,1)S(1)} %get-tuple-element.31.refs_0_), channel_id=1, source_target_pairs={{4,0},{0,4},{5,1},{1,5},{6,2},{2,6},{7,3},{3,7},{12,8},{8,12},{13,... | collective-permute-start | bytes 1486856 | tf_op jit(solution)/shard_map/ppermute | solution.py:41
  5.2 5.1 %collective-permute-start.1 = (bf16[528,128]{1,0:T(8,128)(2,1)S(1)}, bf16[528,128]{1,0:T(8,128)(2,1)S(1)}, u32[]{:S(2)}, u32[]{:S(2)}) collective-permute-start(bf16[528,128]{1,0:T(8,128)(2,1)S(1)} %get-tuple-element.32.refs_2_), channel_id=1, source_target_pairs={{0,16},{8,24},{16,0},{24,8},{1,17},{9,25},{17,1},{25,9},{2,18},{10... | collective-permute-start | bytes 405512 | tf_op jit(solution)/shard_map/ppermute | solution.py:27
  6.8 3.5 %collective-permute-start = (bf16[528,128]{1,0:T(8,128)(2,1)S(1)}, bf16[528,128]{1,0:T(8,128)(2,1)S(1)}, u32[]{:S(2)}, u32[]{:S(2)}) collective-permute-start(bf16[528,128]{1,0:T(8,128)(2,1)S(1)} %get-tuple-element.32.refs_2_), channel_id=1, source_target_pairs={{0,8},{8,0},{16,24},{24,16},{1,9},{9,1},{17,25},{25,17},{2,10},{10... | collective-permute-start | bytes 405512 | tf_op jit(solution)/shard_map/ppermute | solution.py:27
  10.4 1.4 %collective-permute-start.2 = (bf16[528,128]{1,0:T(8,128)(2,1)S(1)}, bf16[528,128]{1,0:T(8,128)(2,1)S(1)}, u32[]{:S(2)}, u32[]{:S(2)}) collective-permute-start(bf16[528,128]{1,0:T(8,128)(2,1)S(1)} %collective-permute-done.1.refs_4_), channel_id=1, source_target_pairs={{0,8},{8,0},{16,24},{24,16},{1,9},{9,1},{17,25},{25,17},{2,10},{10... | collective-permute-start | bytes 405512 | tf_op jit(solution)/shard_map/ppermute | solution.py:27
  13.5 8.7 %collective-permute-start.7 = (bf16[1152,128]{1,0:T(8,128)(2,1)S(1)}, bf16[1152,128]{1,0:T(8,128)(2,1)S(1)}, u32[]{:S(2)}, u32[]{:S(2)}) collective-permute-start(bf16[1152,128]{1,0:T(8,128)(2,1)S(1)} %get-tuple-element.42.refs_1_), channel_id=1, source_target_pairs={{4,0},{0,4},{5,1},{1,5},{6,2},{2,6},{7,3},{3,7},{12,8},{8,12},{13,... | collective-permute-start | bytes 884744 | tf_op jit(solution)/shard_map/ppermute | solution.py:41
  17.1 10.3 %collective-permute-start.4 = (s32[160,128]{1,0:T(8,128)S(1)}, s32[160,128]{1,0:T(8,128)S(1)}, u32[]{:S(2)}, u32[]{:S(2)}) collective-permute-start(s32[160,128]{1,0:T(8,128)S(1)} %get-tuple-element.38), channel_id=1, source_target_pairs={{0,2},{1,3},{2,0},{3,1},{4,6},{5,7},{6,4},{7,5},{8,10},{9,11},{10,... | collective-permute-start | bytes 245768 | tf_op jit(solution)/shard_map/ppermute | solution.py:27
  19.6 7.9 %collective-permute-start.5 = (s32[160,128]{1,0:T(8,128)S(1)}, s32[160,128]{1,0:T(8,128)S(1)}, u32[]{:S(2)}, u32[]{:S(2)}) collective-permute-start(s32[160,128]{1,0:T(8,128)S(1)} %get-tuple-element.39), channel_id=1, source_target_pairs={{0,3},{1,2},{2,1},{3,0},{4,7},{5,6},{6,5},{7,4},{8,11},{9,10},{10,... | collective-permute-start | bytes 245768 | tf_op jit(solution)/shard_map/ppermute | solution.py:27
  21.2 6.3 %collective-permute-start.6 = (s32[160,128]{1,0:T(8,128)S(1)}, s32[160,128]{1,0:T(8,128)S(1)}, u32[]{:S(2)}, u32[]{:S(2)}) collective-permute-start(s32[160,128]{1,0:T(8,128)S(1)} %get-tuple-element.40), channel_id=1, source_target_pairs={{0,1},{1,0},{2,3},{3,2},{4,5},{5,4},{6,7},{7,6},{8,9},{9,8},{10,11... | collective-permute-start | bytes 245768 | tf_op jit(solution)/shard_map/ppermute | solution.py:27
  23.4 5.1 %collective-permute-start.10 = (s32[96,128]{1,0:T(8,128)S(1)}, s32[96,128]{1,0:T(8,128)S(1)}, u32[]{:S(2)}, u32[]{:S(2)}) collective-permute-start(s32[96,128]{1,0:T(8,128)S(1)} %get-tuple-element.46), channel_id=1, source_target_pairs={{0,2},{1,3},{2,0},{3,1},{4,6},{5,7},{6,4},{7,5},{8,10},{9,11},{10,... | collective-permute-start | bytes 147464 | tf_op jit(solution)/shard_map/ppermute | solution.py:27
  25.9 6.0 %collective-permute-start.8 = (s32[96,128]{1,0:T(8,128)S(1)}, s32[96,128]{1,0:T(8,128)S(1)}, u32[]{:S(2)}, u32[]{:S(2)}) collective-permute-start(s32[96,128]{1,0:T(8,128)S(1)} %get-tuple-element.44), channel_id=1, source_target_pairs={{0,3},{1,2},{2,1},{3,0},{4,7},{5,6},{6,5},{7,4},{8,11},{9,10},{10,... | collective-permute-start | bytes 147464 | tf_op jit(solution)/shard_map/ppermute | solution.py:27
  27.4 4.6 %collective-permute-start.9 = (s32[96,128]{1,0:T(8,128)S(1)}, s32[96,128]{1,0:T(8,128)S(1)}, u32[]{:S(2)}, u32[]{:S(2)}) collective-permute-start(s32[96,128]{1,0:T(8,128)S(1)} %get-tuple-element.45), channel_id=1, source_target_pairs={{0,1},{1,0},{2,3},{3,2},{4,5},{5,4},{6,7},{7,6},{8,9},{9,8},{10,11... | collective-permute-start | bytes 147464 | tf_op jit(solution)/shard_map/ppermute | solution.py:27

commit v19 on v18

--- a/solution.py
+++ b/solution.py
@@ -55,15 +55,19 @@
     tile[at + height : at + 2 * height, :width] = quotient(value, LANES)
 
 
+def copy_step(count):
+    return pl.cdiv(count, 6)
+
+
 def pack_first_kernel(sizes, a_rows, a_cols, c_cols, x_in, known, x_out, rows, cols, held, tile, sem):
     layers, count, piece_rows, width, local_rows, kept, order, height = sizes
     spot = x_out.at[pl.ds(0, count * height)].reshape(count, height, order)
-    loads = [
-        pltpu.make_async_copy(source, goal, sem.at[p])
-        for p, (source, goal) in enumerate(
-            ((a_rows, rows), (a_cols, cols), (c_cols, held), (x_in.at[:, pl.ds(0, height)], spot))
-        )
-    ]
+    pairs = [(a_rows, rows), (a_cols, cols), (c_cols, held)]
+    step = copy_step(count)
+    for n in range(0, count, step):
+        some = pl.ds(n, min(step, count - n))
+        pairs.append((x_in.at[some, pl.ds(0, height)], spot.at[some]))
+    loads = [pltpu.make_async_copy(*pair, sem.at[p]) for p, pair in enumerate(pairs)]
     for load in loads:
         load.start()
     known[...] = jnp.zeros_like(known)
@@ -87,7 +91,8 @@
         write_digits(tile, 2 * p, value)
     known[8 : 8 + kept, :local_rows] = held[...]
     x_out[count * height :] = tile[...].astype(jnp.float32).astype(jnp.bfloat16)
-    loads[3].wait()
+    for load in loads[3:]:
+        load.wait()
 
 
 def pack_later_kernel(sizes, x_in, s_cols, s_in, s_out, *refs):
@@ -129,25 +134,31 @@
         codes[s : s + 1] = word
 
 
+def list_height(count, width):
+    return (count * width // GROUP + 2 + 7) // 8 * 8
+
+
 def list_pairs(sizes, codes, pairs):
     count, width, trash = sizes
     total = jnp.int32(0)
     for n in range(count):
         for s in range(width):
             word = codes[s, n]
-            pairs[total] = word
+            pairs[quotient(total, GROUP), remainder(total, GROUP)] = word
             total += (word >= 0).astype(jnp.int32)
     for g in range(GROUP):
-        pairs[total + g] = trash
-    return total
-
-
-def add_products(left, panel, totals, pairs, total):
+        pairs[quotient(total + g, GROUP), remainder(total + g, GROUP)] = trash
+    groups = quotient(total + GROUP - 1, GROUP)
+    pairs[pairs.shape[0] - 1, 0] = groups
+    return groups
+
+
+def add_products(left, panel, totals, words_of, groups):
     height = totals.shape[1]
     mask = (1 << FIELD) - 1
 
     def one_group(group, carry):
-        words = [pairs[group * GROUP + g] for g in range(GROUP)]
+        words = words_of(group)
         products = []
         for word in words:
             at = pl.multiple_of((word >> (2 * FIELD)) * height, height)
@@ -162,7 +173,7 @@
             totals[word & mask] += product
         return carry
 
-    lax.fori_loop(0, quotient(total + GROUP - 1, GROUP), one_group, 0)
+    lax.fori_loop(0, groups, one_group, 0)
 
 
 def own_kernel(sizes, ranges, known, *refs):
@@ -184,9 +195,13 @@
         for q in range(piece):
             panel[d * piece + q] = s_in[d][q * order : (q + 1) * order]
     copy.wait()
-    total = list_pairs((count, width, totals.shape[0] - 1), numbers, pairs)
+    groups = list_pairs((count, width, totals.shape[0] - 1), numbers, pairs)
+
+    def words_of(group):
+        return [pairs[group, g] for g in range(GROUP)]
+
     for (first, height), blocks in zip(ranges, x_in):
-        add_products(blocks, panel, totals.at[:, pl.ds(first, height)], pairs, total)
+        add_products(blocks, panel, totals.at[:, pl.ds(first, height)], words_of, groups)
 
 
 def peer_kernel(sizes, span, *refs):
@@ -196,25 +211,44 @@
     if first == 0:
         known, panel_cols, *refs = refs
     else:
-        codes, *refs = refs
+        listed, *refs = refs
     x_in, refs = refs[: cols - 1], refs[cols - 1 :]
     panel, before, own, sent, refs = refs[0], refs[1], refs[2], refs[3 : 2 + layers], refs[2 + layers :]
+    totals = refs[-1]
     if first == 0:
-        codes, *refs = refs
+        listed, codes, numbers, pairs, sem, list_sem = refs[:-1]
         for j in range(cols - 1):
             digits = x_in[j][count * height :].astype(jnp.float32).astype(jnp.int32)
             place = [digits[p : p + 1] + digits[p + 1 : p + 2] * LANES for p in (0, 2, 4)]
             match(
                 (width, local_rows, kept), place, panel_cols[...], known[8 : 8 + kept], codes.at[j]
             )
-    totals, numbers, pairs, sem = refs
-    copy = pltpu.make_async_copy(codes, numbers, sem)
-    copy.start()
-    totals[...] = before[:, first : first + height]
-    copy.wait()
-    for j in range(cols - 1):
-        total = list_pairs((count, width, layers * slots), numbers.at[j], pairs)
-        add_products(x_in[j], panel, totals, pairs, total)
+        copy = pltpu.make_async_copy(codes, numbers, sem)
+        copy.start()
+        totals[...] = before[:, first : first + height]
+        copy.wait()
+        counts = [
+            list_pairs((count, width, layers * slots), numbers.at[j], pairs.at[j])
+            for j in range(cols - 1)
+        ]
+        copy = pltpu.make_async_copy(pairs, listed, list_sem)
+        copy.start()
+        for j in range(cols - 1):
+
+            def words_of(group):
+                return [pairs[j, group, g] for g in range(GROUP)]
+
+            add_products(x_in[j], panel, totals, words_of, counts[j])
+        copy.wait()
+    else:
+        totals[...] = before[:, first : first + height]
+        for j in range(cols - 1):
+
+            def words_of(group):
+                row = listed[j, pl.ds(group, 1)]
+                return [row[0, g] for g in range(GROUP)]
+
+            add_products(x_in[j], panel, totals, words_of, listed[j, listed.shape[1] - 1 :][0, 0])
 
     own[...] = totals[:slots]
     half = height // 2
@@ -290,7 +324,7 @@
             pltpu.VMEM((1, count), jnp.int32),
             pltpu.VMEM((kept, local_rows), jnp.int32),
             pltpu.VMEM((16, LANES), jnp.int32),
-            pltpu.SemaphoreType.DMA((4,)),
+            pltpu.SemaphoreType.DMA((3 + pl.cdiv(count, copy_step(count)),)),
         ],
         compiler_params=pltpu.CompilerParams(
             vmem_limit_bytes=2 * block_size * (count + 1) + 4 * MIB
@@ -336,7 +370,7 @@
         scratch_shapes=[
             pltpu.VMEM((code_height, LANES), jnp.int32),
             pltpu.SMEM((code_height, LANES), jnp.int32),
-            pltpu.SMEM((count * width + GROUP,), jnp.int32),
+            pltpu.SMEM((list_height(count, width), LANES), jnp.int32),
             pltpu.SemaphoreType.DMA,
         ],
         compiler_params=pltpu.CompilerParams(vmem_limit_bytes=moved + 4 * MIB),
@@ -352,13 +386,22 @@
     x_pieces += [[shifted(part, "col", j) for j in range(1, cols)] for part in later]
 
     code_shape = (cols - 1, code_height, LANES)
+    list_shape = (cols - 1, list_height(count, width), LANES)
     finished, plan = [], []
     for (at, height), pieces in zip(ranges, x_pieces):
         code_rows = slots * (height // 2)
         out_shape = [jax.ShapeDtypeStruct((slots, height, order), jnp.float32)]
         out_shape += [jax.ShapeDtypeStruct((code_rows, order), jnp.int32)] * (layers - 1)
+        scratch = []
         if at == 0:
-            out_shape.append(jax.ShapeDtypeStruct(code_shape, jnp.int32))
+            out_shape.append(jax.ShapeDtypeStruct(list_shape, jnp.int32))
+            scratch = [
+                pltpu.VMEM(code_shape, jnp.int32),
+                pltpu.SMEM(code_shape, jnp.int32),
+                pltpu.SMEM(list_shape, jnp.int32),
+                pltpu.SemaphoreType.DMA,
+                pltpu.SemaphoreType.DMA,
+            ]
         given = plan or (known, panel_cols)
         out = pl.pallas_call(
             functools.partial(
@@ -367,12 +410,7 @@
             out_shape=out_shape,
             in_specs=[vector] * (len(given) + cols + 1),
             out_specs=[vector] * len(out_shape),
-            scratch_shapes=[
-                pltpu.VMEM((all_slots + 1, height, order), jnp.float32),
-                pltpu.SMEM(code_shape, jnp.int32),
-                pltpu.SMEM((count * width + GROUP,), jnp.int32),
-                pltpu.SemaphoreType.DMA,
-            ],
+            scratch_shapes=[*scratch, pltpu.VMEM((all_slots + 1, height, order), jnp.float32)],
             compiler_params=pltpu.CompilerParams(vmem_limit_bytes=moved + 4 * MIB),
             cost_estimate=pl.CostEstimate(
                 flops=2 * order**2 * height * count * width // 4 * (cols - 1),

time: 33 us -> 32.6 us (0.988)
  starting transfers between devices: 13 us -> 13.8 us
  Pallas kernels: 7.55 us -> 6.78 us
    ppermute x9, starting transfers between devices: 9.61 us -> 10.4 us  [flipped(): lax.ppermute(value, axis, [(i, i ^ bits) for i in range(lax.axis_size(axi...]
    pallas_call x2, Pallas kernels: 2.73 us -> 2.22 us  [per_device(): pl.pallas_call(functools.partial(peer_kernel, (cols, layers, count, width...]
    pallas_call x1, Pallas kernels: 1.77 us -> 1.4 us  [per_device(): pl.pallas_call(functools.partial(own_kernel, (rows, count, piece_rows, wi...]
  transfers between devices with their start and end apart: 11 -> 11, of which waited for: 7 -> 7; matrix products, arithmetic and copies ran while one was open for 0% -> 0% of each run, Pallas kernels for 17% -> 15%
where the time goes in v19:
time: 32.6 us; the launch traced here: 32.7 us
  starting transfers between devices  13.8 us (42%)
  waiting for transfers between devices  12 us (37%)
  Pallas kernels  6.78 us (21%)
    ppermute x9, starting transfers between devices, flipped(): lax.ppermute(value, axis, [(i, i ^ bits) for i in range(lax.axis_size(axi...  10.4 us
    ppermute x9, waiting for transfers between devices, flipped(): lax.ppermute(value, axis, [(i, i ^ bits) for i in range(lax.axis_size(axi...  9.36 us
    ppermute x2, starting transfers between devices, shifted(): lax.ppermute(value, axis, [((i + offset) % size, i) for i in range(size)])  3.38 us
    ppermute x2, waiting for transfers between devices, shifted(): lax.ppermute(value, axis, [((i + offset) % size, i) for i in range(size)])  2.66 us
    pallas_call x2, Pallas kernels, per_device(): pl.pallas_call(functools.partial(peer_kernel, (cols, layers, count, width...  2.22 us
    pallas_call x1, Pallas kernels, per_device(): pl.pallas_call(functools.partial(own_kernel, (rows, count, piece_rows, wi...  1.4 us
    pallas_call x1, Pallas kernels, per_device(): pl.pallas_call(functools.partial(pack_first_kernel, (layers, count, piece...  1.21 us
    pallas_call x1, Pallas kernels, per_device(): pl.pallas_call(functools.partial(pack_later_kernel, (count, piece, order,...  1.11 us
  transfers between devices with their start and end apart: 11, of which 7 were waited for; matrix products, arithmetic and copies ran while one was open for 0% of the time, Pallas kernels for 15%

profile of v19, /device:TPU:0, one launch (start us, length us, event | category | flops | bytes accessed | tf_op | source)
XLA Modules:
  0.0 32.7 jit_solution(12277922471404433646)
XLA Ops:
  0.0 1.2 %pack_first.1 = (s32[16,128]{1,0:T(8,128)S(1)}, bf16[1936,128]{1,0:T(8,128)(2,1)S(1)}) custom-call(s32[1,24]{1,0:T(1,128)} %bitcast.6, s32[1,24]{1,0:T(1,128)} %bitcast.7, s32[2,8]{1,0:T(2,128)} %bitcast.5, bf16[24,128,128]{2,1,0:T(8,128)(2,1)} %x_in.2), custom_call_target="tpu_custom_call" | custom-call | tf_op jit(solution)/shard_map/pack_first/pallas_call | solution.py:311
  1.2 3.0 %collective-permute-start.3 = (bf16[1936,128]{1,0:T(8,128)(2,1)S(1)}, bf16[1936,128]{1,0:T(8,128)(2,1)S(1)}, u32[]{:S(2)}, u32[]{:S(2)}) collective-permute-start(bf16[1936,128]{1,0:T(8,128)(2,1)S(1)} %get-tuple-element.31.refs_0_), channel_id=1, source_target_pairs={{4,0},{0,4},{5,1},{1,5},{6,2},{2,6},{7,3},{3,7},{12,8},{8,12},{13,... | collective-permute-start | bytes 1486856 | tf_op jit(solution)/shard_map/ppermute | solution.py:41
  4.2 1.1 %pack_later.1 = (bf16[528,128]{1,0:T(8,128)(2,1)S(1)}, bf16[1152,128]{1,0:T(8,128)(2,1)S(1)}) custom-call(bf16[24,128,128]{2,1,0:T(8,128)(2,1)} %x_in.2, s32[2,2]{1,0:T(2,128)} %s_cols, bf16[4,128,128]{2,1,0:T(8,128)(2,1)} %bitcast.4), custom_call_target="tpu_custom_call" | custom-call | tf_op jit(solution)/shard_map/pack_later/pallas_call | solution.py:338
  5.3 1.6 %collective-permute-start.1 = (bf16[528,128]{1,0:T(8,128)(2,1)S(1)}, bf16[528,128]{1,0:T(8,128)(2,1)S(1)}, u32[]{:S(2)}, u32[]{:S(2)}) collective-permute-start(bf16[528,128]{1,0:T(8,128)(2,1)S(1)} %get-tuple-element.32.refs_2_), channel_id=1, source_target_pairs={{0,16},{8,24},{16,0},{24,8},{1,17},{9,25},{17,1},{25,9},{2,18},{10... | collective-permute-start | bytes 405512 | tf_op jit(solution)/shard_map/ppermute | solution.py:27
  6.9 0.0 collective-permute-start
  6.9 3.5 %collective-permute-done.1.refs_4_ = bf16[528,128]{1,0:T(8,128)(2,1)S(1)} collective-permute-done((bf16[528,128]{1,0:T(8,128)(2,1)S(1)}, bf16[528,128]{1,0:T(8,128)(2,1)S(1)}, u32[]{:S(2)}, u32[]{:S(2)}) %collective-permute-start.1) | collective-permute-done | bytes 135200 | tf_op jit(solution)/shard_map/ppermute | solution.py:27
  10.4 0.0 collective-permute-start.2
  10.5 0.0 collective-permute-done.refs_3_
  10.5 1.3 %collective-permute-done.2.refs_5_ = bf16[528,128]{1,0:T(8,128)(2,1)S(1)} collective-permute-done((bf16[528,128]{1,0:T(8,128)(2,1)S(1)}, bf16[528,128]{1,0:T(8,128)(2,1)S(1)}, u32[]{:S(2)}, u32[]{:S(2)}) %collective-permute-start.2) | collective-permute-done | bytes 135200 | tf_op jit(solution)/shard_map/ppermute | solution.py:27
  11.8 1.4 %own_products.1 = (f32[17,128,128]{2,1,0:T(8,128)S(1)}, bf16[16,128,128]{2,1,0:T(8,128)(2,1)S(1)}, s32[8,128]{1,0:T(8,128)S(1)}) custom-call(s32[16,128]{1,0:T(8,128)S(1)} %get-tuple-element.26.known.refs_0_, bf16[1936,128]{1,0:T(8,128)(2,1)S(1)} %get-tuple-element.31.refs_0_, bf16[1152,128]{1,0:T(8,128)(2,1)S(1)} %get-tuple-element.42.refs_1_, ...), custom_call_target="tpu_custom_call" | custom-call | flops 50331648 | bytes 2883584 | tf_op jit(solution)/shard_map/own_products/pallas_call | solution.py:359
  13.2 0.4 %collective-permute-start.7 = (bf16[1152,128]{1,0:T(8,128)(2,1)S(1)}, bf16[1152,128]{1,0:T(8,128)(2,1)S(1)}, u32[]{:S(2)}, u32[]{:S(2)}) collective-permute-start(bf16[1152,128]{1,0:T(8,128)(2,1)S(1)} %get-tuple-element.42.refs_1_), channel_id=1, source_target_pairs={{4,0},{0,4},{5,1},{1,5},{6,2},{2,6},{7,3},{3,7},{12,8},{8,12},{13,... | collective-permute-start | bytes 884744 | tf_op jit(solution)/shard_map/ppermute | solution.py:41
  13.6 2.1 %collective-permute-done.3.refs_2_ = bf16[1936,128]{1,0:T(8,128)(2,1)S(1)} collective-permute-done((bf16[1936,128]{1,0:T(8,128)(2,1)S(1)}, bf16[1936,128]{1,0:T(8,128)(2,1)S(1)}, u32[]{:S(2)}, u32[]{:S(2)}) %collective-permute-start.3) | collective-permute-done | bytes 495648 | tf_op jit(solution)/shard_map/ppermute | solution.py:41
  15.7 1.7 %peer_products_0.1 = (f32[4,80,128]{2,1,0:T(8,128)S(1)}, s32[160,128]{1,0:T(8,128)S(1)}, s32[160,128]{1,0:T(8,128)S(1)}, s32[160,128]{1,0:T(8,128)S(1)}, s32[1,8,128]{2,1,0:T(8,128)S(1)}) custom-call(s32[16,128]{1,0:T(8,128)S(1)} %get-tuple-element.26.known.refs_0_, s32[8,128]{1,0:T(8,128)S(1)} %get-tuple-element.34.refs_1_, ...), custom_call_target="tpu_custom_call" | custom-call | flops 31457280 | bytes 1703936 | tf_op jit(solution)/shard_map/peer_products_0/pallas_call | solution.py:406
  17.4 2.8 %collective-permute-start.4 = (s32[160,128]{1,0:T(8,128)S(1)}, s32[160,128]{1,0:T(8,128)S(1)}, u32[]{:S(2)}, u32[]{:S(2)}) collective-permute-start(s32[160,128]{1,0:T(8,128)S(1)} %get-tuple-element.38), channel_id=1, source_target_pairs={{0,2},{1,3},{2,0},{3,1},{4,6},{5,7},{6,4},{7,5},{8,10},{9,11},{10,... | collective-permute-start | bytes 245768 | tf_op jit(solution)/shard_map/ppermute | solution.py:27
  20.2 1.3 %collective-permute-start.5 = (s32[160,128]{1,0:T(8,128)S(1)}, s32[160,128]{1,0:T(8,128)S(1)}, u32[]{:S(2)}, u32[]{:S(2)}) collective-permute-start(s32[160,128]{1,0:T(8,128)S(1)} %get-tuple-element.39), channel_id=1, source_target_pairs={{0,3},{1,2},{2,1},{3,0},{4,7},{5,6},{6,5},{7,4},{8,11},{9,10},{10,... | collective-permute-start | bytes 245768 | tf_op jit(solution)/shard_map/ppermute | solution.py:27
  21.5 0.2 collective-permute-start.6
  21.8 0.6 %collective-permute-done.7.refs_1_ = bf16[1152,128]{1,0:T(8,128)(2,1)S(1)} collective-permute-done((bf16[1152,128]{1,0:T(8,128)(2,1)S(1)}, bf16[1152,128]{1,0:T(8,128)(2,1)S(1)}, u32[]{:S(2)}, u32[]{:S(2)}) %collective-permute-start.7) | collective-permute-done | bytes 294944 | tf_op jit(solution)/shard_map/ppermute | solution.py:41
  22.3 0.5 %peer_products_80.1 = (f32[4,48,128]{2,1,0:T(8,128)S(1)}, s32[96,128]{1,0:T(8,128)S(1)}, s32[96,128]{1,0:T(8,128)S(1)}, s32[96,128]{1,0:T(8,128)S(1)}) custom-call(s32[1,8,128]{2,1,0:T(8,128)S(1)} %get-tuple-element.41.refs_0_, bf16[1152,128]{1,0:T(8,128)(2,1)S(1)} %collective-permute-done.7.refs_1_, ...), custom_call_target="tpu_custom_call" | custom-call | flops 18874368 | bytes 1703936 | tf_op jit(solution)/shard_map/peer_products_80/pallas_call | solution.py:406
  22.8 2.6 %collective-permute-start.10 = (s32[96,128]{1,0:T(8,128)S(1)}, s32[96,128]{1,0:T(8,128)S(1)}, u32[]{:S(2)}, u32[]{:S(2)}) collective-permute-start(s32[96,128]{1,0:T(8,128)S(1)} %get-tuple-element.46), channel_id=1, source_target_pairs={{0,2},{1,3},{2,0},{3,1},{4,6},{5,7},{6,4},{7,5},{8,10},{9,11},{10,... | collective-permute-start | bytes 147464 | tf_op jit(solution)/shard_map/ppermute | solution.py:27
  25.5 1.8 %collective-permute-start.8 = (s32[96,128]{1,0:T(8,128)S(1)}, s32[96,128]{1,0:T(8,128)S(1)}, u32[]{:S(2)}, u32[]{:S(2)}) collective-permute-start(s32[96,128]{1,0:T(8,128)S(1)} %get-tuple-element.44), channel_id=1, source_target_pairs={{0,3},{1,2},{2,1},{3,0},{4,7},{5,6},{6,5},{7,4},{8,11},{9,10},{10,... | collective-permute-start | bytes 147464 | tf_op jit(solution)/shard_map/ppermute | solution.py:27
  27.3 0.0 collective-permute-done.4.refs_1_
  27.3 0.0 collective-permute-start.9
  27.3 0.0 collective-permute-done.5.refs_2_
  27.3 0.0 collective-permute-done.6.refs_3_
  27.3 0.1 finish_0.1.refs_0_
  27.4 2.8 %collective-permute-done.10.refs_4_ = s32[96,128]{1,0:T(8,128)S(1)} collective-permute-done((s32[96,128]{1,0:T(8,128)S(1)}, s32[96,128]{1,0:T(8,128)S(1)}, u32[]{:S(2)}, u32[]{:S(2)}) %collective-permute-start.10) | collective-permute-done | bytes 49184 | tf_op jit(solution)/shard_map/ppermute | solution.py:27
  30.2 1.3 %collective-permute-done.8.refs_2_ = s32[96,128]{1,0:T(8,128)S(1)} collective-permute-done((s32[96,128]{1,0:T(8,128)S(1)}, s32[96,128]{1,0:T(8,128)S(1)}, u32[]{:S(2)}, u32[]{:S(2)}) %collective-permute-start.8) | collective-permute-done | bytes 49184 | tf_op jit(solution)/shard_map/ppermute | solution.py:27
  31.5 0.4 %collective-permute-done.9.refs_3_ = s32[96,128]{1,0:T(8,128)S(1)} collective-permute-done((s32[96,128]{1,0:T(8,128)S(1)}, s32[96,128]{1,0:T(8,128)S(1)}, u32[]{:S(2)}, u32[]{:S(2)}) %collective-permute-start.9) | collective-permute-done | bytes 49184 | tf_op jit(solution)/shard_map/ppermute | solution.py:27
  31.9 0.7 %finish_80.1 = bf16[2,2,128,128]{3,2,1,0:T(8,128)(2,1)} custom-call(bf16[2,2,80,128]{3,2,1,0:T(8,128)(2,1)S(1)} %finish_0.1.refs_0_, f32[4,48,128]{2,1,0:T(8,128)S(1)} %get-tuple-element.43.refs_1_, s32[96,128]{1,0:T(8,128)S(1)} %collective-permute-done.8.refs_2_, s32[96,128]{1,0:T(8,128)S(1)} %collective-permute-done.9.refs_3_, ...), custom_call_target="tpu_custom_call" | custom-call | tf_op jit(solution)/shard_map/finish_80/pallas_call | solution.py:429
Async XLA Ops:
  1.2 14.4 %collective-permute-start.3 = (bf16[1936,128]{1,0:T(8,128)(2,1)S(1)}, bf16[1936,128]{1,0:T(8,128)(2,1)S(1)}, u32[]{:S(2)}, u32[]{:S(2)}) collective-permute-start(bf16[1936,128]{1,0:T(8,128)(2,1)S(1)} %get-tuple-element.31.refs_0_), channel_id=1, source_target_pairs={{4,0},{0,4},{5,1},{1,5},{6,2},{2,6},{7,3},{3,7},{12,8},{8,12},{13,... | collective-permute-start | bytes 1486856 | tf_op jit(solution)/shard_map/ppermute | solution.py:41
  5.3 5.1 %collective-permute-start.1 = (bf16[528,128]{1,0:T(8,128)(2,1)S(1)}, bf16[528,128]{1,0:T(8,128)(2,1)S(1)}, u32[]{:S(2)}, u32[]{:S(2)}) collective-permute-start(bf16[528,128]{1,0:T(8,128)(2,1)S(1)} %get-tuple-element.32.refs_2_), channel_id=1, source_target_pairs={{0,16},{8,24},{16,0},{24,8},{1,17},{9,25},{17,1},{25,9},{2,18},{10... | collective-permute-start | bytes 405512 | tf_op jit(solution)/shard_map/ppermute | solution.py:27
  6.9 3.5 %collective-permute-start = (bf16[528,128]{1,0:T(8,128)(2,1)S(1)}, bf16[528,128]{1,0:T(8,128)(2,1)S(1)}, u32[]{:S(2)}, u32[]{:S(2)}) collective-permute-start(bf16[528,128]{1,0:T(8,128)(2,1)S(1)} %get-tuple-element.32.refs_2_), channel_id=1, source_target_pairs={{0,8},{8,0},{16,24},{24,16},{1,9},{9,1},{17,25},{25,17},{2,10},{10... | collective-permute-start | bytes 405512 | tf_op jit(solution)/shard_map/ppermute | solution.py:27
  10.4 1.4 %collective-permute-start.2 = (bf16[528,128]{1,0:T(8,128)(2,1)S(1)}, bf16[528,128]{1,0:T(8,128)(2,1)S(1)}, u32[]{:S(2)}, u32[]{:S(2)}) collective-permute-start(bf16[528,128]{1,0:T(8,128)(2,1)S(1)} %collective-permute-done.1.refs_4_), channel_id=1, source_target_pairs={{0,8},{8,0},{16,24},{24,16},{1,9},{9,1},{17,25},{25,17},{2,10},{10... | collective-permute-start | bytes 405512 | tf_op jit(solution)/shard_map/ppermute | solution.py:27
  13.2 9.1 %collective-permute-start.7 = (bf16[1152,128]{1,0:T(8,128)(2,1)S(1)}, bf16[1152,128]{1,0:T(8,128)(2,1)S(1)}, u32[]{:S(2)}, u32[]{:S(2)}) collective-permute-start(bf16[1152,128]{1,0:T(8,128)(2,1)S(1)} %get-tuple-element.42.refs_1_), channel_id=1, source_target_pairs={{4,0},{0,4},{5,1},{1,5},{6,2},{2,6},{7,3},{3,7},{12,8},{8,12},{13,... | collective-permute-start | bytes 884744 | tf_op jit(solution)/shard_map/ppermute | solution.py:41
  17.4 9.9 %collective-permute-start.4 = (s32[160,128]{1,0:T(8,128)S(1)}, s32[160,128]{1,0:T(8,128)S(1)}, u32[]{:S(2)}, u32[]{:S(2)}) collective-permute-start(s32[160,128]{1,0:T(8,128)S(1)} %get-tuple-element.38), channel_id=1, source_target_pairs={{0,2},{1,3},{2,0},{3,1},{4,6},{5,7},{6,4},{7,5},{8,10},{9,11},{10,... | collective-permute-start | bytes 245768 | tf_op jit(solution)/shard_map/ppermute | solution.py:27
  20.2 7.2 %collective-permute-start.5 = (s32[160,128]{1,0:T(8,128)S(1)}, s32[160,128]{1,0:T(8,128)S(1)}, u32[]{:S(2)}, u32[]{:S(2)}) collective-permute-start(s32[160,128]{1,0:T(8,128)S(1)} %get-tuple-element.39), channel_id=1, source_target_pairs={{0,3},{1,2},{2,1},{3,0},{4,7},{5,6},{6,5},{7,4},{8,11},{9,10},{10,... | collective-permute-start | bytes 245768 | tf_op jit(solution)/shard_map/ppermute | solution.py:27
  21.5 5.8 %collective-permute-start.6 = (s32[160,128]{1,0:T(8,128)S(1)}, s32[160,128]{1,0:T(8,128)S(1)}, u32[]{:S(2)}, u32[]{:S(2)}) collective-permute-start(s32[160,128]{1,0:T(8,128)S(1)} %get-tuple-element.40), channel_id=1, source_target_pairs={{0,1},{1,0},{2,3},{3,2},{4,5},{5,4},{6,7},{7,6},{8,9},{9,8},{10,11... | collective-permute-start | bytes 245768 | tf_op jit(solution)/shard_map/ppermute | solution.py:27
  22.8 7.4 %collective-permute-start.10 = (s32[96,128]{1,0:T(8,128)S(1)}, s32[96,128]{1,0:T(8,128)S(1)}, u32[]{:S(2)}, u32[]{:S(2)}) collective-permute-start(s32[96,128]{1,0:T(8,128)S(1)} %get-tuple-element.46), channel_id=1, source_target_pairs={{0,2},{1,3},{2,0},{3,1},{4,6},{5,7},{6,4},{7,5},{8,10},{9,11},{10,... | collective-permute-start | bytes 147464 | tf_op jit(solution)/shard_map/ppermute | solution.py:27
  25.5 6.0 %collective-permute-start.8 = (s32[96,128]{1,0:T(8,128)S(1)}, s32[96,128]{1,0:T(8,128)S(1)}, u32[]{:S(2)}, u32[]{:S(2)}) collective-permute-start(s32[96,128]{1,0:T(8,128)S(1)} %get-tuple-element.44), channel_id=1, source_target_pairs={{0,3},{1,2},{2,1},{3,0},{4,7},{5,6},{6,5},{7,4},{8,11},{9,10},{10,... | collective-permute-start | bytes 147464 | tf_op jit(solution)/shard_map/ppermute | solution.py:27
  27.3 4.6 %collective-permute-start.9 = (s32[96,128]{1,0:T(8,128)S(1)}, s32[96,128]{1,0:T(8,128)S(1)}, u32[]{:S(2)}, u32[]{:S(2)}) collective-permute-start(s32[96,128]{1,0:T(8,128)S(1)} %get-tuple-element.45), channel_id=1, source_target_pairs={{0,1},{1,0},{2,3},{3,2},{4,5},{5,4},{6,7},{7,6},{8,9},{9,8},{10,11... | collective-permute-start | bytes 147464 | tf_op jit(solution)/shard_map/ppermute | solution.py:27

commit v20 on v19

--- a/solution.py
+++ b/solution.py
@@ -55,18 +55,10 @@
     tile[at + height : at + 2 * height, :width] = quotient(value, LANES)
 
 
-def copy_step(count):
-    return pl.cdiv(count, 6)
-
-
 def pack_first_kernel(sizes, a_rows, a_cols, c_cols, x_in, known, x_out, rows, cols, held, tile, sem):
     layers, count, piece_rows, width, local_rows, kept, order, height = sizes
     spot = x_out.at[pl.ds(0, count * height)].reshape(count, height, order)
-    pairs = [(a_rows, rows), (a_cols, cols), (c_cols, held)]
-    step = copy_step(count)
-    for n in range(0, count, step):
-        some = pl.ds(n, min(step, count - n))
-        pairs.append((x_in.at[some, pl.ds(0, height)], spot.at[some]))
+    pairs = [(a_rows, rows), (a_cols, cols), (c_cols, held), (x_in.at[:, pl.ds(0, height)], spot)]
     loads = [pltpu.make_async_copy(*pair, sem.at[p]) for p, pair in enumerate(pairs)]
     for load in loads:
         load.start()
@@ -91,8 +83,7 @@
         write_digits(tile, 2 * p, value)
     known[8 : 8 + kept, :local_rows] = held[...]
     x_out[count * height :] = tile[...].astype(jnp.float32).astype(jnp.bfloat16)
-    for load in loads[3:]:
-        load.wait()
+    loads[3].wait()
 
 
 def pack_later_kernel(sizes, x_in, s_cols, s_in, s_out, *refs):
@@ -115,7 +106,7 @@
         load.wait()
 
 
-def match(sizes, place, panel_cols, kept_cols, codes):
+def match(sizes, place, panel_cols, kept_cols):
     width, local_rows, kept = sizes
     right, goal, local = place
     wanted, held = [jnp.zeros_like(right)] * width, [jnp.zeros_like(right)] * kept
@@ -126,12 +117,14 @@
         for t in range(kept):
             held[t] = jnp.where(local == i, kept_cols[t : t + 1, i : i + 1], held[t])
     block = lax.broadcasted_iota(jnp.int32, right.shape, 1)
+    codes = []
     for s in range(width):
         word = jnp.full_like(right, -1)
         for t in range(kept):
             pair = ((block << FIELD) | (right + s)) << FIELD | (goal + t)
             word = jnp.where(held[t] == wanted[s], pair, word)
-        codes[s : s + 1] = word
+        codes.append(word)
+    return codes
 
 
 def list_height(count, width):
@@ -139,18 +132,16 @@
 
 
 def list_pairs(sizes, codes, pairs):
-    count, width, trash = sizes
+    count, trash = sizes
     total = jnp.int32(0)
     for n in range(count):
-        for s in range(width):
-            word = codes[s, n]
-            pairs[quotient(total, GROUP), remainder(total, GROUP)] = word
+        for code in codes:
+            word = code[0, n]
+            pairs[total] = word
             total += (word >= 0).astype(jnp.int32)
     for g in range(GROUP):
-        pairs[quotient(total + g, GROUP), remainder(total + g, GROUP)] = trash
-    groups = quotient(total + GROUP - 1, GROUP)
-    pairs[pairs.shape[0] - 1, 0] = groups
-    return groups
+        pairs[total + g] = trash
+    return quotient(total + GROUP - 1, GROUP)
 
 
 def add_products(left, panel, totals, words_of, groups):
@@ -179,7 +170,7 @@
 def own_kernel(sizes, ranges, known, *refs):
     rows, count, piece_rows, width, local_rows, kept, order = sizes
     x_in, s_in, refs = refs[: len(ranges)], refs[len(ranges) :][:rows], refs[len(ranges) + rows :]
-    totals, panel, panel_cols, codes, numbers, pairs, sem = refs
+    totals, panel, panel_cols, pairs = refs
     piece = piece_rows * width
     for d in range(rows):
         tile = s_in[d][piece * order :].astype(jnp.float32).astype(jnp.int32)
@@ -187,18 +178,15 @@
             tile[:piece_rows] + tile[piece_rows : 2 * piece_rows] * LANES
         )
     place = known[0:1], known[1:2], known[2:3]
-    match((width, local_rows, kept), place, panel_cols[...], known[8 : 8 + kept], codes)
-    copy = pltpu.make_async_copy(codes, numbers, sem)
-    copy.start()
+    codes = match((width, local_rows, kept), place, panel_cols[...], known[8 : 8 + kept])
     totals[...] = jnp.zeros_like(totals)
     for d in range(rows):
         for q in range(piece):
             panel[d * piece + q] = s_in[d][q * order : (q + 1) * order]
-    copy.wait()
-    groups = list_pairs((count, width, totals.shape[0] - 1), numbers, pairs)
+    groups = list_pairs((count, totals.shape[0] - 1), codes, pairs)
 
     def words_of(group):
-        return [pairs[group, g] for g in range(GROUP)]
+        return [pairs[group * GROUP + g] for g in range(GROUP)]
 
     for (first, height), blocks in zip(ranges, x_in):
         add_products(blocks, panel, totals.at[:, pl.ds(first, height)], words_of, groups)
@@ -216,30 +204,27 @@
     panel, before, own, sent, refs = refs[0], refs[1], refs[2], refs[3 : 2 + layers], refs[2 + layers :]
     totals = refs[-1]
     if first == 0:
-        listed, codes, numbers, pairs, sem, list_sem = refs[:-1]
+        listed, pairs = refs[:-1]
+        lane = lax.broadcasted_iota(jnp.int32, (1, listed.shape[2]), 1)
+        totals[...] = before[:, first : first + height]
         for j in range(cols - 1):
             digits = x_in[j][count * height :].astype(jnp.float32).astype(jnp.int32)
             place = [digits[p : p + 1] + digits[p + 1 : p + 2] * LANES for p in (0, 2, 4)]
-            match(
-                (width, local_rows, kept), place, panel_cols[...], known[8 : 8 + kept], codes.at[j]
+            codes = match(
+                (width, local_rows, kept), place, panel_cols[...], known[8 : 8 + kept]
             )
-        copy = pltpu.make_async_copy(codes, numbers, sem)
-        copy.start()
-        totals[...] = before[:, first : first + height]
-        copy.wait()
-        counts = [
-            list_pairs((count, width, layers * slots), numbers.at[j], pairs.at[j])
-            for j in range(cols - 1)
-        ]
-        copy = pltpu.make_async_copy(pairs, listed, list_sem)
-        copy.start()
-        for j in range(cols - 1):
+            groups = list_pairs((count, layers * slots), codes, pairs)
+            listed[j, listed.shape[1] - 1 :] = jnp.full(lane.shape, groups, jnp.int32)
 
             def words_of(group):
-                return [pairs[j, group, g] for g in range(GROUP)]
-
-            add_products(x_in[j], panel, totals, words_of, counts[j])
-        copy.wait()
+                words = [pairs[group * GROUP + g] for g in range(GROUP)]
+                row = jnp.zeros(lane.shape, jnp.int32)
+                for g, word in enumerate(words):
+                    row = jnp.where(lane == g, word, row)
+                listed[j, pl.ds(group, 1)] = row
+                return words
+
+            add_products(x_in[j], panel, totals, words_of, groups)
     else:
         totals[...] = before[:, first : first + height]
         for j in range(cols - 1):
@@ -302,7 +287,6 @@
     block_size = order * order
     flat_s = s_blocks.reshape(piece, order, order)
     note_height = (2 * piece_rows + 15) // 16 * 16
-    code_height = (width + 7) // 8 * 8
 
     vector = pl.BlockSpec(memory_space=pltpu.VMEM)
     far = pl.BlockSpec(memory_space=HBM)
@@ -324,7 +308,7 @@
             pltpu.VMEM((1, count), jnp.int32),
             pltpu.VMEM((kept, local_rows), jnp.int32),
             pltpu.VMEM((16, LANES), jnp.int32),
-            pltpu.SemaphoreType.DMA((3 + pl.cdiv(count, copy_step(count)),)),
+            pltpu.SemaphoreType.DMA((4,)),
         ],
         compiler_params=pltpu.CompilerParams(
             vmem_limit_bytes=2 * block_size * (count + 1) + 4 * MIB
@@ -368,10 +352,7 @@
         in_specs=[vector] * (1 + len(ranges) + rows),
         out_specs=[vector] * 3,
         scratch_shapes=[
-            pltpu.VMEM((code_height, LANES), jnp.int32),
-            pltpu.SMEM((code_height, LANES), jnp.int32),
-            pltpu.SMEM((list_height(count, width), LANES), jnp.int32),
-            pltpu.SemaphoreType.DMA,
+            pltpu.SMEM((count * width + GROUP,), jnp.int32),
         ],
         compiler_params=pltpu.CompilerParams(vmem_limit_bytes=moved + 4 * MIB),
         cost_estimate=pl.CostEstimate(
@@ -385,7 +366,6 @@
     x_pieces = [first_piece]
     x_pieces += [[shifted(part, "col", j) for j in range(1, cols)] for part in later]
 
-    code_shape = (cols - 1, code_height, LANES)
     list_shape = (cols - 1, list_height(count, width), LANES)
     finished, plan = [], []
     for (at, height), pieces in zip(ranges, x_pieces):
@@ -395,13 +375,7 @@
         scratch = []
         if at == 0:
             out_shape.append(jax.ShapeDtypeStruct(list_shape, jnp.int32))
-            scratch = [
-                pltpu.VMEM(code_shape, jnp.int32),
-                pltpu.SMEM(code_shape, jnp.int32),
-                pltpu.SMEM(list_shape, jnp.int32),
-                pltpu.SemaphoreType.DMA,
-                pltpu.SemaphoreType.DMA,
-            ]
+            scratch = [pltpu.SMEM((count * width + GROUP,), jnp.int32)]
         given = plan or (known, panel_cols)
         out = pl.pallas_call(
             functools.partial(

time: 32.6 us -> 32.1 us (0.985)
  Pallas kernels: 6.78 us -> 5.59 us
  waiting for transfers between devices: 12 us -> 12.6 us
    ppermute x2, waiting for transfers between devices: 2.66 us -> 3.53 us  [shifted(): lax.ppermute(value, axis, [((i + offset) % size, i) for i in range(size)])]
    pallas_call x1, Pallas kernels: 1.4 us -> 0.78 us  [per_device(): pl.pallas_call(functools.partial(own_kernel, (rows, count, piece_rows, wi...]
    pallas_call x2, Pallas kernels: 2.22 us -> 1.76 us  [per_device(): pl.pallas_call(functools.partial(peer_kernel, (cols, layers, count, width...]
  transfers between devices with their start and end apart: 11 -> 11, of which waited for: 7 -> 6; matrix products, arithmetic and copies ran while one was open for 0% -> 0% of each run, Pallas kernels for 15% -> 12%
where the time goes in v20:
time: 32.1 us
  starting transfers between devices  13.8 us (43%)
  waiting for transfers between devices  12.6 us (39%)
  Pallas kernels  5.59 us (17%)
    ppermute x9, starting transfers between devices, flipped(): lax.ppermute(value, axis, [(i, i ^ bits) for i in range(lax.axis_size(axi...  10.5 us
    ppermute x9, waiting for transfers between devices, flipped(): lax.ppermute(value, axis, [(i, i ^ bits) for i in range(lax.axis_size(axi...  9.07 us
    ppermute x2, waiting for transfers between devices, shifted(): lax.ppermute(value, axis, [((i + offset) % size, i) for i in range(size)])  3.53 us
    ppermute x2, starting transfers between devices, shifted(): lax.ppermute(value, axis, [((i + offset) % size, i) for i in range(size)])  3.38 us
    pallas_call x2, Pallas kernels, per_device(): pl.pallas_call(functools.partial(peer_kernel, (cols, layers, count, width...  1.76 us
    pallas_call x1, Pallas kernels, per_device(): pl.pallas_call(functools.partial(pack_first_kernel, (layers, count, piece...  1.11 us
    pallas_call x1, Pallas kernels, per_device(): pl.pallas_call(functools.partial(pack_later_kernel, (count, piece, order,...  1.11 us
    pallas_call x2, Pallas kernels, per_device(): pl.pallas_call(functools.partial(finish_kernel, (layers, slots), (at, hei...  0.83 us
  transfers between devices with their start and end apart: 11, of which 6 were waited for; matrix products, arithmetic and copies ran while one was open for 0% of the time, Pallas kernels for 12%

profile of v20, /device:TPU:0, one launch (start us, length us, event | category | flops | bytes accessed | tf_op | source)
XLA Modules:
  0.0 32.1 jit_solution(10776982566123741208)
XLA Ops:
  0.0 1.1 %pack_first.1 = (s32[16,128]{1,0:T(8,128)S(1)}, bf16[1936,128]{1,0:T(8,128)(2,1)S(1)}) custom-call(s32[1,24]{1,0:T(1,128)} %bitcast.6, s32[1,24]{1,0:T(1,128)} %bitcast.7, s32[2,8]{1,0:T(2,128)} %bitcast.5, bf16[24,128,128]{2,1,0:T(8,128)(2,1)} %x_in.2), custom_call_target="tpu_custom_call" | custom-call | tf_op jit(solution)/shard_map/pack_first/pallas_call | solution.py:295
  1.1 3.0 %collective-permute-start.3 = (bf16[1936,128]{1,0:T(8,128)(2,1)S(1)}, bf16[1936,128]{1,0:T(8,128)(2,1)S(1)}, u32[]{:S(2)}, u32[]{:S(2)}) collective-permute-start(bf16[1936,128]{1,0:T(8,128)(2,1)S(1)} %get-tuple-element.31.refs_0_), channel_id=1, source_target_pairs={{4,0},{0,4},{5,1},{1,5},{6,2},{2,6},{7,3},{3,7},{12,8},{8,12},{13,... | collective-permute-start | bytes 1486856 | tf_op jit(solution)/shard_map/ppermute | solution.py:41
  4.1 1.1 %pack_later.1 = (bf16[528,128]{1,0:T(8,128)(2,1)S(1)}, bf16[1152,128]{1,0:T(8,128)(2,1)S(1)}) custom-call(bf16[24,128,128]{2,1,0:T(8,128)(2,1)} %x_in.2, s32[2,2]{1,0:T(2,128)} %s_cols, bf16[4,128,128]{2,1,0:T(8,128)(2,1)} %bitcast.4), custom_call_target="tpu_custom_call" | custom-call | tf_op jit(solution)/shard_map/pack_later/pallas_call | solution.py:322
  5.2 1.6 %collective-permute-start.1 = (bf16[528,128]{1,0:T(8,128)(2,1)S(1)}, bf16[528,128]{1,0:T(8,128)(2,1)S(1)}, u32[]{:S(2)}, u32[]{:S(2)}) collective-permute-start(bf16[528,128]{1,0:T(8,128)(2,1)S(1)} %get-tuple-element.32.refs_2_), channel_id=1, source_target_pairs={{0,16},{8,24},{16,0},{24,8},{1,17},{9,25},{17,1},{25,9},{2,18},{10... | collective-permute-start | bytes 405512 | tf_op jit(solution)/shard_map/ppermute | solution.py:27
  6.8 0.0 collective-permute-start
  6.8 3.5 %collective-permute-done.1.refs_4_ = bf16[528,128]{1,0:T(8,128)(2,1)S(1)} collective-permute-done((bf16[528,128]{1,0:T(8,128)(2,1)S(1)}, bf16[528,128]{1,0:T(8,128)(2,1)S(1)}, u32[]{:S(2)}, u32[]{:S(2)}) %collective-permute-start.1) | collective-permute-done | bytes 135200 | tf_op jit(solution)/shard_map/ppermute | solution.py:27
  10.4 0.0 collective-permute-start.2
  10.4 0.0 collective-permute-done.refs_3_
  10.4 1.3 %collective-permute-done.2.refs_5_ = bf16[528,128]{1,0:T(8,128)(2,1)S(1)} collective-permute-done((bf16[528,128]{1,0:T(8,128)(2,1)S(1)}, bf16[528,128]{1,0:T(8,128)(2,1)S(1)}, u32[]{:S(2)}, u32[]{:S(2)}) %collective-permute-start.2) | collective-permute-done | bytes 135200 | tf_op jit(solution)/shard_map/ppermute | solution.py:27
  11.7 0.8 %own_products.1 = (f32[17,128,128]{2,1,0:T(8,128)S(1)}, bf16[16,128,128]{2,1,0:T(8,128)(2,1)S(1)}, s32[8,128]{1,0:T(8,128)S(1)}) custom-call(s32[16,128]{1,0:T(8,128)S(1)} %get-tuple-element.26.known.refs_0_, bf16[1936,128]{1,0:T(8,128)(2,1)S(1)} %get-tuple-element.31.refs_0_, bf16[1152,128]{1,0:T(8,128)(2,1)S(1)} %get-tuple-element.42.refs_1_, ...), custom_call_target="tpu_custom_call" | custom-call | flops 50331648 | bytes 2883584 | tf_op jit(solution)/shard_map/own_products/pallas_call | solution.py:343
  12.5 0.4 %collective-permute-start.7 = (bf16[1152,128]{1,0:T(8,128)(2,1)S(1)}, bf16[1152,128]{1,0:T(8,128)(2,1)S(1)}, u32[]{:S(2)}, u32[]{:S(2)}) collective-permute-start(bf16[1152,128]{1,0:T(8,128)(2,1)S(1)} %get-tuple-element.42.refs_1_), channel_id=1, source_target_pairs={{4,0},{0,4},{5,1},{1,5},{6,2},{2,6},{7,3},{3,7},{12,8},{8,12},{13,... | collective-permute-start | bytes 884744 | tf_op jit(solution)/shard_map/ppermute | solution.py:41
  12.9 3.0 %collective-permute-done.3.refs_2_ = bf16[1936,128]{1,0:T(8,128)(2,1)S(1)} collective-permute-done((bf16[1936,128]{1,0:T(8,128)(2,1)S(1)}, bf16[1936,128]{1,0:T(8,128)(2,1)S(1)}, u32[]{:S(2)}, u32[]{:S(2)}) %collective-permute-start.3) | collective-permute-done | bytes 495648 | tf_op jit(solution)/shard_map/ppermute | solution.py:41
  15.8 1.0 %peer_products_0.1 = (f32[4,80,128]{2,1,0:T(8,128)S(1)}, s32[160,128]{1,0:T(8,128)S(1)}, s32[160,128]{1,0:T(8,128)S(1)}, s32[160,128]{1,0:T(8,128)S(1)}, s32[1,8,128]{2,1,0:T(8,128)S(1)}) custom-call(s32[16,128]{1,0:T(8,128)S(1)} %get-tuple-element.26.known.refs_0_, s32[8,128]{1,0:T(8,128)S(1)} %get-tuple-element.34.refs_1_, ...), custom_call_target="tpu_custom_call" | custom-call | flops 31457280 | bytes 1703936 | tf_op jit(solution)/shard_map/peer_products_0/pallas_call | solution.py:380
  16.8 2.8 %collective-permute-start.4 = (s32[160,128]{1,0:T(8,128)S(1)}, s32[160,128]{1,0:T(8,128)S(1)}, u32[]{:S(2)}, u32[]{:S(2)}) collective-permute-start(s32[160,128]{1,0:T(8,128)S(1)} %get-tuple-element.38), channel_id=1, source_target_pairs={{0,2},{1,3},{2,0},{3,1},{4,6},{5,7},{6,4},{7,5},{8,10},{9,11},{10,... | collective-permute-start | bytes 245768 | tf_op jit(solution)/shard_map/ppermute | solution.py:27
  19.6 1.1 %collective-permute-start.5 = (s32[160,128]{1,0:T(8,128)S(1)}, s32[160,128]{1,0:T(8,128)S(1)}, u32[]{:S(2)}, u32[]{:S(2)}) collective-permute-start(s32[160,128]{1,0:T(8,128)S(1)} %get-tuple-element.39), channel_id=1, source_target_pairs={{0,3},{1,2},{2,1},{3,0},{4,7},{5,6},{6,5},{7,4},{8,11},{9,10},{10,... | collective-permute-start | bytes 245768 | tf_op jit(solution)/shard_map/ppermute | solution.py:27
  20.7 0.5 %collective-permute-start.6 = (s32[160,128]{1,0:T(8,128)S(1)}, s32[160,128]{1,0:T(8,128)S(1)}, u32[]{:S(2)}, u32[]{:S(2)}) collective-permute-start(s32[160,128]{1,0:T(8,128)S(1)} %get-tuple-element.40), channel_id=1, source_target_pairs={{0,1},{1,0},{2,3},{3,2},{4,5},{5,4},{6,7},{7,6},{8,9},{9,8},{10,11... | collective-permute-start | bytes 245768 | tf_op jit(solution)/shard_map/ppermute | solution.py:27
  21.2 0.6 %collective-permute-done.7.refs_1_ = bf16[1152,128]{1,0:T(8,128)(2,1)S(1)} collective-permute-done((bf16[1152,128]{1,0:T(8,128)(2,1)S(1)}, bf16[1152,128]{1,0:T(8,128)(2,1)S(1)}, u32[]{:S(2)}, u32[]{:S(2)}) %collective-permute-start.7) | collective-permute-done | bytes 294944 | tf_op jit(solution)/shard_map/ppermute | solution.py:41
  21.8 0.8 %peer_products_80.1 = (f32[4,48,128]{2,1,0:T(8,128)S(1)}, s32[96,128]{1,0:T(8,128)S(1)}, s32[96,128]{1,0:T(8,128)S(1)}, s32[96,128]{1,0:T(8,128)S(1)}) custom-call(s32[1,8,128]{2,1,0:T(8,128)S(1)} %get-tuple-element.41.refs_0_, bf16[1152,128]{1,0:T(8,128)(2,1)S(1)} %collective-permute-done.7.refs_1_, ...), custom_call_target="tpu_custom_call" | custom-call | flops 18874368 | bytes 1703936 | tf_op jit(solution)/shard_map/peer_products_80/pallas_call | solution.py:380
  22.6 2.9 %collective-permute-start.10 = (s32[96,128]{1,0:T(8,128)S(1)}, s32[96,128]{1,0:T(8,128)S(1)}, u32[]{:S(2)}, u32[]{:S(2)}) collective-permute-start(s32[96,128]{1,0:T(8,128)S(1)} %get-tuple-element.46), channel_id=1, source_target_pairs={{0,2},{1,3},{2,0},{3,1},{4,6},{5,7},{6,4},{7,5},{8,10},{9,11},{10,... | collective-permute-start | bytes 147464 | tf_op jit(solution)/shard_map/ppermute | solution.py:27
  25.5 1.1 %collective-permute-start.8 = (s32[96,128]{1,0:T(8,128)S(1)}, s32[96,128]{1,0:T(8,128)S(1)}, u32[]{:S(2)}, u32[]{:S(2)}) collective-permute-start(s32[96,128]{1,0:T(8,128)S(1)} %get-tuple-element.44), channel_id=1, source_target_pairs={{0,3},{1,2},{2,1},{3,0},{4,7},{5,6},{6,5},{7,4},{8,11},{9,10},{10,... | collective-permute-start | bytes 147464 | tf_op jit(solution)/shard_map/ppermute | solution.py:27
  26.6 0.0 collective-permute-done.4.refs_1_
  26.6 0.5 %collective-permute-start.9 = (s32[96,128]{1,0:T(8,128)S(1)}, s32[96,128]{1,0:T(8,128)S(1)}, u32[]{:S(2)}, u32[]{:S(2)}) collective-permute-start(s32[96,128]{1,0:T(8,128)S(1)} %get-tuple-element.45), channel_id=1, source_target_pairs={{0,1},{1,0},{2,3},{3,2},{4,5},{5,4},{6,7},{7,6},{8,9},{9,8},{10,11... | collective-permute-start | bytes 147464 | tf_op jit(solution)/shard_map/ppermute | solution.py:27
  27.1 0.0 collective-permute-done.5.refs_2_
  27.1 0.0 collective-permute-done.6.refs_3_
  27.1 0.1 finish_0.1.refs_0_
  27.2 2.1 %collective-permute-done.10.refs_4_ = s32[96,128]{1,0:T(8,128)S(1)} collective-permute-done((s32[96,128]{1,0:T(8,128)S(1)}, s32[96,128]{1,0:T(8,128)S(1)}, u32[]{:S(2)}, u32[]{:S(2)}) %collective-permute-start.10) | collective-permute-done | bytes 49184 | tf_op jit(solution)/shard_map/ppermute | solution.py:27
  29.3 2.1 %collective-permute-done.8.refs_2_ = s32[96,128]{1,0:T(8,128)S(1)} collective-permute-done((s32[96,128]{1,0:T(8,128)S(1)}, s32[96,128]{1,0:T(8,128)S(1)}, u32[]{:S(2)}, u32[]{:S(2)}) %collective-permute-start.8) | collective-permute-done | bytes 49184 | tf_op jit(solution)/shard_map/ppermute | solution.py:27
  31.4 0.0 collective-permute-done.9.refs_3_
  31.4 0.7 %finish_80.1 = bf16[2,2,128,128]{3,2,1,0:T(8,128)(2,1)} custom-call(bf16[2,2,80,128]{3,2,1,0:T(8,128)(2,1)S(1)} %finish_0.1.refs_0_, f32[4,48,128]{2,1,0:T(8,128)S(1)} %get-tuple-element.43.refs_1_, s32[96,128]{1,0:T(8,128)S(1)} %collective-permute-done.8.refs_2_, s32[96,128]{1,0:T(8,128)S(1)} %collective-permute-done.9.refs_3_, ...), custom_call_target="tpu_custom_call" | custom-call | tf_op jit(solution)/shard_map/finish_80/pallas_call | solution.py:403
Async XLA Ops:
  1.1 14.7 %collective-permute-start.3 = (bf16[1936,128]{1,0:T(8,128)(2,1)S(1)}, bf16[1936,128]{1,0:T(8,128)(2,1)S(1)}, u32[]{:S(2)}, u32[]{:S(2)}) collective-permute-start(bf16[1936,128]{1,0:T(8,128)(2,1)S(1)} %get-tuple-element.31.refs_0_), channel_id=1, source_target_pairs={{4,0},{0,4},{5,1},{1,5},{6,2},{2,6},{7,3},{3,7},{12,8},{8,12},{13,... | collective-permute-start | bytes 1486856 | tf_op jit(solution)/shard_map/ppermute | solution.py:41
  5.2 5.1 %collective-permute-start.1 = (bf16[528,128]{1,0:T(8,128)(2,1)S(1)}, bf16[528,128]{1,0:T(8,128)(2,1)S(1)}, u32[]{:S(2)}, u32[]{:S(2)}) collective-permute-start(bf16[528,128]{1,0:T(8,128)(2,1)S(1)} %get-tuple-element.32.refs_2_), channel_id=1, source_target_pairs={{0,16},{8,24},{16,0},{24,8},{1,17},{9,25},{17,1},{25,9},{2,18},{10... | collective-permute-start | bytes 405512 | tf_op jit(solution)/shard_map/ppermute | solution.py:27
  6.8 3.5 %collective-permute-start = (bf16[528,128]{1,0:T(8,128)(2,1)S(1)}, bf16[528,128]{1,0:T(8,128)(2,1)S(1)}, u32[]{:S(2)}, u32[]{:S(2)}) collective-permute-start(bf16[528,128]{1,0:T(8,128)(2,1)S(1)} %get-tuple-element.32.refs_2_), channel_id=1, source_target_pairs={{0,8},{8,0},{16,24},{24,16},{1,9},{9,1},{17,25},{25,17},{2,10},{10... | collective-permute-start | bytes 405512 | tf_op jit(solution)/shard_map/ppermute | solution.py:27
  10.4 1.4 %collective-permute-start.2 = (bf16[528,128]{1,0:T(8,128)(2,1)S(1)}, bf16[528,128]{1,0:T(8,128)(2,1)S(1)}, u32[]{:S(2)}, u32[]{:S(2)}) collective-permute-start(bf16[528,128]{1,0:T(8,128)(2,1)S(1)} %collective-permute-done.1.refs_4_), channel_id=1, source_target_pairs={{0,8},{8,0},{16,24},{24,16},{1,9},{9,1},{17,25},{25,17},{2,10},{10... | collective-permute-start | bytes 405512 | tf_op jit(solution)/shard_map/ppermute | solution.py:27
  12.5 9.3 %collective-permute-start.7 = (bf16[1152,128]{1,0:T(8,128)(2,1)S(1)}, bf16[1152,128]{1,0:T(8,128)(2,1)S(1)}, u32[]{:S(2)}, u32[]{:S(2)}) collective-permute-start(bf16[1152,128]{1,0:T(8,128)(2,1)S(1)} %get-tuple-element.42.refs_1_), channel_id=1, source_target_pairs={{4,0},{0,4},{5,1},{1,5},{6,2},{2,6},{7,3},{3,7},{12,8},{8,12},{13,... | collective-permute-start | bytes 884744 | tf_op jit(solution)/shard_map/ppermute | solution.py:41
  16.8 9.8 %collective-permute-start.4 = (s32[160,128]{1,0:T(8,128)S(1)}, s32[160,128]{1,0:T(8,128)S(1)}, u32[]{:S(2)}, u32[]{:S(2)}) collective-permute-start(s32[160,128]{1,0:T(8,128)S(1)} %get-tuple-element.38), channel_id=1, source_target_pairs={{0,2},{1,3},{2,0},{3,1},{4,6},{5,7},{6,4},{7,5},{8,10},{9,11},{10,... | collective-permute-start | bytes 245768 | tf_op jit(solution)/shard_map/ppermute | solution.py:27
  19.6 7.4 %collective-permute-start.5 = (s32[160,128]{1,0:T(8,128)S(1)}, s32[160,128]{1,0:T(8,128)S(1)}, u32[]{:S(2)}, u32[]{:S(2)}) collective-permute-start(s32[160,128]{1,0:T(8,128)S(1)} %get-tuple-element.39), channel_id=1, source_target_pairs={{0,3},{1,2},{2,1},{3,0},{4,7},{5,6},{6,5},{7,4},{8,11},{9,10},{10,... | collective-permute-start | bytes 245768 | tf_op jit(solution)/shard_map/ppermute | solution.py:27
  20.7 6.3 %collective-permute-start.6 = (s32[160,128]{1,0:T(8,128)S(1)}, s32[160,128]{1,0:T(8,128)S(1)}, u32[]{:S(2)}, u32[]{:S(2)}) collective-permute-start(s32[160,128]{1,0:T(8,128)S(1)} %get-tuple-element.40), channel_id=1, source_target_pairs={{0,1},{1,0},{2,3},{3,2},{4,5},{5,4},{6,7},{7,6},{8,9},{9,8},{10,11... | collective-permute-start | bytes 245768 | tf_op jit(solution)/shard_map/ppermute | solution.py:27
  22.6 6.7 %collective-permute-start.10 = (s32[96,128]{1,0:T(8,128)S(1)}, s32[96,128]{1,0:T(8,128)S(1)}, u32[]{:S(2)}, u32[]{:S(2)}) collective-permute-start(s32[96,128]{1,0:T(8,128)S(1)} %get-tuple-element.46), channel_id=1, source_target_pairs={{0,2},{1,3},{2,0},{3,1},{4,6},{5,7},{6,4},{7,5},{8,10},{9,11},{10,... | collective-permute-start | bytes 147464 | tf_op jit(solution)/shard_map/ppermute | solution.py:27
  25.5 5.9 %collective-permute-start.8 = (s32[96,128]{1,0:T(8,128)S(1)}, s32[96,128]{1,0:T(8,128)S(1)}, u32[]{:S(2)}, u32[]{:S(2)}) collective-permute-start(s32[96,128]{1,0:T(8,128)S(1)} %get-tuple-element.44), channel_id=1, source_target_pairs={{0,3},{1,2},{2,1},{3,0},{4,7},{5,6},{6,5},{7,4},{8,11},{9,10},{10,... | collective-permute-start | bytes 147464 | tf_op jit(solution)/shard_map/ppermute | solution.py:27
  26.6 4.8 %collective-permute-start.9 = (s32[96,128]{1,0:T(8,128)S(1)}, s32[96,128]{1,0:T(8,128)S(1)}, u32[]{:S(2)}, u32[]{:S(2)}) collective-permute-start(s32[96,128]{1,0:T(8,128)S(1)} %get-tuple-element.45), channel_id=1, source_target_pairs={{0,1},{1,0},{2,3},{3,2},{4,5},{5,4},{6,7},{7,6},{8,9},{9,8},{10,11... | collective-permute-start | bytes 147464 | tf_op jit(solution)/shard_map/ppermute | solution.py:27

commit v21 on v20

--- a/solution.py
+++ b/solution.py
@@ -243,8 +243,8 @@
         for u in range(slots):
             value = totals[d * slots + u]
             peak = jnp.max(jnp.abs(value), axis=0, keepdims=True)
-            power = jnp.floor(jnp.log2(jnp.maximum(peak, 1e-30)) + 1e-3) + 1.0
-            whole = jnp.floor(value * jnp.exp2(15.0 - power) + 0.5).astype(jnp.int32)
+            power = jnp.floor(jnp.log2(jnp.maximum(peak, 1e-36)) + 1e-3) + 1.0
+            whole = jnp.floor(value * jnp.exp2(-power) * 32768.0 + 0.5).astype(jnp.int32)
             word = (whole[:half] << 16) | (whole[half:] & 0xFFFF)
             bits = ((power.astype(jnp.int32) + 128) >> sublane) & 1
             code[pl.ds(u * half, 8)] = (word[:8] & ~1) | bits
@@ -265,10 +265,10 @@
         for code in codes:
             word = code[pl.ds(u * half, half)]
             power = jnp.sum((word[:8] & 1) << sublane, axis=0, keepdims=True).astype(jnp.float32)
-            scale = jnp.exp2(power - (128.0 + 15.0))
+            scale = jnp.exp2(power - 128.0)
             word = jnp.concatenate([word[:8] & ~1, word[8:]])
-            high += (word >> 16).astype(jnp.float32) * scale
-            low += ((word << 16) >> 16).astype(jnp.float32) * scale
+            high += (word >> 16).astype(jnp.float32) * (1 / 32768) * scale
+            low += ((word << 16) >> 16).astype(jnp.float32) * (1 / 32768) * scale
         result[u // kept, u % kept, first : first + half] = high.astype(jnp.bfloat16)
         result[u // kept, u % kept, first + half : first + height] = low.astype(jnp.bfloat16)
 

time: 32.1 us -> 32.1 us (level)
  starting transfers between devices: 13.8 us -> 13.4 us
    pallas_call x2, Pallas kernels: 1.76 us -> 1.21 us  [per_device(): pl.pallas_call(functools.partial(peer_kernel, (cols, layers, count, width...]
    pallas_call x1, Pallas kernels: 0.78 us -> 1.25 us  [per_device(): pl.pallas_call(functools.partial(own_kernel, (rows, count, piece_rows, wi...]
where the time goes in v21:
time: 32.1 us; the launch traced here: 31.9 us
  starting transfers between devices  13.4 us (42%)
  waiting for transfers between devices  12.9 us (40%)
  Pallas kernels  5.53 us (17%)
    ppermute x9, starting transfers between devices, flipped(): lax.ppermute(value, axis, [(i, i ^ bits) for i in range(lax.axis_size(axi...  10.3 us
    ppermute x9, waiting for transfers between devices, flipped(): lax.ppermute(value, axis, [(i, i ^ bits) for i in range(lax.axis_size(axi...  9.06 us
    ppermute x2, waiting for transfers between devices, shifted(): lax.ppermute(value, axis, [((i + offset) % size, i) for i in range(size)])  3.84 us
    ppermute x2, starting transfers between devices, shifted(): lax.ppermute(value, axis, [((i + offset) % size, i) for i in range(size)])  3.07 us
    pallas_call x1, Pallas kernels, per_device(): pl.pallas_call(functools.partial(own_kernel, (rows, count, piece_rows, wi...  1.25 us
    pallas_call x2, Pallas kernels, per_device(): pl.pallas_call(functools.partial(peer_kernel, (cols, layers, count, width...  1.21 us
    pallas_call x1, Pallas kernels, per_device(): pl.pallas_call(functools.partial(pack_first_kernel, (layers, count, piece...  1.11 us
    pallas_call x1, Pallas kernels, per_device(): pl.pallas_call(functools.partial(pack_later_kernel, (count, piece, order,...  1.11 us
  transfers between devices with their start and end apart: 11, of which 6 were waited for; matrix products, arithmetic and copies ran while one was open for 0% of the time, Pallas kernels for 12%

profile of v21, /device:TPU:0, one launch (start us, length us, event | category | flops | bytes accessed | tf_op | source)
XLA Modules:
  0.0 31.9 jit_solution(8060578984856776872)
XLA Ops:
  0.0 1.1 %pack_first.1 = (s32[16,128]{1,0:T(8,128)S(1)}, bf16[1936,128]{1,0:T(8,128)(2,1)S(1)}) custom-call(s32[1,24]{1,0:T(1,128)} %bitcast.6, s32[1,24]{1,0:T(1,128)} %bitcast.7, s32[2,8]{1,0:T(2,128)} %bitcast.5, bf16[24,128,128]{2,1,0:T(8,128)(2,1)} %x_in.2), custom_call_target="tpu_custom_call" | custom-call | tf_op jit(solution)/shard_map/pack_first/pallas_call | solution.py:295
  1.1 3.0 %collective-permute-start.3 = (bf16[1936,128]{1,0:T(8,128)(2,1)S(1)}, bf16[1936,128]{1,0:T(8,128)(2,1)S(1)}, u32[]{:S(2)}, u32[]{:S(2)}) collective-permute-start(bf16[1936,128]{1,0:T(8,128)(2,1)S(1)} %get-tuple-element.31.refs_0_), channel_id=1, source_target_pairs={{4,0},{0,4},{5,1},{1,5},{6,2},{2,6},{7,3},{3,7},{12,8},{8,12},{13,... | collective-permute-start | bytes 1486856 | tf_op jit(solution)/shard_map/ppermute | solution.py:41
  4.1 1.1 %pack_later.1 = (bf16[528,128]{1,0:T(8,128)(2,1)S(1)}, bf16[1152,128]{1,0:T(8,128)(2,1)S(1)}) custom-call(bf16[24,128,128]{2,1,0:T(8,128)(2,1)} %x_in.2, s32[2,2]{1,0:T(2,128)} %s_cols, bf16[4,128,128]{2,1,0:T(8,128)(2,1)} %bitcast.4), custom_call_target="tpu_custom_call" | custom-call | tf_op jit(solution)/shard_map/pack_later/pallas_call | solution.py:322
  5.2 1.6 %collective-permute-start.1 = (bf16[528,128]{1,0:T(8,128)(2,1)S(1)}, bf16[528,128]{1,0:T(8,128)(2,1)S(1)}, u32[]{:S(2)}, u32[]{:S(2)}) collective-permute-start(bf16[528,128]{1,0:T(8,128)(2,1)S(1)} %get-tuple-element.32.refs_2_), channel_id=1, source_target_pairs={{0,16},{8,24},{16,0},{24,8},{1,17},{9,25},{17,1},{25,9},{2,18},{10... | collective-permute-start | bytes 405512 | tf_op jit(solution)/shard_map/ppermute | solution.py:27
  6.8 0.0 collective-permute-start
  6.8 3.5 %collective-permute-done.1.refs_4_ = bf16[528,128]{1,0:T(8,128)(2,1)S(1)} collective-permute-done((bf16[528,128]{1,0:T(8,128)(2,1)S(1)}, bf16[528,128]{1,0:T(8,128)(2,1)S(1)}, u32[]{:S(2)}, u32[]{:S(2)}) %collective-permute-start.1) | collective-permute-done | bytes 135200 | tf_op jit(solution)/shard_map/ppermute | solution.py:27
  10.4 0.0 collective-permute-start.2
  10.4 0.0 collective-permute-done.refs_3_
  10.4 1.3 %collective-permute-done.2.refs_5_ = bf16[528,128]{1,0:T(8,128)(2,1)S(1)} collective-permute-done((bf16[528,128]{1,0:T(8,128)(2,1)S(1)}, bf16[528,128]{1,0:T(8,128)(2,1)S(1)}, u32[]{:S(2)}, u32[]{:S(2)}) %collective-permute-start.2) | collective-permute-done | bytes 135200 | tf_op jit(solution)/shard_map/ppermute | solution.py:27
  11.7 1.2 %own_products.1 = (f32[17,128,128]{2,1,0:T(8,128)S(1)}, bf16[16,128,128]{2,1,0:T(8,128)(2,1)S(1)}, s32[8,128]{1,0:T(8,128)S(1)}) custom-call(s32[16,128]{1,0:T(8,128)S(1)} %get-tuple-element.26.known.refs_0_, bf16[1936,128]{1,0:T(8,128)(2,1)S(1)} %get-tuple-element.31.refs_0_, bf16[1152,128]{1,0:T(8,128)(2,1)S(1)} %get-tuple-element.42.refs_1_, ...), custom_call_target="tpu_custom_call" | custom-call | flops 50331648 | bytes 2883584 | tf_op jit(solution)/shard_map/own_products/pallas_call | solution.py:343
  13.0 0.1 collective-permute-start.7
  13.0 2.8 %collective-permute-done.3.refs_2_ = bf16[1936,128]{1,0:T(8,128)(2,1)S(1)} collective-permute-done((bf16[1936,128]{1,0:T(8,128)(2,1)S(1)}, bf16[1936,128]{1,0:T(8,128)(2,1)S(1)}, u32[]{:S(2)}, u32[]{:S(2)}) %collective-permute-start.3) | collective-permute-done | bytes 495648 | tf_op jit(solution)/shard_map/ppermute | solution.py:41
  15.8 0.7 %peer_products_0.1 = (f32[4,80,128]{2,1,0:T(8,128)S(1)}, s32[160,128]{1,0:T(8,128)S(1)}, s32[160,128]{1,0:T(8,128)S(1)}, s32[160,128]{1,0:T(8,128)S(1)}, s32[1,8,128]{2,1,0:T(8,128)S(1)}) custom-call(s32[16,128]{1,0:T(8,128)S(1)} %get-tuple-element.26.known.refs_0_, s32[8,128]{1,0:T(8,128)S(1)} %get-tuple-element.34.refs_1_, ...), custom_call_target="tpu_custom_call" | custom-call | flops 31457280 | bytes 1703936 | tf_op jit(solution)/shard_map/peer_products_0/pallas_call | solution.py:380
  16.6 2.8 %collective-permute-start.4 = (s32[160,128]{1,0:T(8,128)S(1)}, s32[160,128]{1,0:T(8,128)S(1)}, u32[]{:S(2)}, u32[]{:S(2)}) collective-permute-start(s32[160,128]{1,0:T(8,128)S(1)} %get-tuple-element.38), channel_id=1, source_target_pairs={{0,2},{1,3},{2,0},{3,1},{4,6},{5,7},{6,4},{7,5},{8,10},{9,11},{10,... | collective-permute-start | bytes 245768 | tf_op jit(solution)/shard_map/ppermute | solution.py:27
  19.4 1.3 %collective-permute-start.5 = (s32[160,128]{1,0:T(8,128)S(1)}, s32[160,128]{1,0:T(8,128)S(1)}, u32[]{:S(2)}, u32[]{:S(2)}) collective-permute-start(s32[160,128]{1,0:T(8,128)S(1)} %get-tuple-element.39), channel_id=1, source_target_pairs={{0,3},{1,2},{2,1},{3,0},{4,7},{5,6},{6,5},{7,4},{8,11},{9,10},{10,... | collective-permute-start | bytes 245768 | tf_op jit(solution)/shard_map/ppermute | solution.py:27
  20.7 0.0 collective-permute-start.6
  20.7 1.0 %collective-permute-done.7.refs_1_ = bf16[1152,128]{1,0:T(8,128)(2,1)S(1)} collective-permute-done((bf16[1152,128]{1,0:T(8,128)(2,1)S(1)}, bf16[1152,128]{1,0:T(8,128)(2,1)S(1)}, u32[]{:S(2)}, u32[]{:S(2)}) %collective-permute-start.7) | collective-permute-done | bytes 294944 | tf_op jit(solution)/shard_map/ppermute | solution.py:41
  21.8 0.5 %peer_products_80.1 = (f32[4,48,128]{2,1,0:T(8,128)S(1)}, s32[96,128]{1,0:T(8,128)S(1)}, s32[96,128]{1,0:T(8,128)S(1)}, s32[96,128]{1,0:T(8,128)S(1)}) custom-call(s32[1,8,128]{2,1,0:T(8,128)S(1)} %get-tuple-element.41.refs_0_, bf16[1152,128]{1,0:T(8,128)(2,1)S(1)} %collective-permute-done.7.refs_1_, ...), custom_call_target="tpu_custom_call" | custom-call | flops 18874368 | bytes 1703936 | tf_op jit(solution)/shard_map/peer_products_80/pallas_call | solution.py:380
  22.3 2.9 %collective-permute-start.10 = (s32[96,128]{1,0:T(8,128)S(1)}, s32[96,128]{1,0:T(8,128)S(1)}, u32[]{:S(2)}, u32[]{:S(2)}) collective-permute-start(s32[96,128]{1,0:T(8,128)S(1)} %get-tuple-element.46), channel_id=1, source_target_pairs={{0,2},{1,3},{2,0},{3,1},{4,6},{5,7},{6,4},{7,5},{8,10},{9,11},{10,... | collective-permute-start | bytes 147464 | tf_op jit(solution)/shard_map/ppermute | solution.py:27
  25.2 1.3 %collective-permute-start.8 = (s32[96,128]{1,0:T(8,128)S(1)}, s32[96,128]{1,0:T(8,128)S(1)}, u32[]{:S(2)}, u32[]{:S(2)}) collective-permute-start(s32[96,128]{1,0:T(8,128)S(1)} %get-tuple-element.44), channel_id=1, source_target_pairs={{0,3},{1,2},{2,1},{3,0},{4,7},{5,6},{6,5},{7,4},{8,11},{9,10},{10,... | collective-permute-start | bytes 147464 | tf_op jit(solution)/shard_map/ppermute | solution.py:27
  26.5 0.0 collective-permute-done.4.refs_1_
  26.5 0.3 collective-permute-start.9
  26.8 0.0 collective-permute-done.5.refs_2_
  26.8 0.0 collective-permute-done.6.refs_3_
  26.8 0.1 finish_0.1.refs_0_
  27.0 1.0 %collective-permute-done.10.refs_4_ = s32[96,128]{1,0:T(8,128)S(1)} collective-permute-done((s32[96,128]{1,0:T(8,128)S(1)}, s32[96,128]{1,0:T(8,128)S(1)}, u32[]{:S(2)}, u32[]{:S(2)}) %collective-permute-start.10) | collective-permute-done | bytes 49184 | tf_op jit(solution)/shard_map/ppermute | solution.py:27
  27.9 3.2 %collective-permute-done.8.refs_2_ = s32[96,128]{1,0:T(8,128)S(1)} collective-permute-done((s32[96,128]{1,0:T(8,128)S(1)}, s32[96,128]{1,0:T(8,128)S(1)}, u32[]{:S(2)}, u32[]{:S(2)}) %collective-permute-start.8) | collective-permute-done | bytes 49184 | tf_op jit(solution)/shard_map/ppermute | solution.py:27
  31.1 0.0 collective-permute-done.9.refs_3_
  31.1 0.7 %finish_80.1 = bf16[2,2,128,128]{3,2,1,0:T(8,128)(2,1)} custom-call(bf16[2,2,80,128]{3,2,1,0:T(8,128)(2,1)S(1)} %finish_0.1.refs_0_, f32[4,48,128]{2,1,0:T(8,128)S(1)} %get-tuple-element.43.refs_1_, s32[96,128]{1,0:T(8,128)S(1)} %collective-permute-done.8.refs_2_, s32[96,128]{1,0:T(8,128)S(1)} %collective-permute-done.9.refs_3_, ...), custom_call_target="tpu_custom_call" | custom-call | tf_op jit(solution)/shard_map/finish_80/pallas_call | solution.py:403
Async XLA Ops:
  1.1 14.7 %collective-permute-start.3 = (bf16[1936,128]{1,0:T(8,128)(2,1)S(1)}, bf16[1936,128]{1,0:T(8,128)(2,1)S(1)}, u32[]{:S(2)}, u32[]{:S(2)}) collective-permute-start(bf16[1936,128]{1,0:T(8,128)(2,1)S(1)} %get-tuple-element.31.refs_0_), channel_id=1, source_target_pairs={{4,0},{0,4},{5,1},{1,5},{6,2},{2,6},{7,3},{3,7},{12,8},{8,12},{13,... | collective-permute-start | bytes 1486856 | tf_op jit(solution)/shard_map/ppermute | solution.py:41
  5.2 5.1 %collective-permute-start.1 = (bf16[528,128]{1,0:T(8,128)(2,1)S(1)}, bf16[528,128]{1,0:T(8,128)(2,1)S(1)}, u32[]{:S(2)}, u32[]{:S(2)}) collective-permute-start(bf16[528,128]{1,0:T(8,128)(2,1)S(1)} %get-tuple-element.32.refs_2_), channel_id=1, source_target_pairs={{0,16},{8,24},{16,0},{24,8},{1,17},{9,25},{17,1},{25,9},{2,18},{10... | collective-permute-start | bytes 405512 | tf_op jit(solution)/shard_map/ppermute | solution.py:27
  6.8 3.5 %collective-permute-start = (bf16[528,128]{1,0:T(8,128)(2,1)S(1)}, bf16[528,128]{1,0:T(8,128)(2,1)S(1)}, u32[]{:S(2)}, u32[]{:S(2)}) collective-permute-start(bf16[528,128]{1,0:T(8,128)(2,1)S(1)} %get-tuple-element.32.refs_2_), channel_id=1, source_target_pairs={{0,8},{8,0},{16,24},{24,16},{1,9},{9,1},{17,25},{25,17},{2,10},{10... | collective-permute-start | bytes 405512 | tf_op jit(solution)/shard_map/ppermute | solution.py:27
  10.4 1.4 %collective-permute-start.2 = (bf16[528,128]{1,0:T(8,128)(2,1)S(1)}, bf16[528,128]{1,0:T(8,128)(2,1)S(1)}, u32[]{:S(2)}, u32[]{:S(2)}) collective-permute-start(bf16[528,128]{1,0:T(8,128)(2,1)S(1)} %collective-permute-done.1.refs_4_), channel_id=1, source_target_pairs={{0,8},{8,0},{16,24},{24,16},{1,9},{9,1},{17,25},{25,17},{2,10},{10... | collective-permute-start | bytes 405512 | tf_op jit(solution)/shard_map/ppermute | solution.py:27
  13.0 8.8 %collective-permute-start.7 = (bf16[1152,128]{1,0:T(8,128)(2,1)S(1)}, bf16[1152,128]{1,0:T(8,128)(2,1)S(1)}, u32[]{:S(2)}, u32[]{:S(2)}) collective-permute-start(bf16[1152,128]{1,0:T(8,128)(2,1)S(1)} %get-tuple-element.42.refs_1_), channel_id=1, source_target_pairs={{4,0},{0,4},{5,1},{1,5},{6,2},{2,6},{7,3},{3,7},{12,8},{8,12},{13,... | collective-permute-start | bytes 884744 | tf_op jit(solution)/shard_map/ppermute | solution.py:41
  16.6 10.0 %collective-permute-start.4 = (s32[160,128]{1,0:T(8,128)S(1)}, s32[160,128]{1,0:T(8,128)S(1)}, u32[]{:S(2)}, u32[]{:S(2)}) collective-permute-start(s32[160,128]{1,0:T(8,128)S(1)} %get-tuple-element.38), channel_id=1, source_target_pairs={{0,2},{1,3},{2,0},{3,1},{4,6},{5,7},{6,4},{7,5},{8,10},{9,11},{10,... | collective-permute-start | bytes 245768 | tf_op jit(solution)/shard_map/ppermute | solution.py:27
  19.4 7.4 %collective-permute-start.5 = (s32[160,128]{1,0:T(8,128)S(1)}, s32[160,128]{1,0:T(8,128)S(1)}, u32[]{:S(2)}, u32[]{:S(2)}) collective-permute-start(s32[160,128]{1,0:T(8,128)S(1)} %get-tuple-element.39), channel_id=1, source_target_pairs={{0,3},{1,2},{2,1},{3,0},{4,7},{5,6},{6,5},{7,4},{8,11},{9,10},{10,... | collective-permute-start | bytes 245768 | tf_op jit(solution)/shard_map/ppermute | solution.py:27
  20.7 6.1 %collective-permute-start.6 = (s32[160,128]{1,0:T(8,128)S(1)}, s32[160,128]{1,0:T(8,128)S(1)}, u32[]{:S(2)}, u32[]{:S(2)}) collective-permute-start(s32[160,128]{1,0:T(8,128)S(1)} %get-tuple-element.40), channel_id=1, source_target_pairs={{0,1},{1,0},{2,3},{3,2},{4,5},{5,4},{6,7},{7,6},{8,9},{9,8},{10,11... | collective-permute-start | bytes 245768 | tf_op jit(solution)/shard_map/ppermute | solution.py:27
  22.3 5.7 %collective-permute-start.10 = (s32[96,128]{1,0:T(8,128)S(1)}, s32[96,128]{1,0:T(8,128)S(1)}, u32[]{:S(2)}, u32[]{:S(2)}) collective-permute-start(s32[96,128]{1,0:T(8,128)S(1)} %get-tuple-element.46), channel_id=1, source_target_pairs={{0,2},{1,3},{2,0},{3,1},{4,6},{5,7},{6,4},{7,5},{8,10},{9,11},{10,... | collective-permute-start | bytes 147464 | tf_op jit(solution)/shard_map/ppermute | solution.py:27
  25.2 6.0 %collective-permute-start.8 = (s32[96,128]{1,0:T(8,128)S(1)}, s32[96,128]{1,0:T(8,128)S(1)}, u32[]{:S(2)}, u32[]{:S(2)}) collective-permute-start(s32[96,128]{1,0:T(8,128)S(1)} %get-tuple-element.44), channel_id=1, source_target_pairs={{0,3},{1,2},{2,1},{3,0},{4,7},{5,6},{6,5},{7,4},{8,11},{9,10},{10,... | collective-permute-start | bytes 147464 | tf_op jit(solution)/shard_map/ppermute | solution.py:27
  26.5 4.6 %collective-permute-start.9 = (s32[96,128]{1,0:T(8,128)S(1)}, s32[96,128]{1,0:T(8,128)S(1)}, u32[]{:S(2)}, u32[]{:S(2)}) collective-permute-start(s32[96,128]{1,0:T(8,128)S(1)} %get-tuple-element.45), channel_id=1, source_target_pairs={{0,1},{1,0},{2,3},{3,2},{4,5},{5,4},{6,7},{7,6},{8,9},{9,8},{10,11... | collective-permute-start | bytes 147464 | tf_op jit(solution)/shard_map/ppermute | solution.py:27

commit v22 on v21

--- a/solution.py
+++ b/solution.py
@@ -394,10 +394,8 @@
             name=f"peer_products_{at}",
         )(*given, *pieces, panel, totals)
         plan = plan or out[layers:]
-        far = [d for d in range(layers // 2, layers)]
-        turn = far + [d for d in range(1, layers) if d not in far]
-        if at > 0:
-            turn = turn[1:] + turn[:1]
+        far, near = list(range(layers // 2, layers)), list(range(1, layers // 2))
+        turn = far + near if at == 0 else far[:-1] + near + far[-1:]
         codes = [flipped(out[d], "layer", d) for d in turn]
         finished = [
             pl.pallas_call(

time: 32.1 us -> 32.2 us (level)
  starting transfers between devices: 13.4 us -> 13.9 us
  Pallas kernels: 5.53 us -> 5.08 us
    pallas_call x1, Pallas kernels: 1.25 us -> 0.78 us  [per_device(): pl.pallas_call(functools.partial(own_kernel, (rows, count, piece_rows, wi...]
  transfers between devices with their start and end apart: 11 -> 11, of which waited for: 6 -> 6; matrix products, arithmetic and copies ran while one was open for 0% -> 0% of each run, Pallas kernels for 12% -> 10%
where the time goes in v22:
time: 32.2 us; the launch traced here: 31.9 us
  starting transfers between devices  13.9 us (43%)
  waiting for transfers between devices  12.8 us (40%)
  Pallas kernels  5.08 us (16%)
    ppermute x9, starting transfers between devices, flipped(): lax.ppermute(value, axis, [(i, i ^ bits) for i in range(lax.axis_size(axi...  10.6 us
    ppermute x9, waiting for transfers between devices, flipped(): lax.ppermute(value, axis, [(i, i ^ bits) for i in range(lax.axis_size(axi...  9.1 us
    ppermute x2, waiting for transfers between devices, shifted(): lax.ppermute(value, axis, [((i + offset) % size, i) for i in range(size)])  3.74 us
    ppermute x2, starting transfers between devices, shifted(): lax.ppermute(value, axis, [((i + offset) % size, i) for i in range(size)])  3.37 us
    pallas_call x2, Pallas kernels, per_device(): pl.pallas_call(functools.partial(peer_kernel, (cols, layers, count, width...  1.22 us
    pallas_call x1, Pallas kernels, per_device(): pl.pallas_call(functools.partial(pack_first_kernel, (layers, count, piece...  1.11 us
    pallas_call x1, Pallas kernels, per_device(): pl.pallas_call(functools.partial(pack_later_kernel, (count, piece, order,...  1.11 us
    pallas_call x2, Pallas kernels, per_device(): pl.pallas_call(functools.partial(finish_kernel, (layers, slots), (at, hei...  0.86 us
  transfers between devices with their start and end apart: 11, of which 6 were waited for; matrix products, arithmetic and copies ran while one was open for 0% of the time, Pallas kernels for 10%

profile of v22, /device:TPU:0, one launch (start us, length us, event | category | flops | bytes accessed | tf_op | source)
XLA Modules:
  0.0 31.9 jit_solution(17738168270777753525)
XLA Ops:
  0.0 1.1 %pack_first.1 = (s32[16,128]{1,0:T(8,128)S(1)}, bf16[1936,128]{1,0:T(8,128)(2,1)S(1)}) custom-call(s32[1,24]{1,0:T(1,128)} %bitcast.6, s32[1,24]{1,0:T(1,128)} %bitcast.7, s32[2,8]{1,0:T(2,128)} %bitcast.5, bf16[24,128,128]{2,1,0:T(8,128)(2,1)} %x_in.2), custom_call_target="tpu_custom_call" | custom-call | tf_op jit(solution)/shard_map/pack_first/pallas_call | solution.py:295
  1.1 3.0 %collective-permute-start.3 = (bf16[1936,128]{1,0:T(8,128)(2,1)S(1)}, bf16[1936,128]{1,0:T(8,128)(2,1)S(1)}, u32[]{:S(2)}, u32[]{:S(2)}) collective-permute-start(bf16[1936,128]{1,0:T(8,128)(2,1)S(1)} %get-tuple-element.31.refs_0_), channel_id=1, source_target_pairs={{4,0},{0,4},{5,1},{1,5},{6,2},{2,6},{7,3},{3,7},{12,8},{8,12},{13,... | collective-permute-start | bytes 1486856 | tf_op jit(solution)/shard_map/ppermute | solution.py:41
  4.1 1.1 %pack_later.1 = (bf16[528,128]{1,0:T(8,128)(2,1)S(1)}, bf16[1152,128]{1,0:T(8,128)(2,1)S(1)}) custom-call(bf16[24,128,128]{2,1,0:T(8,128)(2,1)} %x_in.2, s32[2,2]{1,0:T(2,128)} %s_cols, bf16[4,128,128]{2,1,0:T(8,128)(2,1)} %bitcast.4), custom_call_target="tpu_custom_call" | custom-call | tf_op jit(solution)/shard_map/pack_later/pallas_call | solution.py:322
  5.2 1.6 %collective-permute-start.1 = (bf16[528,128]{1,0:T(8,128)(2,1)S(1)}, bf16[528,128]{1,0:T(8,128)(2,1)S(1)}, u32[]{:S(2)}, u32[]{:S(2)}) collective-permute-start(bf16[528,128]{1,0:T(8,128)(2,1)S(1)} %get-tuple-element.32.refs_2_), channel_id=1, source_target_pairs={{0,16},{8,24},{16,0},{24,8},{1,17},{9,25},{17,1},{25,9},{2,18},{10... | collective-permute-start | bytes 405512 | tf_op jit(solution)/shard_map/ppermute | solution.py:27
  6.8 0.0 collective-permute-start
  6.8 3.5 %collective-permute-done.1.refs_4_ = bf16[528,128]{1,0:T(8,128)(2,1)S(1)} collective-permute-done((bf16[528,128]{1,0:T(8,128)(2,1)S(1)}, bf16[528,128]{1,0:T(8,128)(2,1)S(1)}, u32[]{:S(2)}, u32[]{:S(2)}) %collective-permute-start.1) | collective-permute-done | bytes 135200 | tf_op jit(solution)/shard_map/ppermute | solution.py:27
  10.4 0.0 collective-permute-start.2
  10.4 0.0 collective-permute-done.refs_3_
  10.4 1.3 %collective-permute-done.2.refs_5_ = bf16[528,128]{1,0:T(8,128)(2,1)S(1)} collective-permute-done((bf16[528,128]{1,0:T(8,128)(2,1)S(1)}, bf16[528,128]{1,0:T(8,128)(2,1)S(1)}, u32[]{:S(2)}, u32[]{:S(2)}) %collective-permute-start.2) | collective-permute-done | bytes 135200 | tf_op jit(solution)/shard_map/ppermute | solution.py:27
  11.7 0.8 %own_products.1 = (f32[17,128,128]{2,1,0:T(8,128)S(1)}, bf16[16,128,128]{2,1,0:T(8,128)(2,1)S(1)}, s32[8,128]{1,0:T(8,128)S(1)}) custom-call(s32[16,128]{1,0:T(8,128)S(1)} %get-tuple-element.26.known.refs_0_, bf16[1936,128]{1,0:T(8,128)(2,1)S(1)} %get-tuple-element.31.refs_0_, bf16[1152,128]{1,0:T(8,128)(2,1)S(1)} %get-tuple-element.42.refs_1_, ...), custom_call_target="tpu_custom_call" | custom-call | flops 50331648 | bytes 2883584 | tf_op jit(solution)/shard_map/own_products/pallas_call | solution.py:343
  12.5 0.4 %collective-permute-start.7 = (bf16[1152,128]{1,0:T(8,128)(2,1)S(1)}, bf16[1152,128]{1,0:T(8,128)(2,1)S(1)}, u32[]{:S(2)}, u32[]{:S(2)}) collective-permute-start(bf16[1152,128]{1,0:T(8,128)(2,1)S(1)} %get-tuple-element.42.refs_1_), channel_id=1, source_target_pairs={{4,0},{0,4},{5,1},{1,5},{6,2},{2,6},{7,3},{3,7},{12,8},{8,12},{13,... | collective-permute-start | bytes 884744 | tf_op jit(solution)/shard_map/ppermute | solution.py:41
  12.9 3.0 %collective-permute-done.3.refs_2_ = bf16[1936,128]{1,0:T(8,128)(2,1)S(1)} collective-permute-done((bf16[1936,128]{1,0:T(8,128)(2,1)S(1)}, bf16[1936,128]{1,0:T(8,128)(2,1)S(1)}, u32[]{:S(2)}, u32[]{:S(2)}) %collective-permute-start.3) | collective-permute-done | bytes 495648 | tf_op jit(solution)/shard_map/ppermute | solution.py:41
  15.8 0.7 %peer_products_0.1 = (f32[4,80,128]{2,1,0:T(8,128)S(1)}, s32[160,128]{1,0:T(8,128)S(1)}, s32[160,128]{1,0:T(8,128)S(1)}, s32[160,128]{1,0:T(8,128)S(1)}, s32[1,8,128]{2,1,0:T(8,128)S(1)}) custom-call(s32[16,128]{1,0:T(8,128)S(1)} %get-tuple-element.26.known.refs_0_, s32[8,128]{1,0:T(8,128)S(1)} %get-tuple-element.34.refs_1_, ...), custom_call_target="tpu_custom_call" | custom-call | flops 31457280 | bytes 1703936 | tf_op jit(solution)/shard_map/peer_products_0/pallas_call | solution.py:380
  16.6 2.8 %collective-permute-start.4 = (s32[160,128]{1,0:T(8,128)S(1)}, s32[160,128]{1,0:T(8,128)S(1)}, u32[]{:S(2)}, u32[]{:S(2)}) collective-permute-start(s32[160,128]{1,0:T(8,128)S(1)} %get-tuple-element.38), channel_id=1, source_target_pairs={{0,2},{1,3},{2,0},{3,1},{4,6},{5,7},{6,4},{7,5},{8,10},{9,11},{10,... | collective-permute-start | bytes 245768 | tf_op jit(solution)/shard_map/ppermute | solution.py:27
  19.4 1.6 %collective-permute-start.5 = (s32[160,128]{1,0:T(8,128)S(1)}, s32[160,128]{1,0:T(8,128)S(1)}, u32[]{:S(2)}, u32[]{:S(2)}) collective-permute-start(s32[160,128]{1,0:T(8,128)S(1)} %get-tuple-element.39), channel_id=1, source_target_pairs={{0,3},{1,2},{2,1},{3,0},{4,7},{5,6},{6,5},{7,4},{8,11},{9,10},{10,... | collective-permute-start | bytes 245768 | tf_op jit(solution)/shard_map/ppermute | solution.py:27
  21.0 0.0 collective-permute-start.6
  21.0 0.8 %collective-permute-done.7.refs_1_ = bf16[1152,128]{1,0:T(8,128)(2,1)S(1)} collective-permute-done((bf16[1152,128]{1,0:T(8,128)(2,1)S(1)}, bf16[1152,128]{1,0:T(8,128)(2,1)S(1)}, u32[]{:S(2)}, u32[]{:S(2)}) %collective-permute-start.7) | collective-permute-done | bytes 294944 | tf_op jit(solution)/shard_map/ppermute | solution.py:41
  21.8 0.5 %peer_products_80.1 = (f32[4,48,128]{2,1,0:T(8,128)S(1)}, s32[96,128]{1,0:T(8,128)S(1)}, s32[96,128]{1,0:T(8,128)S(1)}, s32[96,128]{1,0:T(8,128)S(1)}) custom-call(s32[1,8,128]{2,1,0:T(8,128)S(1)} %get-tuple-element.41.refs_0_, bf16[1152,128]{1,0:T(8,128)(2,1)S(1)} %collective-permute-done.7.refs_1_, ...), custom_call_target="tpu_custom_call" | custom-call | flops 18874368 | bytes 1703936 | tf_op jit(solution)/shard_map/peer_products_80/pallas_call | solution.py:380
  22.3 3.9 %collective-permute-start.10 = (s32[96,128]{1,0:T(8,128)S(1)}, s32[96,128]{1,0:T(8,128)S(1)}, u32[]{:S(2)}, u32[]{:S(2)}) collective-permute-start(s32[96,128]{1,0:T(8,128)S(1)} %get-tuple-element.46), channel_id=1, source_target_pairs={{0,3},{1,2},{2,1},{3,0},{4,7},{5,6},{6,5},{7,4},{8,11},{9,10},{10,... | collective-permute-start | bytes 147464 | tf_op jit(solution)/shard_map/ppermute | solution.py:27
  26.2 0.0 collective-permute-start.8
  26.2 0.0 collective-permute-done.4.refs_1_
  26.2 0.6 %collective-permute-start.9 = (s32[96,128]{1,0:T(8,128)S(1)}, s32[96,128]{1,0:T(8,128)S(1)}, u32[]{:S(2)}, u32[]{:S(2)}) collective-permute-start(s32[96,128]{1,0:T(8,128)S(1)} %get-tuple-element.45), channel_id=1, source_target_pairs={{0,1},{1,0},{2,3},{3,2},{4,5},{5,4},{6,7},{7,6},{8,9},{9,8},{10,11... | collective-permute-start | bytes 147464 | tf_op jit(solution)/shard_map/ppermute | solution.py:27
  26.8 0.0 collective-permute-done.5.refs_2_
  26.8 0.0 collective-permute-done.6.refs_3_
  26.8 0.1 finish_0.1.refs_0_
  27.0 1.6 %collective-permute-done.10.refs_4_ = s32[96,128]{1,0:T(8,128)S(1)} collective-permute-done((s32[96,128]{1,0:T(8,128)S(1)}, s32[96,128]{1,0:T(8,128)S(1)}, u32[]{:S(2)}, u32[]{:S(2)}) %collective-permute-start.10) | collective-permute-done | bytes 49184 | tf_op jit(solution)/shard_map/ppermute | solution.py:27
  28.6 2.6 %collective-permute-done.8.refs_2_ = s32[96,128]{1,0:T(8,128)S(1)} collective-permute-done((s32[96,128]{1,0:T(8,128)S(1)}, s32[96,128]{1,0:T(8,128)S(1)}, u32[]{:S(2)}, u32[]{:S(2)}) %collective-permute-start.8) | collective-permute-done | bytes 49184 | tf_op jit(solution)/shard_map/ppermute | solution.py:27
  31.2 0.0 collective-permute-done.9.refs_3_
  31.2 0.7 %finish_80.1 = bf16[2,2,128,128]{3,2,1,0:T(8,128)(2,1)} custom-call(bf16[2,2,80,128]{3,2,1,0:T(8,128)(2,1)S(1)} %finish_0.1.refs_0_, f32[4,48,128]{2,1,0:T(8,128)S(1)} %get-tuple-element.43.refs_1_, s32[96,128]{1,0:T(8,128)S(1)} %collective-permute-done.8.refs_2_, s32[96,128]{1,0:T(8,128)S(1)} %collective-permute-done.9.refs_3_, ...), custom_call_target="tpu_custom_call" | custom-call | tf_op jit(solution)/shard_map/finish_80/pallas_call | solution.py:401
Async XLA Ops:
  1.1 14.7 %collective-permute-start.3 = (bf16[1936,128]{1,0:T(8,128)(2,1)S(1)}, bf16[1936,128]{1,0:T(8,128)(2,1)S(1)}, u32[]{:S(2)}, u32[]{:S(2)}) collective-permute-start(bf16[1936,128]{1,0:T(8,128)(2,1)S(1)} %get-tuple-element.31.refs_0_), channel_id=1, source_target_pairs={{4,0},{0,4},{5,1},{1,5},{6,2},{2,6},{7,3},{3,7},{12,8},{8,12},{13,... | collective-permute-start | bytes 1486856 | tf_op jit(solution)/shard_map/ppermute | solution.py:41
  5.2 5.1 %collective-permute-start.1 = (bf16[528,128]{1,0:T(8,128)(2,1)S(1)}, bf16[528,128]{1,0:T(8,128)(2,1)S(1)}, u32[]{:S(2)}, u32[]{:S(2)}) collective-permute-start(bf16[528,128]{1,0:T(8,128)(2,1)S(1)} %get-tuple-element.32.refs_2_), channel_id=1, source_target_pairs={{0,16},{8,24},{16,0},{24,8},{1,17},{9,25},{17,1},{25,9},{2,18},{10... | collective-permute-start | bytes 405512 | tf_op jit(solution)/shard_map/ppermute | solution.py:27
  6.8 3.5 %collective-permute-start = (bf16[528,128]{1,0:T(8,128)(2,1)S(1)}, bf16[528,128]{1,0:T(8,128)(2,1)S(1)}, u32[]{:S(2)}, u32[]{:S(2)}) collective-permute-start(bf16[528,128]{1,0:T(8,128)(2,1)S(1)} %get-tuple-element.32.refs_2_), channel_id=1, source_target_pairs={{0,8},{8,0},{16,24},{24,16},{1,9},{9,1},{17,25},{25,17},{2,10},{10... | collective-permute-start | bytes 405512 | tf_op jit(solution)/shard_map/ppermute | solution.py:27
  10.4 1.4 %collective-permute-start.2 = (bf16[528,128]{1,0:T(8,128)(2,1)S(1)}, bf16[528,128]{1,0:T(8,128)(2,1)S(1)}, u32[]{:S(2)}, u32[]{:S(2)}) collective-permute-start(bf16[528,128]{1,0:T(8,128)(2,1)S(1)} %collective-permute-done.1.refs_4_), channel_id=1, source_target_pairs={{0,8},{8,0},{16,24},{24,16},{1,9},{9,1},{17,25},{25,17},{2,10},{10... | collective-permute-start | bytes 405512 | tf_op jit(solution)/shard_map/ppermute | solution.py:27
  12.5 9.3 %collective-permute-start.7 = (bf16[1152,128]{1,0:T(8,128)(2,1)S(1)}, bf16[1152,128]{1,0:T(8,128)(2,1)S(1)}, u32[]{:S(2)}, u32[]{:S(2)}) collective-permute-start(bf16[1152,128]{1,0:T(8,128)(2,1)S(1)} %get-tuple-element.42.refs_1_), channel_id=1, source_target_pairs={{4,0},{0,4},{5,1},{1,5},{6,2},{2,6},{7,3},{3,7},{12,8},{8,12},{13,... | collective-permute-start | bytes 884744 | tf_op jit(solution)/shard_map/ppermute | solution.py:41
  16.6 9.6 %collective-permute-start.4 = (s32[160,128]{1,0:T(8,128)S(1)}, s32[160,128]{1,0:T(8,128)S(1)}, u32[]{:S(2)}, u32[]{:S(2)}) collective-permute-start(s32[160,128]{1,0:T(8,128)S(1)} %get-tuple-element.38), channel_id=1, source_target_pairs={{0,2},{1,3},{2,0},{3,1},{4,6},{5,7},{6,4},{7,5},{8,10},{9,11},{10,... | collective-permute-start | bytes 245768 | tf_op jit(solution)/shard_map/ppermute | solution.py:27
  19.4 7.5 %collective-permute-start.5 = (s32[160,128]{1,0:T(8,128)S(1)}, s32[160,128]{1,0:T(8,128)S(1)}, u32[]{:S(2)}, u32[]{:S(2)}) collective-permute-start(s32[160,128]{1,0:T(8,128)S(1)} %get-tuple-element.39), channel_id=1, source_target_pairs={{0,3},{1,2},{2,1},{3,0},{4,7},{5,6},{6,5},{7,4},{8,11},{9,10},{10,... | collective-permute-start | bytes 245768 | tf_op jit(solution)/shard_map/ppermute | solution.py:27
  21.0 5.9 %collective-permute-start.6 = (s32[160,128]{1,0:T(8,128)S(1)}, s32[160,128]{1,0:T(8,128)S(1)}, u32[]{:S(2)}, u32[]{:S(2)}) collective-permute-start(s32[160,128]{1,0:T(8,128)S(1)} %get-tuple-element.40), channel_id=1, source_target_pairs={{0,1},{1,0},{2,3},{3,2},{4,5},{5,4},{6,7},{7,6},{8,9},{9,8},{10,11... | collective-permute-start | bytes 245768 | tf_op jit(solution)/shard_map/ppermute | solution.py:27
  22.3 6.3 %collective-permute-start.10 = (s32[96,128]{1,0:T(8,128)S(1)}, s32[96,128]{1,0:T(8,128)S(1)}, u32[]{:S(2)}, u32[]{:S(2)}) collective-permute-start(s32[96,128]{1,0:T(8,128)S(1)} %get-tuple-element.46), channel_id=1, source_target_pairs={{0,3},{1,2},{2,1},{3,0},{4,7},{5,6},{6,5},{7,4},{8,11},{9,10},{10,... | collective-permute-start | bytes 147464 | tf_op jit(solution)/shard_map/ppermute | solution.py:27
  26.2 5.0 %collective-permute-start.8 = (s32[96,128]{1,0:T(8,128)S(1)}, s32[96,128]{1,0:T(8,128)S(1)}, u32[]{:S(2)}, u32[]{:S(2)}) collective-permute-start(s32[96,128]{1,0:T(8,128)S(1)} %get-tuple-element.44), channel_id=1, source_target_pairs={{0,2},{1,3},{2,0},{3,1},{4,6},{5,7},{6,4},{7,5},{8,10},{9,11},{10,... | collective-permute-start | bytes 147464 | tf_op jit(solution)/shard_map/ppermute | solution.py:27
  26.2 5.0 %collective-permute-start.9 = (s32[96,128]{1,0:T(8,128)S(1)}, s32[96,128]{1,0:T(8,128)S(1)}, u32[]{:S(2)}, u32[]{:S(2)}) collective-permute-start(s32[96,128]{1,0:T(8,128)S(1)} %get-tuple-element.45), channel_id=1, source_target_pairs={{0,1},{1,0},{2,3},{3,2},{4,5},{5,4},{6,7},{7,6},{8,9},{9,8},{10,11... | collective-permute-start | bytes 147464 | tf_op jit(solution)/shard_map/ppermute | solution.py:27

commit v23 on v22

--- a/solution.py
+++ b/solution.py
@@ -15,7 +15,7 @@
 
 
 def row_ranges(order):
-    first = order * 5 // 8
+    first = order * 3 // 4
     return [(0, first), (first, order - first)]
 
 

time: 32.2 us -> 34.6 us (1.075)
  waiting for transfers between devices: 12.8 us -> 15.8 us
  starting transfers between devices: 13.9 us -> 13.2 us
    ppermute x2, waiting for transfers between devices: 3.74 us -> 5.47 us  [shifted(): lax.ppermute(value, axis, [((i + offset) % size, i) for i in range(size)])]
    ppermute x9, waiting for transfers between devices: 9.1 us -> 10.3 us  [flipped(): lax.ppermute(value, axis, [(i, i ^ bits) for i in range(lax.axis_size(axi...]
    ppermute x9, starting transfers between devices: 10.6 us -> 10.1 us  [flipped(): lax.ppermute(value, axis, [(i, i ^ bits) for i in range(lax.axis_size(axi...]
    pallas_call x1, Pallas kernels: 0.78 us -> 1.15 us  [per_device(): pl.pallas_call(functools.partial(own_kernel, (rows, count, piece_rows, wi...]
  transfers between devices with their start and end apart: 11 -> 11, of which waited for: 6 -> 7; matrix products, arithmetic and copies ran while one was open for 0% -> 0% of each run, Pallas kernels for 10% -> 10%
where the time goes in v23:
time: 34.6 us; the launch traced here: 34.4 us
  waiting for transfers between devices  15.8 us (46%)
  starting transfers between devices  13.2 us (38%)
  Pallas kernels  5.39 us (16%)
    ppermute x9, waiting for transfers between devices, flipped(): lax.ppermute(value, axis, [(i, i ^ bits) for i in range(lax.axis_size(axi...  10.3 us
    ppermute x9, starting transfers between devices, flipped(): lax.ppermute(value, axis, [(i, i ^ bits) for i in range(lax.axis_size(axi...  10.1 us
    ppermute x2, waiting for transfers between devices, shifted(): lax.ppermute(value, axis, [((i + offset) % size, i) for i in range(size)])  5.47 us
    ppermute x2, starting transfers between devices, shifted(): lax.ppermute(value, axis, [((i + offset) % size, i) for i in range(size)])  3.07 us
    pallas_call x2, Pallas kernels, per_device(): pl.pallas_call(functools.partial(peer_kernel, (cols, layers, count, width...  1.16 us
    pallas_call x1, Pallas kernels, per_device(): pl.pallas_call(functools.partial(own_kernel, (rows, count, piece_rows, wi...  1.15 us
    pallas_call x1, Pallas kernels, per_device(): pl.pallas_call(functools.partial(pack_first_kernel, (layers, count, piece...  1.15 us
    pallas_call x1, Pallas kernels, per_device(): pl.pallas_call(functools.partial(pack_later_kernel, (count, piece, order,...  1.07 us
  transfers between devices with their start and end apart: 11, of which 7 were waited for; matrix products, arithmetic and copies ran while one was open for 0% of the time, Pallas kernels for 10%

profile of v23, /device:TPU:0, one launch (start us, length us, event | category | flops | bytes accessed | tf_op | source)
XLA Modules:
  0.0 34.4 jit_solution(5627313449282359287)
XLA Ops:
  0.0 1.1 %pack_first.1 = (s32[16,128]{1,0:T(8,128)S(1)}, bf16[2320,128]{1,0:T(8,128)(2,1)S(1)}) custom-call(s32[1,24]{1,0:T(1,128)} %bitcast.6, s32[1,24]{1,0:T(1,128)} %bitcast.7, s32[2,8]{1,0:T(2,128)} %bitcast.5, bf16[24,128,128]{2,1,0:T(8,128)(2,1)} %x_in.2), custom_call_target="tpu_custom_call" | custom-call | tf_op jit(solution)/shard_map/pack_first/pallas_call | solution.py:295
  1.2 3.0 %collective-permute-start.3 = (bf16[2320,128]{1,0:T(8,128)(2,1)S(1)}, bf16[2320,128]{1,0:T(8,128)(2,1)S(1)}, u32[]{:S(2)}, u32[]{:S(2)}) collective-permute-start(bf16[2320,128]{1,0:T(8,128)(2,1)S(1)} %get-tuple-element.31.refs_0_), channel_id=1, source_target_pairs={{4,0},{0,4},{5,1},{1,5},{6,2},{2,6},{7,3},{3,7},{12,8},{8,12},{13,... | collective-permute-start | bytes 1781768 | tf_op jit(solution)/shard_map/ppermute | solution.py:41
  4.2 1.1 %pack_later.1 = (bf16[528,128]{1,0:T(8,128)(2,1)S(1)}, bf16[768,128]{1,0:T(8,128)(2,1)S(1)}) custom-call(bf16[24,128,128]{2,1,0:T(8,128)(2,1)} %x_in.2, s32[2,2]{1,0:T(2,128)} %s_cols, bf16[4,128,128]{2,1,0:T(8,128)(2,1)} %bitcast.4), custom_call_target="tpu_custom_call" | custom-call | tf_op jit(solution)/shard_map/pack_later/pallas_call | solution.py:322
  5.2 1.6 %collective-permute-start.1 = (bf16[528,128]{1,0:T(8,128)(2,1)S(1)}, bf16[528,128]{1,0:T(8,128)(2,1)S(1)}, u32[]{:S(2)}, u32[]{:S(2)}) collective-permute-start(bf16[528,128]{1,0:T(8,128)(2,1)S(1)} %get-tuple-element.32.refs_2_), channel_id=1, source_target_pairs={{0,16},{8,24},{16,0},{24,8},{1,17},{9,25},{17,1},{25,9},{2,18},{10... | collective-permute-start | bytes 405512 | tf_op jit(solution)/shard_map/ppermute | solution.py:27
  6.8 0.0 collective-permute-start
  6.8 3.5 %collective-permute-done.1.refs_4_ = bf16[528,128]{1,0:T(8,128)(2,1)S(1)} collective-permute-done((bf16[528,128]{1,0:T(8,128)(2,1)S(1)}, bf16[528,128]{1,0:T(8,128)(2,1)S(1)}, u32[]{:S(2)}, u32[]{:S(2)}) %collective-permute-start.1) | collective-permute-done | bytes 135200 | tf_op jit(solution)/shard_map/ppermute | solution.py:27
  10.4 0.0 collective-permute-start.2
  10.4 0.0 collective-permute-done.refs_3_
  10.4 1.3 %collective-permute-done.2.refs_5_ = bf16[528,128]{1,0:T(8,128)(2,1)S(1)} collective-permute-done((bf16[528,128]{1,0:T(8,128)(2,1)S(1)}, bf16[528,128]{1,0:T(8,128)(2,1)S(1)}, u32[]{:S(2)}, u32[]{:S(2)}) %collective-permute-start.2) | collective-permute-done | bytes 135200 | tf_op jit(solution)/shard_map/ppermute | solution.py:27
  11.7 1.1 %own_products.1 = (f32[17,128,128]{2,1,0:T(8,128)S(1)}, bf16[16,128,128]{2,1,0:T(8,128)(2,1)S(1)}, s32[8,128]{1,0:T(8,128)S(1)}) custom-call(s32[16,128]{1,0:T(8,128)S(1)} %get-tuple-element.26.known.refs_0_, bf16[2320,128]{1,0:T(8,128)(2,1)S(1)} %get-tuple-element.31.refs_0_, bf16[768,128]{1,0:T(8,128)(2,1)S(1)} %get-tuple-element.42.refs_1_, ...), custom_call_target="tpu_custom_call" | custom-call | flops 50331648 | bytes 2883584 | tf_op jit(solution)/shard_map/own_products/pallas_call | solution.py:343
  12.9 0.1 collective-permute-start.7
  12.9 5.5 %collective-permute-done.3.refs_2_ = bf16[2320,128]{1,0:T(8,128)(2,1)S(1)} collective-permute-done((bf16[2320,128]{1,0:T(8,128)(2,1)S(1)}, bf16[2320,128]{1,0:T(8,128)(2,1)S(1)}, u32[]{:S(2)}, u32[]{:S(2)}) %collective-permute-start.3) | collective-permute-done | bytes 593952 | tf_op jit(solution)/shard_map/ppermute | solution.py:41
  18.4 0.7 %peer_products_0.1 = (f32[4,96,128]{2,1,0:T(8,128)S(1)}, s32[192,128]{1,0:T(8,128)S(1)}, s32[192,128]{1,0:T(8,128)S(1)}, s32[192,128]{1,0:T(8,128)S(1)}, s32[1,8,128]{2,1,0:T(8,128)S(1)}) custom-call(s32[16,128]{1,0:T(8,128)S(1)} %get-tuple-element.26.known.refs_0_, s32[8,128]{1,0:T(8,128)S(1)} %get-tuple-element.34.refs_1_, ...), custom_call_target="tpu_custom_call" | custom-call | flops 37748736 | bytes 1703936 | tf_op jit(solution)/shard_map/peer_products_0/pallas_call | solution.py:380
  19.1 3.2 %collective-permute-start.4 = (s32[192,128]{1,0:T(8,128)S(1)}, s32[192,128]{1,0:T(8,128)S(1)}, u32[]{:S(2)}, u32[]{:S(2)}) collective-permute-start(s32[192,128]{1,0:T(8,128)S(1)} %get-tuple-element.38), channel_id=1, source_target_pairs={{0,2},{1,3},{2,0},{3,1},{4,6},{5,7},{6,4},{7,5},{8,10},{9,11},{10,... | collective-permute-start | bytes 294920 | tf_op jit(solution)/shard_map/ppermute | solution.py:27
  22.4 1.3 %collective-permute-start.5 = (s32[192,128]{1,0:T(8,128)S(1)}, s32[192,128]{1,0:T(8,128)S(1)}, u32[]{:S(2)}, u32[]{:S(2)}) collective-permute-start(s32[192,128]{1,0:T(8,128)S(1)} %get-tuple-element.39), channel_id=1, source_target_pairs={{0,3},{1,2},{2,1},{3,0},{4,7},{5,6},{6,5},{7,4},{8,11},{9,10},{10,... | collective-permute-start | bytes 294920 | tf_op jit(solution)/shard_map/ppermute | solution.py:27
  23.7 0.5 %collective-permute-start.6 = (s32[192,128]{1,0:T(8,128)S(1)}, s32[192,128]{1,0:T(8,128)S(1)}, u32[]{:S(2)}, u32[]{:S(2)}) collective-permute-start(s32[192,128]{1,0:T(8,128)S(1)} %get-tuple-element.40), channel_id=1, source_target_pairs={{0,1},{1,0},{2,3},{3,2},{4,5},{5,4},{6,7},{7,6},{8,9},{9,8},{10,11... | collective-permute-start | bytes 294920 | tf_op jit(solution)/shard_map/ppermute | solution.py:27
  24.2 0.0 collective-permute-done.7.refs_1_
  24.2 0.4 %peer_products_96.1 = (f32[4,32,128]{2,1,0:T(8,128)S(1)}, s32[64,128]{1,0:T(8,128)S(1)}, s32[64,128]{1,0:T(8,128)S(1)}, s32[64,128]{1,0:T(8,128)S(1)}) custom-call(s32[1,8,128]{2,1,0:T(8,128)S(1)} %get-tuple-element.41.refs_0_, bf16[768,128]{1,0:T(8,128)(2,1)S(1)} %collective-permute-done.7.refs_1_, ...), custom_call_target="tpu_custom_call" | custom-call | flops 12582912 | bytes 1703936 | tf_op jit(solution)/shard_map/peer_products_96/pallas_call | solution.py:380
  24.6 3.3 %collective-permute-start.10 = (s32[64,128]{1,0:T(8,128)S(1)}, s32[64,128]{1,0:T(8,128)S(1)}, u32[]{:S(2)}, u32[]{:S(2)}) collective-permute-start(s32[64,128]{1,0:T(8,128)S(1)} %get-tuple-element.46), channel_id=1, source_target_pairs={{0,3},{1,2},{2,1},{3,0},{4,7},{5,6},{6,5},{7,4},{8,11},{9,10},{10,... | collective-permute-start | bytes 98312 | tf_op jit(solution)/shard_map/ppermute | solution.py:27
  27.9 0.0 collective-permute-start.8
  27.9 1.9 %collective-permute-done.4.refs_1_ = s32[192,128]{1,0:T(8,128)S(1)} collective-permute-done((s32[192,128]{1,0:T(8,128)S(1)}, s32[192,128]{1,0:T(8,128)S(1)}, u32[]{:S(2)}, u32[]{:S(2)}) %collective-permute-start.4) | collective-permute-done | bytes 98336 | tf_op jit(solution)/shard_map/ppermute | solution.py:27
  29.8 0.2 collective-permute-start.9
  30.0 0.0 collective-permute-done.5.refs_2_
  30.0 1.0 %collective-permute-done.6.refs_3_ = s32[192,128]{1,0:T(8,128)S(1)} collective-permute-done((s32[192,128]{1,0:T(8,128)S(1)}, s32[192,128]{1,0:T(8,128)S(1)}, u32[]{:S(2)}, u32[]{:S(2)}) %collective-permute-start.6) | collective-permute-done | bytes 98336 | tf_op jit(solution)/shard_map/ppermute | solution.py:27
  31.0 0.1 finish_0.1.refs_0_
  31.2 0.0 collective-permute-done.10.refs_4_
  31.2 1.5 %collective-permute-done.8.refs_2_ = s32[64,128]{1,0:T(8,128)S(1)} collective-permute-done((s32[64,128]{1,0:T(8,128)S(1)}, s32[64,128]{1,0:T(8,128)S(1)}, u32[]{:S(2)}, u32[]{:S(2)}) %collective-permute-start.8) | collective-permute-done | bytes 32800 | tf_op jit(solution)/shard_map/ppermute | solution.py:27
  32.7 1.0 %collective-permute-done.9.refs_3_ = s32[64,128]{1,0:T(8,128)S(1)} collective-permute-done((s32[64,128]{1,0:T(8,128)S(1)}, s32[64,128]{1,0:T(8,128)S(1)}, u32[]{:S(2)}, u32[]{:S(2)}) %collective-permute-start.9) | collective-permute-done | bytes 32800 | tf_op jit(solution)/shard_map/ppermute | solution.py:27
  33.7 0.7 %finish_96.1 = bf16[2,2,128,128]{3,2,1,0:T(8,128)(2,1)} custom-call(bf16[2,2,96,128]{3,2,1,0:T(8,128)(2,1)S(1)} %finish_0.1.refs_0_, f32[4,32,128]{2,1,0:T(8,128)S(1)} %get-tuple-element.43.refs_1_, s32[64,128]{1,0:T(8,128)S(1)} %collective-permute-done.8.refs_2_, s32[64,128]{1,0:T(8,128)S(1)} %collective-permute-done.9.refs_3_, ...), custom_call_target="tpu_custom_call" | custom-call | tf_op jit(solution)/shard_map/finish_96/pallas_call | solution.py:401
Async XLA Ops:
  1.2 17.2 %collective-permute-start.3 = (bf16[2320,128]{1,0:T(8,128)(2,1)S(1)}, bf16[2320,128]{1,0:T(8,128)(2,1)S(1)}, u32[]{:S(2)}, u32[]{:S(2)}) collective-permute-start(bf16[2320,128]{1,0:T(8,128)(2,1)S(1)} %get-tuple-element.31.refs_0_), channel_id=1, source_target_pairs={{4,0},{0,4},{5,1},{1,5},{6,2},{2,6},{7,3},{3,7},{12,8},{8,12},{13,... | collective-permute-start | bytes 1781768 | tf_op jit(solution)/shard_map/ppermute | solution.py:41
  5.2 5.1 %collective-permute-start.1 = (bf16[528,128]{1,0:T(8,128)(2,1)S(1)}, bf16[528,128]{1,0:T(8,128)(2,1)S(1)}, u32[]{:S(2)}, u32[]{:S(2)}) collective-permute-start(bf16[528,128]{1,0:T(8,128)(2,1)S(1)} %get-tuple-element.32.refs_2_), channel_id=1, source_target_pairs={{0,16},{8,24},{16,0},{24,8},{1,17},{9,25},{17,1},{25,9},{2,18},{10... | collective-permute-start | bytes 405512 | tf_op jit(solution)/shard_map/ppermute | solution.py:27
  6.8 3.5 %collective-permute-start = (bf16[528,128]{1,0:T(8,128)(2,1)S(1)}, bf16[528,128]{1,0:T(8,128)(2,1)S(1)}, u32[]{:S(2)}, u32[]{:S(2)}) collective-permute-start(bf16[528,128]{1,0:T(8,128)(2,1)S(1)} %get-tuple-element.32.refs_2_), channel_id=1, source_target_pairs={{0,8},{8,0},{16,24},{24,16},{1,9},{9,1},{17,25},{25,17},{2,10},{10... | collective-permute-start | bytes 405512 | tf_op jit(solution)/shard_map/ppermute | solution.py:27
  10.4 1.4 %collective-permute-start.2 = (bf16[528,128]{1,0:T(8,128)(2,1)S(1)}, bf16[528,128]{1,0:T(8,128)(2,1)S(1)}, u32[]{:S(2)}, u32[]{:S(2)}) collective-permute-start(bf16[528,128]{1,0:T(8,128)(2,1)S(1)} %collective-permute-done.1.refs_4_), channel_id=1, source_target_pairs={{0,8},{8,0},{16,24},{24,16},{1,9},{9,1},{17,25},{25,17},{2,10},{10... | collective-permute-start | bytes 405512 | tf_op jit(solution)/shard_map/ppermute | solution.py:27
  12.9 11.3 %collective-permute-start.7 = (bf16[768,128]{1,0:T(8,128)(2,1)S(1)}, bf16[768,128]{1,0:T(8,128)(2,1)S(1)}, u32[]{:S(2)}, u32[]{:S(2)}) collective-permute-start(bf16[768,128]{1,0:T(8,128)(2,1)S(1)} %get-tuple-element.42.refs_1_), channel_id=1, source_target_pairs={{4,0},{0,4},{5,1},{1,5},{6,2},{2,6},{7,3},{3,7},{12,8},{8,12},{13,... | collective-permute-start | bytes 589832 | tf_op jit(solution)/shard_map/ppermute | solution.py:41
  19.1 10.7 %collective-permute-start.4 = (s32[192,128]{1,0:T(8,128)S(1)}, s32[192,128]{1,0:T(8,128)S(1)}, u32[]{:S(2)}, u32[]{:S(2)}) collective-permute-start(s32[192,128]{1,0:T(8,128)S(1)} %get-tuple-element.38), channel_id=1, source_target_pairs={{0,2},{1,3},{2,0},{3,1},{4,6},{5,7},{6,4},{7,5},{8,10},{9,11},{10,... | collective-permute-start | bytes 294920 | tf_op jit(solution)/shard_map/ppermute | solution.py:27
  22.4 7.7 %collective-permute-start.5 = (s32[192,128]{1,0:T(8,128)S(1)}, s32[192,128]{1,0:T(8,128)S(1)}, u32[]{:S(2)}, u32[]{:S(2)}) collective-permute-start(s32[192,128]{1,0:T(8,128)S(1)} %get-tuple-element.39), channel_id=1, source_target_pairs={{0,3},{1,2},{2,1},{3,0},{4,7},{5,6},{6,5},{7,4},{8,11},{9,10},{10,... | collective-permute-start | bytes 294920 | tf_op jit(solution)/shard_map/ppermute | solution.py:27
  23.7 7.3 %collective-permute-start.6 = (s32[192,128]{1,0:T(8,128)S(1)}, s32[192,128]{1,0:T(8,128)S(1)}, u32[]{:S(2)}, u32[]{:S(2)}) collective-permute-start(s32[192,128]{1,0:T(8,128)S(1)} %get-tuple-element.40), channel_id=1, source_target_pairs={{0,1},{1,0},{2,3},{3,2},{4,5},{5,4},{6,7},{7,6},{8,9},{9,8},{10,11... | collective-permute-start | bytes 294920 | tf_op jit(solution)/shard_map/ppermute | solution.py:27
  24.6 6.6 %collective-permute-start.10 = (s32[64,128]{1,0:T(8,128)S(1)}, s32[64,128]{1,0:T(8,128)S(1)}, u32[]{:S(2)}, u32[]{:S(2)}) collective-permute-start(s32[64,128]{1,0:T(8,128)S(1)} %get-tuple-element.46), channel_id=1, source_target_pairs={{0,3},{1,2},{2,1},{3,0},{4,7},{5,6},{6,5},{7,4},{8,11},{9,10},{10,... | collective-permute-start | bytes 98312 | tf_op jit(solution)/shard_map/ppermute | solution.py:27
  27.9 4.8 %collective-permute-start.8 = (s32[64,128]{1,0:T(8,128)S(1)}, s32[64,128]{1,0:T(8,128)S(1)}, u32[]{:S(2)}, u32[]{:S(2)}) collective-permute-start(s32[64,128]{1,0:T(8,128)S(1)} %get-tuple-element.44), channel_id=1, source_target_pairs={{0,2},{1,3},{2,0},{3,1},{4,6},{5,7},{6,4},{7,5},{8,10},{9,11},{10,... | collective-permute-start | bytes 98312 | tf_op jit(solution)/shard_map/ppermute | solution.py:27
  29.8 3.9 %collective-permute-start.9 = (s32[64,128]{1,0:T(8,128)S(1)}, s32[64,128]{1,0:T(8,128)S(1)}, u32[]{:S(2)}, u32[]{:S(2)}) collective-permute-start(s32[64,128]{1,0:T(8,128)S(1)} %get-tuple-element.45), channel_id=1, source_target_pairs={{0,1},{1,0},{2,3},{3,2},{4,5},{5,4},{6,7},{7,6},{8,9},{9,8},{10,11... | collective-permute-start | bytes 98312 | tf_op jit(solution)/shard_map/ppermute | solution.py:27

commit v24 on v22

--- a/solution.py
+++ b/solution.py
@@ -106,6 +106,14 @@
         load.wait()
 
 
+def range_kernel(span, x_in, out, sem):
+    first, height = span
+    spot = out.reshape(x_in.shape[0], height, x_in.shape[2])
+    load = pltpu.make_async_copy(x_in.at[:, pl.ds(first, height)], spot, sem)
+    load.start()
+    load.wait()
+
+
 def match(sizes, place, panel_cols, kept_cols):
     width, local_rows, kept = sizes
     right, goal, local = place
@@ -362,7 +370,21 @@
     )(known, *x_sent, *s_pieces)
 
     moved = block_size * (8 * all_slots + 2 * panel_size + 2 * count * (cols - 1))
-    later, panel_cols = lax.optimization_barrier((x_sent[1:], panel_cols))
+    late_blocks, panel_cols = lax.optimization_barrier((a_blocks, panel_cols))
+    later = [
+        pl.pallas_call(
+            functools.partial(range_kernel, span),
+            out_shape=jax.ShapeDtypeStruct((count * span[1], order), jnp.bfloat16),
+            in_specs=[far],
+            out_specs=vector,
+            scratch_shapes=[pltpu.SemaphoreType.DMA],
+            compiler_params=pltpu.CompilerParams(
+                vmem_limit_bytes=2 * block_size * count + 4 * MIB
+            ),
+            name=f"pack_{span[0]}",
+        )(*in_hbm(late_blocks))
+        for span in ranges[1:]
+    ]
     x_pieces = [first_piece]
     x_pieces += [[shifted(part, "col", j) for j in range(1, cols)] for part in later]
 

time: 32.2 us -> 32.8 us (1.019)
  Pallas kernels: 5.08 us -> 6.04 us
    pallas_call x0 -> x1, Pallas kernels: none -> 0.97 us  [per_device(): pl.pallas_call(functools.partial(range_kernel, span), out_shape=jax.Shape...]
  transfers between devices with their start and end apart: 11 -> 11, of which waited for: 6 -> 6; matrix products, arithmetic and copies ran while one was open for 0% -> 0% of each run, Pallas kernels for 10% -> 13%
where the time goes in v24:
time: 32.8 us; the launch traced here: 32.5 us
  starting transfers between devices  13.9 us (42%)
  waiting for transfers between devices  12.5 us (38%)
  Pallas kernels  6.04 us (18%)
    ppermute x9, starting transfers between devices, flipped(): lax.ppermute(value, axis, [(i, i ^ bits) for i in range(lax.axis_size(axi...  10.5 us
    ppermute x9, waiting for transfers between devices, flipped(): lax.ppermute(value, axis, [(i, i ^ bits) for i in range(lax.axis_size(axi...  8.95 us
    ppermute x2, waiting for transfers between devices, shifted(): lax.ppermute(value, axis, [((i + offset) % size, i) for i in range(size)])  3.55 us
    ppermute x2, starting transfers between devices, shifted(): lax.ppermute(value, axis, [((i + offset) % size, i) for i in range(size)])  3.38 us
    pallas_call x2, Pallas kernels, per_device(): pl.pallas_call(functools.partial(peer_kernel, (cols, layers, count, width...  1.21 us
    pallas_call x1, Pallas kernels, per_device(): pl.pallas_call(functools.partial(pack_first_kernel, (layers, count, piece...  1.11 us
    pallas_call x1, Pallas kernels, per_device(): pl.pallas_call(functools.partial(pack_later_kernel, (count, piece, order,...  1.11 us
    pallas_call x1, Pallas kernels, per_device(): pl.pallas_call(functools.partial(range_kernel, span), out_shape=jax.Shape...  0.97 us
  transfers between devices with their start and end apart: 11, of which 6 were waited for; matrix products, arithmetic and copies ran while one was open for 0% of the time, Pallas kernels for 13%

profile of v24, /device:TPU:0, one launch (start us, length us, event | category | flops | bytes accessed | tf_op | source)
XLA Modules:
  0.0 32.5 jit_solution(15281763904600742634)
XLA Ops:
  0.0 1.1 %pack_first.1 = (s32[16,128]{1,0:T(8,128)S(1)}, bf16[1936,128]{1,0:T(8,128)(2,1)S(1)}) custom-call(s32[1,24]{1,0:T(1,128)} %bitcast.6, s32[1,24]{1,0:T(1,128)} %bitcast.7, s32[2,8]{1,0:T(2,128)} %bitcast.5, bf16[24,128,128]{2,1,0:T(8,128)(2,1)} %x_in.3), custom_call_target="tpu_custom_call" | custom-call | tf_op jit(solution)/shard_map/pack_first/pallas_call | solution.py:303
  1.1 3.0 %collective-permute-start.3 = (bf16[1936,128]{1,0:T(8,128)(2,1)S(1)}, bf16[1936,128]{1,0:T(8,128)(2,1)S(1)}, u32[]{:S(2)}, u32[]{:S(2)}) collective-permute-start(bf16[1936,128]{1,0:T(8,128)(2,1)S(1)} %get-tuple-element.27.refs_0_), channel_id=1, source_target_pairs={{4,0},{0,4},{5,1},{1,5},{6,2},{2,6},{7,3},{3,7},{12,8},{8,12},{13,... | collective-permute-start | bytes 1486856 | tf_op jit(solution)/shard_map/ppermute | solution.py:41
  4.1 1.1 %pack_later.1 = (bf16[528,128]{1,0:T(8,128)(2,1)S(1)}, bf16[1152,128]{1,0:T(8,128)(2,1)S(1)}) custom-call(bf16[24,128,128]{2,1,0:T(8,128)(2,1)} %x_in.3, s32[2,2]{1,0:T(2,128)} %s_cols, bf16[4,128,128]{2,1,0:T(8,128)(2,1)} %bitcast.4), custom_call_target="tpu_custom_call" | custom-call | tf_op jit(solution)/shard_map/pack_later/pallas_call | solution.py:330
  5.2 1.6 %collective-permute-start.1 = (bf16[528,128]{1,0:T(8,128)(2,1)S(1)}, bf16[528,128]{1,0:T(8,128)(2,1)S(1)}, u32[]{:S(2)}, u32[]{:S(2)}) collective-permute-start(bf16[528,128]{1,0:T(8,128)(2,1)S(1)} %get-tuple-element.32.refs_2_), channel_id=1, source_target_pairs={{0,16},{8,24},{16,0},{24,8},{1,17},{9,25},{17,1},{25,9},{2,18},{10... | collective-permute-start | bytes 405512 | tf_op jit(solution)/shard_map/ppermute | solution.py:27
  6.8 0.0 collective-permute-start
  6.8 3.5 %collective-permute-done.1.refs_4_ = bf16[528,128]{1,0:T(8,128)(2,1)S(1)} collective-permute-done((bf16[528,128]{1,0:T(8,128)(2,1)S(1)}, bf16[528,128]{1,0:T(8,128)(2,1)S(1)}, u32[]{:S(2)}, u32[]{:S(2)}) %collective-permute-start.1) | collective-permute-done | bytes 135200 | tf_op jit(solution)/shard_map/ppermute | solution.py:27
  10.4 0.0 collective-permute-start.2
  10.4 0.0 collective-permute-done.refs_3_
  10.4 1.3 %collective-permute-done.2.refs_5_ = bf16[528,128]{1,0:T(8,128)(2,1)S(1)} collective-permute-done((bf16[528,128]{1,0:T(8,128)(2,1)S(1)}, bf16[528,128]{1,0:T(8,128)(2,1)S(1)}, u32[]{:S(2)}, u32[]{:S(2)}) %collective-permute-start.2) | collective-permute-done | bytes 135200 | tf_op jit(solution)/shard_map/ppermute | solution.py:27
  11.7 0.8 %own_products.1 = (f32[17,128,128]{2,1,0:T(8,128)S(1)}, bf16[16,128,128]{2,1,0:T(8,128)(2,1)S(1)}, s32[8,128]{1,0:T(8,128)S(1)}) custom-call(s32[16,128]{1,0:T(8,128)S(1)} %get-tuple-element.26.known.refs_0_, bf16[1936,128]{1,0:T(8,128)(2,1)S(1)} %get-tuple-element.27.refs_0_, bf16[1152,128]{1,0:T(8,128)(2,1)S(1)} %get-tuple-element.31.refs_1_, ...), custom_call_target="tpu_custom_call" | custom-call | flops 50331648 | bytes 2883584 | tf_op jit(solution)/shard_map/own_products/pallas_call | solution.py:351
  12.5 1.0 %pack_80.1 = bf16[1152,128]{1,0:T(8,128)(2,1)S(1)} custom-call(bf16[24,128,128]{2,1,0:T(8,128)(2,1)} %x_in.3), custom_call_target="tpu_custom_call" | custom-call | tf_op jit(solution)/shard_map/pack_80/pallas_call | solution.py:375
  13.5 0.4 %collective-permute-start.7 = (bf16[1152,128]{1,0:T(8,128)(2,1)S(1)}, bf16[1152,128]{1,0:T(8,128)(2,1)S(1)}, u32[]{:S(2)}, u32[]{:S(2)}) collective-permute-start(bf16[1152,128]{1,0:T(8,128)(2,1)S(1)} %pack_80.1), channel_id=1, source_target_pairs={{4,0},{0,4},{5,1},{1,5},{6,2},{2,6},{7,3},{3,7},{12,8},{8,12},{13,... | collective-permute-start | bytes 884744 | tf_op jit(solution)/shard_map/ppermute | solution.py:41
  13.8 1.6 %collective-permute-done.3.refs_2_ = bf16[1936,128]{1,0:T(8,128)(2,1)S(1)} collective-permute-done((bf16[1936,128]{1,0:T(8,128)(2,1)S(1)}, bf16[1936,128]{1,0:T(8,128)(2,1)S(1)}, u32[]{:S(2)}, u32[]{:S(2)}) %collective-permute-start.3) | collective-permute-done | bytes 495648 | tf_op jit(solution)/shard_map/ppermute | solution.py:41
  15.4 0.7 %peer_products_0.1 = (f32[4,80,128]{2,1,0:T(8,128)S(1)}, s32[160,128]{1,0:T(8,128)S(1)}, s32[160,128]{1,0:T(8,128)S(1)}, s32[160,128]{1,0:T(8,128)S(1)}, s32[1,8,128]{2,1,0:T(8,128)S(1)}) custom-call(s32[16,128]{1,0:T(8,128)S(1)} %get-tuple-element.26.known.refs_0_, s32[8,128]{1,0:T(8,128)S(1)} %get-tuple-element.34.refs_1_, ...), custom_call_target="tpu_custom_call" | custom-call | flops 31457280 | bytes 1703936 | tf_op jit(solution)/shard_map/peer_products_0/pallas_call | solution.py:402
  16.2 2.9 %collective-permute-start.4 = (s32[160,128]{1,0:T(8,128)S(1)}, s32[160,128]{1,0:T(8,128)S(1)}, u32[]{:S(2)}, u32[]{:S(2)}) collective-permute-start(s32[160,128]{1,0:T(8,128)S(1)} %get-tuple-element.38), channel_id=1, source_target_pairs={{0,2},{1,3},{2,0},{3,1},{4,6},{5,7},{6,4},{7,5},{8,10},{9,11},{10,... | collective-permute-start | bytes 245768 | tf_op jit(solution)/shard_map/ppermute | solution.py:27
  19.1 1.4 %collective-permute-start.5 = (s32[160,128]{1,0:T(8,128)S(1)}, s32[160,128]{1,0:T(8,128)S(1)}, u32[]{:S(2)}, u32[]{:S(2)}) collective-permute-start(s32[160,128]{1,0:T(8,128)S(1)} %get-tuple-element.39), channel_id=1, source_target_pairs={{0,3},{1,2},{2,1},{3,0},{4,7},{5,6},{6,5},{7,4},{8,11},{9,10},{10,... | collective-permute-start | bytes 245768 | tf_op jit(solution)/shard_map/ppermute | solution.py:27
  20.4 0.2 collective-permute-start.6
  20.6 2.0 %collective-permute-done.7.refs_1_ = bf16[1152,128]{1,0:T(8,128)(2,1)S(1)} collective-permute-done((bf16[1152,128]{1,0:T(8,128)(2,1)S(1)}, bf16[1152,128]{1,0:T(8,128)(2,1)S(1)}, u32[]{:S(2)}, u32[]{:S(2)}) %collective-permute-start.7) | collective-permute-done | bytes 294944 | tf_op jit(solution)/shard_map/ppermute | solution.py:41
  22.6 0.5 %peer_products_80.1 = (f32[4,48,128]{2,1,0:T(8,128)S(1)}, s32[96,128]{1,0:T(8,128)S(1)}, s32[96,128]{1,0:T(8,128)S(1)}, s32[96,128]{1,0:T(8,128)S(1)}) custom-call(s32[1,8,128]{2,1,0:T(8,128)S(1)} %get-tuple-element.41.refs_0_, bf16[1152,128]{1,0:T(8,128)(2,1)S(1)} %collective-permute-done.7.refs_1_, ...), custom_call_target="tpu_custom_call" | custom-call | flops 18874368 | bytes 1703936 | tf_op jit(solution)/shard_map/peer_products_80/pallas_call | solution.py:402
  23.1 3.7 %collective-permute-start.10 = (s32[96,128]{1,0:T(8,128)S(1)}, s32[96,128]{1,0:T(8,128)S(1)}, u32[]{:S(2)}, u32[]{:S(2)}) collective-permute-start(s32[96,128]{1,0:T(8,128)S(1)} %get-tuple-element.46), channel_id=1, source_target_pairs={{0,3},{1,2},{2,1},{3,0},{4,7},{5,6},{6,5},{7,4},{8,11},{9,10},{10,... | collective-permute-start | bytes 147464 | tf_op jit(solution)/shard_map/ppermute | solution.py:27
  26.8 0.0 collective-permute-start.8
  26.8 0.0 collective-permute-done.4.refs_1_
  26.8 0.8 %collective-permute-start.9 = (s32[96,128]{1,0:T(8,128)S(1)}, s32[96,128]{1,0:T(8,128)S(1)}, u32[]{:S(2)}, u32[]{:S(2)}) collective-permute-start(s32[96,128]{1,0:T(8,128)S(1)} %get-tuple-element.45), channel_id=1, source_target_pairs={{0,1},{1,0},{2,3},{3,2},{4,5},{5,4},{6,7},{7,6},{8,9},{9,8},{10,11... | collective-permute-start | bytes 147464 | tf_op jit(solution)/shard_map/ppermute | solution.py:27
  27.6 0.0 collective-permute-done.5.refs_2_
  27.6 0.0 collective-permute-done.6.refs_3_
  27.6 0.1 finish_0.1.refs_0_
  27.7 1.8 %collective-permute-done.10.refs_4_ = s32[96,128]{1,0:T(8,128)S(1)} collective-permute-done((s32[96,128]{1,0:T(8,128)S(1)}, s32[96,128]{1,0:T(8,128)S(1)}, u32[]{:S(2)}, u32[]{:S(2)}) %collective-permute-start.10) | collective-permute-done | bytes 49184 | tf_op jit(solution)/shard_map/ppermute | solution.py:27
  29.5 2.3 %collective-permute-done.8.refs_2_ = s32[96,128]{1,0:T(8,128)S(1)} collective-permute-done((s32[96,128]{1,0:T(8,128)S(1)}, s32[96,128]{1,0:T(8,128)S(1)}, u32[]{:S(2)}, u32[]{:S(2)}) %collective-permute-start.8) | collective-permute-done | bytes 49184 | tf_op jit(solution)/shard_map/ppermute | solution.py:27
  31.8 0.0 collective-permute-done.9.refs_3_
  31.8 0.7 %finish_80.1 = bf16[2,2,128,128]{3,2,1,0:T(8,128)(2,1)} custom-call(bf16[2,2,80,128]{3,2,1,0:T(8,128)(2,1)S(1)} %finish_0.1.refs_0_, f32[4,48,128]{2,1,0:T(8,128)S(1)} %get-tuple-element.43.refs_1_, s32[96,128]{1,0:T(8,128)S(1)} %collective-permute-done.8.refs_2_, s32[96,128]{1,0:T(8,128)S(1)} %collective-permute-done.9.refs_3_, ...), custom_call_target="tpu_custom_call" | custom-call | tf_op jit(solution)/shard_map/finish_80/pallas_call | solution.py:423
Async XLA Ops:
  1.1 14.3 %collective-permute-start.3 = (bf16[1936,128]{1,0:T(8,128)(2,1)S(1)}, bf16[1936,128]{1,0:T(8,128)(2,1)S(1)}, u32[]{:S(2)}, u32[]{:S(2)}) collective-permute-start(bf16[1936,128]{1,0:T(8,128)(2,1)S(1)} %get-tuple-element.27.refs_0_), channel_id=1, source_target_pairs={{4,0},{0,4},{5,1},{1,5},{6,2},{2,6},{7,3},{3,7},{12,8},{8,12},{13,... | collective-permute-start | bytes 1486856 | tf_op jit(solution)/shard_map/ppermute | solution.py:41
  5.2 5.1 %collective-permute-start.1 = (bf16[528,128]{1,0:T(8,128)(2,1)S(1)}, bf16[528,128]{1,0:T(8,128)(2,1)S(1)}, u32[]{:S(2)}, u32[]{:S(2)}) collective-permute-start(bf16[528,128]{1,0:T(8,128)(2,1)S(1)} %get-tuple-element.32.refs_2_), channel_id=1, source_target_pairs={{0,16},{8,24},{16,0},{24,8},{1,17},{9,25},{17,1},{25,9},{2,18},{10... | collective-permute-start | bytes 405512 | tf_op jit(solution)/shard_map/ppermute | solution.py:27
  6.8 3.5 %collective-permute-start = (bf16[528,128]{1,0:T(8,128)(2,1)S(1)}, bf16[528,128]{1,0:T(8,128)(2,1)S(1)}, u32[]{:S(2)}, u32[]{:S(2)}) collective-permute-start(bf16[528,128]{1,0:T(8,128)(2,1)S(1)} %get-tuple-element.32.refs_2_), channel_id=1, source_target_pairs={{0,8},{8,0},{16,24},{24,16},{1,9},{9,1},{17,25},{25,17},{2,10},{10... | collective-permute-start | bytes 405512 | tf_op jit(solution)/shard_map/ppermute | solution.py:27
  10.4 1.4 %collective-permute-start.2 = (bf16[528,128]{1,0:T(8,128)(2,1)S(1)}, bf16[528,128]{1,0:T(8,128)(2,1)S(1)}, u32[]{:S(2)}, u32[]{:S(2)}) collective-permute-start(bf16[528,128]{1,0:T(8,128)(2,1)S(1)} %collective-permute-done.1.refs_4_), channel_id=1, source_target_pairs={{0,8},{8,0},{16,24},{24,16},{1,9},{9,1},{17,25},{25,17},{2,10},{10... | collective-permute-start | bytes 405512 | tf_op jit(solution)/shard_map/ppermute | solution.py:27
  13.5 9.1 %collective-permute-start.7 = (bf16[1152,128]{1,0:T(8,128)(2,1)S(1)}, bf16[1152,128]{1,0:T(8,128)(2,1)S(1)}, u32[]{:S(2)}, u32[]{:S(2)}) collective-permute-start(bf16[1152,128]{1,0:T(8,128)(2,1)S(1)} %pack_80.1), channel_id=1, source_target_pairs={{4,0},{0,4},{5,1},{1,5},{6,2},{2,6},{7,3},{3,7},{12,8},{8,12},{13,... | collective-permute-start | bytes 884744 | tf_op jit(solution)/shard_map/ppermute | solution.py:41
  16.2 10.6 %collective-permute-start.4 = (s32[160,128]{1,0:T(8,128)S(1)}, s32[160,128]{1,0:T(8,128)S(1)}, u32[]{:S(2)}, u32[]{:S(2)}) collective-permute-start(s32[160,128]{1,0:T(8,128)S(1)} %get-tuple-element.38), channel_id=1, source_target_pairs={{0,2},{1,3},{2,0},{3,1},{4,6},{5,7},{6,4},{7,5},{8,10},{9,11},{10,... | collective-permute-start | bytes 245768 | tf_op jit(solution)/shard_map/ppermute | solution.py:27
  19.1 8.5 %collective-permute-start.5 = (s32[160,128]{1,0:T(8,128)S(1)}, s32[160,128]{1,0:T(8,128)S(1)}, u32[]{:S(2)}, u32[]{:S(2)}) collective-permute-start(s32[160,128]{1,0:T(8,128)S(1)} %get-tuple-element.39), channel_id=1, source_target_pairs={{0,3},{1,2},{2,1},{3,0},{4,7},{5,6},{6,5},{7,4},{8,11},{9,10},{10,... | collective-permute-start | bytes 245768 | tf_op jit(solution)/shard_map/ppermute | solution.py:27
  20.4 7.2 %collective-permute-start.6 = (s32[160,128]{1,0:T(8,128)S(1)}, s32[160,128]{1,0:T(8,128)S(1)}, u32[]{:S(2)}, u32[]{:S(2)}) collective-permute-start(s32[160,128]{1,0:T(8,128)S(1)} %get-tuple-element.40), channel_id=1, source_target_pairs={{0,1},{1,0},{2,3},{3,2},{4,5},{5,4},{6,7},{7,6},{8,9},{9,8},{10,11... | collective-permute-start | bytes 245768 | tf_op jit(solution)/shard_map/ppermute | solution.py:27
  23.1 6.4 %collective-permute-start.10 = (s32[96,128]{1,0:T(8,128)S(1)}, s32[96,128]{1,0:T(8,128)S(1)}, u32[]{:S(2)}, u32[]{:S(2)}) collective-permute-start(s32[96,128]{1,0:T(8,128)S(1)} %get-tuple-element.46), channel_id=1, source_target_pairs={{0,3},{1,2},{2,1},{3,0},{4,7},{5,6},{6,5},{7,4},{8,11},{9,10},{10,... | collective-permute-start | bytes 147464 | tf_op jit(solution)/shard_map/ppermute | solution.py:27
  26.8 5.0 %collective-permute-start.8 = (s32[96,128]{1,0:T(8,128)S(1)}, s32[96,128]{1,0:T(8,128)S(1)}, u32[]{:S(2)}, u32[]{:S(2)}) collective-permute-start(s32[96,128]{1,0:T(8,128)S(1)} %get-tuple-element.44), channel_id=1, source_target_pairs={{0,2},{1,3},{2,0},{3,1},{4,6},{5,7},{6,4},{7,5},{8,10},{9,11},{10,... | collective-permute-start | bytes 147464 | tf_op jit(solution)/shard_map/ppermute | solution.py:27
  26.8 5.0 %collective-permute-start.9 = (s32[96,128]{1,0:T(8,128)S(1)}, s32[96,128]{1,0:T(8,128)S(1)}, u32[]{:S(2)}, u32[]{:S(2)}) collective-permute-start(s32[96,128]{1,0:T(8,128)S(1)} %get-tuple-element.45), channel_id=1, source_target_pairs={{0,1},{1,0},{2,3},{3,2},{4,5},{5,4},{6,7},{7,6},{8,9},{9,8},{10,11... | collective-permute-start | bytes 147464 | tf_op jit(solution)/shard_map/ppermute | solution.py:27

commit v25 on v22

--- a/solution.py
+++ b/solution.py
@@ -362,7 +362,7 @@
     )(known, *x_sent, *s_pieces)
 
     moved = block_size * (8 * all_slots + 2 * panel_size + 2 * count * (cols - 1))
-    later, panel_cols = lax.optimization_barrier((x_sent[1:], panel_cols))
+    later, _ = lax.optimization_barrier((x_sent[1:], s_pieces))
     x_pieces = [first_piece]
     x_pieces += [[shifted(part, "col", j) for j in range(1, cols)] for part in later]
 

time: 32.2 us -> 32.1 us (level)
    ppermute x9, starting transfers between devices: 10.6 us -> 10.9 us  [flipped(): lax.ppermute(value, axis, [(i, i ^ bits) for i in range(lax.axis_size(axi...]
  transfers between devices with their start and end apart: 11 -> 11, of which waited for: 6 -> 7; matrix products, arithmetic and copies ran while one was open for 0% -> 0% of each run, Pallas kernels for 10% -> 10%
where the time goes in v25:
time: 32.1 us; the launch traced here: 31.9 us
  starting transfers between devices  14.2 us (44%)
  waiting for transfers between devices  12.6 us (39%)
  Pallas kernels  5.06 us (16%)
    ppermute x9, starting transfers between devices, flipped(): lax.ppermute(value, axis, [(i, i ^ bits) for i in range(lax.axis_size(axi...  10.9 us
    ppermute x9, waiting for transfers between devices, flipped(): lax.ppermute(value, axis, [(i, i ^ bits) for i in range(lax.axis_size(axi...  9.1 us
    ppermute x2, waiting for transfers between devices, shifted(): lax.ppermute(value, axis, [((i + offset) % size, i) for i in range(size)])  3.47 us
    ppermute x2, starting transfers between devices, shifted(): lax.ppermute(value, axis, [((i + offset) % size, i) for i in range(size)])  3.32 us
    pallas_call x2, Pallas kernels, per_device(): pl.pallas_call(functools.partial(peer_kernel, (cols, layers, count, width...  1.22 us
    pallas_call x1, Pallas kernels, per_device(): pl.pallas_call(functools.partial(pack_first_kernel, (layers, count, piece...  1.11 us
    pallas_call x1, Pallas kernels, per_device(): pl.pallas_call(functools.partial(pack_later_kernel, (count, piece, order,...  1.11 us
    pallas_call x2, Pallas kernels, per_device(): pl.pallas_call(functools.partial(finish_kernel, (layers, slots), (at, hei...  0.86 us
  transfers between devices with their start and end apart: 11, of which 7 were waited for; matrix products, arithmetic and copies ran while one was open for 0% of the time, Pallas kernels for 10%

profile of v25, /device:TPU:0, one launch (start us, length us, event | category | flops | bytes accessed | tf_op | source)
XLA Modules:
  0.0 31.9 jit_solution(7370344555049660653)
XLA Ops:
  0.0 1.1 %pack_first.1 = (s32[16,128]{1,0:T(8,128)S(1)}, bf16[1936,128]{1,0:T(8,128)(2,1)S(1)}) custom-call(s32[1,24]{1,0:T(1,128)} %bitcast.6, s32[1,24]{1,0:T(1,128)} %bitcast.7, s32[2,8]{1,0:T(2,128)} %bitcast.5, bf16[24,128,128]{2,1,0:T(8,128)(2,1)} %x_in.2), custom_call_target="tpu_custom_call" | custom-call | tf_op jit(solution)/shard_map/pack_first/pallas_call | solution.py:295
  1.1 3.0 %collective-permute-start.3 = (bf16[1936,128]{1,0:T(8,128)(2,1)S(1)}, bf16[1936,128]{1,0:T(8,128)(2,1)S(1)}, u32[]{:S(2)}, u32[]{:S(2)}) collective-permute-start(bf16[1936,128]{1,0:T(8,128)(2,1)S(1)} %get-tuple-element.26.refs_0_), channel_id=1, source_target_pairs={{4,0},{0,4},{5,1},{1,5},{6,2},{2,6},{7,3},{3,7},{12,8},{8,12},{13,... | collective-permute-start | bytes 1486856 | tf_op jit(solution)/shard_map/ppermute | solution.py:41
  4.1 1.1 %pack_later.1 = (bf16[528,128]{1,0:T(8,128)(2,1)S(1)}, bf16[1152,128]{1,0:T(8,128)(2,1)S(1)}) custom-call(bf16[24,128,128]{2,1,0:T(8,128)(2,1)} %x_in.2, s32[2,2]{1,0:T(2,128)} %s_cols, bf16[4,128,128]{2,1,0:T(8,128)(2,1)} %bitcast.4), custom_call_target="tpu_custom_call" | custom-call | tf_op jit(solution)/shard_map/pack_later/pallas_call | solution.py:322
  5.2 1.6 %collective-permute-start.1 = (bf16[528,128]{1,0:T(8,128)(2,1)S(1)}, bf16[528,128]{1,0:T(8,128)(2,1)S(1)}, u32[]{:S(2)}, u32[]{:S(2)}) collective-permute-start(bf16[528,128]{1,0:T(8,128)(2,1)S(1)} %get-tuple-element.31.refs_2_), channel_id=1, source_target_pairs={{0,16},{8,24},{16,0},{24,8},{1,17},{9,25},{17,1},{25,9},{2,18},{10... | collective-permute-start | bytes 405512 | tf_op jit(solution)/shard_map/ppermute | solution.py:27
  6.8 0.0 collective-permute-start
  6.8 3.5 %collective-permute-done.1.refs_4_ = bf16[528,128]{1,0:T(8,128)(2,1)S(1)} collective-permute-done((bf16[528,128]{1,0:T(8,128)(2,1)S(1)}, bf16[528,128]{1,0:T(8,128)(2,1)S(1)}, u32[]{:S(2)}, u32[]{:S(2)}) %collective-permute-start.1) | collective-permute-done | bytes 135200 | tf_op jit(solution)/shard_map/ppermute | solution.py:27
  10.4 0.0 collective-permute-start.2
  10.4 0.0 collective-permute-done.refs_3_
  10.4 1.3 %collective-permute-done.2.refs_5_ = bf16[528,128]{1,0:T(8,128)(2,1)S(1)} collective-permute-done((bf16[528,128]{1,0:T(8,128)(2,1)S(1)}, bf16[528,128]{1,0:T(8,128)(2,1)S(1)}, u32[]{:S(2)}, u32[]{:S(2)}) %collective-permute-start.2) | collective-permute-done | bytes 135200 | tf_op jit(solution)/shard_map/ppermute | solution.py:27
  11.7 0.3 collective-permute-start.7
  12.0 0.8 %own_products.1 = (f32[17,128,128]{2,1,0:T(8,128)S(1)}, bf16[16,128,128]{2,1,0:T(8,128)(2,1)S(1)}, s32[8,128]{1,0:T(8,128)S(1)}) custom-call(s32[16,128]{1,0:T(8,128)S(1)} %get-tuple-element.25.known.refs_0_, bf16[1936,128]{1,0:T(8,128)(2,1)S(1)} %get-tuple-element.26.refs_0_, bf16[1152,128]{1,0:T(8,128)(2,1)S(1)} %get-tuple-element.40.refs_1_, ...), custom_call_target="tpu_custom_call" | custom-call | flops 50331648 | bytes 2883584 | tf_op jit(solution)/shard_map/own_products/pallas_call | solution.py:343
  12.8 3.5 %collective-permute-done.3.refs_2_ = bf16[1936,128]{1,0:T(8,128)(2,1)S(1)} collective-permute-done((bf16[1936,128]{1,0:T(8,128)(2,1)S(1)}, bf16[1936,128]{1,0:T(8,128)(2,1)S(1)}, u32[]{:S(2)}, u32[]{:S(2)}) %collective-permute-start.3) | collective-permute-done | bytes 495648 | tf_op jit(solution)/shard_map/ppermute | solution.py:41
  16.3 0.7 %peer_products_0.1 = (f32[4,80,128]{2,1,0:T(8,128)S(1)}, s32[160,128]{1,0:T(8,128)S(1)}, s32[160,128]{1,0:T(8,128)S(1)}, s32[160,128]{1,0:T(8,128)S(1)}, s32[1,8,128]{2,1,0:T(8,128)S(1)}) custom-call(s32[16,128]{1,0:T(8,128)S(1)} %get-tuple-element.25.known.refs_0_, s32[8,128]{1,0:T(8,128)S(1)} %get-tuple-element.32.refs_1_, ...), custom_call_target="tpu_custom_call" | custom-call | flops 31457280 | bytes 1703936 | tf_op jit(solution)/shard_map/peer_products_0/pallas_call | solution.py:380
  17.0 3.2 %collective-permute-start.4 = (s32[160,128]{1,0:T(8,128)S(1)}, s32[160,128]{1,0:T(8,128)S(1)}, u32[]{:S(2)}, u32[]{:S(2)}) collective-permute-start(s32[160,128]{1,0:T(8,128)S(1)} %get-tuple-element.36), channel_id=1, source_target_pairs={{0,2},{1,3},{2,0},{3,1},{4,6},{5,7},{6,4},{7,5},{8,10},{9,11},{10,... | collective-permute-start | bytes 245768 | tf_op jit(solution)/shard_map/ppermute | solution.py:27
  20.2 1.4 %collective-permute-start.5 = (s32[160,128]{1,0:T(8,128)S(1)}, s32[160,128]{1,0:T(8,128)S(1)}, u32[]{:S(2)}, u32[]{:S(2)}) collective-permute-start(s32[160,128]{1,0:T(8,128)S(1)} %get-tuple-element.37), channel_id=1, source_target_pairs={{0,3},{1,2},{2,1},{3,0},{4,7},{5,6},{6,5},{7,4},{8,11},{9,10},{10,... | collective-permute-start | bytes 245768 | tf_op jit(solution)/shard_map/ppermute | solution.py:27
  21.6 0.2 collective-permute-start.6
  21.8 0.0 collective-permute-done.7.refs_1_
  21.8 0.5 %peer_products_80.1 = (f32[4,48,128]{2,1,0:T(8,128)S(1)}, s32[96,128]{1,0:T(8,128)S(1)}, s32[96,128]{1,0:T(8,128)S(1)}, s32[96,128]{1,0:T(8,128)S(1)}) custom-call(s32[1,8,128]{2,1,0:T(8,128)S(1)} %get-tuple-element.39.refs_0_, bf16[1152,128]{1,0:T(8,128)(2,1)S(1)} %collective-permute-done.7.refs_1_, ...), custom_call_target="tpu_custom_call" | custom-call | flops 18874368 | bytes 1703936 | tf_op jit(solution)/shard_map/peer_products_80/pallas_call | solution.py:380
  22.3 3.9 %collective-permute-start.10 = (s32[96,128]{1,0:T(8,128)S(1)}, s32[96,128]{1,0:T(8,128)S(1)}, u32[]{:S(2)}, u32[]{:S(2)}) collective-permute-start(s32[96,128]{1,0:T(8,128)S(1)} %get-tuple-element.44), channel_id=1, source_target_pairs={{0,3},{1,2},{2,1},{3,0},{4,7},{5,6},{6,5},{7,4},{8,11},{9,10},{10,... | collective-permute-start | bytes 147464 | tf_op jit(solution)/shard_map/ppermute | solution.py:27
  26.2 0.0 collective-permute-start.8
  26.2 0.0 collective-permute-done.4.refs_1_
  26.2 0.6 %collective-permute-start.9 = (s32[96,128]{1,0:T(8,128)S(1)}, s32[96,128]{1,0:T(8,128)S(1)}, u32[]{:S(2)}, u32[]{:S(2)}) collective-permute-start(s32[96,128]{1,0:T(8,128)S(1)} %get-tuple-element.43), channel_id=1, source_target_pairs={{0,1},{1,0},{2,3},{3,2},{4,5},{5,4},{6,7},{7,6},{8,9},{9,8},{10,11... | collective-permute-start | bytes 147464 | tf_op jit(solution)/shard_map/ppermute | solution.py:27
  26.8 0.3 collective-permute-done.5.refs_2_
  27.1 0.3 collective-permute-done.6.refs_3_
  27.4 0.1 finish_0.1.refs_0_
  27.5 1.4 %collective-permute-done.10.refs_4_ = s32[96,128]{1,0:T(8,128)S(1)} collective-permute-done((s32[96,128]{1,0:T(8,128)S(1)}, s32[96,128]{1,0:T(8,128)S(1)}, u32[]{:S(2)}, u32[]{:S(2)}) %collective-permute-start.10) | collective-permute-done | bytes 49184 | tf_op jit(solution)/shard_map/ppermute | solution.py:27
  29.0 2.2 %collective-permute-done.8.refs_2_ = s32[96,128]{1,0:T(8,128)S(1)} collective-permute-done((s32[96,128]{1,0:T(8,128)S(1)}, s32[96,128]{1,0:T(8,128)S(1)}, u32[]{:S(2)}, u32[]{:S(2)}) %collective-permute-start.8) | collective-permute-done | bytes 49184 | tf_op jit(solution)/shard_map/ppermute | solution.py:27
  31.2 0.0 collective-permute-done.9.refs_3_
  31.2 0.7 %finish_80.1 = bf16[2,2,128,128]{3,2,1,0:T(8,128)(2,1)} custom-call(bf16[2,2,80,128]{3,2,1,0:T(8,128)(2,1)S(1)} %finish_0.1.refs_0_, f32[4,48,128]{2,1,0:T(8,128)S(1)} %get-tuple-element.41.refs_1_, s32[96,128]{1,0:T(8,128)S(1)} %collective-permute-done.8.refs_2_, s32[96,128]{1,0:T(8,128)S(1)} %collective-permute-done.9.refs_3_, ...), custom_call_target="tpu_custom_call" | custom-call | tf_op jit(solution)/shard_map/finish_80/pallas_call | solution.py:401
Async XLA Ops:
  1.1 15.1 %collective-permute-start.3 = (bf16[1936,128]{1,0:T(8,128)(2,1)S(1)}, bf16[1936,128]{1,0:T(8,128)(2,1)S(1)}, u32[]{:S(2)}, u32[]{:S(2)}) collective-permute-start(bf16[1936,128]{1,0:T(8,128)(2,1)S(1)} %get-tuple-element.26.refs_0_), channel_id=1, source_target_pairs={{4,0},{0,4},{5,1},{1,5},{6,2},{2,6},{7,3},{3,7},{12,8},{8,12},{13,... | collective-permute-start | bytes 1486856 | tf_op jit(solution)/shard_map/ppermute | solution.py:41
  5.2 5.1 %collective-permute-start.1 = (bf16[528,128]{1,0:T(8,128)(2,1)S(1)}, bf16[528,128]{1,0:T(8,128)(2,1)S(1)}, u32[]{:S(2)}, u32[]{:S(2)}) collective-permute-start(bf16[528,128]{1,0:T(8,128)(2,1)S(1)} %get-tuple-element.31.refs_2_), channel_id=1, source_target_pairs={{0,16},{8,24},{16,0},{24,8},{1,17},{9,25},{17,1},{25,9},{2,18},{10... | collective-permute-start | bytes 405512 | tf_op jit(solution)/shard_map/ppermute | solution.py:27
  6.8 3.5 %collective-permute-start = (bf16[528,128]{1,0:T(8,128)(2,1)S(1)}, bf16[528,128]{1,0:T(8,128)(2,1)S(1)}, u32[]{:S(2)}, u32[]{:S(2)}) collective-permute-start(bf16[528,128]{1,0:T(8,128)(2,1)S(1)} %get-tuple-element.31.refs_2_), channel_id=1, source_target_pairs={{0,8},{8,0},{16,24},{24,16},{1,9},{9,1},{17,25},{25,17},{2,10},{10... | collective-permute-start | bytes 405512 | tf_op jit(solution)/shard_map/ppermute | solution.py:27
  10.4 1.4 %collective-permute-start.2 = (bf16[528,128]{1,0:T(8,128)(2,1)S(1)}, bf16[528,128]{1,0:T(8,128)(2,1)S(1)}, u32[]{:S(2)}, u32[]{:S(2)}) collective-permute-start(bf16[528,128]{1,0:T(8,128)(2,1)S(1)} %collective-permute-done.1.refs_4_), channel_id=1, source_target_pairs={{0,8},{8,0},{16,24},{24,16},{1,9},{9,1},{17,25},{25,17},{2,10},{10... | collective-permute-start | bytes 405512 | tf_op jit(solution)/shard_map/ppermute | solution.py:27
  11.7 10.1 %collective-permute-start.7 = (bf16[1152,128]{1,0:T(8,128)(2,1)S(1)}, bf16[1152,128]{1,0:T(8,128)(2,1)S(1)}, u32[]{:S(2)}, u32[]{:S(2)}) collective-permute-start(bf16[1152,128]{1,0:T(8,128)(2,1)S(1)} %get-tuple-element.40.refs_1_), channel_id=1, source_target_pairs={{4,0},{0,4},{5,1},{1,5},{6,2},{2,6},{7,3},{3,7},{12,8},{8,12},{13,... | collective-permute-start | bytes 884744 | tf_op jit(solution)/shard_map/ppermute | solution.py:41
  17.0 9.2 %collective-permute-start.4 = (s32[160,128]{1,0:T(8,128)S(1)}, s32[160,128]{1,0:T(8,128)S(1)}, u32[]{:S(2)}, u32[]{:S(2)}) collective-permute-start(s32[160,128]{1,0:T(8,128)S(1)} %get-tuple-element.36), channel_id=1, source_target_pairs={{0,2},{1,3},{2,0},{3,1},{4,6},{5,7},{6,4},{7,5},{8,10},{9,11},{10,... | collective-permute-start | bytes 245768 | tf_op jit(solution)/shard_map/ppermute | solution.py:27
  20.2 6.9 %collective-permute-start.5 = (s32[160,128]{1,0:T(8,128)S(1)}, s32[160,128]{1,0:T(8,128)S(1)}, u32[]{:S(2)}, u32[]{:S(2)}) collective-permute-start(s32[160,128]{1,0:T(8,128)S(1)} %get-tuple-element.37), channel_id=1, source_target_pairs={{0,3},{1,2},{2,1},{3,0},{4,7},{5,6},{6,5},{7,4},{8,11},{9,10},{10,... | collective-permute-start | bytes 245768 | tf_op jit(solution)/shard_map/ppermute | solution.py:27
  21.6 5.8 %collective-permute-start.6 = (s32[160,128]{1,0:T(8,128)S(1)}, s32[160,128]{1,0:T(8,128)S(1)}, u32[]{:S(2)}, u32[]{:S(2)}) collective-permute-start(s32[160,128]{1,0:T(8,128)S(1)} %get-tuple-element.38), channel_id=1, source_target_pairs={{0,1},{1,0},{2,3},{3,2},{4,5},{5,4},{6,7},{7,6},{8,9},{9,8},{10,11... | collective-permute-start | bytes 245768 | tf_op jit(solution)/shard_map/ppermute | solution.py:27
  22.3 6.7 %collective-permute-start.10 = (s32[96,128]{1,0:T(8,128)S(1)}, s32[96,128]{1,0:T(8,128)S(1)}, u32[]{:S(2)}, u32[]{:S(2)}) collective-permute-start(s32[96,128]{1,0:T(8,128)S(1)} %get-tuple-element.44), channel_id=1, source_target_pairs={{0,3},{1,2},{2,1},{3,0},{4,7},{5,6},{6,5},{7,4},{8,11},{9,10},{10,... | collective-permute-start | bytes 147464 | tf_op jit(solution)/shard_map/ppermute | solution.py:27
  26.2 5.0 %collective-permute-start.8 = (s32[96,128]{1,0:T(8,128)S(1)}, s32[96,128]{1,0:T(8,128)S(1)}, u32[]{:S(2)}, u32[]{:S(2)}) collective-permute-start(s32[96,128]{1,0:T(8,128)S(1)} %get-tuple-element.42), channel_id=1, source_target_pairs={{0,2},{1,3},{2,0},{3,1},{4,6},{5,7},{6,4},{7,5},{8,10},{9,11},{10,... | collective-permute-start | bytes 147464 | tf_op jit(solution)/shard_map/ppermute | solution.py:27
  26.2 5.0 %collective-permute-start.9 = (s32[96,128]{1,0:T(8,128)S(1)}, s32[96,128]{1,0:T(8,128)S(1)}, u32[]{:S(2)}, u32[]{:S(2)}) collective-permute-start(s32[96,128]{1,0:T(8,128)S(1)} %get-tuple-element.43), channel_id=1, source_target_pairs={{0,1},{1,0},{2,3},{3,2},{4,5},{5,4},{6,7},{7,6},{8,9},{9,8},{10,11... | collective-permute-start | bytes 147464 | tf_op jit(solution)/shard_map/ppermute | solution.py:27

commit v26 on v25

--- a/solution.py
+++ b/solution.py
@@ -362,7 +362,7 @@
     )(known, *x_sent, *s_pieces)
 
     moved = block_size * (8 * all_slots + 2 * panel_size + 2 * count * (cols - 1))
-    later, _ = lax.optimization_barrier((x_sent[1:], s_pieces))
+    later = x_sent[1:]
     x_pieces = [first_piece]
     x_pieces += [[shifted(part, "col", j) for j in range(1, cols)] for part in later]
 

time: 32.1 us -> 32.1 us (level)
    ppermute x9, waiting for transfers between devices: 9.1 us -> 8.56 us  [flipped(): lax.ppermute(value, axis, [(i, i ^ bits) for i in range(lax.axis_size(axi...]
where the time goes in v26:
time: 32.1 us; the launch traced here: 31.9 us
  starting transfers between devices  14.4 us (45%)
  waiting for transfers between devices  12.3 us (38%)
  Pallas kernels  5.08 us (16%)
    ppermute x9, starting transfers between devices, flipped(): lax.ppermute(value, axis, [(i, i ^ bits) for i in range(lax.axis_size(axi...  10.9 us
    ppermute x9, waiting for transfers between devices, flipped(): lax.ppermute(value, axis, [(i, i ^ bits) for i in range(lax.axis_size(axi...  8.56 us
    ppermute x2, waiting for transfers between devices, shifted(): lax.ppermute(value, axis, [((i + offset) % size, i) for i in range(size)])  3.77 us
    ppermute x2, starting transfers between devices, shifted(): lax.ppermute(value, axis, [((i + offset) % size, i) for i in range(size)])  3.54 us
    pallas_call x2, Pallas kernels, per_device(): pl.pallas_call(functools.partial(peer_kernel, (cols, layers, count, width...  1.22 us
    pallas_call x1, Pallas kernels, per_device(): pl.pallas_call(functools.partial(pack_first_kernel, (layers, count, piece...  1.11 us
    pallas_call x1, Pallas kernels, per_device(): pl.pallas_call(functools.partial(pack_later_kernel, (count, piece, order,...  1.11 us
    pallas_call x2, Pallas kernels, per_device(): pl.pallas_call(functools.partial(finish_kernel, (layers, slots), (at, hei...  0.86 us
  transfers between devices with their start and end apart: 11, of which 7 were waited for; matrix products, arithmetic and copies ran while one was open for 0% of the time, Pallas kernels for 10%

profile of v26, /device:TPU:0, one launch (start us, length us, event | category | flops | bytes accessed | tf_op | source)
XLA Modules:
  0.0 31.9 jit_solution(12220111050983357565)
XLA Ops:
  0.0 1.1 %pack_first.1 = (s32[16,128]{1,0:T(8,128)S(1)}, bf16[1936,128]{1,0:T(8,128)(2,1)S(1)}) custom-call(s32[1,24]{1,0:T(1,128)} %bitcast.6, s32[1,24]{1,0:T(1,128)} %bitcast.7, s32[2,8]{1,0:T(2,128)} %bitcast.5, bf16[24,128,128]{2,1,0:T(8,128)(2,1)} %x_in.2), custom_call_target="tpu_custom_call" | custom-call | tf_op jit(solution)/shard_map/pack_first/pallas_call | solution.py:295
  1.1 3.0 %collective-permute-start.3 = (bf16[1936,128]{1,0:T(8,128)(2,1)S(1)}, bf16[1936,128]{1,0:T(8,128)(2,1)S(1)}, u32[]{:S(2)}, u32[]{:S(2)}) collective-permute-start(bf16[1936,128]{1,0:T(8,128)(2,1)S(1)} %get-tuple-element.25.refs_0_), channel_id=1, source_target_pairs={{4,0},{0,4},{5,1},{1,5},{6,2},{2,6},{7,3},{3,7},{12,8},{8,12},{13,... | collective-permute-start | bytes 1486856 | tf_op jit(solution)/shard_map/ppermute | solution.py:41
  4.1 1.1 %pack_later.1 = (bf16[528,128]{1,0:T(8,128)(2,1)S(1)}, bf16[1152,128]{1,0:T(8,128)(2,1)S(1)}) custom-call(bf16[24,128,128]{2,1,0:T(8,128)(2,1)} %x_in.2, s32[2,2]{1,0:T(2,128)} %s_cols, bf16[4,128,128]{2,1,0:T(8,128)(2,1)} %bitcast.4), custom_call_target="tpu_custom_call" | custom-call | tf_op jit(solution)/shard_map/pack_later/pallas_call | solution.py:322
  5.2 1.6 %collective-permute-start.1 = (bf16[528,128]{1,0:T(8,128)(2,1)S(1)}, bf16[528,128]{1,0:T(8,128)(2,1)S(1)}, u32[]{:S(2)}, u32[]{:S(2)}) collective-permute-start(bf16[528,128]{1,0:T(8,128)(2,1)S(1)} %get-tuple-element.30.refs_2_), channel_id=1, source_target_pairs={{0,16},{8,24},{16,0},{24,8},{1,17},{9,25},{17,1},{25,9},{2,18},{10... | collective-permute-start | bytes 405512 | tf_op jit(solution)/shard_map/ppermute | solution.py:27
  6.8 0.5 %collective-permute-start.7 = (bf16[1152,128]{1,0:T(8,128)(2,1)S(1)}, bf16[1152,128]{1,0:T(8,128)(2,1)S(1)}, u32[]{:S(2)}, u32[]{:S(2)}) collective-permute-start(bf16[1152,128]{1,0:T(8,128)(2,1)S(1)} %get-tuple-element.29.refs_1_), channel_id=1, source_target_pairs={{4,0},{0,4},{5,1},{1,5},{6,2},{2,6},{7,3},{3,7},{12,8},{8,12},{13,... | collective-permute-start | bytes 884744 | tf_op jit(solution)/shard_map/ppermute | solution.py:41
  7.4 0.0 collective-permute-start
  7.4 3.0 %collective-permute-done.1.refs_4_ = bf16[528,128]{1,0:T(8,128)(2,1)S(1)} collective-permute-done((bf16[528,128]{1,0:T(8,128)(2,1)S(1)}, bf16[528,128]{1,0:T(8,128)(2,1)S(1)}, u32[]{:S(2)}, u32[]{:S(2)}) %collective-permute-start.1) | collective-permute-done | bytes 135200 | tf_op jit(solution)/shard_map/ppermute | solution.py:27
  10.4 0.0 collective-permute-start.2
  10.4 0.0 collective-permute-done.refs_3_
  10.4 1.3 %collective-permute-done.2.refs_5_ = bf16[528,128]{1,0:T(8,128)(2,1)S(1)} collective-permute-done((bf16[528,128]{1,0:T(8,128)(2,1)S(1)}, bf16[528,128]{1,0:T(8,128)(2,1)S(1)}, u32[]{:S(2)}, u32[]{:S(2)}) %collective-permute-start.2) | collective-permute-done | bytes 135200 | tf_op jit(solution)/shard_map/ppermute | solution.py:27
  11.7 0.8 %own_products.1 = (f32[17,128,128]{2,1,0:T(8,128)S(1)}, bf16[16,128,128]{2,1,0:T(8,128)(2,1)S(1)}, s32[8,128]{1,0:T(8,128)S(1)}) custom-call(s32[16,128]{1,0:T(8,128)S(1)} %get-tuple-element.24.known.refs_0_, bf16[1936,128]{1,0:T(8,128)(2,1)S(1)} %get-tuple-element.25.refs_0_, bf16[1152,128]{1,0:T(8,128)(2,1)S(1)} %get-tuple-element.29.refs_1_, ...), custom_call_target="tpu_custom_call" | custom-call | flops 50331648 | bytes 2883584 | tf_op jit(solution)/shard_map/own_products/pallas_call | solution.py:343
  12.5 3.8 %collective-permute-done.3.refs_2_ = bf16[1936,128]{1,0:T(8,128)(2,1)S(1)} collective-permute-done((bf16[1936,128]{1,0:T(8,128)(2,1)S(1)}, bf16[1936,128]{1,0:T(8,128)(2,1)S(1)}, u32[]{:S(2)}, u32[]{:S(2)}) %collective-permute-start.3) | collective-permute-done | bytes 495648 | tf_op jit(solution)/shard_map/ppermute | solution.py:41
  16.3 0.7 %peer_products_0.1 = (f32[4,80,128]{2,1,0:T(8,128)S(1)}, s32[160,128]{1,0:T(8,128)S(1)}, s32[160,128]{1,0:T(8,128)S(1)}, s32[160,128]{1,0:T(8,128)S(1)}, s32[1,8,128]{2,1,0:T(8,128)S(1)}) custom-call(s32[16,128]{1,0:T(8,128)S(1)} %get-tuple-element.24.known.refs_0_, s32[8,128]{1,0:T(8,128)S(1)} %get-tuple-element.31.refs_1_, ...), custom_call_target="tpu_custom_call" | custom-call | flops 31457280 | bytes 1703936 | tf_op jit(solution)/shard_map/peer_products_0/pallas_call | solution.py:380
  17.0 3.2 %collective-permute-start.4 = (s32[160,128]{1,0:T(8,128)S(1)}, s32[160,128]{1,0:T(8,128)S(1)}, u32[]{:S(2)}, u32[]{:S(2)}) collective-permute-start(s32[160,128]{1,0:T(8,128)S(1)} %get-tuple-element.35), channel_id=1, source_target_pairs={{0,2},{1,3},{2,0},{3,1},{4,6},{5,7},{6,4},{7,5},{8,10},{9,11},{10,... | collective-permute-start | bytes 245768 | tf_op jit(solution)/shard_map/ppermute | solution.py:27
  20.2 1.3 %collective-permute-start.5 = (s32[160,128]{1,0:T(8,128)S(1)}, s32[160,128]{1,0:T(8,128)S(1)}, u32[]{:S(2)}, u32[]{:S(2)}) collective-permute-start(s32[160,128]{1,0:T(8,128)S(1)} %get-tuple-element.36), channel_id=1, source_target_pairs={{0,3},{1,2},{2,1},{3,0},{4,7},{5,6},{6,5},{7,4},{8,11},{9,10},{10,... | collective-permute-start | bytes 245768 | tf_op jit(solution)/shard_map/ppermute | solution.py:27
  21.5 0.2 collective-permute-start.6
  21.8 0.0 collective-permute-done.7.refs_1_
  21.8 0.5 %peer_products_80.1 = (f32[4,48,128]{2,1,0:T(8,128)S(1)}, s32[96,128]{1,0:T(8,128)S(1)}, s32[96,128]{1,0:T(8,128)S(1)}, s32[96,128]{1,0:T(8,128)S(1)}) custom-call(s32[1,8,128]{2,1,0:T(8,128)S(1)} %get-tuple-element.38.refs_0_, bf16[1152,128]{1,0:T(8,128)(2,1)S(1)} %collective-permute-done.7.refs_1_, ...), custom_call_target="tpu_custom_call" | custom-call | flops 18874368 | bytes 1703936 | tf_op jit(solution)/shard_map/peer_products_80/pallas_call | solution.py:380
  22.3 3.9 %collective-permute-start.10 = (s32[96,128]{1,0:T(8,128)S(1)}, s32[96,128]{1,0:T(8,128)S(1)}, u32[]{:S(2)}, u32[]{:S(2)}) collective-permute-start(s32[96,128]{1,0:T(8,128)S(1)} %get-tuple-element.42), channel_id=1, source_target_pairs={{0,3},{1,2},{2,1},{3,0},{4,7},{5,6},{6,5},{7,4},{8,11},{9,10},{10,... | collective-permute-start | bytes 147464 | tf_op jit(solution)/shard_map/ppermute | solution.py:27
  26.2 0.0 collective-permute-start.8
  26.2 0.0 collective-permute-done.4.refs_1_
  26.2 0.6 %collective-permute-start.9 = (s32[96,128]{1,0:T(8,128)S(1)}, s32[96,128]{1,0:T(8,128)S(1)}, u32[]{:S(2)}, u32[]{:S(2)}) collective-permute-start(s32[96,128]{1,0:T(8,128)S(1)} %get-tuple-element.41), channel_id=1, source_target_pairs={{0,1},{1,0},{2,3},{3,2},{4,5},{5,4},{6,7},{7,6},{8,9},{9,8},{10,11... | collective-permute-start | bytes 147464 | tf_op jit(solution)/shard_map/ppermute | solution.py:27
  26.8 0.3 collective-permute-done.5.refs_2_
  27.1 0.3 collective-permute-done.6.refs_3_
  27.4 0.1 finish_0.1.refs_0_
  27.5 1.4 %collective-permute-done.10.refs_4_ = s32[96,128]{1,0:T(8,128)S(1)} collective-permute-done((s32[96,128]{1,0:T(8,128)S(1)}, s32[96,128]{1,0:T(8,128)S(1)}, u32[]{:S(2)}, u32[]{:S(2)}) %collective-permute-start.10) | collective-permute-done | bytes 49184 | tf_op jit(solution)/shard_map/ppermute | solution.py:27
  29.0 2.2 %collective-permute-done.8.refs_2_ = s32[96,128]{1,0:T(8,128)S(1)} collective-permute-done((s32[96,128]{1,0:T(8,128)S(1)}, s32[96,128]{1,0:T(8,128)S(1)}, u32[]{:S(2)}, u32[]{:S(2)}) %collective-permute-start.8) | collective-permute-done | bytes 49184 | tf_op jit(solution)/shard_map/ppermute | solution.py:27
  31.2 0.0 collective-permute-done.9.refs_3_
  31.2 0.7 %finish_80.1 = bf16[2,2,128,128]{3,2,1,0:T(8,128)(2,1)} custom-call(bf16[2,2,80,128]{3,2,1,0:T(8,128)(2,1)S(1)} %finish_0.1.refs_0_, f32[4,48,128]{2,1,0:T(8,128)S(1)} %get-tuple-element.39.refs_1_, s32[96,128]{1,0:T(8,128)S(1)} %collective-permute-done.8.refs_2_, s32[96,128]{1,0:T(8,128)S(1)} %collective-permute-done.9.refs_3_, ...), custom_call_target="tpu_custom_call" | custom-call | tf_op jit(solution)/shard_map/finish_80/pallas_call | solution.py:401
Async XLA Ops:
  1.1 15.1 %collective-permute-start.3 = (bf16[1936,128]{1,0:T(8,128)(2,1)S(1)}, bf16[1936,128]{1,0:T(8,128)(2,1)S(1)}, u32[]{:S(2)}, u32[]{:S(2)}) collective-permute-start(bf16[1936,128]{1,0:T(8,128)(2,1)S(1)} %get-tuple-element.25.refs_0_), channel_id=1, source_target_pairs={{4,0},{0,4},{5,1},{1,5},{6,2},{2,6},{7,3},{3,7},{12,8},{8,12},{13,... | collective-permute-start | bytes 1486856 | tf_op jit(solution)/shard_map/ppermute | solution.py:41
  5.2 5.1 %collective-permute-start.1 = (bf16[528,128]{1,0:T(8,128)(2,1)S(1)}, bf16[528,128]{1,0:T(8,128)(2,1)S(1)}, u32[]{:S(2)}, u32[]{:S(2)}) collective-permute-start(bf16[528,128]{1,0:T(8,128)(2,1)S(1)} %get-tuple-element.30.refs_2_), channel_id=1, source_target_pairs={{0,16},{8,24},{16,0},{24,8},{1,17},{9,25},{17,1},{25,9},{2,18},{10... | collective-permute-start | bytes 405512 | tf_op jit(solution)/shard_map/ppermute | solution.py:27
  6.8 15.0 %collective-permute-start.7 = (bf16[1152,128]{1,0:T(8,128)(2,1)S(1)}, bf16[1152,128]{1,0:T(8,128)(2,1)S(1)}, u32[]{:S(2)}, u32[]{:S(2)}) collective-permute-start(bf16[1152,128]{1,0:T(8,128)(2,1)S(1)} %get-tuple-element.29.refs_1_), channel_id=1, source_target_pairs={{4,0},{0,4},{5,1},{1,5},{6,2},{2,6},{7,3},{3,7},{12,8},{8,12},{13,... | collective-permute-start | bytes 884744 | tf_op jit(solution)/shard_map/ppermute | solution.py:41
  7.4 3.0 %collective-permute-start = (bf16[528,128]{1,0:T(8,128)(2,1)S(1)}, bf16[528,128]{1,0:T(8,128)(2,1)S(1)}, u32[]{:S(2)}, u32[]{:S(2)}) collective-permute-start(bf16[528,128]{1,0:T(8,128)(2,1)S(1)} %get-tuple-element.30.refs_2_), channel_id=1, source_target_pairs={{0,8},{8,0},{16,24},{24,16},{1,9},{9,1},{17,25},{25,17},{2,10},{10... | collective-permute-start | bytes 405512 | tf_op jit(solution)/shard_map/ppermute | solution.py:27
  10.4 1.4 %collective-permute-start.2 = (bf16[528,128]{1,0:T(8,128)(2,1)S(1)}, bf16[528,128]{1,0:T(8,128)(2,1)S(1)}, u32[]{:S(2)}, u32[]{:S(2)}) collective-permute-start(bf16[528,128]{1,0:T(8,128)(2,1)S(1)} %collective-permute-done.1.refs_4_), channel_id=1, source_target_pairs={{0,8},{8,0},{16,24},{24,16},{1,9},{9,1},{17,25},{25,17},{2,10},{10... | collective-permute-start | bytes 405512 | tf_op jit(solution)/shard_map/ppermute | solution.py:27
  17.0 9.2 %collective-permute-start.4 = (s32[160,128]{1,0:T(8,128)S(1)}, s32[160,128]{1,0:T(8,128)S(1)}, u32[]{:S(2)}, u32[]{:S(2)}) collective-permute-start(s32[160,128]{1,0:T(8,128)S(1)} %get-tuple-element.35), channel_id=1, source_target_pairs={{0,2},{1,3},{2,0},{3,1},{4,6},{5,7},{6,4},{7,5},{8,10},{9,11},{10,... | collective-permute-start | bytes 245768 | tf_op jit(solution)/shard_map/ppermute | solution.py:27
  20.2 6.9 %collective-permute-start.5 = (s32[160,128]{1,0:T(8,128)S(1)}, s32[160,128]{1,0:T(8,128)S(1)}, u32[]{:S(2)}, u32[]{:S(2)}) collective-permute-start(s32[160,128]{1,0:T(8,128)S(1)} %get-tuple-element.36), channel_id=1, source_target_pairs={{0,3},{1,2},{2,1},{3,0},{4,7},{5,6},{6,5},{7,4},{8,11},{9,10},{10,... | collective-permute-start | bytes 245768 | tf_op jit(solution)/shard_map/ppermute | solution.py:27
  21.5 5.8 %collective-permute-start.6 = (s32[160,128]{1,0:T(8,128)S(1)}, s32[160,128]{1,0:T(8,128)S(1)}, u32[]{:S(2)}, u32[]{:S(2)}) collective-permute-start(s32[160,128]{1,0:T(8,128)S(1)} %get-tuple-element.37), channel_id=1, source_target_pairs={{0,1},{1,0},{2,3},{3,2},{4,5},{5,4},{6,7},{7,6},{8,9},{9,8},{10,11... | collective-permute-start | bytes 245768 | tf_op jit(solution)/shard_map/ppermute | solution.py:27
  22.3 6.7 %collective-permute-start.10 = (s32[96,128]{1,0:T(8,128)S(1)}, s32[96,128]{1,0:T(8,128)S(1)}, u32[]{:S(2)}, u32[]{:S(2)}) collective-permute-start(s32[96,128]{1,0:T(8,128)S(1)} %get-tuple-element.42), channel_id=1, source_target_pairs={{0,3},{1,2},{2,1},{3,0},{4,7},{5,6},{6,5},{7,4},{8,11},{9,10},{10,... | collective-permute-start | bytes 147464 | tf_op jit(solution)/shard_map/ppermute | solution.py:27
  26.2 5.0 %collective-permute-start.8 = (s32[96,128]{1,0:T(8,128)S(1)}, s32[96,128]{1,0:T(8,128)S(1)}, u32[]{:S(2)}, u32[]{:S(2)}) collective-permute-start(s32[96,128]{1,0:T(8,128)S(1)} %get-tuple-element.40), channel_id=1, source_target_pairs={{0,2},{1,3},{2,0},{3,1},{4,6},{5,7},{6,4},{7,5},{8,10},{9,11},{10,... | collective-permute-start | bytes 147464 | tf_op jit(solution)/shard_map/ppermute | solution.py:27
  26.2 5.0 %collective-permute-start.9 = (s32[96,128]{1,0:T(8,128)S(1)}, s32[96,128]{1,0:T(8,128)S(1)}, u32[]{:S(2)}, u32[]{:S(2)}) collective-permute-start(s32[96,128]{1,0:T(8,128)S(1)} %get-tuple-element.41), channel_id=1, source_target_pairs={{0,1},{1,0},{2,3},{3,2},{4,5},{5,4},{6,7},{7,6},{8,9},{9,8},{10,11... | collective-permute-start | bytes 147464 | tf_op jit(solution)/shard_map/ppermute | solution.py:27
